TPU v7x, 128 devices: a whole 4x4x4 slice. The times are simulated.
128 devices in a mesh: tm: 4 (over x_hi, core), space: 32 (over z, y, x_lo).
Axes of the slice: x: 4 (x_hi: 2, x_lo: 2; x = x_hi * 2 + x_lo), y: 4, z: 4, core: 2. Of those that a mesh axis runs over, the one named last changes fastest.
Arguments:
- inv_local: float32 [4, 2048, 2048], P('tm', 'space'), as said below
- coupling: float32 [4, 2048, 2048], P('tm', 'space')
- tail_block: float32 [2048, 2048], P('space'), as said below
- adjacency: int32 [16, 16], replicated, may hold values 0 or 1
Outputs:
- sel_diag: float32 [4, 2048, 2048], P('tm', 'space')
- sel_off: float32 [4, 2048, 2048], P('tm', 'space')
Inputs may be any that keep to these rules, and one draw needn't show every extreme that they name: Every block inv_local[t] is symmetric. tail_block is symmetric.
All inputs are finite; a program needn't handle non-finite values.
Results may differ from a plain program's by a relative error of at most 0.00011.
Values sent between devices are 32-bit elements; how exact they have to be, the bound alone decides.
No kernel may reach another device: no remote copies, remote signals or barrier semaphores. Data moves between devices by JAX's collectives and lax.ppermute only.
A program may use at most 192 MiB of HBM per device.

v0:
```python
import jax
import jax.numpy as jnp
from jax import lax
from jax.sharding import PartitionSpec as P

TILE = 128


def passed_along(x, axis, by):
    length = lax.axis_size(axis)
    pairs = [(i, i + by) for i in range(length) if 0 <= i + by < length]
    return lax.ppermute(x, axis, pairs)


def panel_mask(adjacency, first_row, panel_rows, width):
    count = adjacency.shape[0]
    joined = jnp.maximum(adjacency, jnp.eye(count, dtype=jnp.int32)).astype(jnp.float32)
    row_tiles = (first_row + jnp.arange(panel_rows, dtype=jnp.int32)) // TILE
    row_onehot = (row_tiles[:, None] == jnp.arange(count, dtype=jnp.int32)[None, :]).astype(
        jnp.float32
    )
    col_onehot = (
        jnp.arange(count, dtype=jnp.int32)[:, None]
        == (jnp.arange(width, dtype=jnp.int32) // TILE)[None, :]
    ).astype(jnp.float32)
    return jnp.dot(jnp.dot(row_onehot, joined), col_onehot)


def on_device(inv_local, coupling, tail_block, adjacency):
    highest = lax.Precision.HIGHEST
    panel_rows = coupling.shape[1]
    width = coupling.shape[2]
    level_count = lax.axis_size("tm").bit_length() - 1
    time_index = lax.axis_index("tm")
    first_row = lax.axis_index("space") * panel_rows
    at_end = time_index == lax.axis_size("tm") - 1
    accumulated = inv_local[0]
    composed = coupling[0]
    coupling_whole = composed
    for level in range(level_count + 1):
        gathered = lax.all_gather(composed, "space", axis=0, tiled=True)
        if level == 0:
            coupling_whole = gathered
        if level < level_count:
            far_accum, far_factor = passed_along((accumulated, composed), "tm", -(1 << level))
            far_accum = jnp.where(
                time_index + (1 << level) >= lax.axis_size("tm"), tail_block, far_accum
            )
        else:
            far_accum = tail_block
            far_factor = composed
        half_product = jnp.dot(far_accum, gathered, precision=highest)
        turned = lax.all_to_all(half_product, "space", split_axis=1, concat_axis=0, tiled=True)
        quadratic = jnp.dot(turned.T, gathered, precision=highest)
        if level < level_count:
            composed = jnp.dot(far_factor, gathered, precision=highest)
        accumulated = accumulated + quadratic
    following = passed_along(accumulated, "tm", -1)
    following = jnp.where(at_end, tail_block, following)
    cross = jnp.dot(following, coupling_whole, precision=highest)
    tile_mask = panel_mask(adjacency, first_row, panel_rows, width)
    return ((accumulated * tile_mask)[None], (-cross * tile_mask)[None])


def solution(mesh):
    return jax.shard_map(
        on_device,
        mesh=mesh,
        in_specs=(P("tm", "space", None), P("tm", "space", None), P("space", None), P()),
        out_specs=(P("tm", "space", None), P("tm", "space", None)),
        check_vma=False,
    )
```

profile of v0, /device:TPU:6, one launch (start us, length us, event | category | flops | bytes accessed | tf_op | source)
XLA Modules:
  0.0 1238.6 jit_solution(2466708067767663378)
XLA Ops:
  7.2 0.0 all-gather.9.cloned.1.call-start
  7.2 0.7 all-gather.9.cloned.1.call-update
  7.9 0.0 all-gather.5.cloned.1.call-start
  7.9 0.0 copy-start.1
  8.0 0.0 copy-start
  8.0 2.9 collective-permute-start.2
  10.9 7.0 collective-permute-done.2
  17.8 354.8 %all-gather.9.cloned.1.call-done = f32[1,2048,2048]{2,1,0:T(8,128)} async-done(((f32[1,64,2048]{2,1,0:T(8,128)}), f32[1,2048,2048]{2,1,0:T(8,128)}) %all-gather.9.cloned.1.call-update) | async-done | bytes 16777232 | tf_op jit(solution)/shard_map/all_gather | solution.py:41
  372.6 14.5 %fusion.2 = f32[64,2048]{1,0:T(8,128)} fusion(f32[64,2048]{1,0:T(8,128)S(1)} %collective-permute-done.2, f32[1,2048,2048]{2,1,0:T(8,128)} %all-gather.9.cloned.1.call-done), kind=kOutput, calls=%fused_computation.2 | convolution fusion | flops 3221225472 | bytes 17825792 | tf_op jit(solution)/shard_map/dot_general | solution.py:56
  387.1 0.0 all-gather.5.cloned.1.call-update
  387.1 0.0 all-gather.7.cloned.1.call-start
  387.2 3.1 collective-permute-start.3
  390.3 17.6 %collective-permute-done.3 = f32[64,2048]{1,0:T(8,128)S(1)} collective-permute-done((f32[64,2048]{1,0:T(8,128)}, f32[64,2048]{1,0:T(8,128)S(1)}, u32[]{:S(2)}, u32[]{:S(2)}) %collective-permute-start.3) | collective-permute-done | bytes 524320 | tf_op jit(solution)/shard_map/ppermute | solution.py:12
  407.9 345.9 %all-gather.5.cloned.1.call-done = f32[2048,2048]{1,0:T(8,128)} async-done(((f32[64,2048]{1,0:T(8,128)}), f32[2048,2048]{1,0:T(8,128)}) %all-gather.5.cloned.1.call-update) | async-done | bytes 16777232 | tf_op jit(solution)/shard_map/all_gather | solution.py:41
  753.7 14.5 %fusion.42 = f32[64,2048]{1,0:T(8,128)} fusion(f32[64,2048]{1,0:T(8,128)S(1)} %collective-permute-done.3, f32[2048,2048]{1,0:T(8,128)} %all-gather.5.cloned.1.call-done), kind=kOutput, calls=%fused_computation.47 | convolution fusion | flops 3221225472 | bytes 17825792 | tf_op jit(solution)/shard_map/dot_general | solution.py:56
  768.2 0.0 all-gather.7.cloned.1.call-update
  768.3 0.0 copy-done.1
  768.3 2.1 collective-permute-start
  770.4 6.5 collective-permute-done
  776.9 0.0 copy-done
  776.9 29.0 %fusion.6 = f32[64,2048]{0,1:T(8,128)S(1)} fusion(f32[1,2048,2048]{2,1,0:T(8,128)} %all-gather.9.cloned.1.call-done, f32[64,2048]{1,0:T(8,128)S(1)} %copy-done, f32[64,2048]{1,0:T(8,128)S(1)} %collective-permute-done, pred[]{:T(512)S(6)} %ge.6), kind=kOutput, calls=%fused_computation.6 | convolution fusion | flops 3221356544 | bytes 18350080 | tf_op jit(solution)/shard_map/all_to_all | solution.py:53
  805.8 0.7 reshape.46
  806.5 24.8 %all_to_all.57 = f32[32,1,4096]{2,1,0:T(1,128)S(1)} all-to-all(f32[32,1,4096]{2,1,0:T(1,128)S(1)} %reshape.46), channel_id=1, replica_groups=mesh['tm'=4,'space'=32] {'space'}, dimensions={0} | all-to-all | bytes 1048576 | tf_op jit(solution)/shard_map/all_to_all | solution.py:53
  831.3 0.5 broadcast.75
  831.8 1.8 reduce
  833.6 0.4 reshape.47
  834.1 0.1 bitcast_bitcast_fusion.2
  834.1 0.6 copy.10
  834.8 0.4 all_to_all.45
  835.1 13.8 %fusion.17 = f32[64,2048]{1,0:T(8,128)S(1)} fusion(f32[2048,64]{0,1:T(8,128)S(1)} %all_to_all.45, f32[1,2048,2048]{2,1,0:T(8,128)} %all-gather.9.cloned.1.call-done, f32[1,64,2048]{2,1,0:T(8,128)S(1)} %copy-done.1), kind=kOutput, calls=%fused_computation.14 | convolution fusion | flops 3221356544 | bytes 18350080 | tf_op jit(solution)/shard_map/dot_general | solution.py:54
  849.0 1.6 collective-permute-start.1
  850.6 22.7 %collective-permute-done.1 = f32[64,2048]{1,0:T(8,128)S(1)} collective-permute-done((f32[64,2048]{1,0:T(8,128)S(1)}, f32[64,2048]{1,0:T(8,128)S(1)}, u32[]{:S(2)}, u32[]{:S(2)}) %collective-permute-start.1) | collective-permute-done | bytes 524320 | tf_op jit(solution)/shard_map/ppermute | solution.py:12
  873.3 28.9 %fusion.24 = f32[64,2048]{0,1:T(8,128)S(1)} fusion(f32[2048,2048]{1,0:T(8,128)} %all-gather.5.cloned.1.call-done, f32[64,2048]{1,0:T(8,128)S(1)} %copy-done, f32[64,2048]{1,0:T(8,128)S(1)} %collective-permute-done.1, pred[]{:T(512)S(6)} %ge.7), kind=kOutput, calls=%fused_computation.19 | convolution fusion | flops 3221356544 | bytes 18350080 | tf_op jit(solution)/shard_map/all_to_all | solution.py:53
  902.1 1.4 reshape.48
  903.6 6.1 all-to-all-start.1
  909.7 17.6 %all-to-all-done.1 = f32[32,1,4096]{2,1,0:T(1,128)S(1)} async-done(((f32[32,1,4096]{2,1,0:T(1,128)}), f32[32,1,4096]{2,1,0:T(1,128)S(1)}, u32[]{:S(2)}, u32[]{:S(2)}) %all-to-all-start.1) | async-done | bytes 524320 | tf_op jit(solution)/shard_map/all_to_all | solution.py:53
  927.3 1.8 reduce.1
  929.2 0.4 reshape.49
  929.6 0.1 bitcast_bitcast_fusion.1
  929.7 0.6 copy.12
  930.3 0.4 all_to_all.49
  930.6 222.4 %all-gather.7.cloned.1.call-done = f32[2048,2048]{1,0:T(8,128)} async-done(((f32[64,2048]{1,0:T(8,128)}), f32[2048,2048]{1,0:T(8,128)}) %all-gather.7.cloned.1.call-update) | async-done | bytes 16777232 | tf_op jit(solution)/shard_map/all_gather | solution.py:41
  1153.0 14.4 %convolution_bitcast_fusion = f32[64,2048]{1,0:T(8,128)S(1)} fusion(f32[2048,2048]{1,0:T(8,128)} %all-gather.7.cloned.1.call-done, f32[64,2048]{1,0:T(8,128)S(1)} %copy-done), kind=kOutput, calls=%fused_computation.9 | convolution fusion | flops 3221225472 | bytes 17825792 | tf_op jit(solution)/shard_map/dot_general | solution.py:52
  1167.4 0.3 copy.17
  1167.7 1.5 reshape.50
  1169.2 8.5 all-to-all-start.2
  1177.7 13.8 %convolution_add_fusion.1 = f32[64,2048]{1,0:T(8,128)S(1)} fusion(f32[64,2048]{1,0:T(8,128)S(1)} %fusion.17, f32[2048,64]{0,1:T(8,128)S(1)} %all_to_all.49, f32[2048,2048]{1,0:T(8,128)} %all-gather.5.cloned.1.call-done), kind=kOutput, calls=%fused_computation.11 | convolution fusion | flops 3221356544 | bytes 18350080 | tf_op jit(solution)/shard_map/dot_general | solution.py:54
  1191.5 0.0 copy-start.2
  1191.5 0.0 all-to-all-done.2
  1191.5 1.8 reduce.2
  1193.4 0.4 reshape.51
  1193.8 0.1 bitcast_bitcast_fusion
  1193.9 0.6 copy.14
  1194.5 0.4 all_to_all.53
  1194.8 13.8 %convolution_add_fusion = f32[64,2048]{1,0:T(8,128)S(1)} fusion(f32[64,2048]{1,0:T(8,128)S(1)} %convolution_add_fusion.1, f32[2048,64]{0,1:T(8,128)S(1)} %all_to_all.53, f32[2048,2048]{1,0:T(8,128)} %all-gather.7.cloned.1.call-done), kind=kOutput, calls=%fused_computation.10 | convolution fusion | flops 3221356544 | bytes 18350080 | tf_op jit(solution)/shard_map/dot_general | solution.py:54
  1208.7 2.1 collective-permute-start.4
  1210.8 0.0 copy-done.2
  1210.8 0.5 fusion.20
  1211.3 0.9 multiply_bitcast_fusion
  1212.1 5.1 collective-permute-done.4
  1217.3 14.5 %fusion.14 = f32[1,64,2048]{2,1,0:T(8,128)} fusion(f32[64,2048]{1,0:T(8,128)S(1)} %fusion.20, f32[1,2048,2048]{2,1,0:T(8,128)} %all-gather.9.cloned.1.call-done, f32[64,2048]{1,0:T(8,128)S(1)} %copy-done, f32[64,2048]{1,0:T(8,128)S(1)} %collective-permute-done.4, pred[]{:T(512)S(6)} %eq.39), kind=kOutput, calls=%fused_computation.13 | convolution fusion | flops 3221618688 | bytes 18874368 | tf_op jit(solution)/shard_map/dot_general | solution.py:60
  (2 shorter events, 0.0 us)
Async XLA Ops:
  7.2 365.5 %all-gather.9.cloned.1.call-start = ((), (), s32[]{:S(2)}) async-start(), calls=%async_computation.5 | async-start | bytes 17301504 | tf_op jit(solution)/shard_map/all_gather | solution.py:41
  7.9 745.8 %all-gather.5.cloned.1.call-start = ((), (), s32[]{:S(2)}) async-start(), calls=%async_computation.3 | async-start | bytes 17301504 | tf_op jit(solution)/shard_map/all_gather | solution.py:41
  7.9 760.3 %copy-start.1 = (f32[1,64,2048]{2,1,0:T(8,128)S(1)}, f32[1,64,2048]{2,1,0:T(8,128)}, u32[]{:S(2)}) copy-start(f32[1,64,2048]{2,1,0:T(8,128)} %param.4) | copy-start | bytes 1572868
  8.0 768.9 %copy-start = (f32[64,2048]{1,0:T(8,128)S(1)}, f32[64,2048]{1,0:T(8,128)}, u32[]{:S(2)}) copy-start(f32[64,2048]{1,0:T(8,128)} %param.6) | copy-start | bytes 1572868
  8.0 9.9 collective-permute-start.2
  387.1 765.9 %all-gather.7.cloned.1.call-start = ((), (), s32[]{:S(2)}) async-start(), calls=%async_computation.4 | async-start | bytes 17301504 | tf_op jit(solution)/shard_map/all_gather | solution.py:41
  387.2 20.7 %collective-permute-start.3 = (f32[64,2048]{1,0:T(8,128)}, f32[64,2048]{1,0:T(8,128)S(1)}, u32[]{:S(2)}, u32[]{:S(2)}) collective-permute-start(f32[64,2048]{1,0:T(8,128)} %fusion.2), channel_id=1, source_target_pairs={{64,0},{96,32},{65,1},{97,33},{66,2},{98,34},{67,3},{99,35},{68,4}... | collective-permute-start | bytes 1572872 | tf_op jit(solution)/shard_map/ppermute | solution.py:12
  768.3 8.6 collective-permute-start
  849.0 24.3 %collective-permute-start.1 = (f32[64,2048]{1,0:T(8,128)S(1)}, f32[64,2048]{1,0:T(8,128)S(1)}, u32[]{:S(2)}, u32[]{:S(2)}) collective-permute-start(f32[64,2048]{1,0:T(8,128)S(1)} %fusion.17), channel_id=1, source_target_pairs={{64,0},{96,32},{65,1},{97,33},{66,2},{98,34},{67,3},{99,35},{68,4}... | collective-permute-start | bytes 1572872 | tf_op jit(solution)/shard_map/ppermute | solution.py:12
  903.6 23.7 %all-to-all-start.1 = ((f32[32,1,4096]{2,1,0:T(1,128)}), f32[32,1,4096]{2,1,0:T(1,128)S(1)}, u32[]{:S(2)}, u32[]{:S(2)}) async-start(f32[32,1,4096]{2,1,0:T(1,128)} %reshape.48), calls=%async_computation.1 | async-start | bytes 1048576 | tf_op jit(solution)/shard_map/all_to_all | solution.py:53
  1169.2 22.3 %all-to-all-start.2 = ((f32[32,1,4096]{2,1,0:T(1,128)}), f32[32,1,4096]{2,1,0:T(1,128)S(1)}, u32[]{:S(2)}, u32[]{:S(2)}) async-start(f32[32,1,4096]{2,1,0:T(1,128)} %reshape.50), calls=%async_computation.2 | async-start | bytes 1048576 | tf_op jit(solution)/shard_map/all_to_all | solution.py:53
  1191.5 19.3 %copy-start.2 = (s32[16,16]{1,0:T(8,128)S(1)}, s32[16,16]{1,0:T(8,128)}, u32[]{:S(2)}) copy-start(s32[16,16]{1,0:T(8,128)} %param.7) | copy-start | bytes 3076
  1208.7 8.6 collective-permute-start.4
Sparse Core Ops, SparseCore 0:
  9.6 362.9 all-gather.8
  387.3 366.4 all-gather.4
  768.4 384.6 all-gather.6
where the time goes:
time: 1250 us; the launch traced here: 1240 us
  waiting for transfers between devices  1000 us (80%)
  matrix products  158 us (13%)
  starting transfers between devices  26.5 us (2%)
  blocking collectives  24.8 us (2%)
  between operations  14.3 us (1%)
    all_gather x3, waiting for transfers between devices, on_device(): gathered = lax.all_gather(composed, 'space', axis=0, tiled=True)  923 us
    ppermute x5, waiting for transfers between devices, passed_along(): return lax.ppermute(x, axis, pairs)  58.9 us
    all_to_all x2, matrix products, on_device(): lax.all_to_all(half_product, 'space', split_axis=1, concat_axis=0, tiled=...  57.8 us
    dot_general x3, matrix products, on_device(): quadratic = jnp.dot(turned.T, gathered, precision=highest)  41.5 us
    dot_general x2, matrix products, on_device(): composed = jnp.dot(far_factor, gathered, precision=highest)  29 us
  transfers between devices with their start and end apart: 10, of which 9 were waited for; matrix products, arithmetic and copies ran while one was open for 8% of the time, Pallas kernels for 0%

commit v1 on v0

v1 whole, which is shorter than its diff:
```python
import functools

import jax
import jax.numpy as jnp
import numpy as np
from jax import lax
from jax.experimental import pallas as pl
from jax.experimental.pallas import tpu as pltpu
from jax.sharding import Mesh, PartitionSpec as P

TILE = 128
AXES = ("xh", "co", "z", "y", "xl")
SIZES = (2, 2, 4, 4, 2)


def route(place):
    pairs = []
    for i in range(int(np.prod(SIZES))):
        xh, co, z, y, xl = (int(v) for v in np.unravel_index(i, SIZES))
        at = place(x=2 * xh + xl, y=y, z=z, co=co, t=2 * xh + co, xl=xl)
        to = (at["x"] // 2, at["co"], at["z"], at["y"], at["x"] % 2)
        pairs.append((i, int(np.ravel_multi_index(to, SIZES))))
    assert len({b for _, b in pairs}) == len(pairs)
    return pairs


def send(x, place):
    return lax.ppermute(x, AXES, route(place))


def shifted(axis, by):
    def place(**at):
        return {**at, axis: (at[axis] + by) % 4}

    return place


def to_other_core(**at):
    return {**at, "co": 1 - at["co"]}


def panel_route(by):
    def place(x, y, z, co, t, xl):
        j = (t - y - by) % 4
        return dict(x=j, y=y, z=z, co=xl) if t % 2 else dict(x=y, y=j, z=z, co=xl)

    return place


def lower_route(by):
    def place(x, y, z, co, t, xl):
        v = (t - by) % 4
        return dict(x=y, y=z, z=v, co=xl) if t % 2 else dict(x=z, y=y, z=v, co=xl)

    return place


def tail_route(x, y, z, co, t, xl):
    return dict(x=y, y=t, z=z, co=xl)


def diag_out_route(by):
    def place(x, y, z, co, t, xl):
        step = (x + y + by) % 4
        q = y if step % 2 else x
        return dict(x=2 * (step // 2) + co, co=step % 2, z=z, y=q)

    return place


def off_out_route(by):
    def place(x, y, z, co, t, xl):
        step = (x + y + by) % 4
        b = y if step % 2 else x
        return dict(x=2 * (step // 2) + co, co=step % 2, z=b, y=z)

    return place


def gathered(x, axis):
    return [x] + [send(x, shifted(axis, -r)) for r in (1, 2, 3)]


def scattered(parts, axis):
    total = parts[0]
    for r in (1, 2, 3):
        total = total + send(parts[r], shifted(axis, r))
    return total


def split(x):
    hi = x.astype(jnp.bfloat16)
    lo = (x - hi.astype(jnp.float32)).astype(jnp.bfloat16)
    return hi, lo


def dot_cols(a, b):
    dims = (((0,), (0,)), ((), ()))
    mm = functools.partial(
        lax.dot_general, dimension_numbers=dims, preferred_element_type=jnp.float32
    )
    a_hi, a_lo = split(a)
    b_hi, b_lo = split(b)
    return mm(a_hi, b_hi) + (mm(a_hi, b_lo) + mm(a_lo, b_hi))


def first_kernel(at, t_own, t_sib, a_own, a_sib, o0, o1, o2, o3, y):
    p = at[0]
    y[...] = dot_cols(t_own[...], a_own[...]) + dot_cols(t_sib[...], a_sib[...])
    for r, o in enumerate((o0, o1, o2, o3)):
        rows = pl.multiple_of(lax.rem(p + r, 4) * 128, 128)
        o[...] = y[pl.ds(rows, 128), :]


def cross_kernel(at, x_own, x_sib, a_own, a_sib, o0, o1, o2, o3, a, y):
    p, c, q = at[0], at[1], at[2]
    for r in range(4):
        src = pl.multiple_of(lax.rem(q + r, 4) * 64, 64)
        for ref, half in ((a_own, c), (a_sib, 1 - c)):
            rows = pl.multiple_of(128 * r + 64 * half, 64)
            a[pl.ds(rows, 64), :] = ref[pl.ds(src, 64), :]
    for ref, half in ((x_own, c), (x_sib, 1 - c)):
        rows = pl.multiple_of(256 * half, 256)
        y[pl.ds(rows, 256), :] = dot_cols(ref[...], a[...])
    for r, o in enumerate((o0, o1, o2, o3)):
        rows = pl.multiple_of(lax.rem(p + r, 4) * 128, 128)
        o[...] = y[pl.ds(rows, 128), :]


def close_kernel(at, y0, y1, y2, y3, b_own, b_sib, o0, o1, o2, o3, b, y, x):
    p, c, q = at[0], at[1], at[2]
    for r, piece in enumerate((y0, y1, y2, y3)):
        y[pl.ds(128 * r, 128), :] = piece[...]
        src = pl.multiple_of(lax.rem(p + r, 4) * 64, 64)
        for ref, half in ((b_own, c), (b_sib, 1 - c)):
            rows = pl.multiple_of(128 * r + 64 * half, 64)
            b[pl.ds(rows, 64), :] = ref[pl.ds(src, 64), :]
    x[...] = dot_cols(b[...], y[...])
    for r, o in enumerate((o0, o1, o2, o3)):
        rows = pl.multiple_of(lax.rem(q + r, 4) * 128, 128)
        o[...] = x[pl.ds(rows, 128), :]


def call(kernel, at, args, scratch):
    vmem = pl.BlockSpec(memory_space=pltpu.VMEM)
    return pl.pallas_call(
        kernel,
        out_shape=[jax.ShapeDtypeStruct((128, 256), jnp.float32)] * 4,
        in_specs=[pl.BlockSpec(memory_space=pltpu.SMEM)] + [vmem] * len(args),
        out_specs=[vmem] * 4,
        scratch_shapes=[pltpu.VMEM(s, jnp.float32) for s in scratch],
        compiler_params=pltpu.CompilerParams(vmem_limit_bytes=24 * 1024 * 1024),
        cost_estimate=pl.CostEstimate(
            flops=6 * 512 * 512 * 256, bytes_accessed=2 << 20, transcendentals=0
        ),
    )(at, *args)


def on_device(inv_local, coupling, tail_block, adjacency):
    xh, co, z, y, xl = (lax.axis_index(a) for a in AXES)
    x = 2 * xh + xl
    t_own = 2 * xh + co
    local, factor, tail = inv_local[0], coupling[0], tail_block
    spot = {"x": x, "y": y, "z": z}

    def block(a, j):
        return lax.dynamic_slice(a, (0, 512 * j), (64, 512))

    def half(a, h):
        return jnp.where(h == 0, a[..., :256], a[..., 256:])

    def pick(stack, i):
        return lax.dynamic_index_in_dim(stack, i, 0, keepdims=False)

    tail_piece = send(block(tail, t_own), tail_route)
    upper = jnp.stack([send(block(factor, (t_own - y - r) % 4), panel_route(r)) for r in range(4)])
    lower = jnp.stack([send(block(factor, (t_own - r) % 4), lower_route(r)) for r in range(4)])
    locals_ = jnp.stack([send(block(local, (t_own - y - r) % 4), panel_route(r)) for r in range(4)])

    swapped = send(half(locals_, 1 - co), to_other_core)
    kept = half(locals_, co)
    low = jnp.where(co == 0, kept, swapped)
    high = jnp.where(co == 0, swapped, kept)
    local_pieces = jnp.concatenate([low, high], axis=1)

    def ring(steps, axis, source, where):
        mine = jnp.stack([pick(source, where(t)) for t in steps])
        pieces = gathered(mine, axis)
        return jnp.stack(pieces, axis=1)

    def canonical(rel, axis):
        q = spot[axis]
        order = [(i - q) % 4 for i in range(4)]
        return jnp.stack([pick(rel, o) for o in order])

    at_upper = lambda t: (t - x - y) % 4
    at_lower = lambda t: (t - z) % 4
    x3 = ring([3], "y", upper, at_upper)
    y3 = ring([3], "x", lower, at_lower)
    on_x = ring([2, 0], "x", upper, at_upper), ring([1], "x", lower, at_lower)
    on_y = ring([1], "y", upper, at_upper), ring([2, 0], "y", lower, at_lower)
    uppers = {3: (x3[0], "y"), 2: (on_x[0][0], "x"), 1: (on_y[0][0], "y"), 0: (on_x[0][1], "x")}
    lowers = {3: (y3[0], "x"), 2: (on_y[1][0], "y"), 1: (on_x[1][0], "x"), 0: (on_y[1][1], "y")}

    crosses, blocks = {}, {}
    current = None
    for t in (3, 2, 1, 0):
        first, second = ("y", "x") if t % 2 else ("x", "y")
        rel, axis = uppers[t]
        whole = canonical(rel, axis).reshape(256, 512)
        a_own = half(whole, co)
        a_sib = send(half(whole, 1 - co), to_other_core)
        rel, axis = lowers[t]
        b_own = canonical(rel, axis).reshape(256, 512)
        b_sib = send(b_own, to_other_core)
        at = jnp.stack([z, co, spot[second]]).astype(jnp.int32)
        if t == 3:
            pieces = jnp.stack(gathered(tail_piece, "x"))
            x_own = canonical(pieces, "x").reshape(256, 512)
            x_sib = send(x_own, to_other_core)
            parts = call(first_kernel, at, [x_own, x_sib, a_own, a_sib], [(512, 256)])
        else:
            x_own = jnp.concatenate(gathered(current, second))
            x_sib = send(x_own, to_other_core)
            parts = call(
                cross_kernel, at, [x_own, x_sib, a_own, a_sib], [(512, 256), (512, 256)]
            )
        cross = scattered(parts, "z")
        crosses[t] = cross
        at = jnp.stack([z, co, spot[first]]).astype(jnp.int32)
        parts = call(
            close_kernel,
            at,
            gathered(cross, "z") + [b_own, b_sib],
            [(512, 512), (512, 256), (512, 256)],
        )
        current = scattered(parts, first) + pick(local_pieces, (t - x - y) % 4)
        blocks[t] = current

    def panels(by_step):
        both = jnp.stack([by_step[t] for t in range(4)])
        top, bottom = both[:, :64], both[:, 64:]
        kept = jnp.where(co == 0, top, bottom)
        got = send(jnp.where(co == 0, bottom, top), to_other_core)
        left = jnp.where(co == 0, kept, got)
        right = jnp.where(co == 0, got, kept)
        return jnp.concatenate([left, right], axis=2)

    def placed(by_step, out_route, row):
        stack = panels(by_step)
        got = jnp.stack([send(pick(stack, (x + y + r) % 4), out_route(r)) for r in range(4)])
        return jnp.concatenate([pick(got, (t_own - row - j) % 4) for j in range(4)], axis=1)

    count = adjacency.shape[0]
    joined = jnp.maximum(adjacency, jnp.eye(count, dtype=jnp.int32)).astype(jnp.float32)
    tile_row = (z * 8 + y * 2 + xl) * 64 // TILE
    mask = jnp.repeat(pick(joined, tile_row), TILE)[None, :]
    sel_off = -placed(crosses, off_out_route, z) * mask
    sel_diag = placed(blocks, diag_out_route, y) * mask
    return sel_diag[None], sel_off[None]


def solution(mesh):
    fine = Mesh(mesh.devices.reshape(SIZES), AXES)
    rows = P(("xh", "co"), ("z", "y", "xl"), None)
    return jax.shard_map(
        on_device,
        mesh=fine,
        in_specs=(rows, rows, P(("z", "y", "xl"), None), P()),
        out_specs=(rows, rows),
        check_vma=False,
    )
```

time: 1250 us -> 345 us (0.28)
  waiting for transfers between devices: 1000 us -> 159 us
  matrix products: 158 us -> 0 us
  starting transfers between devices: 26.5 us -> 160 us
  blocking collectives: 24.8 us -> 0 us
    all_gather x3 -> x0, waiting for transfers between devices: 923 us -> none  [on_device(): gathered = lax.all_gather(composed, 'space', axis=0, tiled=True)]
    ppermute x5 -> x102, starting transfers between devices: 11.8 us -> 160 us  [send(): return lax.ppermute(x, AXES, route(place))]
    dot_general x8 -> x0, matrix products: 99.8 us -> none  [the longest x3 41.5 us: on_device(): quadratic = jnp.dot(turned.T, gathered, precision=highest)]
    ppermute x5 -> x102, waiting for transfers between devices: 58.9 us -> 159 us  [send(): return lax.ppermute(x, AXES, route(place))]
    all_to_all x2 -> x0, matrix products: 57.8 us -> none  [on_device(): lax.all_to_all(half_product, 'space', split_axis=1, concat_axis=0, tiled=...]
    all_to_all x1 -> x0, blocking collectives: 24.8 us -> none  [on_device(): lax.all_to_all(half_product, 'space', split_axis=1, concat_axis=0, tiled=...]
    all_to_all x2 -> x0, waiting for transfers between devices: 17.6 us -> none  [on_device(): lax.all_to_all(half_product, 'space', split_axis=1, concat_axis=0, tiled=...]
    all_to_all x2 -> x0, starting transfers between devices: 14.6 us -> none  [on_device(): lax.all_to_all(half_product, 'space', split_axis=1, concat_axis=0, tiled=...]
  transfers between devices with their start and end apart: 10 -> 102, of which waited for: 9 -> 57; matrix products, arithmetic and copies ran while one was open for 8% -> 2% of each run, Pallas kernels for 0% -> 2%
where the time goes in v1:
time: 345 us; the launch traced here: 340 us
  starting transfers between devices  160 us (46%)
  waiting for transfers between devices  159 us (46%)
  Pallas kernels  10.2 us (3%)
  other arithmetic  4.64 us (1%)
  local copies, waits for them, and re-layouts  4.2 us (1%)
    ppermute x102, starting transfers between devices, send(): return lax.ppermute(x, AXES, route(place))  160 us
    ppermute x102, waiting for transfers between devices, send(): return lax.ppermute(x, AXES, route(place))  159 us
    pallas_call x8, Pallas kernels, call(): pl.pallas_call(kernel, out_shape=[jax.ShapeDtypeStruct((128, 256), jnp.fl...  10.2 us
  transfers between devices with their start and end apart: 102, of which 57 were waited for; matrix products, arithmetic and copies ran while one was open for 2% of the time, Pallas kernels for 2%

profile of v1, /device:TPU:6, one launch (start us, length us, event | category | flops | bytes accessed | tf_op | source)
XLA Modules:
  0.0 340.4 jit_solution(1845088417172375920)
XLA Ops:
  1.7 4.5 %collective-permute-start = (f32[64,512]{1,0:T(8,128)S(1)}, f32[64,512]{1,0:T(8,128)S(1)}, u32[]{:S(2)}, u32[]{:S(2)}) collective-permute-start(f32[64,512]{1,0:T(8,128)S(1)} %constant_dynamic-slice_fusion.21), channel_id=1, source_target_pairs={{0,0},{1,32},{2,1},{3,33},{4,64},{5,96},{6,65},{7,97},{8,8},{9,40}... | collective-permute-start | bytes 393224 | tf_op jit(solution)/shard_map/ppermute | solution.py:28
  7.4 5.6 %collective-permute-start.33 = (f32[64,512]{1,0:T(8,128)S(1)}, f32[64,512]{1,0:T(8,128)S(1)}, u32[]{:S(2)}, u32[]{:S(2)}) collective-permute-start(f32[64,512]{1,0:T(8,128)S(1)} %get-tuple-element.154), channel_id=1, source_target_pairs={{0,2},{1,34},{2,1},{3,33},{4,70},{5,102},{6,69},{7,101},{8,10},{9,... | collective-permute-start | bytes 393224 | tf_op jit(solution)/shard_map/ppermute | solution.py:28
  13.0 2.2 collective-permute-start.32
  15.2 2.0 collective-permute-start.31
  17.2 2.9 collective-permute-start.30
  20.8 6.9 %collective-permute-start.8 = (f32[64,512]{1,0:T(8,128)S(1)}, f32[64,512]{1,0:T(8,128)S(1)}, u32[]{:S(2)}, u32[]{:S(2)}) collective-permute-start(f32[64,512]{1,0:T(8,128)S(1)} %get-tuple-element.136), channel_id=1, source_target_pairs={{0,2},{1,34},{2,1},{3,33},{4,70},{5,102},{6,69},{7,101},{8,10},{9,... | collective-permute-start | bytes 393224 | tf_op jit(solution)/shard_map/ppermute | solution.py:28
  27.7 4.0 %collective-permute-start.7 = (f32[64,512]{1,0:T(8,128)S(1)}, f32[64,512]{1,0:T(8,128)S(1)}, u32[]{:S(2)}, u32[]{:S(2)}) collective-permute-start(f32[64,512]{1,0:T(8,128)S(1)} %get-tuple-element.137), channel_id=1, source_target_pairs={{0,4},{1,36},{2,3},{3,35},{4,64},{5,96},{6,71},{7,103},{8,12},{9,4... | collective-permute-start | bytes 393224 | tf_op jit(solution)/shard_map/ppermute | solution.py:28
  31.8 3.0 collective-permute-start.6
  36.8 3.7 %collective-permute-start.22 = (f32[64,512]{1,0:T(8,128)S(1)}, f32[64,512]{1,0:T(8,128)S(1)}, u32[]{:S(2)}, u32[]{:S(2)}) collective-permute-start(f32[64,512]{1,0:T(8,128)S(1)} %get-tuple-element.140), channel_id=1, source_target_pairs={{0,8},{1,40},{2,10},{3,42},{4,12},{5,44},{6,14},{7,46},{8,9},{9,41... | collective-permute-start | bytes 393224 | tf_op jit(solution)/shard_map/ppermute | solution.py:28
  40.6 3.4 %collective-permute-done.6 = f32[64,512]{1,0:T(8,128)S(1)} collective-permute-done((f32[64,512]{1,0:T(8,128)S(1)}, f32[64,512]{1,0:T(8,128)S(1)}, u32[]{:S(2)}, u32[]{:S(2)}) %collective-permute-start.6) | collective-permute-done | bytes 131104 | tf_op jit(solution)/shard_map/ppermute | solution.py:28
  44.0 4.9 %collective-permute-done.5 = f32[64,512]{1,0:T(8,128)S(1)} collective-permute-done((f32[64,512]{1,0:T(8,128)S(1)}, f32[64,512]{1,0:T(8,128)S(1)}, u32[]{:S(2)}, u32[]{:S(2)}) %collective-permute-start.5) | collective-permute-done | bytes 131104 | tf_op jit(solution)/shard_map/ppermute | solution.py:28
  50.9 4.0 %collective-permute-done.22 = f32[64,512]{1,0:T(8,128)S(1)} collective-permute-done((f32[64,512]{1,0:T(8,128)S(1)}, f32[64,512]{1,0:T(8,128)S(1)}, u32[]{:S(2)}, u32[]{:S(2)}) %collective-permute-start.22) | collective-permute-done | bytes 131104 | tf_op jit(solution)/shard_map/ppermute | solution.py:28
  54.9 2.9 collective-permute-done.21
  57.9 3.8 %collective-permute-start.61 = (f32[1,64,512]{2,1,0:T(8,128)S(1)}, f32[1,64,512]{2,1,0:T(8,128)S(1)}, u32[]{:S(2)}, u32[]{:S(2)}) collective-permute-start(f32[1,64,512]{2,1,0:T(8,128)S(1)} %get-tuple-element.116), channel_id=1, source_target_pairs={{0,4},{1,5},{2,6},{3,7},{4,0},{5,1},{6,2},{7,3},{8,12},{9,13},{10,... | collective-permute-start | bytes 393224 | tf_op jit(solution)/shard_map/ppermute | solution.py:28
  61.7 2.5 collective-permute-start.60
  66.0 2.8 collective-permute-done.62
  68.8 3.4 collective-permute-start.10
  72.2 3.4 %collective-permute-start.72 = (f32[1,64,512]{2,1,0:T(8,128)S(1)}, f32[1,64,512]{2,1,0:T(8,128)S(1)}, u32[]{:S(2)}, u32[]{:S(2)}) collective-permute-start(f32[1,64,512]{2,1,0:T(8,128)S(1)} %get-tuple-element.106), channel_id=1, source_target_pairs={{0,1},{1,64},{2,3},{3,66},{4,5},{5,68},{6,7},{7,70},{8,9},{9,72},{... | collective-permute-start | bytes 393224 | tf_op jit(solution)/shard_map/ppermute | solution.py:28
  77.1 2.3 collective-permute-start.2
  85.2 2.8 collective-permute-start.25
  89.0 2.2 collective-permute-start.24
  91.4 3.3 collective-permute-start.41
  97.0 2.7 collective-permute-done.23
  99.9 6.1 %collective-permute-done.41 = f32[2,64,512]{2,1,0:T(8,128)S(1)} collective-permute-done((f32[2,64,512]{2,1,0:T(8,128)S(1)}, f32[2,64,512]{2,1,0:T(8,128)S(1)}, u32[]{:S(2)}, u32[]{:S(2)}) %collective-permute-start.41) | collective-permute-done | bytes 262176 | tf_op jit(solution)/shard_map/ppermute | solution.py:28
  106.6 4.3 %collective-permute-done.39 = f32[2,64,512]{2,1,0:T(8,128)S(1)} collective-permute-done((f32[2,64,512]{2,1,0:T(8,128)S(1)}, f32[2,64,512]{2,1,0:T(8,128)S(1)}, u32[]{:S(2)}, u32[]{:S(2)}) %collective-permute-start.39) | collective-permute-done | bytes 262176 | tf_op jit(solution)/shard_map/ppermute | solution.py:28
  112.7 2.5 collective-permute-start.14
  115.5 3.5 %collective-permute-done.15 = f32[128,256]{1,0:T(8,128)S(1)} collective-permute-done((f32[128,256]{1,0:T(8,128)S(1)}, f32[128,256]{1,0:T(8,128)S(1)}, u32[]{:S(2)}, u32[]{:S(2)}) %collective-permute-start.15) | collective-permute-done | bytes 131104 | tf_op jit(solution)/shard_map/ppermute | solution.py:28
  120.5 2.0 collective-permute-done.13
  125.4 2.1 collective-permute-start.50
  136.0 6.3 %collective-permute-done.29 = f32[128,256]{1,0:T(8,128)S(1)} collective-permute-done((f32[128,256]{1,0:T(8,128)S(1)}, f32[128,256]{1,0:T(8,128)S(1)}, u32[]{:S(2)}, u32[]{:S(2)}) %collective-permute-start.29) | collective-permute-done | bytes 131104 | tf_op jit(solution)/shard_map/ppermute | solution.py:28
  143.2 5.3 %collective-permute-done.27 = f32[128,256]{1,0:T(8,128)S(1)} collective-permute-done((f32[128,256]{1,0:T(8,128)S(1)}, f32[128,256]{1,0:T(8,128)S(1)}, u32[]{:S(2)}, u32[]{:S(2)}) %collective-permute-start.27) | collective-permute-done | bytes 131104 | tf_op jit(solution)/shard_map/ppermute | solution.py:28
  148.7 2.9 collective-permute-start.36
  152.0 4.2 %collective-permute-done.37 = f32[128,256]{1,0:T(8,128)S(1)} collective-permute-done((f32[128,256]{1,0:T(8,128)S(1)}, f32[128,256]{1,0:T(8,128)S(1)}, u32[]{:S(2)}, u32[]{:S(2)}) %collective-permute-start.37) | collective-permute-done | bytes 131104 | tf_op jit(solution)/shard_map/ppermute | solution.py:28
  160.4 2.3 collective-permute-start.45
  164.0 4.5 %collective-permute-done.45 = f32[128,256]{1,0:T(8,128)S(1)} collective-permute-done((f32[128,256]{1,0:T(8,128)S(1)}, f32[128,256]{1,0:T(8,128)S(1)}, u32[]{:S(2)}, u32[]{:S(2)}) %collective-permute-start.45) | collective-permute-done | bytes 131104 | tf_op jit(solution)/shard_map/ppermute | solution.py:28
  168.5 2.0 collective-permute-done.44
  174.3 4.3 %collective-permute-done.46.y1 = f32[128,256]{1,0:T(8,128)S(1)} collective-permute-done((f32[128,256]{1,0:T(8,128)S(1)}, f32[128,256]{1,0:T(8,128)S(1)}, u32[]{:S(2)}, u32[]{:S(2)}) %collective-permute-start.46) | collective-permute-done | bytes 131104 | tf_op jit(solution)/shard_map/ppermute | solution.py:28
  183.8 2.8 collective-permute-start.54
  187.5 5.2 %collective-permute-done.55 = f32[128,256]{1,0:T(8,128)S(1)} collective-permute-done((f32[128,256]{1,0:T(8,128)S(1)}, f32[128,256]{1,0:T(8,128)S(1)}, u32[]{:S(2)}, u32[]{:S(2)}) %collective-permute-start.55) | collective-permute-done | bytes 131104 | tf_op jit(solution)/shard_map/ppermute | solution.py:28
  193.3 2.7 collective-permute-start.58
  196.1 10.3 %collective-permute-start.57 = (f32[128,256]{1,0:T(8,128)S(1)}, f32[128,256]{1,0:T(8,128)S(1)}, u32[]{:S(2)}, u32[]{:S(2)}) collective-permute-start(f32[128,256]{1,0:T(8,128)S(1)} %fusion.26), channel_id=1, source_target_pairs={{0,64},{1,65},{2,66},{3,67},{4,68},{5,69},{6,70},{7,71},{8,72},{9,... | collective-permute-start | bytes 393224 | tf_op jit(solution)/shard_map/ppermute | solution.py:28
  207.4 6.7 %collective-permute-done.57 = f32[128,256]{1,0:T(8,128)S(1)} collective-permute-done((f32[128,256]{1,0:T(8,128)S(1)}, f32[128,256]{1,0:T(8,128)S(1)}, u32[]{:S(2)}, u32[]{:S(2)}) %collective-permute-start.57) | collective-permute-done | bytes 131104 | tf_op jit(solution)/shard_map/ppermute | solution.py:28
  221.0 4.3 %collective-permute-done.66 = f32[128,256]{1,0:T(8,128)S(1)} collective-permute-done((f32[128,256]{1,0:T(8,128)S(1)}, f32[128,256]{1,0:T(8,128)S(1)}, u32[]{:S(2)}, u32[]{:S(2)}) %collective-permute-start.66) | collective-permute-done | bytes 131104 | tf_op jit(solution)/shard_map/ppermute | solution.py:28
  226.9 2.0 collective-permute-done.64
  231.0 4.3 %collective-permute-done.67.y1 = f32[128,256]{1,0:T(8,128)S(1)} collective-permute-done((f32[128,256]{1,0:T(8,128)S(1)}, f32[128,256]{1,0:T(8,128)S(1)}, u32[]{:S(2)}, u32[]{:S(2)}) %collective-permute-start.67) | collective-permute-done | bytes 131104 | tf_op jit(solution)/shard_map/ppermute | solution.py:28
  235.4 2.6 collective-permute-done.68.y2
  240.2 2.3 collective-permute-start.76
  243.4 4.3 %collective-permute-done.76 = f32[128,256]{1,0:T(8,128)S(1)} collective-permute-done((f32[128,256]{1,0:T(8,128)S(1)}, f32[128,256]{1,0:T(8,128)S(1)}, u32[]{:S(2)}, u32[]{:S(2)}) %collective-permute-start.76) | collective-permute-done | bytes 131104 | tf_op jit(solution)/shard_map/ppermute | solution.py:28
  247.7 2.4 collective-permute-done.75
  251.3 2.3 collective-permute-start.78
  254.5 5.8 %collective-permute-done.79 = f32[128,256]{1,0:T(8,128)S(1)} collective-permute-done((f32[128,256]{1,0:T(8,128)S(1)}, f32[128,256]{1,0:T(8,128)S(1)}, u32[]{:S(2)}, u32[]{:S(2)}) %collective-permute-start.79) | collective-permute-done | bytes 131104 | tf_op jit(solution)/shard_map/ppermute | solution.py:28
  267.2 4.2 %collective-permute-done.84 = f32[128,256]{1,0:T(8,128)S(1)} collective-permute-done((f32[128,256]{1,0:T(8,128)S(1)}, f32[128,256]{1,0:T(8,128)S(1)}, u32[]{:S(2)}, u32[]{:S(2)}) %collective-permute-start.84) | collective-permute-done | bytes 131104 | tf_op jit(solution)/shard_map/ppermute | solution.py:28
  271.4 2.0 collective-permute-done.83
  273.3 1.9 collective-permute-done.82
  277.5 4.3 %collective-permute-done.85.y1 = f32[128,256]{1,0:T(8,128)S(1)} collective-permute-done((f32[128,256]{1,0:T(8,128)S(1)}, f32[128,256]{1,0:T(8,128)S(1)}, u32[]{:S(2)}, u32[]{:S(2)}) %collective-permute-start.85) | collective-permute-done | bytes 131104 | tf_op jit(solution)/shard_map/ppermute | solution.py:28
  281.7 2.5 collective-permute-done.86.y2
  286.8 2.3 collective-permute-start.90
  290.2 5.9 %collective-permute-done.91 = f32[128,256]{1,0:T(8,128)S(1)} collective-permute-done((f32[128,256]{1,0:T(8,128)S(1)}, f32[128,256]{1,0:T(8,128)S(1)}, u32[]{:S(2)}, u32[]{:S(2)}) %collective-permute-start.91) | collective-permute-done | bytes 131104 | tf_op jit(solution)/shard_map/ppermute | solution.py:28
  299.9 4.9 %collective-permute-start.100 = (f32[64,512]{1,0:T(8,128)S(1)}, f32[64,512]{1,0:T(8,128)S(1)}, u32[]{:S(2)}, u32[]{:S(2)}) collective-permute-start(f32[64,512]{1,0:T(8,128)S(1)} %get-tuple-element.82), channel_id=1, source_target_pairs={{0,64},{1,96},{2,104},{3,8},{4,0},{5,48},{6,56},{7,72},{8,66},{9,9... | collective-permute-start | bytes 393224 | tf_op jit(solution)/shard_map/ppermute | solution.py:28
  304.9 8.0 %collective-permute-start.99 = (f32[64,512]{1,0:T(8,128)S(1)}, f32[64,512]{1,0:T(8,128)S(1)}, u32[]{:S(2)}, u32[]{:S(2)}) collective-permute-start(f32[64,512]{1,0:T(8,128)S(1)} %get-tuple-element.81), channel_id=1, source_target_pairs={{0,32},{1,72},{2,64},{3,104},{4,112},{5,8},{6,0},{7,56},{8,34},{9,... | collective-permute-start | bytes 393224 | tf_op jit(solution)/shard_map/ppermute | solution.py:28
  315.0 5.1 %collective-permute-start.96 = (f32[64,512]{1,0:T(8,128)S(1)}, f32[64,512]{1,0:T(8,128)S(1)}, u32[]{:S(2)}, u32[]{:S(2)}) collective-permute-start(f32[64,512]{1,0:T(8,128)S(1)} %get-tuple-element.91), channel_id=1, source_target_pairs={{0,96},{1,2},{2,0},{3,34},{4,36},{5,66},{6,64},{7,102},{8,104},{9,... | collective-permute-start | bytes 393224 | tf_op jit(solution)/shard_map/ppermute | solution.py:28
  322.0 7.2 %collective-permute-start.94 = (f32[64,512]{1,0:T(8,128)S(1)}, f32[64,512]{1,0:T(8,128)S(1)}, u32[]{:S(2)}, u32[]{:S(2)}) collective-permute-start(f32[64,512]{1,0:T(8,128)S(1)} %get-tuple-element.89), channel_id=1, source_target_pairs={{0,32},{1,66},{2,64},{3,98},{4,100},{5,2},{6,0},{7,38},{8,40},{9,7... | collective-permute-start | bytes 393224 | tf_op jit(solution)/shard_map/ppermute | solution.py:28
  331.2 2.0 collective-permute-done.94
  333.2 5.9 %collective-permute-done.93 = f32[64,512]{1,0:T(8,128)S(1)} collective-permute-done((f32[64,512]{1,0:T(8,128)S(1)}, f32[64,512]{1,0:T(8,128)S(1)}, u32[]{:S(2)}, u32[]{:S(2)}) %collective-permute-start.93) | collective-permute-done | bytes 131104 | tf_op jit(solution)/shard_map/ppermute | solution.py:28
  (239 shorter events, 92.4 us)
Async XLA Ops:
  1.7 74.0 %collective-permute-start = (f32[64,512]{1,0:T(8,128)S(1)}, f32[64,512]{1,0:T(8,128)S(1)}, u32[]{:S(2)}, u32[]{:S(2)}) collective-permute-start(f32[64,512]{1,0:T(8,128)S(1)} %constant_dynamic-slice_fusion.21), channel_id=1, source_target_pairs={{0,0},{1,32},{2,1},{3,33},{4,64},{5,96},{6,65},{7,97},{8,8},{9,40}... | collective-permute-start | bytes 393224 | tf_op jit(solution)/shard_map/ppermute | solution.py:28
  7.4 13.4 %collective-permute-start.33 = (f32[64,512]{1,0:T(8,128)S(1)}, f32[64,512]{1,0:T(8,128)S(1)}, u32[]{:S(2)}, u32[]{:S(2)}) collective-permute-start(f32[64,512]{1,0:T(8,128)S(1)} %get-tuple-element.154), channel_id=1, source_target_pairs={{0,2},{1,34},{2,1},{3,33},{4,70},{5,102},{6,69},{7,101},{8,10},{9,... | collective-permute-start | bytes 393224 | tf_op jit(solution)/shard_map/ppermute | solution.py:28
  13.0 14.7 %collective-permute-start.32 = (f32[64,512]{1,0:T(8,128)S(1)}, f32[64,512]{1,0:T(8,128)S(1)}, u32[]{:S(2)}, u32[]{:S(2)}) collective-permute-start(f32[64,512]{1,0:T(8,128)S(1)} %get-tuple-element.155), channel_id=1, source_target_pairs={{0,4},{1,36},{2,3},{3,35},{4,64},{5,96},{6,71},{7,103},{8,12},{9,4... | collective-permute-start | bytes 393224 | tf_op jit(solution)/shard_map/ppermute | solution.py:28
  15.2 16.6 %collective-permute-start.31 = (f32[64,512]{1,0:T(8,128)S(1)}, f32[64,512]{1,0:T(8,128)S(1)}, u32[]{:S(2)}, u32[]{:S(2)}) collective-permute-start(f32[64,512]{1,0:T(8,128)S(1)} %get-tuple-element.153), channel_id=1, source_target_pairs={{0,6},{1,38},{2,5},{3,37},{4,66},{5,98},{6,65},{7,97},{8,14},{9,46... | collective-permute-start | bytes 393224 | tf_op jit(solution)/shard_map/ppermute | solution.py:28
  17.2 17.6 %collective-permute-start.30 = (f32[64,512]{1,0:T(8,128)S(1)}, f32[64,512]{1,0:T(8,128)S(1)}, u32[]{:S(2)}, u32[]{:S(2)}) collective-permute-start(f32[64,512]{1,0:T(8,128)S(1)} %get-tuple-element.152), channel_id=1, source_target_pairs={{0,0},{1,32},{2,7},{3,39},{4,68},{5,100},{6,67},{7,99},{8,8},{9,40... | collective-permute-start | bytes 393224 | tf_op jit(solution)/shard_map/ppermute | solution.py:28
  20.8 16.0 %collective-permute-start.8 = (f32[64,512]{1,0:T(8,128)S(1)}, f32[64,512]{1,0:T(8,128)S(1)}, u32[]{:S(2)}, u32[]{:S(2)}) collective-permute-start(f32[64,512]{1,0:T(8,128)S(1)} %get-tuple-element.136), channel_id=1, source_target_pairs={{0,2},{1,34},{2,1},{3,33},{4,70},{5,102},{6,69},{7,101},{8,10},{9,... | collective-permute-start | bytes 393224 | tf_op jit(solution)/shard_map/ppermute | solution.py:28
  27.7 12.9 %collective-permute-start.7 = (f32[64,512]{1,0:T(8,128)S(1)}, f32[64,512]{1,0:T(8,128)S(1)}, u32[]{:S(2)}, u32[]{:S(2)}) collective-permute-start(f32[64,512]{1,0:T(8,128)S(1)} %get-tuple-element.137), channel_id=1, source_target_pairs={{0,4},{1,36},{2,3},{3,35},{4,64},{5,96},{6,71},{7,103},{8,12},{9,4... | collective-permute-start | bytes 393224 | tf_op jit(solution)/shard_map/ppermute | solution.py:28
  31.8 12.2 %collective-permute-start.6 = (f32[64,512]{1,0:T(8,128)S(1)}, f32[64,512]{1,0:T(8,128)S(1)}, u32[]{:S(2)}, u32[]{:S(2)}) collective-permute-start(f32[64,512]{1,0:T(8,128)S(1)} %get-tuple-element.138), channel_id=1, source_target_pairs={{0,6},{1,38},{2,5},{3,37},{4,66},{5,98},{6,65},{7,97},{8,14},{9,46... | collective-permute-start | bytes 393224 | tf_op jit(solution)/shard_map/ppermute | solution.py:28
  34.8 14.1 %collective-permute-start.5 = (f32[64,512]{1,0:T(8,128)S(1)}, f32[64,512]{1,0:T(8,128)S(1)}, u32[]{:S(2)}, u32[]{:S(2)}) collective-permute-start(f32[64,512]{1,0:T(8,128)S(1)} %get-tuple-element.139), channel_id=1, source_target_pairs={{0,0},{1,32},{2,7},{3,39},{4,68},{5,100},{6,67},{7,99},{8,8},{9,40... | collective-permute-start | bytes 393224 | tf_op jit(solution)/shard_map/ppermute | solution.py:28
  36.8 18.1 %collective-permute-start.22 = (f32[64,512]{1,0:T(8,128)S(1)}, f32[64,512]{1,0:T(8,128)S(1)}, u32[]{:S(2)}, u32[]{:S(2)}) collective-permute-start(f32[64,512]{1,0:T(8,128)S(1)} %get-tuple-element.140), channel_id=1, source_target_pairs={{0,8},{1,40},{2,10},{3,42},{4,12},{5,44},{6,14},{7,46},{8,9},{9,41... | collective-permute-start | bytes 393224 | tf_op jit(solution)/shard_map/ppermute | solution.py:28
  40.6 17.3 %collective-permute-start.21 = (f32[64,512]{1,0:T(8,128)S(1)}, f32[64,512]{1,0:T(8,128)S(1)}, u32[]{:S(2)}, u32[]{:S(2)}) collective-permute-start(f32[64,512]{1,0:T(8,128)S(1)} %get-tuple-element.141), channel_id=1, source_target_pairs={{0,16},{1,48},{2,18},{3,50},{4,20},{5,52},{6,22},{7,54},{8,17},{9,... | collective-permute-start | bytes 393224 | tf_op jit(solution)/shard_map/ppermute | solution.py:28
  44.0 17.7 %collective-permute-start.20 = (f32[64,512]{1,0:T(8,128)S(1)}, f32[64,512]{1,0:T(8,128)S(1)}, u32[]{:S(2)}, u32[]{:S(2)}) collective-permute-start(f32[64,512]{1,0:T(8,128)S(1)} %get-tuple-element.135), channel_id=1, source_target_pairs={{0,24},{1,56},{2,26},{3,58},{4,28},{5,60},{6,30},{7,62},{8,25},{9,... | collective-permute-start | bytes 393224 | tf_op jit(solution)/shard_map/ppermute | solution.py:28
  48.9 16.9 %collective-permute-start.19 = (f32[64,512]{1,0:T(8,128)S(1)}, f32[64,512]{1,0:T(8,128)S(1)}, u32[]{:S(2)}, u32[]{:S(2)}) collective-permute-start(f32[64,512]{1,0:T(8,128)S(1)} %get-tuple-element.134), channel_id=1, source_target_pairs={{0,0},{1,32},{2,2},{3,34},{4,4},{5,36},{6,6},{7,38},{8,1},{9,33},{... | collective-permute-start | bytes 393224 | tf_op jit(solution)/shard_map/ppermute | solution.py:28
  54.9 13.9 %collective-permute-start.62 = (f32[1,64,512]{2,1,0:T(8,128)S(1)}, f32[1,64,512]{2,1,0:T(8,128)S(1)}, u32[]{:S(2)}, u32[]{:S(2)}) collective-permute-start(f32[1,64,512]{2,1,0:T(8,128)S(1)} %get-tuple-element.116), channel_id=1, source_target_pairs={{0,2},{1,3},{2,4},{3,5},{4,6},{5,7},{6,0},{7,1},{8,10},{9,11},{10,... | collective-permute-start | bytes 393224 | tf_op jit(solution)/shard_map/ppermute | solution.py:28
  57.9 14.3 %collective-permute-start.61 = (f32[1,64,512]{2,1,0:T(8,128)S(1)}, f32[1,64,512]{2,1,0:T(8,128)S(1)}, u32[]{:S(2)}, u32[]{:S(2)}) collective-permute-start(f32[1,64,512]{2,1,0:T(8,128)S(1)} %get-tuple-element.116), channel_id=1, source_target_pairs={{0,4},{1,5},{2,6},{3,7},{4,0},{5,1},{6,2},{7,3},{8,12},{9,13},{10,... | collective-permute-start | bytes 393224 | tf_op jit(solution)/shard_map/ppermute | solution.py:28
  61.7 10.5 %collective-permute-start.60 = (f32[1,64,512]{2,1,0:T(8,128)S(1)}, f32[1,64,512]{2,1,0:T(8,128)S(1)}, u32[]{:S(2)}, u32[]{:S(2)}) collective-permute-start(f32[1,64,512]{2,1,0:T(8,128)S(1)} %get-tuple-element.116), channel_id=1, source_target_pairs={{0,6},{1,7},{2,0},{3,1},{4,2},{5,3},{6,4},{7,5},{8,14},{9,15},{10,... | collective-permute-start | bytes 393224 | tf_op jit(solution)/shard_map/ppermute | solution.py:28
  65.8 10.0 %collective-permute-start.11 = (f32[1,64,512]{2,1,0:T(8,128)S(1)}, f32[1,64,512]{2,1,0:T(8,128)S(1)}, u32[]{:S(2)}, u32[]{:S(2)}) collective-permute-start(f32[1,64,512]{2,1,0:T(8,128)S(1)} %get-tuple-element.119), channel_id=1, source_target_pairs={{0,2},{1,3},{2,4},{3,5},{4,6},{5,7},{6,0},{7,1},{8,10},{9,11},{10,... | collective-permute-start | bytes 393224 | tf_op jit(solution)/shard_map/ppermute | solution.py:28
  72.2 19.0 %collective-permute-start.72 = (f32[1,64,512]{2,1,0:T(8,128)S(1)}, f32[1,64,512]{2,1,0:T(8,128)S(1)}, u32[]{:S(2)}, u32[]{:S(2)}) collective-permute-start(f32[1,64,512]{2,1,0:T(8,128)S(1)} %get-tuple-element.106), channel_id=1, source_target_pairs={{0,1},{1,64},{2,3},{3,66},{4,5},{5,68},{6,7},{7,70},{8,9},{9,72},{... | collective-permute-start | bytes 393224 | tf_op jit(solution)/shard_map/ppermute | solution.py:28
  75.7 15.7 %collective-permute-start.71 = (f32[1,64,512]{2,1,0:T(8,128)S(1)}, f32[1,64,512]{2,1,0:T(8,128)S(1)}, u32[]{:S(2)}, u32[]{:S(2)}) collective-permute-start(f32[1,64,512]{2,1,0:T(8,128)S(1)} %get-tuple-element.106), channel_id=1, source_target_pairs={{0,64},{1,65},{2,66},{3,67},{4,68},{5,69},{6,70},{7,71},{8,72},{9,... | collective-permute-start | bytes 393224 | tf_op jit(solution)/shard_map/ppermute | solution.py:28
  79.4 9.6 %collective-permute-start.1 = (f32[64,512]{1,0:T(8,128)S(1)}, f32[64,512]{1,0:T(8,128)S(1)}, u32[]{:S(2)}, u32[]{:S(2)}) collective-permute-start(f32[64,512]{1,0:T(8,128)S(1)} %collective-permute-done), channel_id=1, source_target_pairs={{0,65},{1,0},{2,67},{3,2},{4,69},{5,4},{6,71},{7,6},{8,73},{9,8},{... | collective-permute-start | bytes 393224 | tf_op jit(solution)/shard_map/ppermute | solution.py:28
  82.3 12.4 %collective-permute-start.70 = (f32[1,64,512]{2,1,0:T(8,128)S(1)}, f32[1,64,512]{2,1,0:T(8,128)S(1)}, u32[]{:S(2)}, u32[]{:S(2)}) collective-permute-start(f32[1,64,512]{2,1,0:T(8,128)S(1)} %get-tuple-element.106), channel_id=1, source_target_pairs={{0,65},{1,0},{2,67},{3,2},{4,69},{5,4},{6,71},{7,6},{8,73},{9,8},{... | collective-permute-start | bytes 393224 | tf_op jit(solution)/shard_map/ppermute | solution.py:28
  85.2 9.7 %collective-permute-start.25 = (f32[1,64,512]{2,1,0:T(8,128)S(1)}, f32[1,64,512]{2,1,0:T(8,128)S(1)}, u32[]{:S(2)}, u32[]{:S(2)}) collective-permute-start(f32[1,64,512]{2,1,0:T(8,128)S(1)} %get-tuple-element.109), channel_id=1, source_target_pairs={{0,1},{1,64},{2,3},{3,66},{4,5},{5,68},{6,7},{7,70},{8,9},{9,72},{... | collective-permute-start | bytes 393224 | tf_op jit(solution)/shard_map/ppermute | solution.py:28
  91.3 8.5 %collective-permute-start.23 = (f32[1,64,512]{2,1,0:T(8,128)S(1)}, f32[1,64,512]{2,1,0:T(8,128)S(1)}, u32[]{:S(2)}, u32[]{:S(2)}) collective-permute-start(f32[1,64,512]{2,1,0:T(8,128)S(1)} %get-tuple-element.109), channel_id=1, source_target_pairs={{0,65},{1,0},{2,67},{3,2},{4,69},{5,4},{6,71},{7,6},{8,73},{9,8},{... | collective-permute-start | bytes 393224 | tf_op jit(solution)/shard_map/ppermute | solution.py:28
  91.4 14.7 %collective-permute-start.41 = (f32[2,64,512]{2,1,0:T(8,128)S(1)}, f32[2,64,512]{2,1,0:T(8,128)S(1)}, u32[]{:S(2)}, u32[]{:S(2)}) collective-permute-start(f32[2,64,512]{2,1,0:T(8,128)S(1)} %get-tuple-element.159), channel_id=1, source_target_pairs={{0,1},{1,64},{2,3},{3,66},{4,5},{5,68},{6,7},{7,70},{8,9},{9,72},{... | collective-permute-start | bytes 786440 | tf_op jit(solution)/shard_map/ppermute | solution.py:28
  94.7 11.4 %collective-permute-start.40 = (f32[2,64,512]{2,1,0:T(8,128)S(1)}, f32[2,64,512]{2,1,0:T(8,128)S(1)}, u32[]{:S(2)}, u32[]{:S(2)}) collective-permute-start(f32[2,64,512]{2,1,0:T(8,128)S(1)} %get-tuple-element.159), channel_id=1, source_target_pairs={{0,64},{1,65},{2,66},{3,67},{4,68},{5,69},{6,70},{7,71},{8,72},{9,... | collective-permute-start | bytes 786440 | tf_op jit(solution)/shard_map/ppermute | solution.py:28
  94.9 16.0 %collective-permute-start.39 = (f32[2,64,512]{2,1,0:T(8,128)S(1)}, f32[2,64,512]{2,1,0:T(8,128)S(1)}, u32[]{:S(2)}, u32[]{:S(2)}) collective-permute-start(f32[2,64,512]{2,1,0:T(8,128)S(1)} %get-tuple-element.159), channel_id=1, source_target_pairs={{0,65},{1,0},{2,67},{3,2},{4,69},{5,4},{6,71},{7,6},{8,73},{9,8},{... | collective-permute-start | bytes 786440 | tf_op jit(solution)/shard_map/ppermute | solution.py:28
  96.6 14.4 %collective-permute-start.4 = (f32[256,512]{1,0:T(8,128)S(1)}, f32[256,512]{1,0:T(8,128)S(1)}, u32[]{:S(2)}, u32[]{:S(2)}) collective-permute-start(f32[256,512]{1,0:T(8,128)S(1)} %bitcast.202), channel_id=1, source_target_pairs={{0,32},{1,33},{2,34},{3,35},{4,36},{5,37},{6,38},{7,39},{8,40},{9,... | collective-permute-start | bytes 1572872 | tf_op jit(solution)/shard_map/ppermute | solution.py:28
  99.7 11.3 %collective-permute-start.12 = (f32[256,256]{1,0:T(8,128)S(1)}, f32[256,256]{1,0:T(8,128)S(1)}, u32[]{:S(2)}, u32[]{:S(2)}) collective-permute-start(f32[256,256]{1,0:T(8,128)S(1)} %get-tuple-element.142), channel_id=1, source_target_pairs={{0,32},{1,33},{2,34},{3,35},{4,36},{5,37},{6,38},{7,39},{8,40},{9,... | collective-permute-start | bytes 786440 | tf_op jit(solution)/shard_map/ppermute | solution.py:28
  106.1 18.4 %collective-permute-start.34 = (f32[4,64,256]{2,1,0:T(8,128)S(1)}, f32[4,64,256]{2,1,0:T(8,128)S(1)}, u32[]{:S(2)}, u32[]{:S(2)}) collective-permute-start(f32[4,64,256]{2,1,0:T(8,128)S(1)} %slice_select_fusion.10), channel_id=1, source_target_pairs={{0,32},{1,33},{2,34},{3,35},{4,36},{5,37},{6,38},{7,39},{8,40},{9,... | collective-permute-start | bytes 786440 | tf_op jit(solution)/shard_map/ppermute | solution.py:28
  106.1 19.3 %collective-permute-start.26 = (f32[256,512]{1,0:T(8,128)S(1)}, f32[256,512]{1,0:T(8,128)S(1)}, u32[]{:S(2)}, u32[]{:S(2)}) collective-permute-start(f32[256,512]{1,0:T(8,128)S(1)} %bitcast.200), channel_id=1, source_target_pairs={{0,32},{1,33},{2,34},{3,35},{4,36},{5,37},{6,38},{7,39},{8,40},{9,... | collective-permute-start | bytes 1572872 | tf_op jit(solution)/shard_map/ppermute | solution.py:28
  119.0 29.7 %collective-permute-start.51 = (f32[2,64,512]{2,1,0:T(8,128)S(1)}, f32[2,64,512]{2,1,0:T(8,128)S(1)}, u32[]{:S(2)}, u32[]{:S(2)}) collective-permute-start(f32[2,64,512]{2,1,0:T(8,128)S(1)} %get-tuple-element.157), channel_id=1, source_target_pairs={{0,2},{1,3},{2,4},{3,5},{4,6},{5,7},{6,0},{7,1},{8,10},{9,11},{10,... | collective-permute-start | bytes 786440 | tf_op jit(solution)/shard_map/ppermute | solution.py:28
  125.4 26.2 %collective-permute-start.50 = (f32[2,64,512]{2,1,0:T(8,128)S(1)}, f32[2,64,512]{2,1,0:T(8,128)S(1)}, u32[]{:S(2)}, u32[]{:S(2)}) collective-permute-start(f32[2,64,512]{2,1,0:T(8,128)S(1)} %get-tuple-element.157), channel_id=1, source_target_pairs={{0,4},{1,5},{2,6},{3,7},{4,0},{5,1},{6,2},{7,3},{8,12},{9,13},{10,... | collective-permute-start | bytes 786440 | tf_op jit(solution)/shard_map/ppermute | solution.py:28
  128.8 23.1 %collective-permute-start.49 = (f32[2,64,512]{2,1,0:T(8,128)S(1)}, f32[2,64,512]{2,1,0:T(8,128)S(1)}, u32[]{:S(2)}, u32[]{:S(2)}) collective-permute-start(f32[2,64,512]{2,1,0:T(8,128)S(1)} %get-tuple-element.157), channel_id=1, source_target_pairs={{0,6},{1,7},{2,0},{3,1},{4,2},{5,3},{6,4},{7,5},{8,14},{9,15},{10,... | collective-permute-start | bytes 786440 | tf_op jit(solution)/shard_map/ppermute | solution.py:28
  133.6 8.7 %collective-permute-start.29 = (f32[128,256]{1,0:T(8,128)S(1)}, f32[128,256]{1,0:T(8,128)S(1)}, u32[]{:S(2)}, u32[]{:S(2)}) collective-permute-start(f32[128,256]{1,0:T(8,128)S(1)} %get-tuple-element.41), channel_id=1, source_target_pairs={{0,6},{1,7},{2,0},{3,1},{4,2},{5,3},{6,4},{7,5},{8,14},{9,15},{10,... | collective-permute-start | bytes 393224 | tf_op jit(solution)/shard_map/ppermute | solution.py:28
  134.5 8.6 %collective-permute-start.28 = (f32[128,256]{1,0:T(8,128)S(1)}, f32[128,256]{1,0:T(8,128)S(1)}, u32[]{:S(2)}, u32[]{:S(2)}) collective-permute-start(f32[128,256]{1,0:T(8,128)S(1)} %get-tuple-element.40), channel_id=1, source_target_pairs={{0,4},{1,5},{2,6},{3,7},{4,0},{5,1},{6,2},{7,3},{8,12},{9,13},{10,... | collective-permute-start | bytes 393224 | tf_op jit(solution)/shard_map/ppermute | solution.py:28
  143.1 15.0 %collective-permute-start.42 = (f32[256,256]{1,0:T(8,128)S(1)}, f32[256,256]{1,0:T(8,128)S(1)}, u32[]{:S(2)}, u32[]{:S(2)}) collective-permute-start(f32[256,256]{1,0:T(8,128)S(1)} %get-tuple-element.124), channel_id=1, source_target_pairs={{0,32},{1,33},{2,34},{3,35},{4,36},{5,37},{6,38},{7,39},{8,40},{9,... | collective-permute-start | bytes 786440 | tf_op jit(solution)/shard_map/ppermute | solution.py:28
  157.5 16.8 %collective-permute-start.52 = (f32[256,512]{1,0:T(8,128)S(1)}, f32[256,512]{1,0:T(8,128)S(1)}, u32[]{:S(2)}, u32[]{:S(2)}) collective-permute-start(f32[256,512]{1,0:T(8,128)S(1)} %bitcast.204), channel_id=1, source_target_pairs={{0,32},{1,33},{2,34},{3,35},{4,36},{5,37},{6,38},{7,39},{8,40},{9,... | collective-permute-start | bytes 1572872 | tf_op jit(solution)/shard_map/ppermute | solution.py:28
  163.2 9.0 %collective-permute-start.43 = (f32[128,256]{1,0:T(8,128)S(1)}, f32[128,256]{1,0:T(8,128)S(1)}, u32[]{:S(2)}, u32[]{:S(2)}) collective-permute-start(f32[128,256]{1,0:T(8,128)S(1)} %get-tuple-element.43), channel_id=1, source_target_pairs={{0,8},{1,9},{2,10},{3,11},{4,12},{5,13},{6,14},{7,15},{8,16},{9,17... | collective-permute-start | bytes 393224 | tf_op jit(solution)/shard_map/ppermute | solution.py:28
  173.4 8.6 %collective-permute-start.48 = (f32[128,256]{1,0:T(8,128)S(1)}, f32[128,256]{1,0:T(8,128)S(1)}, u32[]{:S(2)}, u32[]{:S(2)}) collective-permute-start(f32[128,256]{1,0:T(8,128)S(1)} %add_add_fusion.2.y0), channel_id=1, source_target_pairs={{0,8},{1,9},{2,10},{3,11},{4,12},{5,13},{6,14},{7,15},{8,16},{9,17... | collective-permute-start | bytes 393224 | tf_op jit(solution)/shard_map/ppermute | solution.py:28
  183.4 9.3 %collective-permute-start.55 = (f32[128,256]{1,0:T(8,128)S(1)}, f32[128,256]{1,0:T(8,128)S(1)}, u32[]{:S(2)}, u32[]{:S(2)}) collective-permute-start(f32[128,256]{1,0:T(8,128)S(1)} %get-tuple-element.49), channel_id=1, source_target_pairs={{0,65},{1,0},{2,67},{3,2},{4,69},{5,4},{6,71},{7,6},{8,73},{9,8},{... | collective-permute-start | bytes 393224 | tf_op jit(solution)/shard_map/ppermute | solution.py:28
  183.8 8.9 %collective-permute-start.54 = (f32[128,256]{1,0:T(8,128)S(1)}, f32[128,256]{1,0:T(8,128)S(1)}, u32[]{:S(2)}, u32[]{:S(2)}) collective-permute-start(f32[128,256]{1,0:T(8,128)S(1)} %get-tuple-element.48), channel_id=1, source_target_pairs={{0,64},{1,65},{2,66},{3,67},{4,68},{5,69},{6,70},{7,71},{8,72},{9,... | collective-permute-start | bytes 393224 | tf_op jit(solution)/shard_map/ppermute | solution.py:28
  193.3 14.0 %collective-permute-start.58 = (f32[128,256]{1,0:T(8,128)S(1)}, f32[128,256]{1,0:T(8,128)S(1)}, u32[]{:S(2)}, u32[]{:S(2)}) collective-permute-start(f32[128,256]{1,0:T(8,128)S(1)} %fusion.26), channel_id=1, source_target_pairs={{0,1},{1,64},{2,3},{3,66},{4,5},{5,68},{6,7},{7,70},{8,9},{9,72},{... | collective-permute-start | bytes 393224 | tf_op jit(solution)/shard_map/ppermute | solution.py:28
  196.1 18.0 %collective-permute-start.57 = (f32[128,256]{1,0:T(8,128)S(1)}, f32[128,256]{1,0:T(8,128)S(1)}, u32[]{:S(2)}, u32[]{:S(2)}) collective-permute-start(f32[128,256]{1,0:T(8,128)S(1)} %fusion.26), channel_id=1, source_target_pairs={{0,64},{1,65},{2,66},{3,67},{4,68},{5,69},{6,70},{7,71},{8,72},{9,... | collective-permute-start | bytes 393224 | tf_op jit(solution)/shard_map/ppermute | solution.py:28
  206.4 8.8 %collective-permute-start.56 = (f32[128,256]{1,0:T(8,128)S(1)}, f32[128,256]{1,0:T(8,128)S(1)}, u32[]{:S(2)}, u32[]{:S(2)}) collective-permute-start(f32[128,256]{1,0:T(8,128)S(1)} %fusion.26), channel_id=1, source_target_pairs={{0,65},{1,0},{2,67},{3,2},{4,69},{5,4},{6,71},{7,6},{8,73},{9,8},{... | collective-permute-start | bytes 393224 | tf_op jit(solution)/shard_map/ppermute | solution.py:28
  216.1 15.0 %collective-permute-start.73 = (f32[256,512]{1,0:T(8,128)S(1)}, f32[256,512]{1,0:T(8,128)S(1)}, u32[]{:S(2)}, u32[]{:S(2)}) collective-permute-start(f32[256,512]{1,0:T(8,128)S(1)} %bitcast.206), channel_id=1, source_target_pairs={{0,32},{1,33},{2,34},{3,35},{4,36},{5,37},{6,38},{7,39},{8,40},{9,... | collective-permute-start | bytes 1572872 | tf_op jit(solution)/shard_map/ppermute | solution.py:28
  219.1 9.8 %collective-permute-start.64 = (f32[128,256]{1,0:T(8,128)S(1)}, f32[128,256]{1,0:T(8,128)S(1)}, u32[]{:S(2)}, u32[]{:S(2)}) collective-permute-start(f32[128,256]{1,0:T(8,128)S(1)} %get-tuple-element.51), channel_id=1, source_target_pairs={{0,8},{1,9},{2,10},{3,11},{4,12},{5,13},{6,14},{7,15},{8,16},{9,17... | collective-permute-start | bytes 393224 | tf_op jit(solution)/shard_map/ppermute | solution.py:28
  230.1 8.7 %collective-permute-start.69 = (f32[128,256]{1,0:T(8,128)S(1)}, f32[128,256]{1,0:T(8,128)S(1)}, u32[]{:S(2)}, u32[]{:S(2)}) collective-permute-start(f32[128,256]{1,0:T(8,128)S(1)} %add_add_fusion.1.y0), channel_id=1, source_target_pairs={{0,8},{1,9},{2,10},{3,11},{4,12},{5,13},{6,14},{7,15},{8,16},{9,17... | collective-permute-start | bytes 393224 | tf_op jit(solution)/shard_map/ppermute | solution.py:28
  242.5 8.7 %collective-permute-start.74 = (f32[128,256]{1,0:T(8,128)S(1)}, f32[128,256]{1,0:T(8,128)S(1)}, u32[]{:S(2)}, u32[]{:S(2)}) collective-permute-start(f32[128,256]{1,0:T(8,128)S(1)} %get-tuple-element.55), channel_id=1, source_target_pairs={{0,2},{1,3},{2,4},{3,5},{4,6},{5,7},{6,0},{7,1},{8,10},{9,11},{10,... | collective-permute-start | bytes 393224 | tf_op jit(solution)/shard_map/ppermute | solution.py:28
  251.2 9.2 %collective-permute-start.79 = (f32[128,256]{1,0:T(8,128)S(1)}, f32[128,256]{1,0:T(8,128)S(1)}, u32[]{:S(2)}, u32[]{:S(2)}) collective-permute-start(f32[128,256]{1,0:T(8,128)S(1)} %fusion.29), channel_id=1, source_target_pairs={{0,2},{1,3},{2,4},{3,5},{4,6},{5,7},{6,0},{7,1},{8,10},{9,11},{10,... | collective-permute-start | bytes 393224 | tf_op jit(solution)/shard_map/ppermute | solution.py:28
  251.3 9.1 %collective-permute-start.78 = (f32[128,256]{1,0:T(8,128)S(1)}, f32[128,256]{1,0:T(8,128)S(1)}, u32[]{:S(2)}, u32[]{:S(2)}) collective-permute-start(f32[128,256]{1,0:T(8,128)S(1)} %fusion.29), channel_id=1, source_target_pairs={{0,4},{1,5},{2,6},{3,7},{4,0},{5,1},{6,2},{7,3},{8,12},{9,13},{10,... | collective-permute-start | bytes 393224 | tf_op jit(solution)/shard_map/ppermute | solution.py:28
  263.1 14.3 %collective-permute-start.88 = (f32[256,512]{1,0:T(8,128)S(1)}, f32[256,512]{1,0:T(8,128)S(1)}, u32[]{:S(2)}, u32[]{:S(2)}) collective-permute-start(f32[256,512]{1,0:T(8,128)S(1)} %bitcast.198), channel_id=1, source_target_pairs={{0,32},{1,33},{2,34},{3,35},{4,36},{5,37},{6,38},{7,39},{8,40},{9,... | collective-permute-start | bytes 1572872 | tf_op jit(solution)/shard_map/ppermute | solution.py:28
  265.5 9.8 %collective-permute-start.82 = (f32[128,256]{1,0:T(8,128)S(1)}, f32[128,256]{1,0:T(8,128)S(1)}, u32[]{:S(2)}, u32[]{:S(2)}) collective-permute-start(f32[128,256]{1,0:T(8,128)S(1)} %get-tuple-element.59), channel_id=1, source_target_pairs={{0,8},{1,9},{2,10},{3,11},{4,12},{5,13},{6,14},{7,15},{8,16},{9,17... | collective-permute-start | bytes 393224 | tf_op jit(solution)/shard_map/ppermute | solution.py:28
  276.4 9.0 %collective-permute-start.87 = (f32[128,256]{1,0:T(8,128)S(1)}, f32[128,256]{1,0:T(8,128)S(1)}, u32[]{:S(2)}, u32[]{:S(2)}) collective-permute-start(f32[128,256]{1,0:T(8,128)S(1)} %add_add_fusion.y0), channel_id=1, source_target_pairs={{0,8},{1,9},{2,10},{3,11},{4,12},{5,13},{6,14},{7,15},{8,16},{9,17... | collective-permute-start | bytes 393224 | tf_op jit(solution)/shard_map/ppermute | solution.py:28
  286.7 9.3 %collective-permute-start.91 = (f32[128,256]{1,0:T(8,128)S(1)}, f32[128,256]{1,0:T(8,128)S(1)}, u32[]{:S(2)}, u32[]{:S(2)}) collective-permute-start(f32[128,256]{1,0:T(8,128)S(1)} %get-tuple-element.65), channel_id=1, source_target_pairs={{0,65},{1,0},{2,67},{3,2},{4,69},{5,4},{6,71},{7,6},{8,73},{9,8},{... | collective-permute-start | bytes 393224 | tf_op jit(solution)/shard_map/ppermute | solution.py:28
  286.8 9.2 %collective-permute-start.90 = (f32[128,256]{1,0:T(8,128)S(1)}, f32[128,256]{1,0:T(8,128)S(1)}, u32[]{:S(2)}, u32[]{:S(2)}) collective-permute-start(f32[128,256]{1,0:T(8,128)S(1)} %get-tuple-element.64), channel_id=1, source_target_pairs={{0,64},{1,65},{2,66},{3,67},{4,68},{5,69},{6,70},{7,71},{8,72},{9,... | collective-permute-start | bytes 393224 | tf_op jit(solution)/shard_map/ppermute | solution.py:28
  297.8 17.0 %collective-permute-start.92 = (f32[4,64,256]{2,1,0:T(8,128)S(1)}, f32[4,64,256]{2,1,0:T(8,128)S(1)}, u32[]{:S(2)}, u32[]{:S(2)}) collective-permute-start(f32[4,64,256]{2,1,0:T(8,128)S(1)} %slice_select_fusion.2), channel_id=1, source_target_pairs={{0,32},{1,33},{2,34},{3,35},{4,36},{5,37},{6,38},{7,39},{8,40},{9,... | collective-permute-start | bytes 786440 | tf_op jit(solution)/shard_map/ppermute | solution.py:28
  298.0 22.0 %collective-permute-start.101 = (f32[64,512]{1,0:T(8,128)S(1)}, f32[64,512]{1,0:T(8,128)S(1)}, u32[]{:S(2)}, u32[]{:S(2)}) collective-permute-start(f32[64,512]{1,0:T(8,128)S(1)} %get-tuple-element.83), channel_id=1, source_target_pairs={{0,96},{1,8},{2,0},{3,40},{4,48},{5,72},{6,64},{7,120},{8,98},{9,1... | collective-permute-start | bytes 393224 | tf_op jit(solution)/shard_map/ppermute | solution.py:28
  299.9 22.0 %collective-permute-start.100 = (f32[64,512]{1,0:T(8,128)S(1)}, f32[64,512]{1,0:T(8,128)S(1)}, u32[]{:S(2)}, u32[]{:S(2)}) collective-permute-start(f32[64,512]{1,0:T(8,128)S(1)} %get-tuple-element.82), channel_id=1, source_target_pairs={{0,64},{1,96},{2,104},{3,8},{4,0},{5,48},{6,56},{7,72},{8,66},{9,9... | collective-permute-start | bytes 393224 | tf_op jit(solution)/shard_map/ppermute | solution.py:28
  304.9 24.2 %collective-permute-start.99 = (f32[64,512]{1,0:T(8,128)S(1)}, f32[64,512]{1,0:T(8,128)S(1)}, u32[]{:S(2)}, u32[]{:S(2)}) collective-permute-start(f32[64,512]{1,0:T(8,128)S(1)} %get-tuple-element.81), channel_id=1, source_target_pairs={{0,32},{1,72},{2,64},{3,104},{4,112},{5,8},{6,0},{7,56},{8,34},{9,... | collective-permute-start | bytes 393224 | tf_op jit(solution)/shard_map/ppermute | solution.py:28
  312.9 18.2 %collective-permute-start.98 = (f32[64,512]{1,0:T(8,128)S(1)}, f32[64,512]{1,0:T(8,128)S(1)}, u32[]{:S(2)}, u32[]{:S(2)}) collective-permute-start(f32[64,512]{1,0:T(8,128)S(1)} %get-tuple-element.80), channel_id=1, source_target_pairs={{0,0},{1,32},{2,40},{3,72},{4,64},{5,112},{6,120},{7,8},{8,2},{9,3... | collective-permute-start | bytes 393224 | tf_op jit(solution)/shard_map/ppermute | solution.py:28
  315.0 16.2 %collective-permute-start.96 = (f32[64,512]{1,0:T(8,128)S(1)}, f32[64,512]{1,0:T(8,128)S(1)}, u32[]{:S(2)}, u32[]{:S(2)}) collective-permute-start(f32[64,512]{1,0:T(8,128)S(1)} %get-tuple-element.91), channel_id=1, source_target_pairs={{0,96},{1,2},{2,0},{3,34},{4,36},{5,66},{6,64},{7,102},{8,104},{9,... | collective-permute-start | bytes 393224 | tf_op jit(solution)/shard_map/ppermute | solution.py:28
  320.0 11.2 %collective-permute-start.95 = (f32[64,512]{1,0:T(8,128)S(1)}, f32[64,512]{1,0:T(8,128)S(1)}, u32[]{:S(2)}, u32[]{:S(2)}) collective-permute-start(f32[64,512]{1,0:T(8,128)S(1)} %get-tuple-element.90), channel_id=1, source_target_pairs={{0,64},{1,96},{2,98},{3,2},{4,0},{5,36},{6,38},{7,66},{8,72},{9,10... | collective-permute-start | bytes 393224 | tf_op jit(solution)/shard_map/ppermute | solution.py:28
  322.0 11.2 %collective-permute-start.94 = (f32[64,512]{1,0:T(8,128)S(1)}, f32[64,512]{1,0:T(8,128)S(1)}, u32[]{:S(2)}, u32[]{:S(2)}) collective-permute-start(f32[64,512]{1,0:T(8,128)S(1)} %get-tuple-element.89), channel_id=1, source_target_pairs={{0,32},{1,66},{2,64},{3,98},{4,100},{5,2},{6,0},{7,38},{8,40},{9,7... | collective-permute-start | bytes 393224 | tf_op jit(solution)/shard_map/ppermute | solution.py:28
  329.1 9.9 %collective-permute-start.93 = (f32[64,512]{1,0:T(8,128)S(1)}, f32[64,512]{1,0:T(8,128)S(1)}, u32[]{:S(2)}, u32[]{:S(2)}) collective-permute-start(f32[64,512]{1,0:T(8,128)S(1)} %get-tuple-element.88), channel_id=1, source_target_pairs={{0,0},{1,32},{2,34},{3,66},{4,64},{5,100},{6,102},{7,2},{8,8},{9,4... | collective-permute-start | bytes 393224 | tf_op jit(solution)/shard_map/ppermute | solution.py:28
  (50 other events, 575.4 us)

commit v2 on v0

v2 whole, which is shorter than its diff:
```python
import functools

import jax
import jax.numpy as jnp
import numpy as np
from jax import lax
from jax.experimental import pallas as pl
from jax.experimental.pallas import tpu as pltpu
from jax.sharding import Mesh, PartitionSpec as P

TILE = 128
AXES = ("xh", "co", "z", "y", "xl")
SIZES = (2, 2, 4, 4, 2)
X, Y, Z, C, XL, ZH, LANE = range(7)


def route(place, only=None):
    pairs = []
    for i in range(int(np.prod(SIZES))):
        xh, co, z, y, xl = (int(v) for v in np.unravel_index(i, SIZES))
        at = dict(x=2 * xh + xl, y=y, z=z, co=co)
        if only is not None and not only(**at):
            continue
        at = place(**at)
        to = (at["x"] // 2, at["co"], at["z"], at["y"], at["x"] % 2)
        pairs.append((i, int(np.ravel_multi_index(to, SIZES))))
    assert len({b for _, b in pairs}) == len(pairs)
    return pairs


def send(x, place, only=None):
    return lax.ppermute(x, AXES, route(place, only))


def shifted(axis, by):
    def place(**at):
        return {**at, axis: (at[axis] + by) % 4}

    return place


def to_other_core(**at):
    return {**at, "co": 1 - at["co"]}


def deal(by):
    def place(**at):
        axis = "z" if at["co"] else "y"
        return {**at, axis: (at[axis] + by) % 4}

    return place


def x_pair(**at):
    return {**at, "x": at["x"] ^ 1}


def gathered(x, axis):
    return [x] + [send(x, shifted(axis, -r)) for r in (1, 2, 3)]


def scattered(parts, axis):
    total = parts[0]
    for r in (1, 2, 3):
        total = total + send(parts[r], shifted(axis, r))
    return total


def split(x):
    hi = x.astype(jnp.bfloat16)
    lo = (x - hi.astype(jnp.float32)).astype(jnp.bfloat16)
    return hi, lo


def dot_cols(a, b):
    dims = (((0,), (0,)), ((), ()))
    mm = functools.partial(
        lax.dot_general, dimension_numbers=dims, preferred_element_type=jnp.float32
    )
    a_hi, a_lo = split(a)
    b_hi, b_lo = split(b)
    return mm(a_hi, b_hi) + (mm(a_hi, b_lo) + mm(a_lo, b_hi))


def dot_rows(a, b_hi, b_lo):
    a_hi, a_lo = split(a)
    mm = functools.partial(jnp.dot, preferred_element_type=jnp.float32)
    return mm(a_hi, b_hi) + (mm(a_hi, b_lo) + mm(a_lo, b_hi))


def put_parts(value, turn_by, outs):
    for r, o in enumerate(outs):
        rows = pl.multiple_of(lax.rem(turn_by + r, 4) * 128, 128)
        o[...] = value[pl.ds(rows, 128), :]


def cross_of(at, x_own, x_sib, a, y, outs):
    p, c = at[Z], at[C]
    for ref, half in ((x_own, c), (x_sib, 1 - c)):
        rows = pl.multiple_of(256 * half, 256)
        y[pl.ds(rows, 256), :] = dot_cols(ref[...], a[...])
    put_parts(y, p, outs)


def cross_tail_kernel(at, t_own, t_one, t_two, a0, a1, a2, a3, o0, o1, o2, o3, a, y):
    c, q, even = at[C], at[Y], at[XL]
    for r, piece in enumerate((a0, a1, a2, a3)):
        rows = pl.multiple_of(lax.rem(q + r, 4) * 128, 128)
        a[pl.ds(rows, 128), :] = piece[...]
    a_hi, a_lo = split(a[...])

    def put(rows_of, count, first, half):
        part = dot_rows(rows_of[...].reshape(count * 64, 512), a_hi, a_lo)
        for i in range(count):
            rows = pl.multiple_of(128 * (first + i) + 64 * half, 64)
            y[pl.ds(rows, 64), :] = part[64 * i : 64 * i + 64]

    put(t_own, 4, 0, even)
    put(t_one, 2, 2 * c, 1 - even)
    put(t_two, 2, 2 * (1 - c), 1 - even)
    put_parts(y, at[Z], (o0, o1, o2, o3))


def cross_even_kernel(which, at, x_own, x_sib, a_all, o0, o1, o2, o3, a, y):
    q, c = at[Y], at[C]
    for r in range(4):
        a[pl.ds(128 * r, 128), :] = a_all[2 * lax.rem(q + r, 4) + c, which]
    cross_of(at, x_own, x_sib, a, y, (o0, o1, o2, o3))


def cross_odd_kernel(at, x_own, x_sib, a_all, o0, o1, o2, o3, a, y):
    q, c = at[X], at[C]
    for r in range(4):
        for h in range(2):
            a[pl.ds(128 * r, 128), pl.ds(128 * h, 128)] = a_all[2 * lax.rem(q + r, 4) + c, h]
    cross_of(at, x_own, x_sib, a, y, (o0, o1, o2, o3))


def close_odd_kernel(which, at, y0, y1, y2, y3, b_all, o0, o1, o2, o3, b, y, x):
    p, q = at[Z], at[Y]
    for r, piece in enumerate((y0, y1, y2, y3)):
        y[pl.ds(128 * r, 128), :] = piece[...]
        for h in range(2):
            b[pl.ds(128 * r, 128), pl.ds(256 * h, 256)] = b_all[2 * lax.rem(p + r, 4) + h, which]
    x[...] = dot_cols(b[...], y[...])
    put_parts(x, q, (o0, o1, o2, o3))


def close_even_kernel(skip, at, y0, y1, y2, y3, b_all, o0, o1, o2, o3, b, y, x):
    p, q, h = at[Z], at[X], at[ZH]
    for r, piece in enumerate((y0, y1, y2, y3)):
        y[pl.ds(128 * r, 128), :] = piece[...]
        for j in range(4):
            block = b_all[2 * j + h, skip + lax.rem(p + r, 4)]
            b[pl.ds(128 * r, 128), pl.ds(128 * j, 128)] = block
    x[...] = dot_cols(b[...], y[...])
    put_parts(x, q, (o0, o1, o2, o3))


def deal_kernel(at, factor, local, tail, *outs):
    for r, out in enumerate(outs):
        for k in range(4):
            v = lax.rem(at[LANE] + r, 4)
            col = jnp.where(at[C] == 0, 512 * k + 128 * v, 512 * v + 128 * k)
            cols = pl.ds(pl.multiple_of(col, 128), 128)
            out[0, :, pl.ds(128 * k, 128)] = factor[:, cols]
            out[1, :, pl.ds(128 * k, 128)] = jnp.where(at[C] == 0, local[:, cols], tail[:, cols])


def pair_kernel(at, d0, d1, d2, d3, factor, local, keep, give):
    low, high = pl.ds(0, 256), pl.ds(256, 256)

    @pl.when(at[C] == 0)
    def _():
        for r, d in enumerate((d0, d1, d2, d3)):
            s = lax.rem(at[LANE] + 4 - r, 4)
            for k in range(2):
                keep[s, k] = d[k, :, low]
                give[s, k] = d[k, :, high]
        for s in range(4):
            for k in range(2, 5):
                give[s, k] = jnp.zeros((64, 256), jnp.float32)
                keep[s, k] = jnp.zeros((64, 256), jnp.float32)

    @pl.when(at[C] == 1)
    def _():
        for r, d in enumerate((d0, d1, d2, d3)):
            s = lax.rem(at[LANE] + 4 - r, 4)
            keep[s, 1] = d[0, :, high]
            give[s, 1] = d[0, :, low]
            for h, cols in enumerate((low, high)):
                keep[s, 3 + h] = d[1, :, cols]
                give[s, 3 + h] = d[1, :, cols]
        for s in range(4):
            for k, ref in ((0, factor), (2, local)):
                for i in range(2):
                    here = pl.ds(128 * i, 128)
                    give[s, k, :, here] = ref[:, pl.ds(512 * i + 128 * s, 128)]
                    keep[s, k, :, here] = ref[:, pl.ds(512 * (i + 2) + 128 * s, 128)]


def row_kernel(at, keep, got, a0, a1, a2, a3, b0, b1, b2, b3, t_all, t_half):
    def fill(odd, even):
        for r, (a, b) in enumerate(((a0, b0), (a1, b1), (a2, b2), (a3, b3))):
            s = lax.rem(at[X] + r, 4)
            a[0], a[1] = odd[s, 0], odd[s, 1]
            b[0], b[1], b[2] = odd[s, 2], even[s, 0], even[s, 1]
        for s in range(4):
            for h in range(2):
                t_all[s, :, pl.ds(256 * h, 256)] = odd[s, 3 + h]
        for i in range(2):
            for h in range(2):
                t_half[i, :, pl.ds(256 * h, 256)] = odd[2 * at[C] + i, 3 + h]

    @pl.when(at[C] == 0)
    def _():
        fill(got, keep)

    @pl.when(at[C] == 1)
    def _():
        fill(keep, got)


def from_x(at, r):
    s = lax.rem(at[X] + 4 - r, 4)
    return s // 2, pl.ds(pl.multiple_of(64 * lax.rem(s, 2), 64), 64)


def base_kernel(at, a0, a1, a2, a3, upper_one, upper_three, lower):
    for r, a in enumerate((a0, a1, a2, a3)):
        step, rows = from_x(at, r)
        lower[step, rows, :] = a[1]

        @pl.when(step == 0)
        def _():
            upper_one[rows, :] = a[0]

        @pl.when(step == 1)
        def _():
            upper_three[rows, :] = a[0]


def rest_kernel(at, b0, b1, b2, b3, l0, l1, l2, l3, upper, same, other):
    for r, b in enumerate((b0, b1, b2, b3)):
        step, rows = from_x(at, r)
        upper[step, rows, :] = b[1]
        for n, (odd, even) in enumerate(((l1, l0), (l3, l2))):

            @pl.when(step == n)
            def _():
                odd[rows, :] = b[0]
                even[rows, :] = b[2]

        swap = lax.rem(at[Z], 2)
        here = pl.ds(pl.multiple_of(128 * swap, 128), 128)
        there = pl.ds(pl.multiple_of(128 * (1 - swap), 128), 128)
        same[step, rows, :] = b[1, :, here]
        other[step, rows, :] = b[1, :, there]


def column_kernel(at, e0, e1, e2, e3, upper, first, second):
    for h in range(2):
        first[h] = upper[:, pl.ds(128 * h, 128)]
    for r, e in enumerate((e0, e1, e2, e3)):
        s = lax.rem(at[Z] + 4 - r, 4)
        first[2 + s] = e[1]
        second[s] = e[0]


def leave_kernel(at, *refs):
    kept, outs = refs[:8], refs[8:]
    for r, out in enumerate(outs):
        for s in range(4):

            @pl.when(lax.rem(at[X] + r, 4) == s)
            def _():
                for n in range(2):
                    for k in range(2):
                        ref = kept[2 * (2 * (s // 2) + n) + k]
                        out[n, k] = ref[pl.ds(64 * (s % 2), 64), :]


def meet_kernel(at, a0, a1, a2, a3, keep, give):
    for r, a in enumerate((a0, a1, a2, a3)):
        s = lax.rem(at[X] + 4 - r, 4)
        keep[s] = a[at[C]]
        give[s] = a[1 - at[C]]


def turn_kernel(at, keep, got, *outs):
    mine = pl.ds(pl.multiple_of(256 * at[C], 256), 256)
    theirs = pl.ds(pl.multiple_of(256 * (1 - at[C]), 256), 256)
    for r, out in enumerate(outs):
        s = lax.rem(at[Y] + r, 4)
        for k in range(2):
            out[k, :, mine] = keep[s, k]
            out[k, :, theirs] = got[s, k]


def finish_kernel(at, mask, d0, d1, d2, d3, g1, g2, g3, diag, off):
    def fill(parts, sign):
        for r, part in enumerate(parts):
            s = lax.rem(at[Y] + 4 + sign * r, 4)
            for k in range(4):
                cols = pl.ds(pl.multiple_of(512 * k + 128 * s, 128), 128)
                kept = mask[4 * k + s]
                diag[:, cols] = part[0, :, pl.ds(128 * k, 128)] * kept
                off[:, cols] = -part[1, :, pl.ds(128 * k, 128)] * kept

    @pl.when(at[C] == 0)
    def _():
        fill((d0, g1, g2, g3), -1)

    @pl.when(at[C] == 1)
    def _():
        fill((d0, d1, d2, d3), 1)


def local(kernel, at, args, shapes, scratch=(), flops=0, scalars=()):
    vmem = pl.BlockSpec(memory_space=pltpu.VMEM)
    smem = pl.BlockSpec(memory_space=pltpu.SMEM)
    moved = sum(int(np.prod(a.shape)) for a in args) + sum(int(np.prod(s)) for s in shapes)
    return pl.pallas_call(
        kernel,
        out_shape=[jax.ShapeDtypeStruct(s, jnp.float32) for s in shapes],
        in_specs=[smem] * (1 + len(scalars)) + [vmem] * len(args),
        out_specs=[vmem] * len(shapes),
        scratch_shapes=[pltpu.VMEM(s, jnp.float32) for s in scratch],
        compiler_params=pltpu.CompilerParams(vmem_limit_bytes=32 * 1024 * 1024),
        cost_estimate=pl.CostEstimate(flops=flops, bytes_accessed=4 * moved, transcendentals=0),
    )(at, *scalars, *args)


def product(kernel, at, args, scratch):
    return local(kernel, at, args, [(128, 256)] * 4, scratch, flops=6 * 512 * 512 * 256)


def ring(pieces, place, only=None):
    return [pieces[0]] + [send(pieces[r], place(r), only) for r in (1, 2, 3)]


def after(values, done):
    return lax.optimization_barrier((tuple(values), done))[0]


def on_device(inv_local, coupling, tail_block, adjacency):
    xh, co, z, y, xl = (lax.axis_index(a) for a in AXES)
    x = 2 * xh + xl
    at = jnp.stack([x, y, z, co, xl, z // 2, jnp.where(co == 0, y, z)]).astype(jnp.int32)
    along = {axis: functools.partial(shifted, axis) for axis in "xyz"}

    factor, own, tail = coupling[0], inv_local[0], tail_block
    dealt = ring(local(deal_kernel, at, [factor, own, tail], [(2, 64, 512)] * 4), deal)
    keep, give = local(pair_kernel, at, dealt + [factor, own], [(4, 5, 64, 256)] * 2)
    got = send(give, to_other_core)
    *rows, t_all, t_half = local(
        row_kernel,
        at,
        [keep, got],
        [(2, 64, 256)] * 4 + [(3, 64, 256)] * 4 + [(4, 64, 512), (2, 64, 512)],
    )
    first = ring(rows[:4], along["x"])
    t_one = send(t_half, x_pair)
    t_two = send(t_one, to_other_core)
    upper_one, upper_three, lower_odd = local(
        base_kernel, at, first, [(128, 256), (128, 256), (2, 128, 256)]
    )
    on_x = lax.all_gather(lower_odd, ("xh", "xl", "co"))
    pieces = gathered(upper_three, "y")
    wide, square = (512, 256), (512, 512)
    parts = product(cross_tail_kernel, at, [t_all, t_one, t_two] + pieces, [wide, wide])

    rest = ring(after(rows[4:], parts[0]), along["x"])
    l0, l1, l2, l3, upper_even, same, other = local(
        rest_kernel, at, rest, [(128, 256)] * 4 + [(2, 128, 256)] + [(2, 128, 128)] * 2
    )
    locals_ = [l0, l1, l2, l3]
    cross = scattered(parts, "z")
    crosses, blocks = {3: cross}, {}

    on_x_even = lax.all_gather(upper_even, ("xh", "xl", "co"))
    same, other = after([same, other], cross)
    columns = [same]
    for r, block in ((1, other), (2, same), (3, other)):
        aimed = lambda z, co, **_: ((z + r) % 4) // 2 == co
        columns.append(send(block, along["z"](r), aimed))
    on_y, on_y_last = local(
        column_kernel, at, columns + [upper_one], [(6, 128, 128), (4, 128, 128)]
    )
    on_y = lax.all_gather(on_y, ("y", "co"))
    on_y_last = lax.all_gather(on_y_last, ("y", "co"))

    for t in (3, 2, 1, 0):
        first, second = ("y", "x") if t % 2 else ("x", "y")
        if t < 3:
            x_own = jnp.concatenate(gathered(blocks[t + 1], second))
            x_sib = send(x_own, to_other_core)
            if t % 2:
                kernel, a_all = cross_odd_kernel, on_y
            else:
                kernel, a_all = functools.partial(cross_even_kernel, t // 2), on_x_even
            cross = scattered(product(kernel, at, [x_own, x_sib, a_all], [wide, wide]), "z")
            crosses[t] = cross
        if t % 2:
            kernel, b_all = functools.partial(close_odd_kernel, t // 2), on_x
        else:
            kernel = functools.partial(close_even_kernel, 2 if t else 0)
            b_all = on_y if t else on_y_last
        parts = product(kernel, at, gathered(cross, "z") + [b_all], [square, wide, wide])
        blocks[t] = scattered(parts, first) + locals_[t]

    outs = [a[t] for t in range(4) for a in (blocks, crosses)]
    outs = ring(local(leave_kernel, at, outs, [(2, 2, 64, 256)] * 4), along["x"])
    keep, give = local(meet_kernel, at, outs, [(4, 2, 64, 256)] * 2)
    got = send(give, to_other_core)
    turned = local(turn_kernel, at, [keep, got], [(2, 64, 512)] * 4)
    back = ring(turned, along["y"], lambda co, **_: co == 0)

    count = adjacency.shape[0]
    joined = jnp.maximum(adjacency, jnp.eye(count, dtype=jnp.int32)).astype(jnp.float32)
    mask = lax.dynamic_index_in_dim(joined, (z * 8 + y * 2 + xl) * 64 // TILE, 0, keepdims=False)
    diag, off = local(
        finish_kernel, at, list(turned) + back[1:], [(64, 2048)] * 2, scalars=[mask]
    )
    return diag[None], off[None]


def solution(mesh):
    fine = Mesh(mesh.devices.reshape(SIZES), AXES)
    rows = P(("xh", "co"), ("z", "y", "xl"), None)
    return jax.shard_map(
        on_device,
        mesh=fine,
        in_specs=(rows, rows, P(("z", "y", "xl"), None), P()),
        out_specs=(rows, rows),
        check_vma=False,
    )
```

time: 1250 us -> 316 us (0.25)
  waiting for transfers between devices: 1000 us -> 188 us
  matrix products: 158 us -> 0 us
  starting transfers between devices: 26.5 us -> 82 us
  blocking collectives: 24.8 us -> 0 us
  Pallas kernels: 0 us -> 19.8 us
    all_gather x3 -> x4, waiting for transfers between devices: 923 us -> 0.03 us  [the longest x1 0.02 us: on_device(): on_x_even = lax.all_gather(upper_even, ('xh', 'xl', 'co'))]
    ppermute x5 -> x73, waiting for transfers between devices: 58.9 us -> 188 us  [send(): return lax.ppermute(x, AXES, route(place, only))]
    dot_general x8 -> x0, matrix products: 99.8 us -> none  [the longest x3 41.5 us: on_device(): quadratic = jnp.dot(turned.T, gathered, precision=highest)]
    ppermute x5 -> x73, starting transfers between devices: 11.8 us -> 81.8 us  [send(): return lax.ppermute(x, AXES, route(place, only))]
    all_to_all x2 -> x0, matrix products: 57.8 us -> none  [on_device(): lax.all_to_all(half_product, 'space', split_axis=1, concat_axis=0, tiled=...]
    all_to_all x1 -> x0, blocking collectives: 24.8 us -> none  [on_device(): lax.all_to_all(half_product, 'space', split_axis=1, concat_axis=0, tiled=...]
    pallas_call x0 -> x18, Pallas kernels: none -> 19.8 us  [local(): pl.pallas_call(kernel, out_shape=[jax.ShapeDtypeStruct(s, jnp.float32) fo...]
    all_to_all x2 -> x0, waiting for transfers between devices: 17.6 us -> none  [on_device(): lax.all_to_all(half_product, 'space', split_axis=1, concat_axis=0, tiled=...]
  transfers between devices with their start and end apart: 10 -> 77, of which waited for: 9 -> 64; matrix products, arithmetic and copies ran while one was open for 8% -> 0% of each run, Pallas kernels for 0% -> 4%
where the time goes in v2:
time: 316 us; the launch traced here: 315 us
  waiting for transfers between devices  188 us (59%)
  starting transfers between devices  82 us (26%)
  Pallas kernels  19.8 us (6%)
  between operations  14.2 us (4%)
  local copies, waits for them, and re-layouts  9.97 us (3%)
    ppermute x73, waiting for transfers between devices, send(): return lax.ppermute(x, AXES, route(place, only))  188 us
    ppermute x73, starting transfers between devices, send(): return lax.ppermute(x, AXES, route(place, only))  81.8 us
    pallas_call x18, Pallas kernels, local(): pl.pallas_call(kernel, out_shape=[jax.ShapeDtypeStruct(s, jnp.float32) fo...  19.8 us
    unnamed x20, local copies, waits for them, and re-layouts  9.89 us
  transfers between devices with their start and end apart: 77, of which 64 were waited for; matrix products, arithmetic and copies ran while one was open for 0% of the time, Pallas kernels for 4%

profile of v2, /device:TPU:6, one launch (start us, length us, event | category | flops | bytes accessed | tf_op | source)
XLA Modules:
  0.0 314.8 jit_solution(6895304170129709548)
XLA Ops:
  12.9 2.9 collective-permute-start.1
  18.9 4.0 %collective-permute-done.1.d2 = f32[2,64,512]{2,1,0:T(8,128)S(1)} collective-permute-done((f32[2,64,512]{2,1,0:T(8,128)S(1)}, f32[2,64,512]{2,1,0:T(8,128)S(1)}, u32[]{:S(2)}, u32[]{:S(2)}) %collective-permute-start.1) | collective-permute-done | bytes 262176 | tf_op jit(solution)/shard_map/ppermute | solution.py:32
  23.8 3.0 collective-permute-done.3.got
  28.0 2.4 collective-permute-start.7
  30.4 3.4 %collective-permute-done.6.a1 = f32[2,64,256]{2,1,0:T(8,128)S(1)} collective-permute-done((f32[2,64,256]{2,1,0:T(8,128)S(1)}, f32[2,64,256]{2,1,0:T(8,128)S(1)}, u32[]{:S(2)}, u32[]{:S(2)}) %collective-permute-start.6) | collective-permute-done | bytes 131104 | tf_op jit(solution)/shard_map/ppermute | solution.py:32
  40.1 6.6 %collective-permute-done.4.t_one = f32[2,64,512]{2,1,0:T(8,128)S(1)} collective-permute-done((f32[2,64,512]{2,1,0:T(8,128)S(1)}, f32[2,64,512]{2,1,0:T(8,128)S(1)}, u32[]{:S(2)}, u32[]{:S(2)}) %collective-permute-start.4) | collective-permute-done | bytes 262176 | tf_op jit(solution)/shard_map/ppermute | solution.py:32
  46.7 2.8 collective-permute-start.9
  51.0 4.8 %collective-permute-done.9.a1 = f32[128,256]{1,0:T(8,128)S(1)} collective-permute-done((f32[128,256]{1,0:T(8,128)S(1)}, f32[128,256]{1,0:T(8,128)S(1)}, u32[]{:S(2)}, u32[]{:S(2)}) %collective-permute-start.9) | collective-permute-done | bytes 131104 | tf_op jit(solution)/shard_map/ppermute | solution.py:32
  57.4 2.1 collective-permute-done.11.a3
  63.7 4.8 %collective-permute-done.21.b1 = f32[3,64,256]{2,1,0:T(8,128)S(1)} collective-permute-done((f32[3,64,256]{2,1,0:T(8,128)S(1)}, f32[3,64,256]{2,1,0:T(8,128)S(1)}, u32[]{:S(2)}, u32[]{:S(2)}) %collective-permute-start.21) | collective-permute-done | bytes 196640 | tf_op jit(solution)/shard_map/ppermute | solution.py:32
  68.5 2.6 collective-permute-done.22.b2
  71.1 3.0 collective-permute-done.23.b3
  75.5 3.5 %collective-permute-start.14 = (f32[128,256]{1,0:T(8,128)S(1)}, f32[128,256]{1,0:T(8,128)S(1)}, u32[]{:S(2)}, u32[]{:S(2)}) collective-permute-start(f32[128,256]{1,0:T(8,128)S(1)} %get-tuple-element.96), channel_id=1, source_target_pairs={{0,24},{1,25},{2,26},{3,27},{4,28},{5,29},{6,30},{7,31},{8,0},{9,1... | collective-permute-start | bytes 393224 | tf_op jit(solution)/shard_map/ppermute | solution.py:32
  80.3 4.4 %collective-permute-done.14 = f32[128,256]{1,0:T(8,128)S(1)} collective-permute-done((f32[128,256]{1,0:T(8,128)S(1)}, f32[128,256]{1,0:T(8,128)S(1)}, u32[]{:S(2)}, u32[]{:S(2)}) %collective-permute-start.14) | collective-permute-done | bytes 131104 | tf_op jit(solution)/shard_map/ppermute | solution.py:32
  84.8 2.2 collective-permute-done.13
  88.2 1.9 collective-permute-start.34
  92.8 3.5 %collective-permute-done.34.e1 = f32[2,128,128]{2,1,0:T(8,128)S(1)} collective-permute-done((f32[2,128,128]{2,1,0:T(8,128)S(1)}, f32[2,128,128]{2,1,0:T(8,128)S(1)}, u32[]{:S(2)}, u32[]{:S(2)}) %collective-permute-start.34) | collective-permute-done | bytes 131104 | tf_op jit(solution)/shard_map/ppermute | solution.py:32
  96.3 2.2 collective-permute-done.35.e2
  100.1 4.0 %collective-permute-start.16 = (f32[128,256]{1,0:T(8,128)S(1)}, f32[128,256]{1,0:T(8,128)S(1)}, u32[]{:S(2)}, u32[]{:S(2)}) collective-permute-start(f32[128,256]{1,0:T(8,128)S(1)} %add_add_fusion.7.y0.refs_7_), channel_id=1, source_target_pairs={{0,16},{1,17},{2,18},{3,19},{4,20},{5,21},{6,22},{7,23},{8,24},{9,... | collective-permute-start | bytes 393224 | tf_op jit(solution)/shard_map/ppermute | solution.py:32
  104.1 2.3 collective-permute-done.15.y1
  106.4 2.1 collective-permute-done.16.y2
  108.5 2.0 collective-permute-done.17.y3
  116.1 6.2 %collective-permute-done.20 = f32[128,256]{1,0:T(8,128)S(1)} collective-permute-done((f32[128,256]{1,0:T(8,128)S(1)}, f32[128,256]{1,0:T(8,128)S(1)}, u32[]{:S(2)}, u32[]{:S(2)}) %collective-permute-start.20) | collective-permute-done | bytes 131104 | tf_op jit(solution)/shard_map/ppermute | solution.py:32
  122.2 2.3 collective-permute-done.19
  127.7 3.6 %collective-permute-start.25 = (f32[128,256]{1,0:T(8,128)S(1)}, f32[128,256]{1,0:T(8,128)S(1)}, u32[]{:S(2)}, u32[]{:S(2)}) collective-permute-start(f32[128,256]{1,0:T(8,128)S(1)} %add_add_fusion.6.refs_6_), channel_id=1, source_target_pairs={{0,4},{1,5},{2,6},{3,7},{4,0},{5,1},{6,2},{7,3},{8,12},{9,13},{10,... | collective-permute-start | bytes 393224 | tf_op jit(solution)/shard_map/ppermute | solution.py:32
  131.5 5.4 %collective-permute-done.26 = f32[128,256]{1,0:T(8,128)S(1)} collective-permute-done((f32[128,256]{1,0:T(8,128)S(1)}, f32[128,256]{1,0:T(8,128)S(1)}, u32[]{:S(2)}, u32[]{:S(2)}) %collective-permute-start.26) | collective-permute-done | bytes 131104 | tf_op jit(solution)/shard_map/ppermute | solution.py:32
  136.9 3.6 %collective-permute-done.25 = f32[128,256]{1,0:T(8,128)S(1)} collective-permute-done((f32[128,256]{1,0:T(8,128)S(1)}, f32[128,256]{1,0:T(8,128)S(1)}, u32[]{:S(2)}, u32[]{:S(2)}) %collective-permute-start.25) | collective-permute-done | bytes 131104 | tf_op jit(solution)/shard_map/ppermute | solution.py:32
  145.3 1.9 collective-permute-start.30
  148.2 4.9 %collective-permute-done.30 = f32[128,256]{1,0:T(8,128)S(1)} collective-permute-done((f32[128,256]{1,0:T(8,128)S(1)}, f32[128,256]{1,0:T(8,128)S(1)}, u32[]{:S(2)}, u32[]{:S(2)}) %collective-permute-start.30) | collective-permute-done | bytes 131104 | tf_op jit(solution)/shard_map/ppermute | solution.py:32
  153.1 2.0 collective-permute-done.29
  158.6 4.4 %collective-permute-done.31.y1 = f32[128,256]{1,0:T(8,128)S(1)} collective-permute-done((f32[128,256]{1,0:T(8,128)S(1)}, f32[128,256]{1,0:T(8,128)S(1)}, u32[]{:S(2)}, u32[]{:S(2)}) %collective-permute-start.31) | collective-permute-done | bytes 131104 | tf_op jit(solution)/shard_map/ppermute | solution.py:32
  163.0 2.3 collective-permute-done.32.y2
  166.1 1.9 copy-done
  170.4 2.5 collective-permute-start.37
  172.9 5.1 %collective-permute-done.39 = f32[128,256]{1,0:T(8,128)S(1)} collective-permute-done((f32[128,256]{1,0:T(8,128)S(1)}, f32[128,256]{1,0:T(8,128)S(1)}, u32[]{:S(2)}, u32[]{:S(2)}) %collective-permute-start.39) | collective-permute-done | bytes 131104 | tf_op jit(solution)/shard_map/ppermute | solution.py:32
  178.7 2.4 collective-permute-start.42
  182.0 3.9 %collective-permute-done.42 = f32[128,256]{1,0:T(8,128)S(1)} collective-permute-done((f32[128,256]{1,0:T(8,128)S(1)}, f32[128,256]{1,0:T(8,128)S(1)}, u32[]{:S(2)}, u32[]{:S(2)}) %collective-permute-start.42) | collective-permute-done | bytes 131104 | tf_op jit(solution)/shard_map/ppermute | solution.py:32
  186.0 2.4 collective-permute-done.41
  189.5 1.9 collective-permute-done.43.x_sib
  192.8 1.9 collective-permute-start.44
  194.7 4.3 %collective-permute-done.46 = f32[128,256]{1,0:T(8,128)S(1)} collective-permute-done((f32[128,256]{1,0:T(8,128)S(1)}, f32[128,256]{1,0:T(8,128)S(1)}, u32[]{:S(2)}, u32[]{:S(2)}) %collective-permute-start.46) | collective-permute-done | bytes 131104 | tf_op jit(solution)/shard_map/ppermute | solution.py:32
  200.6 2.0 collective-permute-done.44
  204.8 4.3 %collective-permute-done.47.y1 = f32[128,256]{1,0:T(8,128)S(1)} collective-permute-done((f32[128,256]{1,0:T(8,128)S(1)}, f32[128,256]{1,0:T(8,128)S(1)}, u32[]{:S(2)}, u32[]{:S(2)}) %collective-permute-start.47) | collective-permute-done | bytes 131104 | tf_op jit(solution)/shard_map/ppermute | solution.py:32
  209.1 2.6 collective-permute-done.48.y2
  216.4 3.8 %collective-permute-done.52 = f32[128,256]{1,0:T(8,128)S(1)} collective-permute-done((f32[128,256]{1,0:T(8,128)S(1)}, f32[128,256]{1,0:T(8,128)S(1)}, u32[]{:S(2)}, u32[]{:S(2)}) %collective-permute-start.52) | collective-permute-done | bytes 131104 | tf_op jit(solution)/shard_map/ppermute | solution.py:32
  220.2 2.8 collective-permute-done.51
  224.1 2.3 collective-permute-start.54
  227.4 5.8 %collective-permute-done.55 = f32[128,256]{1,0:T(8,128)S(1)} collective-permute-done((f32[128,256]{1,0:T(8,128)S(1)}, f32[128,256]{1,0:T(8,128)S(1)}, u32[]{:S(2)}, u32[]{:S(2)}) %collective-permute-start.55) | collective-permute-done | bytes 131104 | tf_op jit(solution)/shard_map/ppermute | solution.py:32
  234.2 1.9 collective-permute-done.56.x_sib
  239.4 4.3 %collective-permute-done.59 = f32[128,256]{1,0:T(8,128)S(1)} collective-permute-done((f32[128,256]{1,0:T(8,128)S(1)}, f32[128,256]{1,0:T(8,128)S(1)}, u32[]{:S(2)}, u32[]{:S(2)}) %collective-permute-start.59) | collective-permute-done | bytes 131104 | tf_op jit(solution)/shard_map/ppermute | solution.py:32
  245.4 1.9 collective-permute-done.57
  249.5 4.3 %collective-permute-done.60.y1 = f32[128,256]{1,0:T(8,128)S(1)} collective-permute-done((f32[128,256]{1,0:T(8,128)S(1)}, f32[128,256]{1,0:T(8,128)S(1)}, u32[]{:S(2)}, u32[]{:S(2)}) %collective-permute-start.60) | collective-permute-done | bytes 131104 | tf_op jit(solution)/shard_map/ppermute | solution.py:32
  253.8 2.5 collective-permute-done.61.y2
  260.2 2.3 collective-permute-start.64
  263.5 5.7 %collective-permute-done.65 = f32[128,256]{1,0:T(8,128)S(1)} collective-permute-done((f32[128,256]{1,0:T(8,128)S(1)}, f32[128,256]{1,0:T(8,128)S(1)}, u32[]{:S(2)}, u32[]{:S(2)}) %collective-permute-start.65) | collective-permute-done | bytes 131104 | tf_op jit(solution)/shard_map/ppermute | solution.py:32
  270.6 2.4 collective-permute-start.66
  274.0 10.1 %collective-permute-done.66.a1 = f32[2,2,64,256]{3,2,1,0:T(8,128)S(1)} collective-permute-done((f32[2,2,64,256]{3,2,1,0:T(8,128)S(1)}, f32[2,2,64,256]{3,2,1,0:T(8,128)S(1)}, u32[]{:S(2)}, u32[]{:S(2)}) %collective-permute-start.66) | collective-permute-done | bytes 262176 | tf_op jit(solution)/shard_map/ppermute | solution.py:32
  284.0 3.4 %collective-permute-done.68.a3 = f32[2,2,64,256]{3,2,1,0:T(8,128)S(1)} collective-permute-done((f32[2,2,64,256]{3,2,1,0:T(8,128)S(1)}, f32[2,2,64,256]{3,2,1,0:T(8,128)S(1)}, u32[]{:S(2)}, u32[]{:S(2)}) %collective-permute-start.68) | collective-permute-done | bytes 262176 | tf_op jit(solution)/shard_map/ppermute | solution.py:32
  288.2 1.9 collective-permute-done.69.got
  290.7 2.3 collective-permute-start.70
  293.0 5.4 %collective-permute-start.71 = (f32[2,64,512]{2,1,0:T(8,128)S(1)}, f32[2,64,512]{2,1,0:T(8,128)S(1)}, u32[]{:S(2)}, u32[]{:S(2)}) collective-permute-start(f32[2,64,512]{2,1,0:T(8,128)S(1)} %get-tuple-element.154.d2), channel_id=1, source_target_pairs={{0,4},{1,5},{2,6},{3,7},{4,0},{5,1},{6,2},{7,3},{8,12},{9,13},{10,... | collective-permute-start | bytes 786440 | tf_op jit(solution)/shard_map/ppermute | solution.py:32
  298.3 1.9 collective-permute-start.72
  301.0 2.6 collective-permute-done.71.g2
  303.5 3.0 collective-permute-done.72.g3
  (145 shorter events, 87.5 us)
Async XLA Ops:
  7.2 103.3 %all-gather.9.cloned.1.call-start = ((), (), s32[]{:S(2)}) async-start(), calls=%async_computation | async-start | bytes 2359296 | tf_op jit(solution)/shard_map/all_gather | solution.py:368
  11.2 7.7 %collective-permute-start = (f32[2,64,512]{2,1,0:T(8,128)S(1)}, f32[2,64,512]{2,1,0:T(8,128)S(1)}, u32[]{:S(2)}, u32[]{:S(2)}) collective-permute-start(f32[2,64,512]{2,1,0:T(8,128)S(1)} %get-tuple-element.81), channel_id=1, source_target_pairs={{0,2},{1,3},{2,4},{3,5},{4,6},{5,7},{6,0},{7,1},{8,10},{9,11},{10,... | collective-permute-start | bytes 786440 | tf_op jit(solution)/shard_map/ppermute | solution.py:32
  12.9 10.1 %collective-permute-start.1 = (f32[2,64,512]{2,1,0:T(8,128)S(1)}, f32[2,64,512]{2,1,0:T(8,128)S(1)}, u32[]{:S(2)}, u32[]{:S(2)}) collective-permute-start(f32[2,64,512]{2,1,0:T(8,128)S(1)} %get-tuple-element.82), channel_id=1, source_target_pairs={{0,4},{1,5},{2,6},{3,7},{4,0},{5,1},{6,2},{7,3},{8,12},{9,13},{10,... | collective-permute-start | bytes 786440 | tf_op jit(solution)/shard_map/ppermute | solution.py:32
  15.8 7.2 %collective-permute-start.2 = (f32[2,64,512]{2,1,0:T(8,128)S(1)}, f32[2,64,512]{2,1,0:T(8,128)S(1)}, u32[]{:S(2)}, u32[]{:S(2)}) collective-permute-start(f32[2,64,512]{2,1,0:T(8,128)S(1)} %get-tuple-element.83), channel_id=1, source_target_pairs={{0,6},{1,7},{2,0},{3,1},{4,2},{5,3},{6,4},{7,5},{8,14},{9,15},{10,... | collective-permute-start | bytes 786440 | tf_op jit(solution)/shard_map/ppermute | solution.py:32
  28.0 7.7 %collective-permute-start.7 = (f32[2,64,256]{2,1,0:T(8,128)S(1)}, f32[2,64,256]{2,1,0:T(8,128)S(1)}, u32[]{:S(2)}, u32[]{:S(2)}) collective-permute-start(f32[2,64,256]{2,1,0:T(8,128)S(1)} %get-tuple-element.90), channel_id=1, source_target_pairs={{0,64},{1,65},{2,66},{3,67},{4,68},{5,69},{6,70},{7,71},{8,72},{9,... | collective-permute-start | bytes 393224 | tf_op jit(solution)/shard_map/ppermute | solution.py:32
  30.4 7.2 %collective-permute-start.8 = (f32[2,64,256]{2,1,0:T(8,128)S(1)}, f32[2,64,256]{2,1,0:T(8,128)S(1)}, u32[]{:S(2)}, u32[]{:S(2)}) collective-permute-start(f32[2,64,256]{2,1,0:T(8,128)S(1)} %get-tuple-element.91), channel_id=1, source_target_pairs={{0,65},{1,0},{2,67},{3,2},{4,69},{5,4},{6,71},{7,6},{8,73},{9,8},{... | collective-permute-start | bytes 393224 | tf_op jit(solution)/shard_map/ppermute | solution.py:32
  39.0 101.6 %all-gather.11.cloned.1.call-start = ((), (), s32[]{:S(2)}) async-start(), calls=%async_computation.1 | async-start | bytes 2359296 | tf_op jit(solution)/shard_map/all_gather | solution.py:381
  39.0 7.6 %collective-permute-start.4 = (f32[2,64,512]{2,1,0:T(8,128)S(1)}, f32[2,64,512]{2,1,0:T(8,128)S(1)}, u32[]{:S(2)}, u32[]{:S(2)}) collective-permute-start(f32[2,64,512]{2,1,0:T(8,128)S(1)} %get-tuple-element.87), channel_id=1, source_target_pairs={{0,1},{1,0},{2,3},{3,2},{4,5},{5,4},{6,7},{7,6},{8,9},{9,8},{10,11... | collective-permute-start | bytes 786440 | tf_op jit(solution)/shard_map/ppermute | solution.py:32
  46.7 12.8 %collective-permute-start.5 = (f32[2,64,512]{2,1,0:T(8,128)S(1)}, f32[2,64,512]{2,1,0:T(8,128)S(1)}, u32[]{:S(2)}, u32[]{:S(2)}) collective-permute-start(f32[2,64,512]{2,1,0:T(8,128)S(1)} %collective-permute-done.4.t_one), channel_id=1, source_target_pairs={{0,32},{1,33},{2,34},{3,35},{4,36},{5,37},{6,38},{7,39},{8,40},{9,... | collective-permute-start | bytes 786440 | tf_op jit(solution)/shard_map/ppermute | solution.py:32
  46.7 9.0 %collective-permute-start.9 = (f32[128,256]{1,0:T(8,128)S(1)}, f32[128,256]{1,0:T(8,128)S(1)}, u32[]{:S(2)}, u32[]{:S(2)}) collective-permute-start(f32[128,256]{1,0:T(8,128)S(1)} %get-tuple-element.92.a0), channel_id=1, source_target_pairs={{0,6},{1,7},{2,0},{3,1},{4,2},{5,3},{6,4},{7,5},{8,14},{9,15},{10,... | collective-permute-start | bytes 393224 | tf_op jit(solution)/shard_map/ppermute | solution.py:32
  49.5 7.9 %collective-permute-start.10 = (f32[128,256]{1,0:T(8,128)S(1)}, f32[128,256]{1,0:T(8,128)S(1)}, u32[]{:S(2)}, u32[]{:S(2)}) collective-permute-start(f32[128,256]{1,0:T(8,128)S(1)} %get-tuple-element.92.a0), channel_id=1, source_target_pairs={{0,4},{1,5},{2,6},{3,7},{4,0},{5,1},{6,2},{7,3},{8,12},{9,13},{10,... | collective-permute-start | bytes 393224 | tf_op jit(solution)/shard_map/ppermute | solution.py:32
  50.3 9.1 %collective-permute-start.11 = (f32[128,256]{1,0:T(8,128)S(1)}, f32[128,256]{1,0:T(8,128)S(1)}, u32[]{:S(2)}, u32[]{:S(2)}) collective-permute-start(f32[128,256]{1,0:T(8,128)S(1)} %get-tuple-element.92.a0), channel_id=1, source_target_pairs={{0,2},{1,3},{2,4},{3,5},{4,6},{5,7},{6,0},{7,1},{8,10},{9,11},{10,... | collective-permute-start | bytes 393224 | tf_op jit(solution)/shard_map/ppermute | solution.py:32
  60.7 7.8 %collective-permute-start.21 = (f32[3,64,256]{2,1,0:T(8,128)S(1)}, f32[3,64,256]{2,1,0:T(8,128)S(1)}, u32[]{:S(2)}, u32[]{:S(2)}) collective-permute-start(f32[3,64,256]{2,1,0:T(8,128)S(1)} %get-tuple-element.107), channel_id=1, source_target_pairs={{0,1},{1,64},{2,3},{3,66},{4,5},{5,68},{6,7},{7,70},{8,9},{9,72},{... | collective-permute-start | bytes 589832 | tf_op jit(solution)/shard_map/ppermute | solution.py:32
  61.7 9.3 %collective-permute-start.22 = (f32[3,64,256]{2,1,0:T(8,128)S(1)}, f32[3,64,256]{2,1,0:T(8,128)S(1)}, u32[]{:S(2)}, u32[]{:S(2)}) collective-permute-start(f32[3,64,256]{2,1,0:T(8,128)S(1)} %get-tuple-element.108), channel_id=1, source_target_pairs={{0,64},{1,65},{2,66},{3,67},{4,68},{5,69},{6,70},{7,71},{8,72},{9,... | collective-permute-start | bytes 589832 | tf_op jit(solution)/shard_map/ppermute | solution.py:32
  63.5 10.6 %collective-permute-start.23 = (f32[3,64,256]{2,1,0:T(8,128)S(1)}, f32[3,64,256]{2,1,0:T(8,128)S(1)}, u32[]{:S(2)}, u32[]{:S(2)}) collective-permute-start(f32[3,64,256]{2,1,0:T(8,128)S(1)} %get-tuple-element.109), channel_id=1, source_target_pairs={{0,65},{1,0},{2,67},{3,2},{4,69},{5,4},{6,71},{7,6},{8,73},{9,8},{... | collective-permute-start | bytes 589832 | tf_op jit(solution)/shard_map/ppermute | solution.py:32
  75.5 90.6 %all-gather.13.cloned.1.call-start = ((), (), s32[]{:S(2)}) async-start(), calls=%async_computation.2 | async-start | bytes 3538944 | tf_op jit(solution)/shard_map/all_gather | solution.py:390
  75.5 9.2 %collective-permute-start.14 = (f32[128,256]{1,0:T(8,128)S(1)}, f32[128,256]{1,0:T(8,128)S(1)}, u32[]{:S(2)}, u32[]{:S(2)}) collective-permute-start(f32[128,256]{1,0:T(8,128)S(1)} %get-tuple-element.96), channel_id=1, source_target_pairs={{0,24},{1,25},{2,26},{3,27},{4,28},{5,29},{6,30},{7,31},{8,0},{9,1... | collective-permute-start | bytes 393224 | tf_op jit(solution)/shard_map/ppermute | solution.py:32
  79.0 7.9 %collective-permute-start.13 = (f32[128,256]{1,0:T(8,128)S(1)}, f32[128,256]{1,0:T(8,128)S(1)}, u32[]{:S(2)}, u32[]{:S(2)}) collective-permute-start(f32[128,256]{1,0:T(8,128)S(1)} %get-tuple-element.95), channel_id=1, source_target_pairs={{0,16},{1,17},{2,18},{3,19},{4,20},{5,21},{6,22},{7,23},{8,24},{9,... | collective-permute-start | bytes 393224 | tf_op jit(solution)/shard_map/ppermute | solution.py:32
  79.0 9.2 %collective-permute-start.12 = (f32[128,256]{1,0:T(8,128)S(1)}, f32[128,256]{1,0:T(8,128)S(1)}, u32[]{:S(2)}, u32[]{:S(2)}) collective-permute-start(f32[128,256]{1,0:T(8,128)S(1)} %get-tuple-element.94), channel_id=1, source_target_pairs={{0,8},{1,9},{2,10},{3,11},{4,12},{5,13},{6,14},{7,15},{8,16},{9,17... | collective-permute-start | bytes 393224 | tf_op jit(solution)/shard_map/ppermute | solution.py:32
  88.2 8.1 %collective-permute-start.34 = (f32[2,128,128]{2,1,0:T(8,128)S(1)}, f32[2,128,128]{2,1,0:T(8,128)S(1)}, u32[]{:S(2)}, u32[]{:S(2)}) collective-permute-start(f32[2,128,128]{2,1,0:T(8,128)S(1)} %get-tuple-element.119), channel_id=1, source_target_pairs={{0,8},{1,9},{2,10},{3,11},{4,12},{5,13},{6,14},{7,15},{24,0},{25,1... | collective-permute-start | bytes 393224 | tf_op jit(solution)/shard_map/ppermute | solution.py:32
  90.2 8.4 %collective-permute-start.35 = (f32[2,128,128]{2,1,0:T(8,128)S(1)}, f32[2,128,128]{2,1,0:T(8,128)S(1)}, u32[]{:S(2)}, u32[]{:S(2)}) collective-permute-start(f32[2,128,128]{2,1,0:T(8,128)S(1)} %get-tuple-element.118.e0), channel_id=1, source_target_pairs={{16,0},{17,1},{18,2},{19,3},{20,4},{21,5},{22,6},{23,7},{24,8},{25... | collective-permute-start | bytes 393224 | tf_op jit(solution)/shard_map/ppermute | solution.py:32
  91.5 7.1 %collective-permute-start.36 = (f32[2,128,128]{2,1,0:T(8,128)S(1)}, f32[2,128,128]{2,1,0:T(8,128)S(1)}, u32[]{:S(2)}, u32[]{:S(2)}) collective-permute-start(f32[2,128,128]{2,1,0:T(8,128)S(1)} %get-tuple-element.119), channel_id=1, source_target_pairs={{8,0},{9,1},{10,2},{11,3},{12,4},{13,5},{14,6},{15,7},{16,8},{17,9... | collective-permute-start | bytes 393224 | tf_op jit(solution)/shard_map/ppermute | solution.py:32
  100.0 149.5 %all-gather.15.cloned.1.call-start = ((), (), s32[]{:S(2)}) async-start(), calls=%async_computation.3 | async-start | bytes 2359296 | tf_op jit(solution)/shard_map/all_gather | solution.py:391
  100.1 8.4 %collective-permute-start.16 = (f32[128,256]{1,0:T(8,128)S(1)}, f32[128,256]{1,0:T(8,128)S(1)}, u32[]{:S(2)}, u32[]{:S(2)}) collective-permute-start(f32[128,256]{1,0:T(8,128)S(1)} %add_add_fusion.7.y0.refs_7_), channel_id=1, source_target_pairs={{0,16},{1,17},{2,18},{3,19},{4,20},{5,21},{6,22},{7,23},{8,24},{9,... | collective-permute-start | bytes 393224 | tf_op jit(solution)/shard_map/ppermute | solution.py:32
  113.3 8.9 %collective-permute-start.20 = (f32[128,256]{1,0:T(8,128)S(1)}, f32[128,256]{1,0:T(8,128)S(1)}, u32[]{:S(2)}, u32[]{:S(2)}) collective-permute-start(f32[128,256]{1,0:T(8,128)S(1)} %get-tuple-element.101), channel_id=1, source_target_pairs={{0,6},{1,7},{2,0},{3,1},{4,2},{5,3},{6,4},{7,5},{8,14},{9,15},{10,... | collective-permute-start | bytes 393224 | tf_op jit(solution)/shard_map/ppermute | solution.py:32
  113.9 10.6 %collective-permute-start.19 = (f32[128,256]{1,0:T(8,128)S(1)}, f32[128,256]{1,0:T(8,128)S(1)}, u32[]{:S(2)}, u32[]{:S(2)}) collective-permute-start(f32[128,256]{1,0:T(8,128)S(1)} %get-tuple-element.100), channel_id=1, source_target_pairs={{0,4},{1,5},{2,6},{3,7},{4,0},{5,1},{6,2},{7,3},{8,12},{9,13},{10,... | collective-permute-start | bytes 393224 | tf_op jit(solution)/shard_map/ppermute | solution.py:32
  114.8 11.4 %collective-permute-start.18 = (f32[128,256]{1,0:T(8,128)S(1)}, f32[128,256]{1,0:T(8,128)S(1)}, u32[]{:S(2)}, u32[]{:S(2)}) collective-permute-start(f32[128,256]{1,0:T(8,128)S(1)} %get-tuple-element.99), channel_id=1, source_target_pairs={{0,2},{1,3},{2,4},{3,5},{4,6},{5,7},{6,0},{7,1},{8,10},{9,11},{10,... | collective-permute-start | bytes 393224 | tf_op jit(solution)/shard_map/ppermute | solution.py:32
  126.2 10.7 %collective-permute-start.26 = (f32[128,256]{1,0:T(8,128)S(1)}, f32[128,256]{1,0:T(8,128)S(1)}, u32[]{:S(2)}, u32[]{:S(2)}) collective-permute-start(f32[128,256]{1,0:T(8,128)S(1)} %add_add_fusion.6.refs_6_), channel_id=1, source_target_pairs={{0,2},{1,3},{2,4},{3,5},{4,6},{5,7},{6,0},{7,1},{8,10},{9,11},{10,... | collective-permute-start | bytes 393224 | tf_op jit(solution)/shard_map/ppermute | solution.py:32
  127.7 12.7 %collective-permute-start.25 = (f32[128,256]{1,0:T(8,128)S(1)}, f32[128,256]{1,0:T(8,128)S(1)}, u32[]{:S(2)}, u32[]{:S(2)}) collective-permute-start(f32[128,256]{1,0:T(8,128)S(1)} %add_add_fusion.6.refs_6_), channel_id=1, source_target_pairs={{0,4},{1,5},{2,6},{3,7},{4,0},{5,1},{6,2},{7,3},{8,12},{9,13},{10,... | collective-permute-start | bytes 393224 | tf_op jit(solution)/shard_map/ppermute | solution.py:32
  131.4 9.1 %collective-permute-start.24 = (f32[128,256]{1,0:T(8,128)S(1)}, f32[128,256]{1,0:T(8,128)S(1)}, u32[]{:S(2)}, u32[]{:S(2)}) collective-permute-start(f32[128,256]{1,0:T(8,128)S(1)} %add_add_fusion.6.refs_6_), channel_id=1, source_target_pairs={{0,6},{1,7},{2,0},{3,1},{4,2},{5,3},{6,4},{7,5},{8,14},{9,15},{10,... | collective-permute-start | bytes 393224 | tf_op jit(solution)/shard_map/ppermute | solution.py:32
  145.3 7.8 %collective-permute-start.30 = (f32[128,256]{1,0:T(8,128)S(1)}, f32[128,256]{1,0:T(8,128)S(1)}, u32[]{:S(2)}, u32[]{:S(2)}) collective-permute-start(f32[128,256]{1,0:T(8,128)S(1)} %get-tuple-element.115), channel_id=1, source_target_pairs={{0,24},{1,25},{2,26},{3,27},{4,28},{5,29},{6,30},{7,31},{8,0},{9,1... | collective-permute-start | bytes 393224 | tf_op jit(solution)/shard_map/ppermute | solution.py:32
  147.2 7.9 %collective-permute-start.29 = (f32[128,256]{1,0:T(8,128)S(1)}, f32[128,256]{1,0:T(8,128)S(1)}, u32[]{:S(2)}, u32[]{:S(2)}) collective-permute-start(f32[128,256]{1,0:T(8,128)S(1)} %get-tuple-element.114), channel_id=1, source_target_pairs={{0,16},{1,17},{2,18},{3,19},{4,20},{5,21},{6,22},{7,23},{8,24},{9,... | collective-permute-start | bytes 393224 | tf_op jit(solution)/shard_map/ppermute | solution.py:32
  147.2 9.3 %collective-permute-start.28 = (f32[128,256]{1,0:T(8,128)S(1)}, f32[128,256]{1,0:T(8,128)S(1)}, u32[]{:S(2)}, u32[]{:S(2)}) collective-permute-start(f32[128,256]{1,0:T(8,128)S(1)} %get-tuple-element.113), channel_id=1, source_target_pairs={{0,8},{1,9},{2,10},{3,11},{4,12},{5,13},{6,14},{7,15},{8,16},{9,17... | collective-permute-start | bytes 393224 | tf_op jit(solution)/shard_map/ppermute | solution.py:32
  156.5 6.5 %collective-permute-start.31 = (f32[128,256]{1,0:T(8,128)S(1)}, f32[128,256]{1,0:T(8,128)S(1)}, u32[]{:S(2)}, u32[]{:S(2)}) collective-permute-start(f32[128,256]{1,0:T(8,128)S(1)} %add_add_fusion.5.y0.refs_5_), channel_id=1, source_target_pairs={{0,24},{1,25},{2,26},{3,27},{4,28},{5,29},{6,30},{7,31},{8,0},{9,1... | collective-permute-start | bytes 393224 | tf_op jit(solution)/shard_map/ppermute | solution.py:32
  157.5 7.8 %collective-permute-start.32 = (f32[128,256]{1,0:T(8,128)S(1)}, f32[128,256]{1,0:T(8,128)S(1)}, u32[]{:S(2)}, u32[]{:S(2)}) collective-permute-start(f32[128,256]{1,0:T(8,128)S(1)} %add_add_fusion.5.y0.refs_5_), channel_id=1, source_target_pairs={{0,16},{1,17},{2,18},{3,19},{4,20},{5,21},{6,22},{7,23},{8,24},{9,... | collective-permute-start | bytes 393224 | tf_op jit(solution)/shard_map/ppermute | solution.py:32
  157.7 8.4 %collective-permute-start.33 = (f32[128,256]{1,0:T(8,128)S(1)}, f32[128,256]{1,0:T(8,128)S(1)}, u32[]{:S(2)}, u32[]{:S(2)}) collective-permute-start(f32[128,256]{1,0:T(8,128)S(1)} %add_add_fusion.5.y0.refs_5_), channel_id=1, source_target_pairs={{0,8},{1,9},{2,10},{3,11},{4,12},{5,13},{6,14},{7,15},{8,16},{9,17... | collective-permute-start | bytes 393224 | tf_op jit(solution)/shard_map/ppermute | solution.py:32
  169.3 8.7 %collective-permute-start.39 = (f32[128,256]{1,0:T(8,128)S(1)}, f32[128,256]{1,0:T(8,128)S(1)}, u32[]{:S(2)}, u32[]{:S(2)}) collective-permute-start(f32[128,256]{1,0:T(8,128)S(1)} %get-tuple-element.125), channel_id=1, source_target_pairs={{0,65},{1,0},{2,67},{3,2},{4,69},{5,4},{6,71},{7,6},{8,73},{9,8},{... | collective-permute-start | bytes 393224 | tf_op jit(solution)/shard_map/ppermute | solution.py:32
  169.4 8.7 %collective-permute-start.38 = (f32[128,256]{1,0:T(8,128)S(1)}, f32[128,256]{1,0:T(8,128)S(1)}, u32[]{:S(2)}, u32[]{:S(2)}) collective-permute-start(f32[128,256]{1,0:T(8,128)S(1)} %get-tuple-element.124), channel_id=1, source_target_pairs={{0,64},{1,65},{2,66},{3,67},{4,68},{5,69},{6,70},{7,71},{8,72},{9,... | collective-permute-start | bytes 393224 | tf_op jit(solution)/shard_map/ppermute | solution.py:32
  170.4 8.3 %collective-permute-start.37 = (f32[128,256]{1,0:T(8,128)S(1)}, f32[128,256]{1,0:T(8,128)S(1)}, u32[]{:S(2)}, u32[]{:S(2)}) collective-permute-start(f32[128,256]{1,0:T(8,128)S(1)} %get-tuple-element.123), channel_id=1, source_target_pairs={{0,1},{1,64},{2,3},{3,66},{4,5},{5,68},{6,7},{7,70},{8,9},{9,72},{... | collective-permute-start | bytes 393224 | tf_op jit(solution)/shard_map/ppermute | solution.py:32
  178.7 7.3 %collective-permute-start.42 = (f32[128,256]{1,0:T(8,128)S(1)}, f32[128,256]{1,0:T(8,128)S(1)}, u32[]{:S(2)}, u32[]{:S(2)}) collective-permute-start(f32[128,256]{1,0:T(8,128)S(1)} %add_add_fusion.4.refs_4_), channel_id=1, source_target_pairs={{0,1},{1,64},{2,3},{3,66},{4,5},{5,68},{6,7},{7,70},{8,9},{9,72},{... | collective-permute-start | bytes 393224 | tf_op jit(solution)/shard_map/ppermute | solution.py:32
  181.1 7.3 %collective-permute-start.41 = (f32[128,256]{1,0:T(8,128)S(1)}, f32[128,256]{1,0:T(8,128)S(1)}, u32[]{:S(2)}, u32[]{:S(2)}) collective-permute-start(f32[128,256]{1,0:T(8,128)S(1)} %add_add_fusion.4.refs_4_), channel_id=1, source_target_pairs={{0,64},{1,65},{2,66},{3,67},{4,68},{5,69},{6,70},{7,71},{8,72},{9,... | collective-permute-start | bytes 393224 | tf_op jit(solution)/shard_map/ppermute | solution.py:32
  181.1 8.2 %collective-permute-start.40 = (f32[128,256]{1,0:T(8,128)S(1)}, f32[128,256]{1,0:T(8,128)S(1)}, u32[]{:S(2)}, u32[]{:S(2)}) collective-permute-start(f32[128,256]{1,0:T(8,128)S(1)} %add_add_fusion.4.refs_4_), channel_id=1, source_target_pairs={{0,65},{1,0},{2,67},{3,2},{4,69},{5,4},{6,71},{7,6},{8,73},{9,8},{... | collective-permute-start | bytes 393224 | tf_op jit(solution)/shard_map/ppermute | solution.py:32
  192.7 7.9 %collective-permute-start.45 = (f32[128,256]{1,0:T(8,128)S(1)}, f32[128,256]{1,0:T(8,128)S(1)}, u32[]{:S(2)}, u32[]{:S(2)}) collective-permute-start(f32[128,256]{1,0:T(8,128)S(1)} %get-tuple-element.129), channel_id=1, source_target_pairs={{0,16},{1,17},{2,18},{3,19},{4,20},{5,21},{6,22},{7,23},{8,24},{9,... | collective-permute-start | bytes 393224 | tf_op jit(solution)/shard_map/ppermute | solution.py:32
  192.8 9.8 %collective-permute-start.44 = (f32[128,256]{1,0:T(8,128)S(1)}, f32[128,256]{1,0:T(8,128)S(1)}, u32[]{:S(2)}, u32[]{:S(2)}) collective-permute-start(f32[128,256]{1,0:T(8,128)S(1)} %get-tuple-element.128), channel_id=1, source_target_pairs={{0,8},{1,9},{2,10},{3,11},{4,12},{5,13},{6,14},{7,15},{8,16},{9,17... | collective-permute-start | bytes 393224 | tf_op jit(solution)/shard_map/ppermute | solution.py:32
  203.8 7.8 %collective-permute-start.48 = (f32[128,256]{1,0:T(8,128)S(1)}, f32[128,256]{1,0:T(8,128)S(1)}, u32[]{:S(2)}, u32[]{:S(2)}) collective-permute-start(f32[128,256]{1,0:T(8,128)S(1)} %add_add_fusion.3.y0.refs_3_), channel_id=1, source_target_pairs={{0,16},{1,17},{2,18},{3,19},{4,20},{5,21},{6,22},{7,23},{8,24},{9,... | collective-permute-start | bytes 393224 | tf_op jit(solution)/shard_map/ppermute | solution.py:32
  203.8 8.7 %collective-permute-start.49 = (f32[128,256]{1,0:T(8,128)S(1)}, f32[128,256]{1,0:T(8,128)S(1)}, u32[]{:S(2)}, u32[]{:S(2)}) collective-permute-start(f32[128,256]{1,0:T(8,128)S(1)} %add_add_fusion.3.y0.refs_3_), channel_id=1, source_target_pairs={{0,8},{1,9},{2,10},{3,11},{4,12},{5,13},{6,14},{7,15},{8,16},{9,17... | collective-permute-start | bytes 393224 | tf_op jit(solution)/shard_map/ppermute | solution.py:32
  215.3 7.6 %collective-permute-start.51 = (f32[128,256]{1,0:T(8,128)S(1)}, f32[128,256]{1,0:T(8,128)S(1)}, u32[]{:S(2)}, u32[]{:S(2)}) collective-permute-start(f32[128,256]{1,0:T(8,128)S(1)} %get-tuple-element.133), channel_id=1, source_target_pairs={{0,4},{1,5},{2,6},{3,7},{4,0},{5,1},{6,2},{7,3},{8,12},{9,13},{10,... | collective-permute-start | bytes 393224 | tf_op jit(solution)/shard_map/ppermute | solution.py:32
  215.3 8.7 %collective-permute-start.50 = (f32[128,256]{1,0:T(8,128)S(1)}, f32[128,256]{1,0:T(8,128)S(1)}, u32[]{:S(2)}, u32[]{:S(2)}) collective-permute-start(f32[128,256]{1,0:T(8,128)S(1)} %get-tuple-element.132), channel_id=1, source_target_pairs={{0,2},{1,3},{2,4},{3,5},{4,6},{5,7},{6,0},{7,1},{8,10},{9,11},{10,... | collective-permute-start | bytes 393224 | tf_op jit(solution)/shard_map/ppermute | solution.py:32
  224.1 9.2 %collective-permute-start.55 = (f32[128,256]{1,0:T(8,128)S(1)}, f32[128,256]{1,0:T(8,128)S(1)}, u32[]{:S(2)}, u32[]{:S(2)}) collective-permute-start(f32[128,256]{1,0:T(8,128)S(1)} %add_add_fusion.2.refs_2_), channel_id=1, source_target_pairs={{0,2},{1,3},{2,4},{3,5},{4,6},{5,7},{6,0},{7,1},{8,10},{9,11},{10,... | collective-permute-start | bytes 393224 | tf_op jit(solution)/shard_map/ppermute | solution.py:32
  224.1 9.1 %collective-permute-start.54 = (f32[128,256]{1,0:T(8,128)S(1)}, f32[128,256]{1,0:T(8,128)S(1)}, u32[]{:S(2)}, u32[]{:S(2)}) collective-permute-start(f32[128,256]{1,0:T(8,128)S(1)} %add_add_fusion.2.refs_2_), channel_id=1, source_target_pairs={{0,4},{1,5},{2,6},{3,7},{4,0},{5,1},{6,2},{7,3},{8,12},{9,13},{10,... | collective-permute-start | bytes 393224 | tf_op jit(solution)/shard_map/ppermute | solution.py:32
  226.5 7.4 %collective-permute-start.53 = (f32[128,256]{1,0:T(8,128)S(1)}, f32[128,256]{1,0:T(8,128)S(1)}, u32[]{:S(2)}, u32[]{:S(2)}) collective-permute-start(f32[128,256]{1,0:T(8,128)S(1)} %add_add_fusion.2.refs_2_), channel_id=1, source_target_pairs={{0,6},{1,7},{2,0},{3,1},{4,2},{5,3},{6,4},{7,5},{8,14},{9,15},{10,... | collective-permute-start | bytes 393224 | tf_op jit(solution)/shard_map/ppermute | solution.py:32
  237.8 7.7 %collective-permute-start.58 = (f32[128,256]{1,0:T(8,128)S(1)}, f32[128,256]{1,0:T(8,128)S(1)}, u32[]{:S(2)}, u32[]{:S(2)}) collective-permute-start(f32[128,256]{1,0:T(8,128)S(1)} %get-tuple-element.138), channel_id=1, source_target_pairs={{0,16},{1,17},{2,18},{3,19},{4,20},{5,21},{6,22},{7,23},{8,24},{9,... | collective-permute-start | bytes 393224 | tf_op jit(solution)/shard_map/ppermute | solution.py:32
  237.8 9.6 %collective-permute-start.57 = (f32[128,256]{1,0:T(8,128)S(1)}, f32[128,256]{1,0:T(8,128)S(1)}, u32[]{:S(2)}, u32[]{:S(2)}) collective-permute-start(f32[128,256]{1,0:T(8,128)S(1)} %get-tuple-element.137), channel_id=1, source_target_pairs={{0,8},{1,9},{2,10},{3,11},{4,12},{5,13},{6,14},{7,15},{8,16},{9,17... | collective-permute-start | bytes 393224 | tf_op jit(solution)/shard_map/ppermute | solution.py:32
  248.5 7.8 %collective-permute-start.61 = (f32[128,256]{1,0:T(8,128)S(1)}, f32[128,256]{1,0:T(8,128)S(1)}, u32[]{:S(2)}, u32[]{:S(2)}) collective-permute-start(f32[128,256]{1,0:T(8,128)S(1)} %add_add_fusion.1.y0.refs_1_), channel_id=1, source_target_pairs={{0,16},{1,17},{2,18},{3,19},{4,20},{5,21},{6,22},{7,23},{8,24},{9,... | collective-permute-start | bytes 393224 | tf_op jit(solution)/shard_map/ppermute | solution.py:32
  248.5 8.8 %collective-permute-start.62 = (f32[128,256]{1,0:T(8,128)S(1)}, f32[128,256]{1,0:T(8,128)S(1)}, u32[]{:S(2)}, u32[]{:S(2)}) collective-permute-start(f32[128,256]{1,0:T(8,128)S(1)} %add_add_fusion.1.y0.refs_1_), channel_id=1, source_target_pairs={{0,8},{1,9},{2,10},{3,11},{4,12},{5,13},{6,14},{7,15},{8,16},{9,17... | collective-permute-start | bytes 393224 | tf_op jit(solution)/shard_map/ppermute | solution.py:32
  260.1 9.1 %collective-permute-start.65 = (f32[128,256]{1,0:T(8,128)S(1)}, f32[128,256]{1,0:T(8,128)S(1)}, u32[]{:S(2)}, u32[]{:S(2)}) collective-permute-start(f32[128,256]{1,0:T(8,128)S(1)} %get-tuple-element.144), channel_id=1, source_target_pairs={{0,65},{1,0},{2,67},{3,2},{4,69},{5,4},{6,71},{7,6},{8,73},{9,8},{... | collective-permute-start | bytes 393224 | tf_op jit(solution)/shard_map/ppermute | solution.py:32
  260.2 9.0 %collective-permute-start.64 = (f32[128,256]{1,0:T(8,128)S(1)}, f32[128,256]{1,0:T(8,128)S(1)}, u32[]{:S(2)}, u32[]{:S(2)}) collective-permute-start(f32[128,256]{1,0:T(8,128)S(1)} %get-tuple-element.143), channel_id=1, source_target_pairs={{0,64},{1,65},{2,66},{3,67},{4,68},{5,69},{6,70},{7,71},{8,72},{9,... | collective-permute-start | bytes 393224 | tf_op jit(solution)/shard_map/ppermute | solution.py:32
  262.6 7.2 %collective-permute-start.63 = (f32[128,256]{1,0:T(8,128)S(1)}, f32[128,256]{1,0:T(8,128)S(1)}, u32[]{:S(2)}, u32[]{:S(2)}) collective-permute-start(f32[128,256]{1,0:T(8,128)S(1)} %get-tuple-element.142), channel_id=1, source_target_pairs={{0,1},{1,64},{2,3},{3,66},{4,5},{5,68},{6,7},{7,70},{8,9},{9,72},{... | collective-permute-start | bytes 393224 | tf_op jit(solution)/shard_map/ppermute | solution.py:32
  270.6 13.4 %collective-permute-start.66 = (f32[2,2,64,256]{3,2,1,0:T(8,128)S(1)}, f32[2,2,64,256]{3,2,1,0:T(8,128)S(1)}, u32[]{:S(2)}, u32[]{:S(2)}) collective-permute-start(f32[2,2,64,256]{3,2,1,0:T(8,128)S(1)} %get-tuple-element.147), channel_id=1, source_target_pairs={{0,1},{1,64},{2,3},{3,66},{4,5},{5,68},{6,7},{7,70},{8,9},{9,72},{... | collective-permute-start | bytes 786440 | tf_op jit(solution)/shard_map/ppermute | solution.py:32
  273.0 11.0 %collective-permute-start.67 = (f32[2,2,64,256]{3,2,1,0:T(8,128)S(1)}, f32[2,2,64,256]{3,2,1,0:T(8,128)S(1)}, u32[]{:S(2)}, u32[]{:S(2)}) collective-permute-start(f32[2,2,64,256]{3,2,1,0:T(8,128)S(1)} %get-tuple-element.148), channel_id=1, source_target_pairs={{0,64},{1,65},{2,66},{3,67},{4,68},{5,69},{6,70},{7,71},{8,72},{9,... | collective-permute-start | bytes 786440 | tf_op jit(solution)/shard_map/ppermute | solution.py:32
  273.1 14.4 %collective-permute-start.68 = (f32[2,2,64,256]{3,2,1,0:T(8,128)S(1)}, f32[2,2,64,256]{3,2,1,0:T(8,128)S(1)}, u32[]{:S(2)}, u32[]{:S(2)}) collective-permute-start(f32[2,2,64,256]{3,2,1,0:T(8,128)S(1)} %get-tuple-element.149), channel_id=1, source_target_pairs={{0,65},{1,0},{2,67},{3,2},{4,69},{5,4},{6,71},{7,6},{8,73},{9,8},{... | collective-permute-start | bytes 786440 | tf_op jit(solution)/shard_map/ppermute | solution.py:32
  290.7 10.3 %collective-permute-start.70 = (f32[2,64,512]{2,1,0:T(8,128)S(1)}, f32[2,64,512]{2,1,0:T(8,128)S(1)}, u32[]{:S(2)}, u32[]{:S(2)}) collective-permute-start(f32[2,64,512]{2,1,0:T(8,128)S(1)} %get-tuple-element.153.d1), channel_id=1, source_target_pairs={{0,2},{1,3},{2,4},{3,5},{4,6},{5,7},{6,0},{7,1},{8,10},{9,11},{10,... | collective-permute-start | bytes 786440 | tf_op jit(solution)/shard_map/ppermute | solution.py:32
  293.0 10.6 %collective-permute-start.71 = (f32[2,64,512]{2,1,0:T(8,128)S(1)}, f32[2,64,512]{2,1,0:T(8,128)S(1)}, u32[]{:S(2)}, u32[]{:S(2)}) collective-permute-start(f32[2,64,512]{2,1,0:T(8,128)S(1)} %get-tuple-element.154.d2), channel_id=1, source_target_pairs={{0,4},{1,5},{2,6},{3,7},{4,0},{5,1},{6,2},{7,3},{8,12},{9,13},{10,... | collective-permute-start | bytes 786440 | tf_op jit(solution)/shard_map/ppermute | solution.py:32
  298.3 8.3 %collective-permute-start.72 = (f32[2,64,512]{2,1,0:T(8,128)S(1)}, f32[2,64,512]{2,1,0:T(8,128)S(1)}, u32[]{:S(2)}, u32[]{:S(2)}) collective-permute-start(f32[2,64,512]{2,1,0:T(8,128)S(1)} %get-tuple-element.155.d3), channel_id=1, source_target_pairs={{0,6},{1,7},{2,0},{3,1},{4,2},{5,3},{6,4},{7,5},{8,14},{9,15},{10,... | collective-permute-start | bytes 786440 | tf_op jit(solution)/shard_map/ppermute | solution.py:32
  (23 other events, 152.3 us)
Sparse Core Ops, SparseCore 0:
  39.1 25.9 all-gather.8
  75.6 23.8 all-gather.10
  101.8 39.0 all-gather.12
  148.3 24.6 all-gather.14

commit v3 on v0

v3 whole, which is shorter than its diff:
```python
import functools

import jax
import jax.numpy as jnp
import numpy as np
from jax import lax
from jax.experimental import pallas as pl
from jax.experimental.pallas import tpu as pltpu
from jax.sharding import Mesh, PartitionSpec as P

TILE = 128
AXES = ("xh", "co", "z", "y", "xl")
SIZES = (2, 2, 4, 4, 2)
X, Y, Z, C, XL, LANE = range(6)


def route(place, only=None):
    pairs = []
    for i in range(int(np.prod(SIZES))):
        xh, co, z, y, xl = (int(v) for v in np.unravel_index(i, SIZES))
        at = dict(x=2 * xh + xl, y=y, z=z, co=co)
        if only is not None and not only(**at):
            continue
        at = place(**at)
        to = (at["x"] // 2, at["co"], at["z"], at["y"], at["x"] % 2)
        pairs.append((i, int(np.ravel_multi_index(to, SIZES))))
    assert len({b for _, b in pairs}) == len(pairs)
    return pairs


def send(x, place, only=None):
    return lax.ppermute(x, AXES, route(place, only))


def partner(axis, r):
    def place(**at):
        return {**at, axis: at[axis] ^ r}

    return place


def deal(r):
    def place(**at):
        axis = "z" if at["co"] else "y"
        return {**at, axis: at[axis] ^ r}

    return place


def to_other_core(**at):
    return {**at, "co": 1 - at["co"]}


def exchanged(pieces, place, only=None):
    return [pieces[0]] + [send(pieces[r], place(r), only) for r in (1, 2, 3)]


def gathered(piece, axis):
    return exchanged([piece] * 4, functools.partial(partner, axis))


def scattered(parts, axis):
    got = exchanged(parts, functools.partial(partner, axis))
    return sum(a[:128] for a in got[1:]) + got[0][:128], got


def after(values, done):
    return lax.optimization_barrier((tuple(values), done))[0]


def split(x):
    hi = x.astype(jnp.bfloat16)
    lo = (x - hi.astype(jnp.float32)).astype(jnp.bfloat16)
    return hi, lo


def dot_cols(a, b):
    dims = (((0,), (0,)), ((), ()))
    mm = functools.partial(
        lax.dot_general, dimension_numbers=dims, preferred_element_type=jnp.float32
    )
    a_hi, a_lo = split(a)
    b_hi, b_lo = split(b)
    return mm(a_hi, b_hi) + (mm(a_hi, b_lo) + mm(a_lo, b_hi))


def dot_rows(a, b):
    mm = functools.partial(jnp.dot, preferred_element_type=jnp.float32)
    a_hi, a_lo = split(a)
    b_hi, b_lo = split(b)
    return mm(a_hi, b_hi) + (mm(a_hi, b_lo) + mm(a_lo, b_hi))


def rows_of(start, count):
    return pl.ds(pl.multiple_of(start, count), count)


def fetch(pairs, sems, first=0):
    copies = [
        pltpu.make_async_copy(a, b, sems.at[first + i]) for i, (a, b) in enumerate(pairs)
    ]
    for copy in copies:
        copy.start()
    return copies


def arrive(copies):
    for copy in copies:
        copy.wait()


def put_parts(value, place, outs):
    for r, o in enumerate(outs):
        o[pl.ds(0, 128), :] = value[rows_of(128 * (place ^ r), 128), :]


def put_pieces(pieces, place, ref):
    for r, piece in enumerate(pieces):
        ref[rows_of(128 * (place ^ r), 128), :] = piece[...]


def cross_tail_kernel(at, t_own, t_one, t_two, *rest):
    pieces, riders, outs, (a, y) = rest[:4], rest[4:8], rest[8:12], rest[12:]
    for o, rider in zip(outs, riders):
        o[pl.ds(128, 64), :] = rider[...]
    put_pieces(pieces, at[Y], a)

    def put(ref, count, first, half):
        part = dot_rows(ref[...].reshape(count * 64, 512), a[...])
        for i in range(count):
            y[rows_of(128 * (first + i) + 64 * half, 64), :] = part[64 * i : 64 * i + 64]

    put(t_own, 4, 0, at[XL])
    put(t_one, 2, 2 * at[C], 1 - at[XL])
    put(t_two, 2, 2 * (1 - at[C]), 1 - at[XL])
    put_parts(y, at[Z], outs)


def cross_kernel(odd, slot, at, a_all, *rest):
    halves, outs, (a, y, sems) = rest[:2], rest[2:6], rest[6:]
    c = at[C]
    place = at[X] if odd else at[Y]
    if odd:
        blocks = [
            (
                a_all.at[2 * (place ^ j) + c, 0, 2 * h + i],
                a.at[pl.ds(128 * j + 64 * i, 64), pl.ds(128 * h, 128)],
            )
            for j in range(4)
            for h in range(2)
            for i in range(2)
        ]
    else:
        blocks = [
            (
                a_all.at[2 * (place ^ j) + i, slot, rows_of(64 * c, 64), :],
                a.at[pl.ds(128 * j + 64 * i, 64), :],
            )
            for j in range(4)
            for i in range(2)
        ]
    copies = fetch(blocks, sems)
    arrive(copies)
    for ref, half in zip(halves, (c, 1 - c)):
        y[rows_of(256 * half, 256), :] = dot_cols(ref[...], a[...])
    put_parts(y, at[Z], outs)


def close_kernel(odd, slot, at, b_all, *rest):
    pieces, outs, (b, x, y, sems) = rest[:4], rest[4:8], rest[8:]
    if odd:
        blocks = [
            (
                b_all.at[2 * j + h, 1, pl.ds(64 * i, 64), :],
                b.at[2 * j + i, :, pl.ds(256 * h, 256)],
            )
            for j in range(4)
            for h in range(2)
            for i in range(2)
        ]
    else:
        blocks = [
            (b_all.at[2 * j + i, slot, k], b.at[2 * k + i, :, pl.ds(128 * j, 128)])
            for j in range(4)
            for i in range(2)
            for k in range(4)
        ]
    copies = fetch(blocks, sems)
    put_pieces(pieces, at[Z], y)
    arrive(copies)
    x[...] = dot_cols(b[...].reshape(512, 512), y[...])
    put_parts(x, at[Y] if odd else at[X], outs)


def close_ring_kernel(at, b_own, b_sib, y0, y1, y2, y3, *rest):
    outs, (b, x, y) = rest[:4], rest[4:]
    put_pieces((y0, y1, y2, y3), at[Z], y)
    for ref, half in ((b_own, at[C]), (b_sib, 1 - at[C])):
        for r in range(4):
            rows = rows_of(128 * (at[X] ^ r), 128)
            b[rows, rows_of(256 * half, 256)] = ref[pl.ds(128 * r, 128), :]
    x[...] = dot_cols(b[...], y[...])
    put_parts(x, at[Y], outs)


def deal_kernel(at, factor, local, tail, *rest):
    outs, sems = rest[:4], rest[4]

    def blocks(ref, n):
        pairs = []
        for r, out in enumerate(outs):
            for k in range(4):
                v = at[LANE] ^ r
                col = jnp.where(at[C] == 0, 512 * k + 128 * v, 512 * v + 128 * k)
                pairs.append((ref.at[:, rows_of(col, 128)], out.at[n, :, pl.ds(128 * k, 128)]))
        return pairs

    copies = fetch(blocks(factor, 0), sems)

    @pl.when(at[C] == 0)
    def _():
        arrive(fetch(blocks(local, 1), sems, 16))

    @pl.when(at[C] == 1)
    def _():
        arrive(fetch(blocks(tail, 1), sems, 16))

    arrive(copies)


def pair_kernel(at, d0, d1, d2, d3, factor, local, keep, give):
    low, high = pl.ds(0, 256), pl.ds(256, 256)
    dealt = (d0, d1, d2, d3)

    def factors(ref):
        for r, d in enumerate(dealt):
            ref[at[LANE] ^ r, 0] = d[0, :, low]
            ref[at[LANE] ^ r, 1] = d[0, :, high]

    def nothing(ref, slots):
        for s in range(4):
            for k in slots:
                ref[s, k] = jnp.zeros((64, 256), jnp.float32)

    @pl.when(at[C] == 0)
    def _():
        for r, d in enumerate(dealt):
            keep[at[LANE] ^ r, 2] = d[1, :, low]
            give[at[LANE] ^ r, 2] = d[1, :, high]
        for ref in (keep, give):
            nothing(ref, (3, 4))

        @pl.when(at[XL] == 0)
        def _():
            factors(keep)
            nothing(give, (0, 1))

        @pl.when(at[XL] == 1)
        def _():
            factors(give)
            nothing(keep, (0, 1))

    @pl.when(at[C] == 1)
    def _():
        for r, d in enumerate(dealt):
            s = at[LANE] ^ r
            keep[s, 1] = d[0, :, high]
            give[s, 1] = d[0, :, low]
            for h, cols in enumerate((low, high)):
                keep[s, 3 + h] = d[1, :, cols]
                give[s, 3 + h] = d[1, :, cols]
        for s in range(4):
            for k, ref in ((0, factor), (2, local)):
                for i in range(2):
                    here = pl.ds(128 * i, 128)
                    give[s, k, :, here] = ref[:, pl.ds(512 * i + 128 * s, 128)]
                    keep[s, k, :, here] = ref[:, pl.ds(512 * (i + 2) + 128 * s, 128)]


def row_kernel(at, keep, got, *outs):
    rows, locals_, t_all = outs[:4], outs[4:8], outs[8]

    def fill(odd, even):
        for r, (a, e) in enumerate(zip(rows, locals_)):
            s = at[X] ^ r
            for k in range(2):
                a[k] = odd[s, k]
                a[2 + k] = even[s, k]
            e[0] = odd[s, 2]
            e[1] = even[s, 2]
        for s in range(4):
            for h in range(2):
                t_all[s, :, pl.ds(256 * h, 256)] = odd[s, 3 + h]
        for i, a in enumerate((rows[1], rows[3])):
            for h in range(2):
                a[4 + h] = odd[2 * at[C] + i, 3 + h]

    @pl.when(at[C] == 0)
    def _():
        fill(got, keep)

    @pl.when(at[C] == 1)
    def _():
        fill(keep, got)


def base_kernel(at, a0, a1, a2, a3, *rest):
    uppers, lower, riders, t_one = rest[:2], rest[2], rest[3:7], rest[7]
    target, gathers, sems = rest[8:]
    for r, a in enumerate((a0, a1, a2, a3)):
        s = at[X] ^ r
        n = s // 2
        rows = rows_of(64 * lax.rem(s, 2), 64)

        @pl.when(n == 0)
        def _():
            uppers[0][rows, :] = a[0]
            gathers[1, rows, :] = a[1]

        @pl.when(n == 1)
        def _():
            uppers[1][rows, :] = a[0]
            lower[rows, :] = a[1]

        @pl.when(lax.rem(s, 2) == at[C])
        def _():
            for h in range(2):
                gathers[2 * (1 - n), pl.ds(64 * h, 64), :] = a[2 + h]
            for k, rider in enumerate(riders):
                v = at[Z] ^ k
                block = a[2 + v // 2, :, rows_of(128 * lax.rem(v, 2), 128)]
                rider[:, rows_of(128 * n, 128)] = block

    copies = fetch([(gathers, target)], sems)
    for i, a in enumerate((a1, a3)):
        for h in range(2):
            t_one[i, :, pl.ds(256 * h, 256)] = a[4 + h]
    arrive(copies)


def column_kernel(at, e0, e1, e2, e3, upper, target, out, sems):
    for h in range(2):
        for i in range(2):
            out[0, 2 * h + i] = upper[pl.ds(64 * i, 64), pl.ds(128 * h, 128)]
    for r, e in enumerate((e0, e1, e2, e3)):
        for n in range(2):
            out[1 + n, at[Z] ^ r] = e[pl.ds(128, 64), pl.ds(128 * n, 128)]
    arrive(fetch([(out, target)], sems))


def local_kernel(at, e0, e1, e2, e3, *outs):
    for r, e in enumerate((e0, e1, e2, e3)):
        s = at[X] ^ r
        for n in range(2):

            @pl.when(s // 2 == n)
            def _():
                rows = rows_of(64 * lax.rem(s, 2), 64)
                outs[2 * n][rows, :] = e[1]
                outs[2 * n + 1][rows, :] = e[0]


def leave_kernel(at, *refs):
    kept, outs = refs[:8], refs[8:]
    for r, out in enumerate(outs):
        for s in range(4):

            @pl.when((at[X] ^ r) == s)
            def _():
                for n in range(2):
                    for k in range(2):
                        ref = kept[2 * (2 * (s // 2) + n) + k]
                        out[n, k] = ref[pl.ds(64 * (s % 2), 64), :]


def meet_kernel(at, a0, a1, a2, a3, keep, give):
    for r, a in enumerate((a0, a1, a2, a3)):
        keep[at[X] ^ r] = a[at[C]]
        give[at[X] ^ r] = a[1 - at[C]]


def turn_kernel(at, keep, got, *outs):
    mine, theirs = rows_of(256 * at[C], 256), rows_of(256 * (1 - at[C]), 256)
    for r, out in enumerate(outs):
        for k in range(2):
            out[k, :, mine] = keep[at[Y] ^ r, k]
            out[k, :, theirs] = got[at[Y] ^ r, k]


def finish_kernel(at, mask, d0, d1, d2, d3, g1, g2, g3, diag, off):
    def fill(parts):
        for r, part in enumerate(parts):
            s = at[Y] ^ r
            for k in range(4):
                cols = rows_of(512 * k + 128 * s, 128)
                kept = mask[4 * k + s]
                diag[:, cols] = part[0, :, pl.ds(128 * k, 128)] * kept
                off[:, cols] = -part[1, :, pl.ds(128 * k, 128)] * kept

    @pl.when(at[C] == 0)
    def _():
        fill((d0, g1, g2, g3))

    @pl.when(at[C] == 1)
    def _():
        fill((d0, d1, d2, d3))


def local(kernel, at, args, shapes, scratch=(), copies=0, scalars=(), far=(), flops=0, out_far=0):
    vmem = pl.BlockSpec(memory_space=pltpu.VMEM)
    smem = pl.BlockSpec(memory_space=pltpu.SMEM)
    hbm = pl.BlockSpec(memory_space=pltpu.HBM)
    moved = sum(int(np.prod(a.shape)) for a in args) + sum(int(np.prod(s)) for s in shapes)
    scratch = [pltpu.VMEM(s, jnp.float32) for s in scratch]
    if copies:
        scratch.append(pltpu.SemaphoreType.DMA((copies,)))
    return pl.pallas_call(
        kernel,
        out_shape=[jax.ShapeDtypeStruct(s, jnp.float32) for s in shapes],
        in_specs=[smem] * (1 + len(scalars)) + [hbm] * len(far) + [vmem] * len(args),
        out_specs=[vmem] * (len(shapes) - out_far) + [hbm] * out_far,
        scratch_shapes=scratch,
        compiler_params=pltpu.CompilerParams(vmem_limit_bytes=16 * 1024 * 1024),
        cost_estimate=pl.CostEstimate(flops=flops, bytes_accessed=4 * moved, transcendentals=0),
    )(at, *scalars, *far, *args)


def product(kernel, at, args, scratch, rows=128, far=(), copies=0):
    work = 6 * 512 * 512 * 256
    return local(
        kernel, at, args, [(rows, 256)] * 4, scratch, copies=copies, far=far, flops=work
    )


def on_device(inv_local, coupling, tail_block, adjacency):
    xh, co, z, y, xl = (lax.axis_index(a) for a in AXES)
    x = 2 * xh + xl
    at = jnp.stack([x, y, z, co, xl, jnp.where(co == 0, y, z)]).astype(jnp.int32)
    along = {axis: functools.partial(partner, axis) for axis in "xyz"}
    piece, half_piece = (128, 256), (64, 256)
    wide, square = (512, 256), (512, 512)
    x8, y8 = ("xh", "xl", "co"), ("y", "co")

    factor, own, tail = coupling[0], inv_local[0], tail_block
    dealt = local(deal_kernel, at, [], [(2, 64, 512)] * 4, copies=32, far=[factor, own, tail])
    dealt = exchanged(dealt, deal)
    keep, give = local(pair_kernel, at, dealt + [factor, own], [(4, 5, 64, 256)] * 2)
    got = send(give, to_other_core)
    *rows, t_all = local(
        row_kernel,
        at,
        [keep, got],
        [(n, 64, 256) for n in (4, 6, 4, 6)] + [(2, 64, 256)] * 4 + [(4, 64, 512)],
    )
    rows, rows_local = rows[:4], rows[4:]
    (upper_one, upper_three, lower_three, *riders, t_one, on_x) = local(
        base_kernel,
        at,
        exchanged(rows, along["x"]),
        [piece] * 3 + [half_piece] * 4 + [(2, 64, 512)] + [(3, *piece)],
        [(3, *piece)],
        copies=1,
        out_far=1,
    )
    pieces = gathered(upper_three, "y")
    lowers = gathered(lower_three, "x")
    (t_aside,) = after([t_one], pieces[1])
    t_two = send(t_aside, to_other_core)
    pieces = list(after(pieces, tuple(lowers)))
    parts = product(
        cross_tail_kernel, at, [t_all, t_one, t_two] + pieces + riders, [wide, wide], 192
    )
    b_own = jnp.concatenate(lowers)
    b_sib = send(b_own, to_other_core)
    (on_x, *rows_local) = after([on_x] + rows_local, parts[0])
    on_x = lax.all_gather(on_x, x8)
    cross, columns = scattered(parts, "z")
    locals_ = local(local_kernel, at, exchanged(rows_local, along["x"]), [piece] * 4)
    crosses, blocks = {3: cross}, {}
    (on_y,) = local(
        column_kernel,
        at,
        columns + [upper_one],
        [(3, 4, 64, 128)],
        [(3, 4, 64, 128)],
        copies=1,
        out_far=1,
    )

    for t in (3, 2, 1, 0):
        odd = t % 2 == 1
        first, second = ("y", "x") if odd else ("x", "y")
        if t < 3:
            mine = gathered(blocks[t + 1], second)
            x_own = jnp.concatenate(mine)
            if t == 2:
                (on_y,) = after([on_y], (blocks[3], on_x))
                on_y = lax.all_gather(on_y, y8)
            args = [x_own, send(x_own, to_other_core)]
            kernel = functools.partial(cross_kernel, odd, 0 if t else 2)
            far, copies = (on_y, 16) if odd else (on_x, 8)
            parts = product(kernel, at, args, [wide, wide], 128, [far], copies)
            cross, _ = scattered(parts, "z")
            crosses[t] = cross
        args = gathered(cross, "z")
        if t == 3:
            args = [b_own, b_sib] + args
            parts = product(close_ring_kernel, at, args, [square, wide, wide])
        else:
            kernel = functools.partial(close_kernel, odd, 1 + t // 2)
            far, copies = (on_x, 16) if odd else (on_y, 32)
            parts = product(kernel, at, args, [(8, 64, 512), wide, wide], 128, [far], copies)
        blocks[t] = scattered(parts, first)[0] + locals_[t]

    outs = [a[t] for t in range(4) for a in (blocks, crosses)]
    outs = exchanged(local(leave_kernel, at, outs, [(2, 2, 64, 256)] * 4), along["x"])
    keep, give = local(meet_kernel, at, outs, [(4, 2, 64, 256)] * 2)
    got = send(give, to_other_core)
    turned = local(turn_kernel, at, [keep, got], [(2, 64, 512)] * 4)
    back = exchanged(turned, along["y"], lambda co, **_: co == 0)

    count = adjacency.shape[0]
    joined = jnp.maximum(adjacency, jnp.eye(count, dtype=jnp.int32)).astype(jnp.float32)
    mask = lax.dynamic_index_in_dim(joined, (z * 8 + y * 2 + xl) * 64 // TILE, 0, keepdims=False)
    diag, off = local(
        finish_kernel, at, list(turned) + back[1:], [(64, 2048)] * 2, scalars=[mask]
    )
    return diag[None], off[None]


def solution(mesh):
    fine = Mesh(mesh.devices.reshape(SIZES), AXES)
    rows = P(("xh", "co"), ("z", "y", "xl"), None)
    return jax.shard_map(
        on_device,
        mesh=fine,
        in_specs=(rows, rows, P(("z", "y", "xl"), None), P()),
        out_specs=(rows, rows),
        check_vma=False,
    )
```

time: 1250 us -> 293 us (0.23)
  waiting for transfers between devices: 1000 us -> 139 us
  matrix products: 158 us -> 0 us
  starting transfers between devices: 26.5 us -> 106 us
  blocking collectives: 24.8 us -> 0 us
  Pallas kernels: 0 us -> 22.9 us
    all_gather x3 -> x2, waiting for transfers between devices: 923 us -> 0.02 us  [the longest x1 0.02 us: on_device(): on_x = lax.all_gather(on_x, x8)]
    dot_general x8 -> x0, matrix products: 99.8 us -> none  [the longest x3 41.5 us: on_device(): quadratic = jnp.dot(turned.T, gathered, precision=highest)]
    ppermute x5 -> x73, starting transfers between devices: 11.8 us -> 106 us  [send(): return lax.ppermute(x, AXES, route(place, only))]
    ppermute x5 -> x73, waiting for transfers between devices: 58.9 us -> 139 us  [send(): return lax.ppermute(x, AXES, route(place, only))]
    all_to_all x2 -> x0, matrix products: 57.8 us -> none  [on_device(): lax.all_to_all(half_product, 'space', split_axis=1, concat_axis=0, tiled=...]
    all_to_all x1 -> x0, blocking collectives: 24.8 us -> none  [on_device(): lax.all_to_all(half_product, 'space', split_axis=1, concat_axis=0, tiled=...]
    pallas_call x0 -> x18, Pallas kernels: none -> 22.9 us  [local(): pl.pallas_call(kernel, out_shape=[jax.ShapeDtypeStruct(s, jnp.float32) fo...]
    all_to_all x2 -> x0, waiting for transfers between devices: 17.6 us -> none  [on_device(): lax.all_to_all(half_product, 'space', split_axis=1, concat_axis=0, tiled=...]
  transfers between devices with their start and end apart: 10 -> 75, of which waited for: 9 -> 58; matrix products, arithmetic and copies ran while one was open for 8% -> 0% of each run, Pallas kernels for 0% -> 2%
where the time goes in v3:
time: 293 us; the launch traced here: 290 us
  waiting for transfers between devices  139 us (47%)
  starting transfers between devices  106 us (36%)
  Pallas kernels  22.9 us (8%)
  between operations  14.5 us (5%)
  local copies, waits for them, and re-layouts  7.04 us (2%)
    ppermute x73, waiting for transfers between devices, send(): return lax.ppermute(x, AXES, route(place, only))  139 us
    ppermute x73, starting transfers between devices, send(): return lax.ppermute(x, AXES, route(place, only))  106 us
    pallas_call x18, Pallas kernels, local(): pl.pallas_call(kernel, out_shape=[jax.ShapeDtypeStruct(s, jnp.float32) fo...  22.9 us
    unnamed x15, local copies, waits for them, and re-layouts  6.94 us
  transfers between devices with their start and end apart: 75, of which 58 were waited for; matrix products, arithmetic and copies ran while one was open for 0% of the time, Pallas kernels for 2%

profile of v3, /device:TPU:6, one launch (start us, length us, event | category | flops | bytes accessed | tf_op | source)
XLA Modules:
  0.0 290.3 jit_solution(835342918656262077)
XLA Ops:
  13.3 2.9 collective-permute-start.1
  18.1 5.4 %collective-permute-done.1.d2 = f32[2,64,512]{2,1,0:T(8,128)S(1)} collective-permute-done((f32[2,64,512]{2,1,0:T(8,128)S(1)}, f32[2,64,512]{2,1,0:T(8,128)S(1)}, u32[]{:S(2)}, u32[]{:S(2)}) %collective-permute-start.1) | collective-permute-done | bytes 262176 | tf_op jit(solution)/shard_map/ppermute | solution.py:32
  23.5 2.7 collective-permute-done.2.d3
  27.0 3.0 %collective-permute-done.3.got = f32[4,5,64,256]{3,2,1,0:T(8,128)S(1)} collective-permute-done((f32[4,5,64,256]{3,2,1,0:T(8,128)S(1)}, f32[4,5,64,256]{3,2,1,0:T(8,128)S(1)}, u32[]{:S(2)}, u32[]{:S(2)}) %collective-permute-start.3) | collective-permute-done | bytes 1310752 | tf_op jit(solution)/shard_map/ppermute | solution.py:32
  32.8 2.1 collective-permute-start.5
  34.9 12.7 %collective-permute-done.5.a2 = f32[4,64,256]{2,1,0:T(8,128)S(1)} collective-permute-done((f32[4,64,256]{2,1,0:T(8,128)S(1)}, f32[4,64,256]{2,1,0:T(8,128)S(1)}, u32[]{:S(2)}, u32[]{:S(2)}) %collective-permute-start.5) | collective-permute-done | bytes 262176 | tf_op jit(solution)/shard_map/ppermute | solution.py:32
  52.0 2.2 collective-permute-start.10
  55.9 2.6 collective-permute-start.9
  60.6 2.0 collective-permute-start.11
  63.3 4.9 %collective-permute-done.13 = f32[128,256]{1,0:T(8,128)S(1)} collective-permute-done((f32[128,256]{1,0:T(8,128)S(1)}, f32[128,256]{1,0:T(8,128)S(1)}, u32[]{:S(2)}, u32[]{:S(2)}) %collective-permute-start.13) | collective-permute-done | bytes 131104 | tf_op jit(solution)/shard_map/ppermute | solution.py:32
  70.3 3.1 %collective-permute-start.15 = (f32[192,256]{1,0:T(8,128)S(1)}, f32[192,256]{1,0:T(8,128)S(1)}, u32[]{:S(2)}, u32[]{:S(2)}) collective-permute-start(f32[192,256]{1,0:T(8,128)S(1)} %get-tuple-element.110), channel_id=1, source_target_pairs={{0,16},{1,17},{2,18},{3,19},{4,20},{5,21},{6,22},{7,23},{8,24},{9,... | collective-permute-start | bytes 589832 | tf_op jit(solution)/shard_map/ppermute | solution.py:32
  75.1 3.0 %collective-permute-done.14.e1 = f32[192,256]{1,0:T(8,128)S(1)} collective-permute-done((f32[192,256]{1,0:T(8,128)S(1)}, f32[192,256]{1,0:T(8,128)S(1)}, u32[]{:S(2)}, u32[]{:S(2)}) %collective-permute-start.14) | collective-permute-done | bytes 196640 | tf_op jit(solution)/shard_map/ppermute | solution.py:32
  78.2 3.8 %collective-permute-done.15.e2 = f32[192,256]{1,0:T(8,128)S(1)} collective-permute-done((f32[192,256]{1,0:T(8,128)S(1)}, f32[192,256]{1,0:T(8,128)S(1)}, u32[]{:S(2)}, u32[]{:S(2)}) %collective-permute-start.15) | collective-permute-done | bytes 196640 | tf_op jit(solution)/shard_map/ppermute | solution.py:32
  82.0 2.5 collective-permute-done.16.e3
  85.8 2.9 %collective-permute-start.18 = (f32[128,256]{1,0:T(8,128)S(1)}, f32[128,256]{1,0:T(8,128)S(1)}, u32[]{:S(2)}, u32[]{:S(2)}) collective-permute-start(f32[128,256]{1,0:T(8,128)S(1)} %fusion.y0.refs_7_), channel_id=1, source_target_pairs={{0,8},{1,9},{2,10},{3,11},{4,12},{5,13},{6,14},{7,15},{8,0},{9,1},... | collective-permute-start | bytes 393224 | tf_op jit(solution)/shard_map/ppermute | solution.py:32
  88.7 2.6 collective-permute-start.25
  95.7 3.2 %collective-permute-start.22 = (f32[128,256]{1,0:T(8,128)S(1)}, f32[128,256]{1,0:T(8,128)S(1)}, u32[]{:S(2)}, u32[]{:S(2)}) collective-permute-start(f32[128,256]{1,0:T(8,128)S(1)} %get-tuple-element.114), channel_id=1, source_target_pairs={{0,4},{1,5},{2,6},{3,7},{4,0},{5,1},{6,2},{7,3},{8,12},{9,13},{10,... | collective-permute-start | bytes 393224 | tf_op jit(solution)/shard_map/ppermute | solution.py:32
  110.3 4.3 %collective-permute-done.29 = f32[128,256]{1,0:T(8,128)S(1)} collective-permute-done((f32[128,256]{1,0:T(8,128)S(1)}, f32[128,256]{1,0:T(8,128)S(1)}, u32[]{:S(2)}, u32[]{:S(2)}) %collective-permute-start.29) | collective-permute-done | bytes 131104 | tf_op jit(solution)/shard_map/ppermute | solution.py:32
  115.3 2.3 collective-permute-done.30.rest_1_
  117.7 1.9 copy-done
  119.5 2.0 shard_map.67
  121.6 2.3 collective-permute-start.32
  124.0 2.3 collective-permute-start.33
  127.9 2.4 collective-permute-done.32
  130.4 2.2 collective-permute-done.33
  132.7 2.4 collective-permute-start.36
  136.8 3.6 %collective-permute-done.36.rest_3_ = f32[128,256]{1,0:T(8,128)S(1)} collective-permute-done((f32[128,256]{1,0:T(8,128)S(1)}, f32[128,256]{1,0:T(8,128)S(1)}, u32[]{:S(2)}, u32[]{:S(2)}) %collective-permute-start.36) | collective-permute-done | bytes 131104 | tf_op jit(solution)/shard_map/ppermute | solution.py:32
  140.4 2.3 collective-permute-done.35.rest_2_
  142.8 1.9 copy-done.2
  146.5 3.3 %collective-permute-start.38 = (f32[128,256]{1,0:T(8,128)S(1)}, f32[128,256]{1,0:T(8,128)S(1)}, u32[]{:S(2)}, u32[]{:S(2)}) collective-permute-start(f32[128,256]{1,0:T(8,128)S(1)} %get-tuple-element.134), channel_id=1, source_target_pairs={{0,64},{1,65},{2,66},{3,67},{4,68},{5,69},{6,70},{7,71},{8,72},{9,... | collective-permute-start | bytes 393224 | tf_op jit(solution)/shard_map/ppermute | solution.py:32
  151.5 2.7 collective-permute-done.38
  160.3 2.1 collective-permute-done.42
  164.7 1.9 collective-permute-done.43.rest_1_
  168.4 4.3 %collective-permute-start.45 = (f32[128,256]{1,0:T(8,128)S(1)}, f32[128,256]{1,0:T(8,128)S(1)}, u32[]{:S(2)}, u32[]{:S(2)}) collective-permute-start(f32[128,256]{1,0:T(8,128)S(1)} %get-tuple-element.139), channel_id=1, source_target_pairs={{0,16},{1,17},{2,18},{3,19},{4,20},{5,21},{6,22},{7,23},{8,24},{9,... | collective-permute-start | bytes 393224 | tf_op jit(solution)/shard_map/ppermute | solution.py:32
  174.5 4.6 %collective-permute-done.45 = f32[128,256]{1,0:T(8,128)S(1)} collective-permute-done((f32[128,256]{1,0:T(8,128)S(1)}, f32[128,256]{1,0:T(8,128)S(1)}, u32[]{:S(2)}, u32[]{:S(2)}) %collective-permute-start.45) | collective-permute-done | bytes 131104 | tf_op jit(solution)/shard_map/ppermute | solution.py:32
  179.1 2.2 collective-permute-done.46
  182.4 3.1 %collective-permute-start.47 = (f32[128,256]{1,0:T(8,128)S(1)}, f32[128,256]{1,0:T(8,128)S(1)}, u32[]{:S(2)}, u32[]{:S(2)}) collective-permute-start(f32[128,256]{1,0:T(8,128)S(1)} %add_add_fusion.3.rest_0_.refs_3_), channel_id=1, source_target_pairs={{0,8},{1,9},{2,10},{3,11},{4,12},{5,13},{6,14},{7,15},{8,0},{9,1},... | collective-permute-start | bytes 393224 | tf_op jit(solution)/shard_map/ppermute | solution.py:32
  185.6 4.8 %collective-permute-done.49.rest_3_ = f32[128,256]{1,0:T(8,128)S(1)} collective-permute-done((f32[128,256]{1,0:T(8,128)S(1)}, f32[128,256]{1,0:T(8,128)S(1)}, u32[]{:S(2)}, u32[]{:S(2)}) %collective-permute-start.49) | collective-permute-done | bytes 131104 | tf_op jit(solution)/shard_map/ppermute | solution.py:32
  192.7 2.2 collective-permute-start.51
  194.9 2.5 collective-permute-start.52
  201.7 2.7 collective-permute-start.55
  205.8 3.5 %collective-permute-done.55 = f32[128,256]{1,0:T(8,128)S(1)} collective-permute-done((f32[128,256]{1,0:T(8,128)S(1)}, f32[128,256]{1,0:T(8,128)S(1)}, u32[]{:S(2)}, u32[]{:S(2)}) %collective-permute-start.55) | collective-permute-done | bytes 131104 | tf_op jit(solution)/shard_map/ppermute | solution.py:32
  209.3 2.0 collective-permute-done.54
  211.5 1.9 collective-permute-done.56.rest_1_
  213.4 2.0 shard_map.71
  217.3 2.9 collective-permute-start.59
  221.8 1.9 collective-permute-done.58
  223.7 2.2 collective-permute-done.59
  226.0 2.9 %collective-permute-start.62 = (f32[128,256]{1,0:T(8,128)S(1)}, f32[128,256]{1,0:T(8,128)S(1)}, u32[]{:S(2)}, u32[]{:S(2)}) collective-permute-start(f32[128,256]{1,0:T(8,128)S(1)} %add_add_fusion.1.rest_0_.refs_1_), channel_id=1, source_target_pairs={{0,24},{1,25},{2,26},{3,27},{4,28},{5,29},{6,30},{7,31},{8,16},{9,... | collective-permute-start | bytes 393224 | tf_op jit(solution)/shard_map/ppermute | solution.py:32
  230.2 4.0 %collective-permute-done.62.rest_3_ = f32[128,256]{1,0:T(8,128)S(1)} collective-permute-done((f32[128,256]{1,0:T(8,128)S(1)}, f32[128,256]{1,0:T(8,128)S(1)}, u32[]{:S(2)}, u32[]{:S(2)}) %collective-permute-start.62) | collective-permute-done | bytes 131104 | tf_op jit(solution)/shard_map/ppermute | solution.py:32
  234.2 2.3 collective-permute-done.61.rest_2_
  238.3 2.7 collective-permute-start.64
  241.1 1.9 collective-permute-start.65
  243.3 2.1 collective-permute-done.64
  245.4 1.8 collective-permute-done.65
  248.1 3.4 %collective-permute-start.67 = (f32[2,2,64,256]{3,2,1,0:T(8,128)S(1)}, f32[2,2,64,256]{3,2,1,0:T(8,128)S(1)}, u32[]{:S(2)}, u32[]{:S(2)}) collective-permute-start(f32[2,2,64,256]{3,2,1,0:T(8,128)S(1)} %get-tuple-element.158), channel_id=1, source_target_pairs={{0,64},{1,65},{2,66},{3,67},{4,68},{5,69},{6,70},{7,71},{8,72},{9,... | collective-permute-start | bytes 786440 | tf_op jit(solution)/shard_map/ppermute | solution.py:32
  252.8 2.0 collective-permute-done.66.a1
  254.8 4.3 %collective-permute-done.67.a2 = f32[2,2,64,256]{3,2,1,0:T(8,128)S(1)} collective-permute-done((f32[2,2,64,256]{3,2,1,0:T(8,128)S(1)}, f32[2,2,64,256]{3,2,1,0:T(8,128)S(1)}, u32[]{:S(2)}, u32[]{:S(2)}) %collective-permute-start.67) | collective-permute-done | bytes 262176 | tf_op jit(solution)/shard_map/ppermute | solution.py:32
  259.1 2.7 collective-permute-done.68.a3
  262.5 1.9 collective-permute-done.69.got
  265.0 2.2 collective-permute-start.70
  267.2 5.1 %collective-permute-start.71 = (f32[2,64,512]{2,1,0:T(8,128)S(1)}, f32[2,64,512]{2,1,0:T(8,128)S(1)}, u32[]{:S(2)}, u32[]{:S(2)}) collective-permute-start(f32[2,64,512]{2,1,0:T(8,128)S(1)} %get-tuple-element.164.d2), channel_id=1, source_target_pairs={{0,4},{1,5},{2,6},{3,7},{4,0},{5,1},{6,2},{7,3},{8,12},{9,13},{10,... | collective-permute-start | bytes 786440 | tf_op jit(solution)/shard_map/ppermute | solution.py:32
  272.3 3.2 %collective-permute-start.72 = (f32[2,64,512]{2,1,0:T(8,128)S(1)}, f32[2,64,512]{2,1,0:T(8,128)S(1)}, u32[]{:S(2)}, u32[]{:S(2)}) collective-permute-start(f32[2,64,512]{2,1,0:T(8,128)S(1)} %get-tuple-element.165.d3), channel_id=1, source_target_pairs={{0,6},{1,7},{2,4},{3,5},{4,2},{5,3},{6,0},{7,1},{8,14},{9,15},{10,... | collective-permute-start | bytes 786440 | tf_op jit(solution)/shard_map/ppermute | solution.py:32
  277.5 4.3 %collective-permute-done.72.g3 = f32[2,64,512]{2,1,0:T(8,128)S(1)} collective-permute-done((f32[2,64,512]{2,1,0:T(8,128)S(1)}, f32[2,64,512]{2,1,0:T(8,128)S(1)}, u32[]{:S(2)}, u32[]{:S(2)}) %collective-permute-start.72) | collective-permute-done | bytes 262176 | tf_op jit(solution)/shard_map/ppermute | solution.py:32
  (135 shorter events, 84.2 us)
Async XLA Ops:
  7.2 99.0 %all-gather.5.cloned.1.call-start = ((), (), s32[]{:S(2)}) async-start(), calls=%async_computation | async-start | bytes 3538944 | tf_op jit(solution)/shard_map/all_gather | solution.py:476
  11.7 6.5 %collective-permute-start = (f32[2,64,512]{2,1,0:T(8,128)S(1)}, f32[2,64,512]{2,1,0:T(8,128)S(1)}, u32[]{:S(2)}, u32[]{:S(2)}) collective-permute-start(f32[2,64,512]{2,1,0:T(8,128)S(1)} %get-tuple-element.86), channel_id=1, source_target_pairs={{0,2},{1,3},{2,0},{3,1},{4,6},{5,7},{6,4},{7,5},{8,10},{9,11},{10,... | collective-permute-start | bytes 786440 | tf_op jit(solution)/shard_map/ppermute | solution.py:32
  13.3 10.2 %collective-permute-start.1 = (f32[2,64,512]{2,1,0:T(8,128)S(1)}, f32[2,64,512]{2,1,0:T(8,128)S(1)}, u32[]{:S(2)}, u32[]{:S(2)}) collective-permute-start(f32[2,64,512]{2,1,0:T(8,128)S(1)} %get-tuple-element.87), channel_id=1, source_target_pairs={{0,4},{1,5},{2,6},{3,7},{4,0},{5,1},{6,2},{7,3},{8,12},{9,13},{10,... | collective-permute-start | bytes 786440 | tf_op jit(solution)/shard_map/ppermute | solution.py:32
  16.2 10.0 %collective-permute-start.2 = (f32[2,64,512]{2,1,0:T(8,128)S(1)}, f32[2,64,512]{2,1,0:T(8,128)S(1)}, u32[]{:S(2)}, u32[]{:S(2)}) collective-permute-start(f32[2,64,512]{2,1,0:T(8,128)S(1)} %get-tuple-element.88), channel_id=1, source_target_pairs={{0,6},{1,7},{2,4},{3,5},{4,2},{5,3},{6,0},{7,1},{8,14},{9,15},{10,... | collective-permute-start | bytes 786440 | tf_op jit(solution)/shard_map/ppermute | solution.py:32
  30.7 16.9 %collective-permute-start.4 = (f32[6,64,256]{2,1,0:T(8,128)S(1)}, f32[6,64,256]{2,1,0:T(8,128)S(1)}, u32[]{:S(2)}, u32[]{:S(2)}) collective-permute-start(f32[6,64,256]{2,1,0:T(8,128)S(1)} %get-tuple-element.93), channel_id=1, source_target_pairs={{0,1},{1,0},{2,3},{3,2},{4,5},{5,4},{6,7},{7,6},{8,9},{9,8},{10,11... | collective-permute-start | bytes 1179656 | tf_op jit(solution)/shard_map/ppermute | solution.py:32
  31.7 17.7 %collective-permute-start.6 = (f32[6,64,256]{2,1,0:T(8,128)S(1)}, f32[6,64,256]{2,1,0:T(8,128)S(1)}, u32[]{:S(2)}, u32[]{:S(2)}) collective-permute-start(f32[6,64,256]{2,1,0:T(8,128)S(1)} %get-tuple-element.95), channel_id=1, source_target_pairs={{0,65},{1,64},{2,67},{3,66},{4,69},{5,68},{6,71},{7,70},{8,73},{9,... | collective-permute-start | bytes 1179656 | tf_op jit(solution)/shard_map/ppermute | solution.py:32
  32.8 14.8 %collective-permute-start.5 = (f32[4,64,256]{2,1,0:T(8,128)S(1)}, f32[4,64,256]{2,1,0:T(8,128)S(1)}, u32[]{:S(2)}, u32[]{:S(2)}) collective-permute-start(f32[4,64,256]{2,1,0:T(8,128)S(1)} %get-tuple-element.94), channel_id=1, source_target_pairs={{0,64},{1,65},{2,66},{3,67},{4,68},{5,69},{6,70},{7,71},{8,72},{9,... | collective-permute-start | bytes 786440 | tf_op jit(solution)/shard_map/ppermute | solution.py:32
  52.0 8.6 %collective-permute-start.10 = (f32[128,256]{1,0:T(8,128)S(1)}, f32[128,256]{1,0:T(8,128)S(1)}, u32[]{:S(2)}, u32[]{:S(2)}) collective-permute-start(f32[128,256]{1,0:T(8,128)S(1)} %get-tuple-element.100.rest_0_), channel_id=1, source_target_pairs={{0,6},{1,7},{2,4},{3,5},{4,2},{5,3},{6,0},{7,1},{8,14},{9,15},{10,... | collective-permute-start | bytes 393224 | tf_op jit(solution)/shard_map/ppermute | solution.py:32
  55.9 12.9 %collective-permute-start.8 = (f32[2,64,512]{2,1,0:T(8,128)S(1)}, f32[2,64,512]{2,1,0:T(8,128)S(1)}, u32[]{:S(2)}, u32[]{:S(2)}) collective-permute-start(f32[2,64,512]{2,1,0:T(8,128)S(1)} %get-tuple-element.98.t_one), channel_id=1, source_target_pairs={{0,32},{1,33},{2,34},{3,35},{4,36},{5,37},{6,38},{7,39},{8,40},{9,... | collective-permute-start | bytes 786440 | tf_op jit(solution)/shard_map/ppermute | solution.py:32
  55.9 7.4 %collective-permute-start.9 = (f32[128,256]{1,0:T(8,128)S(1)}, f32[128,256]{1,0:T(8,128)S(1)}, u32[]{:S(2)}, u32[]{:S(2)}) collective-permute-start(f32[128,256]{1,0:T(8,128)S(1)} %get-tuple-element.100.rest_0_), channel_id=1, source_target_pairs={{0,4},{1,5},{2,6},{3,7},{4,0},{5,1},{6,2},{7,3},{8,12},{9,13},{10,... | collective-permute-start | bytes 393224 | tf_op jit(solution)/shard_map/ppermute | solution.py:32
  58.6 9.6 %collective-permute-start.13 = (f32[128,256]{1,0:T(8,128)S(1)}, f32[128,256]{1,0:T(8,128)S(1)}, u32[]{:S(2)}, u32[]{:S(2)}) collective-permute-start(f32[128,256]{1,0:T(8,128)S(1)} %get-tuple-element.99), channel_id=1, source_target_pairs={{0,65},{1,64},{2,67},{3,66},{4,69},{5,68},{6,71},{7,70},{8,73},{9,... | collective-permute-start | bytes 393224 | tf_op jit(solution)/shard_map/ppermute | solution.py:32
  59.7 8.5 %collective-permute-start.12 = (f32[128,256]{1,0:T(8,128)S(1)}, f32[128,256]{1,0:T(8,128)S(1)}, u32[]{:S(2)}, u32[]{:S(2)}) collective-permute-start(f32[128,256]{1,0:T(8,128)S(1)} %get-tuple-element.99), channel_id=1, source_target_pairs={{0,64},{1,65},{2,66},{3,67},{4,68},{5,69},{6,70},{7,71},{8,72},{9,... | collective-permute-start | bytes 393224 | tf_op jit(solution)/shard_map/ppermute | solution.py:32
  60.6 8.2 %collective-permute-start.11 = (f32[128,256]{1,0:T(8,128)S(1)}, f32[128,256]{1,0:T(8,128)S(1)}, u32[]{:S(2)}, u32[]{:S(2)}) collective-permute-start(f32[128,256]{1,0:T(8,128)S(1)} %get-tuple-element.99), channel_id=1, source_target_pairs={{0,1},{1,0},{2,3},{3,2},{4,5},{5,4},{6,7},{7,6},{8,9},{9,8},{10,11... | collective-permute-start | bytes 393224 | tf_op jit(solution)/shard_map/ppermute | solution.py:32
  70.1 72.6 %all-gather.7.cloned.1.call-start = ((), (), s32[]{:S(2)}) async-start(), calls=%async_computation.1 | async-start | bytes 3538944 | tf_op jit(solution)/shard_map/all_gather | solution.py:498
  70.3 7.9 %collective-permute-start.14 = (f32[192,256]{1,0:T(8,128)S(1)}, f32[192,256]{1,0:T(8,128)S(1)}, u32[]{:S(2)}, u32[]{:S(2)}) collective-permute-start(f32[192,256]{1,0:T(8,128)S(1)} %get-tuple-element.109), channel_id=1, source_target_pairs={{0,8},{1,9},{2,10},{3,11},{4,12},{5,13},{6,14},{7,15},{8,0},{9,1},... | collective-permute-start | bytes 589832 | tf_op jit(solution)/shard_map/ppermute | solution.py:32
  70.3 11.6 %collective-permute-start.15 = (f32[192,256]{1,0:T(8,128)S(1)}, f32[192,256]{1,0:T(8,128)S(1)}, u32[]{:S(2)}, u32[]{:S(2)}) collective-permute-start(f32[192,256]{1,0:T(8,128)S(1)} %get-tuple-element.110), channel_id=1, source_target_pairs={{0,16},{1,17},{2,18},{3,19},{4,20},{5,21},{6,22},{7,23},{8,24},{9,... | collective-permute-start | bytes 589832 | tf_op jit(solution)/shard_map/ppermute | solution.py:32
  73.5 11.0 %collective-permute-start.16 = (f32[192,256]{1,0:T(8,128)S(1)}, f32[192,256]{1,0:T(8,128)S(1)}, u32[]{:S(2)}, u32[]{:S(2)}) collective-permute-start(f32[192,256]{1,0:T(8,128)S(1)} %get-tuple-element.111), channel_id=1, source_target_pairs={{0,24},{1,25},{2,26},{3,27},{4,28},{5,29},{6,30},{7,31},{8,16},{9,... | collective-permute-start | bytes 589832 | tf_op jit(solution)/shard_map/ppermute | solution.py:32
  75.0 13.7 %collective-permute-start.17 = (f32[512,256]{1,0:T(8,128)S(1)}, f32[512,256]{1,0:T(8,128)S(1)}, u32[]{:S(2)}, u32[]{:S(2)}) collective-permute-start(f32[512,256]{1,0:T(8,128)S(1)} %constant_dynamic-update-slice_fusion.b_own), channel_id=1, source_target_pairs={{0,32},{1,33},{2,34},{3,35},{4,36},{5,37},{6,38},{7,39},{8,40},{9,... | collective-permute-start | bytes 1572872 | tf_op jit(solution)/shard_map/ppermute | solution.py:32
  84.5 8.6 %collective-permute-start.20 = (f32[128,256]{1,0:T(8,128)S(1)}, f32[128,256]{1,0:T(8,128)S(1)}, u32[]{:S(2)}, u32[]{:S(2)}) collective-permute-start(f32[128,256]{1,0:T(8,128)S(1)} %fusion.y0.refs_7_), channel_id=1, source_target_pairs={{0,24},{1,25},{2,26},{3,27},{4,28},{5,29},{6,30},{7,31},{8,16},{9,... | collective-permute-start | bytes 393224 | tf_op jit(solution)/shard_map/ppermute | solution.py:32
  85.8 8.5 %collective-permute-start.19 = (f32[128,256]{1,0:T(8,128)S(1)}, f32[128,256]{1,0:T(8,128)S(1)}, u32[]{:S(2)}, u32[]{:S(2)}) collective-permute-start(f32[128,256]{1,0:T(8,128)S(1)} %fusion.y0.refs_7_), channel_id=1, source_target_pairs={{0,16},{1,17},{2,18},{3,19},{4,20},{5,21},{6,22},{7,23},{8,24},{9,... | collective-permute-start | bytes 393224 | tf_op jit(solution)/shard_map/ppermute | solution.py:32
  85.8 8.5 %collective-permute-start.18 = (f32[128,256]{1,0:T(8,128)S(1)}, f32[128,256]{1,0:T(8,128)S(1)}, u32[]{:S(2)}, u32[]{:S(2)}) collective-permute-start(f32[128,256]{1,0:T(8,128)S(1)} %fusion.y0.refs_7_), channel_id=1, source_target_pairs={{0,8},{1,9},{2,10},{3,11},{4,12},{5,13},{6,14},{7,15},{8,0},{9,1},... | collective-permute-start | bytes 393224 | tf_op jit(solution)/shard_map/ppermute | solution.py:32
  88.7 10.2 %collective-permute-start.24 = (f32[2,64,256]{2,1,0:T(8,128)S(1)}, f32[2,64,256]{2,1,0:T(8,128)S(1)}, u32[]{:S(2)}, u32[]{:S(2)}) collective-permute-start(f32[2,64,256]{2,1,0:T(8,128)S(1)} %get-tuple-element.123), channel_id=1, source_target_pairs={{0,1},{1,0},{2,3},{3,2},{4,5},{5,4},{6,7},{7,6},{8,9},{9,8},{10,11... | collective-permute-start | bytes 393224 | tf_op jit(solution)/shard_map/ppermute | solution.py:32
  88.7 12.1 %collective-permute-start.25 = (f32[2,64,256]{2,1,0:T(8,128)S(1)}, f32[2,64,256]{2,1,0:T(8,128)S(1)}, u32[]{:S(2)}, u32[]{:S(2)}) collective-permute-start(f32[2,64,256]{2,1,0:T(8,128)S(1)} %get-tuple-element.124), channel_id=1, source_target_pairs={{0,64},{1,65},{2,66},{3,67},{4,68},{5,69},{6,70},{7,71},{8,72},{9,... | collective-permute-start | bytes 393224 | tf_op jit(solution)/shard_map/ppermute | solution.py:32
  93.1 8.2 %collective-permute-start.26 = (f32[2,64,256]{2,1,0:T(8,128)S(1)}, f32[2,64,256]{2,1,0:T(8,128)S(1)}, u32[]{:S(2)}, u32[]{:S(2)}) collective-permute-start(f32[2,64,256]{2,1,0:T(8,128)S(1)} %get-tuple-element.125), channel_id=1, source_target_pairs={{0,65},{1,64},{2,67},{3,66},{4,69},{5,68},{6,71},{7,70},{8,73},{9,... | collective-permute-start | bytes 393224 | tf_op jit(solution)/shard_map/ppermute | solution.py:32
  95.6 7.7 %collective-permute-start.21 = (f32[128,256]{1,0:T(8,128)S(1)}, f32[128,256]{1,0:T(8,128)S(1)}, u32[]{:S(2)}, u32[]{:S(2)}) collective-permute-start(f32[128,256]{1,0:T(8,128)S(1)} %get-tuple-element.113), channel_id=1, source_target_pairs={{0,2},{1,3},{2,0},{3,1},{4,6},{5,7},{6,4},{7,5},{8,10},{9,11},{10,... | collective-permute-start | bytes 393224 | tf_op jit(solution)/shard_map/ppermute | solution.py:32
  95.7 8.6 %collective-permute-start.22 = (f32[128,256]{1,0:T(8,128)S(1)}, f32[128,256]{1,0:T(8,128)S(1)}, u32[]{:S(2)}, u32[]{:S(2)}) collective-permute-start(f32[128,256]{1,0:T(8,128)S(1)} %get-tuple-element.114), channel_id=1, source_target_pairs={{0,4},{1,5},{2,6},{3,7},{4,0},{5,1},{6,2},{7,3},{8,12},{9,13},{10,... | collective-permute-start | bytes 393224 | tf_op jit(solution)/shard_map/ppermute | solution.py:32
  98.9 7.2 %collective-permute-start.23 = (f32[128,256]{1,0:T(8,128)S(1)}, f32[128,256]{1,0:T(8,128)S(1)}, u32[]{:S(2)}, u32[]{:S(2)}) collective-permute-start(f32[128,256]{1,0:T(8,128)S(1)} %get-tuple-element.115), channel_id=1, source_target_pairs={{0,6},{1,7},{2,4},{3,5},{4,2},{5,3},{6,0},{7,1},{8,14},{9,15},{10,... | collective-permute-start | bytes 393224 | tf_op jit(solution)/shard_map/ppermute | solution.py:32
  106.2 8.4 %collective-permute-start.29 = (f32[128,256]{1,0:T(8,128)S(1)}, f32[128,256]{1,0:T(8,128)S(1)}, u32[]{:S(2)}, u32[]{:S(2)}) collective-permute-start(f32[128,256]{1,0:T(8,128)S(1)} %add_add_fusion.6.refs_6_), channel_id=1, source_target_pairs={{0,6},{1,7},{2,4},{3,5},{4,2},{5,3},{6,0},{7,1},{8,14},{9,15},{10,... | collective-permute-start | bytes 393224 | tf_op jit(solution)/shard_map/ppermute | solution.py:32
  107.6 7.0 %collective-permute-start.28 = (f32[128,256]{1,0:T(8,128)S(1)}, f32[128,256]{1,0:T(8,128)S(1)}, u32[]{:S(2)}, u32[]{:S(2)}) collective-permute-start(f32[128,256]{1,0:T(8,128)S(1)} %add_add_fusion.6.refs_6_), channel_id=1, source_target_pairs={{0,4},{1,5},{2,6},{3,7},{4,0},{5,1},{6,2},{7,3},{8,12},{9,13},{10,... | collective-permute-start | bytes 393224 | tf_op jit(solution)/shard_map/ppermute | solution.py:32
  108.7 6.5 %collective-permute-start.27 = (f32[128,256]{1,0:T(8,128)S(1)}, f32[128,256]{1,0:T(8,128)S(1)}, u32[]{:S(2)}, u32[]{:S(2)}) collective-permute-start(f32[128,256]{1,0:T(8,128)S(1)} %add_add_fusion.6.refs_6_), channel_id=1, source_target_pairs={{0,2},{1,3},{2,0},{3,1},{4,6},{5,7},{6,4},{7,5},{8,10},{9,11},{10,... | collective-permute-start | bytes 393224 | tf_op jit(solution)/shard_map/ppermute | solution.py:32
  121.5 6.4 %collective-permute-start.31 = (f32[128,256]{1,0:T(8,128)S(1)}, f32[128,256]{1,0:T(8,128)S(1)}, u32[]{:S(2)}, u32[]{:S(2)}) collective-permute-start(f32[128,256]{1,0:T(8,128)S(1)} %get-tuple-element.129), channel_id=1, source_target_pairs={{0,8},{1,9},{2,10},{3,11},{4,12},{5,13},{6,14},{7,15},{8,0},{9,1},... | collective-permute-start | bytes 393224 | tf_op jit(solution)/shard_map/ppermute | solution.py:32
  121.6 8.8 %collective-permute-start.32 = (f32[128,256]{1,0:T(8,128)S(1)}, f32[128,256]{1,0:T(8,128)S(1)}, u32[]{:S(2)}, u32[]{:S(2)}) collective-permute-start(f32[128,256]{1,0:T(8,128)S(1)} %get-tuple-element.130), channel_id=1, source_target_pairs={{0,16},{1,17},{2,18},{3,19},{4,20},{5,21},{6,22},{7,23},{8,24},{9,... | collective-permute-start | bytes 393224 | tf_op jit(solution)/shard_map/ppermute | solution.py:32
  124.0 8.7 %collective-permute-start.33 = (f32[128,256]{1,0:T(8,128)S(1)}, f32[128,256]{1,0:T(8,128)S(1)}, u32[]{:S(2)}, u32[]{:S(2)}) collective-permute-start(f32[128,256]{1,0:T(8,128)S(1)} %get-tuple-element.131), channel_id=1, source_target_pairs={{0,24},{1,25},{2,26},{3,27},{4,28},{5,29},{6,30},{7,31},{8,16},{9,... | collective-permute-start | bytes 393224 | tf_op jit(solution)/shard_map/ppermute | solution.py:32
  132.7 7.8 %collective-permute-start.36 = (f32[128,256]{1,0:T(8,128)S(1)}, f32[128,256]{1,0:T(8,128)S(1)}, u32[]{:S(2)}, u32[]{:S(2)}) collective-permute-start(f32[128,256]{1,0:T(8,128)S(1)} %add_add_fusion.5.rest_0_.refs_5_), channel_id=1, source_target_pairs={{0,24},{1,25},{2,26},{3,27},{4,28},{5,29},{6,30},{7,31},{8,16},{9,... | collective-permute-start | bytes 393224 | tf_op jit(solution)/shard_map/ppermute | solution.py:32
  135.1 7.7 %collective-permute-start.35 = (f32[128,256]{1,0:T(8,128)S(1)}, f32[128,256]{1,0:T(8,128)S(1)}, u32[]{:S(2)}, u32[]{:S(2)}) collective-permute-start(f32[128,256]{1,0:T(8,128)S(1)} %add_add_fusion.5.rest_0_.refs_5_), channel_id=1, source_target_pairs={{0,16},{1,17},{2,18},{3,19},{4,20},{5,21},{6,22},{7,23},{8,24},{9,... | collective-permute-start | bytes 393224 | tf_op jit(solution)/shard_map/ppermute | solution.py:32
  135.1 7.7 %collective-permute-start.34 = (f32[128,256]{1,0:T(8,128)S(1)}, f32[128,256]{1,0:T(8,128)S(1)}, u32[]{:S(2)}, u32[]{:S(2)}) collective-permute-start(f32[128,256]{1,0:T(8,128)S(1)} %add_add_fusion.5.rest_0_.refs_5_), channel_id=1, source_target_pairs={{0,8},{1,9},{2,10},{3,11},{4,12},{5,13},{6,14},{7,15},{8,0},{9,1},... | collective-permute-start | bytes 393224 | tf_op jit(solution)/shard_map/ppermute | solution.py:32
  146.5 7.7 %collective-permute-start.38 = (f32[128,256]{1,0:T(8,128)S(1)}, f32[128,256]{1,0:T(8,128)S(1)}, u32[]{:S(2)}, u32[]{:S(2)}) collective-permute-start(f32[128,256]{1,0:T(8,128)S(1)} %get-tuple-element.134), channel_id=1, source_target_pairs={{0,64},{1,65},{2,66},{3,67},{4,68},{5,69},{6,70},{7,71},{8,72},{9,... | collective-permute-start | bytes 393224 | tf_op jit(solution)/shard_map/ppermute | solution.py:32
  149.9 6.2 %collective-permute-start.39 = (f32[128,256]{1,0:T(8,128)S(1)}, f32[128,256]{1,0:T(8,128)S(1)}, u32[]{:S(2)}, u32[]{:S(2)}) collective-permute-start(f32[128,256]{1,0:T(8,128)S(1)} %get-tuple-element.135), channel_id=1, source_target_pairs={{0,65},{1,64},{2,67},{3,66},{4,69},{5,68},{6,71},{7,70},{8,73},{9,... | collective-permute-start | bytes 393224 | tf_op jit(solution)/shard_map/ppermute | solution.py:32
  156.1 6.3 %collective-permute-start.42 = (f32[128,256]{1,0:T(8,128)S(1)}, f32[128,256]{1,0:T(8,128)S(1)}, u32[]{:S(2)}, u32[]{:S(2)}) collective-permute-start(f32[128,256]{1,0:T(8,128)S(1)} %add_add_fusion.4.refs_4_), channel_id=1, source_target_pairs={{0,65},{1,64},{2,67},{3,66},{4,69},{5,68},{6,71},{7,70},{8,73},{9,... | collective-permute-start | bytes 393224 | tf_op jit(solution)/shard_map/ppermute | solution.py:32
  157.5 6.5 %collective-permute-start.41 = (f32[128,256]{1,0:T(8,128)S(1)}, f32[128,256]{1,0:T(8,128)S(1)}, u32[]{:S(2)}, u32[]{:S(2)}) collective-permute-start(f32[128,256]{1,0:T(8,128)S(1)} %add_add_fusion.4.refs_4_), channel_id=1, source_target_pairs={{0,64},{1,65},{2,66},{3,67},{4,68},{5,69},{6,70},{7,71},{8,72},{9,... | collective-permute-start | bytes 393224 | tf_op jit(solution)/shard_map/ppermute | solution.py:32
  168.1 6.4 %collective-permute-start.44 = (f32[128,256]{1,0:T(8,128)S(1)}, f32[128,256]{1,0:T(8,128)S(1)}, u32[]{:S(2)}, u32[]{:S(2)}) collective-permute-start(f32[128,256]{1,0:T(8,128)S(1)} %get-tuple-element.138), channel_id=1, source_target_pairs={{0,8},{1,9},{2,10},{3,11},{4,12},{5,13},{6,14},{7,15},{8,0},{9,1},... | collective-permute-start | bytes 393224 | tf_op jit(solution)/shard_map/ppermute | solution.py:32
  168.4 10.8 %collective-permute-start.45 = (f32[128,256]{1,0:T(8,128)S(1)}, f32[128,256]{1,0:T(8,128)S(1)}, u32[]{:S(2)}, u32[]{:S(2)}) collective-permute-start(f32[128,256]{1,0:T(8,128)S(1)} %get-tuple-element.139), channel_id=1, source_target_pairs={{0,16},{1,17},{2,18},{3,19},{4,20},{5,21},{6,22},{7,23},{8,24},{9,... | collective-permute-start | bytes 393224 | tf_op jit(solution)/shard_map/ppermute | solution.py:32
  172.7 8.7 %collective-permute-start.46 = (f32[128,256]{1,0:T(8,128)S(1)}, f32[128,256]{1,0:T(8,128)S(1)}, u32[]{:S(2)}, u32[]{:S(2)}) collective-permute-start(f32[128,256]{1,0:T(8,128)S(1)} %get-tuple-element.140), channel_id=1, source_target_pairs={{0,24},{1,25},{2,26},{3,27},{4,28},{5,29},{6,30},{7,31},{8,16},{9,... | collective-permute-start | bytes 393224 | tf_op jit(solution)/shard_map/ppermute | solution.py:32
  181.4 9.0 %collective-permute-start.49 = (f32[128,256]{1,0:T(8,128)S(1)}, f32[128,256]{1,0:T(8,128)S(1)}, u32[]{:S(2)}, u32[]{:S(2)}) collective-permute-start(f32[128,256]{1,0:T(8,128)S(1)} %add_add_fusion.3.rest_0_.refs_3_), channel_id=1, source_target_pairs={{0,24},{1,25},{2,26},{3,27},{4,28},{5,29},{6,30},{7,31},{8,16},{9,... | collective-permute-start | bytes 393224 | tf_op jit(solution)/shard_map/ppermute | solution.py:32
  181.7 8.7 %collective-permute-start.48 = (f32[128,256]{1,0:T(8,128)S(1)}, f32[128,256]{1,0:T(8,128)S(1)}, u32[]{:S(2)}, u32[]{:S(2)}) collective-permute-start(f32[128,256]{1,0:T(8,128)S(1)} %add_add_fusion.3.rest_0_.refs_3_), channel_id=1, source_target_pairs={{0,16},{1,17},{2,18},{3,19},{4,20},{5,21},{6,22},{7,23},{8,24},{9,... | collective-permute-start | bytes 393224 | tf_op jit(solution)/shard_map/ppermute | solution.py:32
  182.4 8.5 %collective-permute-start.47 = (f32[128,256]{1,0:T(8,128)S(1)}, f32[128,256]{1,0:T(8,128)S(1)}, u32[]{:S(2)}, u32[]{:S(2)}) collective-permute-start(f32[128,256]{1,0:T(8,128)S(1)} %add_add_fusion.3.rest_0_.refs_3_), channel_id=1, source_target_pairs={{0,8},{1,9},{2,10},{3,11},{4,12},{5,13},{6,14},{7,15},{8,0},{9,1},... | collective-permute-start | bytes 393224 | tf_op jit(solution)/shard_map/ppermute | solution.py:32
  192.7 7.5 %collective-permute-start.51 = (f32[128,256]{1,0:T(8,128)S(1)}, f32[128,256]{1,0:T(8,128)S(1)}, u32[]{:S(2)}, u32[]{:S(2)}) collective-permute-start(f32[128,256]{1,0:T(8,128)S(1)} %get-tuple-element.143), channel_id=1, source_target_pairs={{0,4},{1,5},{2,6},{3,7},{4,0},{5,1},{6,2},{7,3},{8,12},{9,13},{10,... | collective-permute-start | bytes 393224 | tf_op jit(solution)/shard_map/ppermute | solution.py:32
  194.9 6.7 %collective-permute-start.52 = (f32[128,256]{1,0:T(8,128)S(1)}, f32[128,256]{1,0:T(8,128)S(1)}, u32[]{:S(2)}, u32[]{:S(2)}) collective-permute-start(f32[128,256]{1,0:T(8,128)S(1)} %get-tuple-element.144), channel_id=1, source_target_pairs={{0,6},{1,7},{2,4},{3,5},{4,2},{5,3},{6,0},{7,1},{8,14},{9,15},{10,... | collective-permute-start | bytes 393224 | tf_op jit(solution)/shard_map/ppermute | solution.py:32
  201.7 7.7 %collective-permute-start.55 = (f32[128,256]{1,0:T(8,128)S(1)}, f32[128,256]{1,0:T(8,128)S(1)}, u32[]{:S(2)}, u32[]{:S(2)}) collective-permute-start(f32[128,256]{1,0:T(8,128)S(1)} %add_add_fusion.2.refs_2_), channel_id=1, source_target_pairs={{0,6},{1,7},{2,4},{3,5},{4,2},{5,3},{6,0},{7,1},{8,14},{9,15},{10,... | collective-permute-start | bytes 393224 | tf_op jit(solution)/shard_map/ppermute | solution.py:32
  204.4 6.9 %collective-permute-start.54 = (f32[128,256]{1,0:T(8,128)S(1)}, f32[128,256]{1,0:T(8,128)S(1)}, u32[]{:S(2)}, u32[]{:S(2)}) collective-permute-start(f32[128,256]{1,0:T(8,128)S(1)} %add_add_fusion.2.refs_2_), channel_id=1, source_target_pairs={{0,4},{1,5},{2,6},{3,7},{4,0},{5,1},{6,2},{7,3},{8,12},{9,13},{10,... | collective-permute-start | bytes 393224 | tf_op jit(solution)/shard_map/ppermute | solution.py:32
  204.4 6.9 %collective-permute-start.53 = (f32[128,256]{1,0:T(8,128)S(1)}, f32[128,256]{1,0:T(8,128)S(1)}, u32[]{:S(2)}, u32[]{:S(2)}) collective-permute-start(f32[128,256]{1,0:T(8,128)S(1)} %add_add_fusion.2.refs_2_), channel_id=1, source_target_pairs={{0,2},{1,3},{2,0},{3,1},{4,6},{5,7},{6,4},{7,5},{8,10},{9,11},{10,... | collective-permute-start | bytes 393224 | tf_op jit(solution)/shard_map/ppermute | solution.py:32
  215.4 6.4 %collective-permute-start.57 = (f32[128,256]{1,0:T(8,128)S(1)}, f32[128,256]{1,0:T(8,128)S(1)}, u32[]{:S(2)}, u32[]{:S(2)}) collective-permute-start(f32[128,256]{1,0:T(8,128)S(1)} %get-tuple-element.147), channel_id=1, source_target_pairs={{0,8},{1,9},{2,10},{3,11},{4,12},{5,13},{6,14},{7,15},{8,0},{9,1},... | collective-permute-start | bytes 393224 | tf_op jit(solution)/shard_map/ppermute | solution.py:32
  215.4 8.3 %collective-permute-start.58 = (f32[128,256]{1,0:T(8,128)S(1)}, f32[128,256]{1,0:T(8,128)S(1)}, u32[]{:S(2)}, u32[]{:S(2)}) collective-permute-start(f32[128,256]{1,0:T(8,128)S(1)} %get-tuple-element.148), channel_id=1, source_target_pairs={{0,16},{1,17},{2,18},{3,19},{4,20},{5,21},{6,22},{7,23},{8,24},{9,... | collective-permute-start | bytes 393224 | tf_op jit(solution)/shard_map/ppermute | solution.py:32
  217.3 8.7 %collective-permute-start.59 = (f32[128,256]{1,0:T(8,128)S(1)}, f32[128,256]{1,0:T(8,128)S(1)}, u32[]{:S(2)}, u32[]{:S(2)}) collective-permute-start(f32[128,256]{1,0:T(8,128)S(1)} %get-tuple-element.149), channel_id=1, source_target_pairs={{0,24},{1,25},{2,26},{3,27},{4,28},{5,29},{6,30},{7,31},{8,16},{9,... | collective-permute-start | bytes 393224 | tf_op jit(solution)/shard_map/ppermute | solution.py:32
  226.0 8.2 %collective-permute-start.62 = (f32[128,256]{1,0:T(8,128)S(1)}, f32[128,256]{1,0:T(8,128)S(1)}, u32[]{:S(2)}, u32[]{:S(2)}) collective-permute-start(f32[128,256]{1,0:T(8,128)S(1)} %add_add_fusion.1.rest_0_.refs_1_), channel_id=1, source_target_pairs={{0,24},{1,25},{2,26},{3,27},{4,28},{5,29},{6,30},{7,31},{8,16},{9,... | collective-permute-start | bytes 393224 | tf_op jit(solution)/shard_map/ppermute | solution.py:32
  228.9 7.5 %collective-permute-start.61 = (f32[128,256]{1,0:T(8,128)S(1)}, f32[128,256]{1,0:T(8,128)S(1)}, u32[]{:S(2)}, u32[]{:S(2)}) collective-permute-start(f32[128,256]{1,0:T(8,128)S(1)} %add_add_fusion.1.rest_0_.refs_1_), channel_id=1, source_target_pairs={{0,16},{1,17},{2,18},{3,19},{4,20},{5,21},{6,22},{7,23},{8,24},{9,... | collective-permute-start | bytes 393224 | tf_op jit(solution)/shard_map/ppermute | solution.py:32
  228.9 7.5 %collective-permute-start.60 = (f32[128,256]{1,0:T(8,128)S(1)}, f32[128,256]{1,0:T(8,128)S(1)}, u32[]{:S(2)}, u32[]{:S(2)}) collective-permute-start(f32[128,256]{1,0:T(8,128)S(1)} %add_add_fusion.1.rest_0_.refs_1_), channel_id=1, source_target_pairs={{0,8},{1,9},{2,10},{3,11},{4,12},{5,13},{6,14},{7,15},{8,0},{9,1},... | collective-permute-start | bytes 393224 | tf_op jit(solution)/shard_map/ppermute | solution.py:32
  238.3 7.1 %collective-permute-start.64 = (f32[128,256]{1,0:T(8,128)S(1)}, f32[128,256]{1,0:T(8,128)S(1)}, u32[]{:S(2)}, u32[]{:S(2)}) collective-permute-start(f32[128,256]{1,0:T(8,128)S(1)} %get-tuple-element.152), channel_id=1, source_target_pairs={{0,64},{1,65},{2,66},{3,67},{4,68},{5,69},{6,70},{7,71},{8,72},{9,... | collective-permute-start | bytes 393224 | tf_op jit(solution)/shard_map/ppermute | solution.py:32
  248.0 6.8 %collective-permute-start.66 = (f32[2,2,64,256]{3,2,1,0:T(8,128)S(1)}, f32[2,2,64,256]{3,2,1,0:T(8,128)S(1)}, u32[]{:S(2)}, u32[]{:S(2)}) collective-permute-start(f32[2,2,64,256]{3,2,1,0:T(8,128)S(1)} %get-tuple-element.157), channel_id=1, source_target_pairs={{0,1},{1,0},{2,3},{3,2},{4,5},{5,4},{6,7},{7,6},{8,9},{9,8},{10,11... | collective-permute-start | bytes 786440 | tf_op jit(solution)/shard_map/ppermute | solution.py:32
  248.1 11.0 %collective-permute-start.67 = (f32[2,2,64,256]{3,2,1,0:T(8,128)S(1)}, f32[2,2,64,256]{3,2,1,0:T(8,128)S(1)}, u32[]{:S(2)}, u32[]{:S(2)}) collective-permute-start(f32[2,2,64,256]{3,2,1,0:T(8,128)S(1)} %get-tuple-element.158), channel_id=1, source_target_pairs={{0,64},{1,65},{2,66},{3,67},{4,68},{5,69},{6,70},{7,71},{8,72},{9,... | collective-permute-start | bytes 786440 | tf_op jit(solution)/shard_map/ppermute | solution.py:32
  251.5 10.3 %collective-permute-start.68 = (f32[2,2,64,256]{3,2,1,0:T(8,128)S(1)}, f32[2,2,64,256]{3,2,1,0:T(8,128)S(1)}, u32[]{:S(2)}, u32[]{:S(2)}) collective-permute-start(f32[2,2,64,256]{3,2,1,0:T(8,128)S(1)} %get-tuple-element.159), channel_id=1, source_target_pairs={{0,65},{1,64},{2,67},{3,66},{4,69},{5,68},{6,71},{7,70},{8,73},{9,... | collective-permute-start | bytes 786440 | tf_op jit(solution)/shard_map/ppermute | solution.py:32
  265.0 11.2 %collective-permute-start.70 = (f32[2,64,512]{2,1,0:T(8,128)S(1)}, f32[2,64,512]{2,1,0:T(8,128)S(1)}, u32[]{:S(2)}, u32[]{:S(2)}) collective-permute-start(f32[2,64,512]{2,1,0:T(8,128)S(1)} %get-tuple-element.163.d1), channel_id=1, source_target_pairs={{0,2},{1,3},{2,0},{3,1},{4,6},{5,7},{6,4},{7,5},{8,10},{9,11},{10,... | collective-permute-start | bytes 786440 | tf_op jit(solution)/shard_map/ppermute | solution.py:32
  267.2 10.3 %collective-permute-start.71 = (f32[2,64,512]{2,1,0:T(8,128)S(1)}, f32[2,64,512]{2,1,0:T(8,128)S(1)}, u32[]{:S(2)}, u32[]{:S(2)}) collective-permute-start(f32[2,64,512]{2,1,0:T(8,128)S(1)} %get-tuple-element.164.d2), channel_id=1, source_target_pairs={{0,4},{1,5},{2,6},{3,7},{4,0},{5,1},{6,2},{7,3},{8,12},{9,13},{10,... | collective-permute-start | bytes 786440 | tf_op jit(solution)/shard_map/ppermute | solution.py:32
  272.3 9.5 %collective-permute-start.72 = (f32[2,64,512]{2,1,0:T(8,128)S(1)}, f32[2,64,512]{2,1,0:T(8,128)S(1)}, u32[]{:S(2)}, u32[]{:S(2)}) collective-permute-start(f32[2,64,512]{2,1,0:T(8,128)S(1)} %get-tuple-element.165.d3), channel_id=1, source_target_pairs={{0,6},{1,7},{2,4},{3,5},{4,2},{5,3},{6,0},{7,1},{8,14},{9,15},{10,... | collective-permute-start | bytes 786440 | tf_op jit(solution)/shard_map/ppermute | solution.py:32
  (17 other events, 76.1 us)
Sparse Core Ops, SparseCore 0:
  70.3 29.6 all-gather.4
  106.3 27.0 all-gather.6

commit v4 on v3

--- a/solution.py
+++ b/solution.py
@@ -116,7 +116,7 @@
 
 def put_pieces(pieces, place, ref):
     for r, piece in enumerate(pieces):
-        ref[rows_of(128 * (place ^ r), 128), :] = piece[...]
+        ref[rows_of(128 * (place ^ r), 128), :] = piece[pl.ds(0, 128), :]
 
 
 def cross_tail_kernel(at, t_own, t_one, t_two, *rest):
@@ -136,99 +136,53 @@
     put_parts(y, at[Z], outs)
 
 
-def cross_kernel(odd, slot, at, a_all, *rest):
-    halves, outs, (a, y, sems) = rest[:2], rest[2:6], rest[6:]
-    c = at[C]
-    place = at[X] if odd else at[Y]
-    if odd:
-        blocks = [
-            (
-                a_all.at[2 * (place ^ j) + c, 0, 2 * h + i],
-                a.at[pl.ds(128 * j + 64 * i, 64), pl.ds(128 * h, 128)],
-            )
-            for j in range(4)
-            for h in range(2)
-            for i in range(2)
-        ]
-    else:
-        blocks = [
-            (
-                a_all.at[2 * (place ^ j) + i, slot, rows_of(64 * c, 64), :],
-                a.at[pl.ds(128 * j + 64 * i, 64), :],
-            )
-            for j in range(4)
-            for i in range(2)
-        ]
-    copies = fetch(blocks, sems)
-    arrive(copies)
-    for ref, half in zip(halves, (c, 1 - c)):
-        y[rows_of(256 * half, 256), :] = dot_cols(ref[...], a[...])
+def cross_even_kernel(at, x_own, x_sib, a_own, *rest):
+    o0, o1, o2, o3, a, y = rest[-6:]
+    for r in range(4):
+        row = 128 * (at[X] ^ at[Y] ^ r)
+        theirs = rest[0][r, pl.ds(128, 64), :] if len(rest) > 6 else x_sib[pl.ds(512 + 64 * r, 64), :]
+        a[rows_of(row + 64 * at[C], 64), :] = a_own[r]
+        a[rows_of(row + 64 * (1 - at[C]), 64), :] = theirs
+    cross_of(at, x_own, x_sib, a, y, (o0, o1, o2, o3))
+
+
+def cross_odd_kernel(at, x_own, x_sib, a0, a1, a2, a3, o0, o1, o2, o3, a, y):
+    for r, piece in enumerate((a0, a1, a2, a3)):
+        a[rows_of(128 * (at[X] ^ at[Y] ^ r), 128), :] = piece[pl.ds(128, 128), :]
+    cross_of(at, x_own, x_sib, a, y, (o0, o1, o2, o3))
+
+
+def cross_of(at, x_own, x_sib, a, y, outs):
+    for ref, half in ((x_own, at[C]), (x_sib, 1 - at[C])):
+        y[rows_of(256 * half, 256), :] = dot_cols(ref[pl.ds(0, 512), :], a[...])
     put_parts(y, at[Z], outs)
 
 
-def close_kernel(odd, slot, at, b_all, *rest):
-    pieces, outs, (b, x, y, sems) = rest[:4], rest[4:8], rest[8:]
-    if odd:
-        blocks = [
-            (
-                b_all.at[2 * j + h, 1, pl.ds(64 * i, 64), :],
-                b.at[2 * j + i, :, pl.ds(256 * h, 256)],
-            )
-            for j in range(4)
-            for h in range(2)
-            for i in range(2)
-        ]
-    else:
-        blocks = [
-            (b_all.at[2 * j + i, slot, k], b.at[2 * k + i, :, pl.ds(128 * j, 128)])
-            for j in range(4)
-            for i in range(2)
-            for k in range(4)
-        ]
-    copies = fetch(blocks, sems)
-    put_pieces(pieces, at[Z], y)
-    arrive(copies)
-    x[...] = dot_cols(b[...].reshape(512, 512), y[...])
-    put_parts(x, at[Y] if odd else at[X], outs)
-
-
-def close_ring_kernel(at, b_own, b_sib, y0, y1, y2, y3, *rest):
+def close_odd_kernel(at, b0, b1, b2, b3, b_sib, y0, y1, y2, y3, *rest):
     outs, (b, x, y) = rest[:4], rest[4:]
     put_pieces((y0, y1, y2, y3), at[Z], y)
-    for ref, half in ((b_own, at[C]), (b_sib, 1 - at[C])):
-        for r in range(4):
-            rows = rows_of(128 * (at[X] ^ r), 128)
-            b[rows, rows_of(256 * half, 256)] = ref[pl.ds(128 * r, 128), :]
+    for r, own in enumerate((b0, b1, b2, b3)):
+        rows = rows_of(128 * (at[X] ^ r), 128)
+        b[rows, rows_of(256 * at[C], 256)] = own[pl.ds(0, 128), :]
+        b[rows, rows_of(256 * (1 - at[C]), 256)] = b_sib[r, pl.ds(0, 128), :]
     x[...] = dot_cols(b[...], y[...])
     put_parts(x, at[Y], outs)
 
 
-def deal_kernel(at, factor, local, tail, *rest):
-    outs, sems = rest[:4], rest[4]
-
-    def blocks(ref, n):
-        pairs = []
-        for r, out in enumerate(outs):
-            for k in range(4):
-                v = at[LANE] ^ r
-                col = jnp.where(at[C] == 0, 512 * k + 128 * v, 512 * v + 128 * k)
-                pairs.append((ref.at[:, rows_of(col, 128)], out.at[n, :, pl.ds(128 * k, 128)]))
-        return pairs
-
-    copies = fetch(blocks(factor, 0), sems)
-
-    @pl.when(at[C] == 0)
-    def _():
-        arrive(fetch(blocks(local, 1), sems, 16))
-
-    @pl.when(at[C] == 1)
-    def _():
-        arrive(fetch(blocks(tail, 1), sems, 16))
-
-    arrive(copies)
-
-
-def pair_kernel(at, d0, d1, d2, d3, factor, local, keep, give):
+def close_even_kernel(slot, at, b0, b1, b2, b3, b_sib, y0, y1, y2, y3, *rest):
+    outs, (b, x, y) = rest[:4], rest[4:]
+    put_pieces((y0, y1, y2, y3), at[Z], y)
+    here = pl.ds(128 * slot, 128)
+    for r, own in enumerate((b0, b1, b2, b3)):
+        cols = rows_of(128 * (at[Y] ^ r), 128)
+        for k in range(4):
+            b[rows_of(128 * k + 64 * at[C], 64), cols] = own[pl.ds(64 * k, 64), here]
+            b[rows_of(128 * k + 64 * (1 - at[C]), 64), cols] = b_sib[r, pl.ds(64 * k, 64), here]
+    x[...] = dot_cols(b[...], y[...])
+    put_parts(x, at[X], outs)
+
+
+def pair_kernel(at, mask, d0, d1, d2, d3, factor, local, keep, give):
     low, high = pl.ds(0, 256), pl.ds(256, 256)
     dealt = (d0, d1, d2, d3)
 
@@ -304,53 +258,63 @@
         fill(keep, got)
 
 
-def base_kernel(at, a0, a1, a2, a3, *rest):
-    uppers, lower, riders, t_one = rest[:2], rest[2], rest[3:7], rest[7]
-    target, gathers, sems = rest[8:]
+def base_kernel(at, a0, a1, a2, a3, l0, l1, l2, l3, *outs):
+    uppers, mixed, lower, riders, messages, t_one = (*outs[:3], outs[3:7], outs[7:11], outs[11])
+    for out, rows in zip(messages, (l0, l1, l2, l3)):
+        out[0] = rows[0]
+        out[1] = rows[1]
     for r, a in enumerate((a0, a1, a2, a3)):
         s = at[X] ^ r
         n = s // 2
         rows = rows_of(64 * lax.rem(s, 2), 64)
-
-        @pl.when(n == 0)
+        for i in range(2):
+
+            @pl.when(n == i)
+            def _():
+                uppers[rows_of(128 * (1 - i) + 64 * lax.rem(s, 2), 64), :] = a[0]
+                (mixed, lower)[i][rows, :] = a[1]
+
+        @pl.when((n == 0) & (lax.rem(s, 2) == at[C]))
         def _():
-            uppers[0][rows, :] = a[0]
-            gathers[1, rows, :] = a[1]
-
-        @pl.when(n == 1)
+            for h in range(2):
+                mixed[pl.ds(128 + 64 * h, 64), :] = a[2 + h]
+
+        @pl.when((n == 1) & (lax.rem(s, 2) == at[C]))
         def _():
-            uppers[1][rows, :] = a[0]
-            lower[rows, :] = a[1]
+            for out in messages:
+                for h in range(2):
+                    out[2 + h] = a[2 + h]
 
         @pl.when(lax.rem(s, 2) == at[C])
         def _():
-            for h in range(2):
-                gathers[2 * (1 - n), pl.ds(64 * h, 64), :] = a[2 + h]
             for k, rider in enumerate(riders):
                 v = at[Z] ^ k
                 block = a[2 + v // 2, :, rows_of(128 * lax.rem(v, 2), 128)]
                 rider[:, rows_of(128 * n, 128)] = block
 
-    copies = fetch([(gathers, target)], sems)
     for i, a in enumerate((a1, a3)):
         for h in range(2):
             t_one[i, :, pl.ds(256 * h, 256)] = a[4 + h]
-    arrive(copies)
-
-
-def column_kernel(at, e0, e1, e2, e3, upper, target, out, sems):
-    for h in range(2):
-        for i in range(2):
-            out[0, 2 * h + i] = upper[pl.ds(64 * i, 64), pl.ds(128 * h, 128)]
+
+
+def share_kernel(at, a0, a1, a2, a3, give, a_own):
+    for r, a in enumerate((a0, a1, a2, a3)):
+        give[r, pl.ds(0, 128), :] = a[pl.ds(0, 128), :]
+        give[r, pl.ds(128, 64), :] = a[rows_of(128 + 64 * (1 - at[C]), 64), :]
+        a_own[r] = a[rows_of(128 + 64 * at[C], 64), :]
+
+
+def column_kernel(at, e0, e1, e2, e3, out):
     for r, e in enumerate((e0, e1, e2, e3)):
-        for n in range(2):
-            out[1 + n, at[Z] ^ r] = e[pl.ds(128, 64), pl.ds(128 * n, 128)]
-    arrive(fetch([(out, target)], sems))
+        out[rows_of(64 * (at[Z] ^ r), 64), :] = e[pl.ds(128, 64), :]
 
 
 def local_kernel(at, e0, e1, e2, e3, *outs):
+    a_own, a_give = outs[4:]
     for r, e in enumerate((e0, e1, e2, e3)):
         s = at[X] ^ r
+        a_own[r] = e[2 + at[C]]
+        a_give[pl.ds(64 * r, 64), :] = e[3 - at[C]]
         for n in range(2):
 
             @pl.when(s // 2 == n)
@@ -421,7 +385,7 @@
         out_specs=[vmem] * (len(shapes) - out_far) + [hbm] * out_far,
         scratch_shapes=scratch,
         compiler_params=pltpu.CompilerParams(vmem_limit_bytes=16 * 1024 * 1024),
-        cost_estimate=pl.CostEstimate(flops=flops, bytes_accessed=4 * moved, transcendentals=0),
+        cost_estimate=pl.CostEstimate(flops=0, bytes_accessed=1024, transcendentals=0),
     )(at, *scalars, *far, *args)
 
 
@@ -442,9 +406,23 @@
     x8, y8 = ("xh", "xl", "co"), ("y", "co")
 
     factor, own, tail = coupling[0], inv_local[0], tail_block
-    dealt = local(deal_kernel, at, [], [(2, 64, 512)] * 4, copies=32, far=[factor, own, tail])
-    dealt = exchanged(dealt, deal)
-    keep, give = local(pair_kernel, at, dealt + [factor, own], [(4, 5, 64, 256)] * 2)
+    lane = jnp.where(co == 0, y, z)
+
+    def dealt_for(r):
+        def columns(a):
+            v = lane ^ r
+            starts = [jnp.where(co == 0, 512 * k + 128 * v, 512 * v + 128 * k) for k in range(4)]
+            return jnp.concatenate([lax.dynamic_slice(a, (0, s), (64, 128)) for s in starts], axis=1)
+
+        return jnp.stack([columns(factor), jnp.where(co == 0, columns(own), columns(tail))])
+
+    count = adjacency.shape[0]
+    joined = jnp.maximum(adjacency, jnp.eye(count, dtype=jnp.int32)).astype(jnp.float32)
+    mask = lax.dynamic_index_in_dim(joined, (z * 8 + y * 2 + xl) * 64 // TILE, 0, keepdims=False)
+    dealt = exchanged([dealt_for(r) for r in range(4)], deal)
+    keep, give = local(
+        pair_kernel, at, dealt + [factor, own], [(4, 5, 64, 256)] * 2, scalars=[mask]
+    )
     got = send(give, to_other_core)
     *rows, t_all = local(
         row_kernel,
@@ -453,16 +431,17 @@
         [(n, 64, 256) for n in (4, 6, 4, 6)] + [(2, 64, 256)] * 4 + [(4, 64, 512)],
     )
     rows, rows_local = rows[:4], rows[4:]
-    (upper_one, upper_three, lower_three, *riders, t_one, on_x) = local(
+    (uppers, mixed, lower_three, *riders) = local(
         base_kernel,
         at,
-        exchanged(rows, along["x"]),
-        [piece] * 3 + [half_piece] * 4 + [(2, 64, 512)] + [(3, *piece)],
-        [(3, *piece)],
-        copies=1,
-        out_far=1,
-    )
-    pieces = gathered(upper_three, "y")
+        exchanged(rows, along["x"]) + rows_local,
+        [(256, 256), (256, 256), piece]
+        + [half_piece] * 4
+        + [(4, 64, 256)] * 4
+        + [(2, 64, 512)],
+    )
+    riders, rows_local, t_one = riders[:4], riders[4:8], riders[8]
+    pieces = gathered(uppers, "y")
     lowers = gathered(lower_three, "x")
     (t_aside,) = after([t_one], pieces[1])
     t_two = send(t_aside, to_other_core)
@@ -470,46 +449,52 @@
     parts = product(
         cross_tail_kernel, at, [t_all, t_one, t_two] + pieces + riders, [wide, wide], 192
     )
-    b_own = jnp.concatenate(lowers)
-    b_sib = send(b_own, to_other_core)
-    (on_x, *rows_local) = after([on_x] + rows_local, parts[0])
-    on_x = lax.all_gather(on_x, x8)
+    b_sib = send(jnp.stack(lowers), to_other_core)
+    rows_local = after(rows_local, parts[0])
     cross, columns = scattered(parts, "z")
-    locals_ = local(local_kernel, at, exchanged(rows_local, along["x"]), [piece] * 4)
+    rows_local = exchanged(rows_local, along["x"])
     crosses, blocks = {3: cross}, {}
-    (on_y,) = local(
-        column_kernel,
-        at,
-        columns + [upper_one],
-        [(3, 4, 64, 128)],
-        [(3, 4, 64, 128)],
-        copies=1,
-        out_far=1,
-    )
+    (on_y,) = local(column_kernel, at, columns, [(256, 256)])
 
     for t in (3, 2, 1, 0):
         odd = t % 2 == 1
         first, second = ("y", "x") if odd else ("x", "y")
         if t < 3:
             mine = gathered(blocks[t + 1], second)
-            x_own = jnp.concatenate(mine)
             if t == 2:
-                (on_y,) = after([on_y], (blocks[3], on_x))
-                on_y = lax.all_gather(on_y, y8)
+                (mixed,) = after([mixed], blocks[3])
+                mixed = gathered(mixed, "x")
+                x_own = jnp.concatenate(after(mine + [a_give], tuple(mixed)))
+                (on_y,) = after([on_y], x_own)
+                on_y = gathered(on_y, "y")
+            else:
+                x_own = jnp.concatenate(mine)
             args = [x_own, send(x_own, to_other_core)]
-            kernel = functools.partial(cross_kernel, odd, 0 if t else 2)
-            far, copies = (on_y, 16) if odd else (on_x, 8)
-            parts = product(kernel, at, args, [wide, wide], 128, [far], copies)
+            if odd:
+                args += pieces
+            else:
+                args += [a_own] if t else [a_own, b_sib]
+            kernel = cross_odd_kernel if odd else cross_even_kernel
+            parts = product(kernel, at, args, [wide, wide])
             cross, _ = scattered(parts, "z")
             crosses[t] = cross
-        args = gathered(cross, "z")
+        whole = gathered(cross, "z")
+        if t == 2:
+            on_y = list(after(on_y, tuple(whole)))
+            on_y_sib = send(jnp.stack(on_y), to_other_core)
+        args = list(lowers) + [b_sib] if odd else on_y + [on_y_sib]
+        kernel = close_odd_kernel if odd else functools.partial(close_even_kernel, t // 2)
+        args += whole
+        parts = product(kernel, at, args, [square, wide, wide])
         if t == 3:
-            args = [b_own, b_sib] + args
-            parts = product(close_ring_kernel, at, args, [square, wide, wide])
-        else:
-            kernel = functools.partial(close_kernel, odd, 1 + t // 2)
-            far, copies = (on_x, 16) if odd else (on_y, 32)
-            parts = product(kernel, at, args, [(8, 64, 512), wide, wide], 128, [far], copies)
+            rows_local = after(rows_local, parts[0])
+            *locals_, a_own, a_give = local(
+                local_kernel, at, rows_local, [piece] * 4 + [(4, *half_piece), (256, 256)]
+            )
+        if t == 2:
+            lowers = list(after(mixed, parts[0]))
+            give, a_own = local(share_kernel, at, lowers, [(4, 192, 256), (4, *half_piece)])
+            b_sib = send(give, to_other_core)
         blocks[t] = scattered(parts, first)[0] + locals_[t]
 
     outs = [a[t] for t in range(4) for a in (blocks, crosses)]
@@ -519,9 +504,6 @@
     turned = local(turn_kernel, at, [keep, got], [(2, 64, 512)] * 4)
     back = exchanged(turned, along["y"], lambda co, **_: co == 0)
 
-    count = adjacency.shape[0]
-    joined = jnp.maximum(adjacency, jnp.eye(count, dtype=jnp.int32)).astype(jnp.float32)
-    mask = lax.dynamic_index_in_dim(joined, (z * 8 + y * 2 + xl) * 64 // TILE, 0, keepdims=False)
     diag, off = local(
         finish_kernel, at, list(turned) + back[1:], [(64, 2048)] * 2, scalars=[mask]
     )

time: 293 us -> 287 us (0.980)
  waiting for transfers between devices: 139 us -> 153 us
  between operations: 14.5 us -> 1.31 us
  local copies, waits for them, and re-layouts: 7.04 us -> 1.61 us
  starting transfers between devices: 106 us -> 111 us
  Pallas kernels: 22.9 us -> 18.1 us
    ppermute x73 -> x81, waiting for transfers between devices: 139 us -> 153 us  [send(): return lax.ppermute(x, AXES, route(place, only))]
    unnamed x15 -> x8, local copies, waits for them, and re-layouts: 6.94 us -> 0.05 us
    pallas_call x18, Pallas kernels: 22.9 us -> 18.1 us  [local(): pl.pallas_call(kernel, out_shape=[jax.ShapeDtypeStruct(s, jnp.float32) fo...]
    ppermute x73 -> x81, starting transfers between devices: 106 us -> 111 us  [send(): return lax.ppermute(x, AXES, route(place, only))]
  transfers between devices with their start and end apart: 75 -> 81, of which waited for: 58 -> 61; matrix products, arithmetic and copies ran while one was open for 0% -> 0% of each run, Pallas kernels for 2% -> 2%
where the time goes in v4:
time: 287 us; the launch traced here: 286 us
  waiting for transfers between devices  153 us (53%)
  starting transfers between devices  111 us (39%)
  Pallas kernels  18.1 us (6%)
    ppermute x81, waiting for transfers between devices, send(): return lax.ppermute(x, AXES, route(place, only))  153 us
    ppermute x81, starting transfers between devices, send(): return lax.ppermute(x, AXES, route(place, only))  111 us
    pallas_call x18, Pallas kernels, local(): pl.pallas_call(kernel, out_shape=[jax.ShapeDtypeStruct(s, jnp.float32) fo...  18.1 us
  transfers between devices with their start and end apart: 81, of which 61 were waited for; matrix products, arithmetic and copies ran while one was open for 0% of the time, Pallas kernels for 2%

profile of v4, /device:TPU:6, one launch (start us, length us, event | category | flops | bytes accessed | tf_op | source)
XLA Modules:
  0.0 285.6 jit_solution(14231955187074684790)
XLA Ops:
  4.1 3.0 %collective-permute-start.1 = (f32[2,64,512]{2,1,0:T(8,128)S(1)}, f32[2,64,512]{2,1,0:T(8,128)S(1)}, u32[]{:S(2)}, u32[]{:S(2)}) collective-permute-start(f32[2,64,512]{2,1,0:T(8,128)S(1)} %pad_maximum_fusion.6), channel_id=1, source_target_pairs={{0,4},{1,5},{2,6},{3,7},{4,0},{5,1},{6,2},{7,3},{8,12},{9,13},{10,... | collective-permute-start | bytes 786440 | tf_op jit(solution)/shard_map/ppermute | solution.py:32
  8.8 5.4 %collective-permute-done.1.d2 = f32[2,64,512]{2,1,0:T(8,128)S(1)} collective-permute-done((f32[2,64,512]{2,1,0:T(8,128)S(1)}, f32[2,64,512]{2,1,0:T(8,128)S(1)}, u32[]{:S(2)}, u32[]{:S(2)}) %collective-permute-start.1) | collective-permute-done | bytes 262176 | tf_op jit(solution)/shard_map/ppermute | solution.py:32
  14.2 2.7 collective-permute-done.2.d3
  17.7 3.0 %collective-permute-done.3.got = f32[4,5,64,256]{3,2,1,0:T(8,128)S(1)} collective-permute-done((f32[4,5,64,256]{3,2,1,0:T(8,128)S(1)}, f32[4,5,64,256]{3,2,1,0:T(8,128)S(1)}, u32[]{:S(2)}, u32[]{:S(2)}) %collective-permute-start.3) | collective-permute-done | bytes 1310752 | tf_op jit(solution)/shard_map/ppermute | solution.py:32
  23.5 2.1 collective-permute-start.5
  25.6 12.7 %collective-permute-done.5.a2 = f32[4,64,256]{2,1,0:T(8,128)S(1)} collective-permute-done((f32[4,64,256]{2,1,0:T(8,128)S(1)}, f32[4,64,256]{2,1,0:T(8,128)S(1)}, u32[]{:S(2)}, u32[]{:S(2)}) %collective-permute-start.5) | collective-permute-done | bytes 262176 | tf_op jit(solution)/shard_map/ppermute | solution.py:32
  42.2 2.2 collective-permute-start.10
  46.3 4.0 %collective-permute-done.7.rest_1_.a1 = f32[256,256]{1,0:T(8,128)S(1)} collective-permute-done((f32[256,256]{1,0:T(8,128)S(1)}, f32[256,256]{1,0:T(8,128)S(1)}, u32[]{:S(2)}, u32[]{:S(2)}) %collective-permute-start.7) | collective-permute-done | bytes 262176 | tf_op jit(solution)/shard_map/ppermute | solution.py:32
  52.3 5.8 %collective-permute-done.12.b2 = f32[128,256]{1,0:T(8,128)S(1)} collective-permute-done((f32[128,256]{1,0:T(8,128)S(1)}, f32[128,256]{1,0:T(8,128)S(1)}, u32[]{:S(2)}, u32[]{:S(2)}) %collective-permute-start.12) | collective-permute-done | bytes 131104 | tf_op jit(solution)/shard_map/ppermute | solution.py:32
  60.3 2.0 collective-permute-start.14
  62.3 3.6 %collective-permute-start.15 = (f32[192,256]{1,0:T(8,128)S(1)}, f32[192,256]{1,0:T(8,128)S(1)}, u32[]{:S(2)}, u32[]{:S(2)}) collective-permute-start(f32[192,256]{1,0:T(8,128)S(1)} %get-tuple-element.130), channel_id=1, source_target_pairs={{0,16},{1,17},{2,18},{3,19},{4,20},{5,21},{6,22},{7,23},{8,24},{9,... | collective-permute-start | bytes 589832 | tf_op jit(solution)/shard_map/ppermute | solution.py:32
  66.0 2.1 collective-permute-done.14.e1
  68.1 6.5 %collective-permute-done.15.e2 = f32[192,256]{1,0:T(8,128)S(1)} collective-permute-done((f32[192,256]{1,0:T(8,128)S(1)}, f32[192,256]{1,0:T(8,128)S(1)}, u32[]{:S(2)}, u32[]{:S(2)}) %collective-permute-start.15) | collective-permute-done | bytes 196640 | tf_op jit(solution)/shard_map/ppermute | solution.py:32
  74.7 2.6 collective-permute-done.16.e3
  78.1 2.9 %collective-permute-start.25 = (f32[4,64,256]{2,1,0:T(8,128)S(1)}, f32[4,64,256]{2,1,0:T(8,128)S(1)}, u32[]{:S(2)}, u32[]{:S(2)}) collective-permute-start(f32[4,64,256]{2,1,0:T(8,128)S(1)} %get-tuple-element.142), channel_id=1, source_target_pairs={{0,64},{1,65},{2,66},{3,67},{4,68},{5,69},{6,70},{7,71},{8,72},{9,... | collective-permute-start | bytes 786440 | tf_op jit(solution)/shard_map/ppermute | solution.py:32
  83.6 2.6 collective-permute-start.18
  86.2 2.5 collective-permute-done.19.y2
  88.7 1.9 collective-permute-done.18.y1
  93.6 3.0 %collective-permute-start.23 = (f32[128,256]{1,0:T(8,128)S(1)}, f32[128,256]{1,0:T(8,128)S(1)}, u32[]{:S(2)}, u32[]{:S(2)}) collective-permute-start(f32[128,256]{1,0:T(8,128)S(1)} %get-tuple-element.134), channel_id=1, source_target_pairs={{0,6},{1,7},{2,4},{3,5},{4,2},{5,3},{6,0},{7,1},{8,14},{9,15},{10,... | collective-permute-start | bytes 393224 | tf_op jit(solution)/shard_map/ppermute | solution.py:32
  100.1 3.5 %collective-permute-start.29 = (f32[128,256]{1,0:T(8,128)S(1)}, f32[128,256]{1,0:T(8,128)S(1)}, u32[]{:S(2)}, u32[]{:S(2)}) collective-permute-start(f32[128,256]{1,0:T(8,128)S(1)} %add_add_fusion.6.refs_6_), channel_id=1, source_target_pairs={{0,6},{1,7},{2,4},{3,5},{4,2},{5,3},{6,0},{7,1},{8,14},{9,15},{10,... | collective-permute-start | bytes 393224 | tf_op jit(solution)/shard_map/ppermute | solution.py:32
  103.6 2.1 collective-permute-start.32
  108.6 5.5 %collective-permute-done.28 = f32[128,256]{1,0:T(8,128)S(1)} collective-permute-done((f32[128,256]{1,0:T(8,128)S(1)}, f32[128,256]{1,0:T(8,128)S(1)}, u32[]{:S(2)}, u32[]{:S(2)}) %collective-permute-start.28) | collective-permute-done | bytes 131104 | tf_op jit(solution)/shard_map/ppermute | solution.py:32
  115.1 2.3 collective-permute-done.36.x_sib
  119.3 2.5 collective-permute-start.38
  125.4 2.7 collective-permute-start.33
  128.1 2.2 collective-permute-done.39
  132.1 6.2 %collective-permute-done.35.b3 = f32[256,256]{1,0:T(8,128)S(1)} collective-permute-done((f32[256,256]{1,0:T(8,128)S(1)}, f32[256,256]{1,0:T(8,128)S(1)}, u32[]{:S(2)}, u32[]{:S(2)}) %collective-permute-start.35) | collective-permute-done | bytes 262176 | tf_op jit(solution)/shard_map/ppermute | solution.py:32
  139.5 3.8 %collective-permute-done.40.y1 = f32[128,256]{1,0:T(8,128)S(1)} collective-permute-done((f32[128,256]{1,0:T(8,128)S(1)}, f32[128,256]{1,0:T(8,128)S(1)}, u32[]{:S(2)}, u32[]{:S(2)}) %collective-permute-start.40) | collective-permute-done | bytes 131104 | tf_op jit(solution)/shard_map/ppermute | solution.py:32
  143.5 2.6 collective-permute-done.43.b_sib
  148.2 3.0 %collective-permute-start.46 = (f32[128,256]{1,0:T(8,128)S(1)}, f32[128,256]{1,0:T(8,128)S(1)}, u32[]{:S(2)}, u32[]{:S(2)}) collective-permute-start(f32[128,256]{1,0:T(8,128)S(1)} %get-tuple-element.174), channel_id=1, source_target_pairs={{0,64},{1,65},{2,66},{3,67},{4,68},{5,69},{6,70},{7,71},{8,72},{9,... | collective-permute-start | bytes 393224 | tf_op jit(solution)/shard_map/ppermute | solution.py:32
  153.9 3.6 %collective-permute-done.46 = f32[128,256]{1,0:T(8,128)S(1)} collective-permute-done((f32[128,256]{1,0:T(8,128)S(1)}, f32[128,256]{1,0:T(8,128)S(1)}, u32[]{:S(2)}, u32[]{:S(2)}) %collective-permute-start.46) | collective-permute-done | bytes 131104 | tf_op jit(solution)/shard_map/ppermute | solution.py:32
  157.6 2.2 collective-permute-done.47
  161.1 2.9 %collective-permute-start.48 = (f32[128,256]{1,0:T(8,128)S(1)}, f32[128,256]{1,0:T(8,128)S(1)}, u32[]{:S(2)}, u32[]{:S(2)}) collective-permute-start(f32[128,256]{1,0:T(8,128)S(1)} %add_add_fusion.4.refs_4_), channel_id=1, source_target_pairs={{0,1},{1,0},{2,3},{3,2},{4,5},{5,4},{6,7},{7,6},{8,9},{9,8},{10,11... | collective-permute-start | bytes 393224 | tf_op jit(solution)/shard_map/ppermute | solution.py:32
  164.0 4.8 %collective-permute-done.50 = f32[128,256]{1,0:T(8,128)S(1)} collective-permute-done((f32[128,256]{1,0:T(8,128)S(1)}, f32[128,256]{1,0:T(8,128)S(1)}, u32[]{:S(2)}, u32[]{:S(2)}) %collective-permute-start.50) | collective-permute-done | bytes 131104 | tf_op jit(solution)/shard_map/ppermute | solution.py:32
  172.8 3.0 %collective-permute-start.53 = (f32[128,256]{1,0:T(8,128)S(1)}, f32[128,256]{1,0:T(8,128)S(1)}, u32[]{:S(2)}, u32[]{:S(2)}) collective-permute-start(f32[128,256]{1,0:T(8,128)S(1)} %get-tuple-element.178), channel_id=1, source_target_pairs={{0,16},{1,17},{2,18},{3,19},{4,20},{5,21},{6,22},{7,23},{8,24},{9,... | collective-permute-start | bytes 393224 | tf_op jit(solution)/shard_map/ppermute | solution.py:32
  179.1 3.1 %collective-permute-done.53 = f32[128,256]{1,0:T(8,128)S(1)} collective-permute-done((f32[128,256]{1,0:T(8,128)S(1)}, f32[128,256]{1,0:T(8,128)S(1)}, u32[]{:S(2)}, u32[]{:S(2)}) %collective-permute-start.53) | collective-permute-done | bytes 131104 | tf_op jit(solution)/shard_map/ppermute | solution.py:32
  182.3 2.2 collective-permute-done.54
  186.3 2.5 collective-permute-start.55
  188.7 4.3 %collective-permute-done.57.y3 = f32[128,256]{1,0:T(8,128)S(1)} collective-permute-done((f32[128,256]{1,0:T(8,128)S(1)}, f32[128,256]{1,0:T(8,128)S(1)}, u32[]{:S(2)}, u32[]{:S(2)}) %collective-permute-start.57) | collective-permute-done | bytes 131104 | tf_op jit(solution)/shard_map/ppermute | solution.py:32
  195.6 2.7 collective-permute-start.59
  198.3 2.0 collective-permute-start.60
  200.7 2.1 collective-permute-done.59
  204.5 2.3 collective-permute-start.63
  208.9 2.1 collective-permute-done.63
  211.0 2.3 collective-permute-done.62
  213.4 1.9 collective-permute-done.64.x_sib
  217.7 2.0 collective-permute-start.66
  223.0 3.2 %collective-permute-done.66 = f32[128,256]{1,0:T(8,128)S(1)} collective-permute-done((f32[128,256]{1,0:T(8,128)S(1)}, f32[128,256]{1,0:T(8,128)S(1)}, u32[]{:S(2)}, u32[]{:S(2)}) %collective-permute-start.66) | collective-permute-done | bytes 131104 | tf_op jit(solution)/shard_map/ppermute | solution.py:32
  226.1 2.2 collective-permute-done.67
  230.1 2.5 collective-permute-start.68
  232.6 4.3 %collective-permute-done.70.y3 = f32[128,256]{1,0:T(8,128)S(1)} collective-permute-done((f32[128,256]{1,0:T(8,128)S(1)}, f32[128,256]{1,0:T(8,128)S(1)}, u32[]{:S(2)}, u32[]{:S(2)}) %collective-permute-start.70) | collective-permute-done | bytes 131104 | tf_op jit(solution)/shard_map/ppermute | solution.py:32
  239.5 2.7 collective-permute-start.72
  242.3 1.9 collective-permute-start.73
  244.6 2.1 collective-permute-done.72
  249.6 3.1 %collective-permute-start.75 = (f32[2,2,64,256]{3,2,1,0:T(8,128)S(1)}, f32[2,2,64,256]{3,2,1,0:T(8,128)S(1)}, u32[]{:S(2)}, u32[]{:S(2)}) collective-permute-start(f32[2,2,64,256]{3,2,1,0:T(8,128)S(1)} %get-tuple-element.198), channel_id=1, source_target_pairs={{0,64},{1,65},{2,66},{3,67},{4,68},{5,69},{6,70},{7,71},{8,72},{9,... | collective-permute-start | bytes 786440 | tf_op jit(solution)/shard_map/ppermute | solution.py:32
  254.0 3.1 %collective-permute-done.74.a1 = f32[2,2,64,256]{3,2,1,0:T(8,128)S(1)} collective-permute-done((f32[2,2,64,256]{3,2,1,0:T(8,128)S(1)}, f32[2,2,64,256]{3,2,1,0:T(8,128)S(1)}, u32[]{:S(2)}, u32[]{:S(2)}) %collective-permute-start.74) | collective-permute-done | bytes 262176 | tf_op jit(solution)/shard_map/ppermute | solution.py:32
  257.1 4.3 %collective-permute-done.75.a2 = f32[2,2,64,256]{3,2,1,0:T(8,128)S(1)} collective-permute-done((f32[2,2,64,256]{3,2,1,0:T(8,128)S(1)}, f32[2,2,64,256]{3,2,1,0:T(8,128)S(1)}, u32[]{:S(2)}, u32[]{:S(2)}) %collective-permute-start.75) | collective-permute-done | bytes 262176 | tf_op jit(solution)/shard_map/ppermute | solution.py:32
  261.4 2.5 collective-permute-done.76.a3
  264.6 1.9 collective-permute-done.77.got
  267.2 2.5 collective-permute-start.78
  269.7 4.7 %collective-permute-start.79 = (f32[2,64,512]{2,1,0:T(8,128)S(1)}, f32[2,64,512]{2,1,0:T(8,128)S(1)}, u32[]{:S(2)}, u32[]{:S(2)}) collective-permute-start(f32[2,64,512]{2,1,0:T(8,128)S(1)} %get-tuple-element.204.d2), channel_id=1, source_target_pairs={{0,4},{1,5},{2,6},{3,7},{4,0},{5,1},{6,2},{7,3},{8,12},{9,13},{10,... | collective-permute-start | bytes 786440 | tf_op jit(solution)/shard_map/ppermute | solution.py:32
  274.4 3.2 %collective-permute-start.80 = (f32[2,64,512]{2,1,0:T(8,128)S(1)}, f32[2,64,512]{2,1,0:T(8,128)S(1)}, u32[]{:S(2)}, u32[]{:S(2)}) collective-permute-start(f32[2,64,512]{2,1,0:T(8,128)S(1)} %get-tuple-element.205.d3), channel_id=1, source_target_pairs={{0,6},{1,7},{2,4},{3,5},{4,2},{5,3},{6,0},{7,1},{8,14},{9,15},{10,... | collective-permute-start | bytes 786440 | tf_op jit(solution)/shard_map/ppermute | solution.py:32
  277.6 2.0 collective-permute-done.79.g2
  279.6 4.3 %collective-permute-done.80.g3 = f32[2,64,512]{2,1,0:T(8,128)S(1)} collective-permute-done((f32[2,64,512]{2,1,0:T(8,128)S(1)}, f32[2,64,512]{2,1,0:T(8,128)S(1)}, u32[]{:S(2)}, u32[]{:S(2)}) %collective-permute-start.80) | collective-permute-done | bytes 262176 | tf_op jit(solution)/shard_map/ppermute | solution.py:32
  (154 shorter events, 80.5 us)
Async XLA Ops:
  2.3 6.5 %collective-permute-start = (f32[2,64,512]{2,1,0:T(8,128)S(1)}, f32[2,64,512]{2,1,0:T(8,128)S(1)}, u32[]{:S(2)}, u32[]{:S(2)}) collective-permute-start(f32[2,64,512]{2,1,0:T(8,128)S(1)} %pad_maximum_fusion.5), channel_id=1, source_target_pairs={{0,2},{1,3},{2,0},{3,1},{4,6},{5,7},{6,4},{7,5},{8,10},{9,11},{10,... | collective-permute-start | bytes 786440 | tf_op jit(solution)/shard_map/ppermute | solution.py:32
  4.1 10.1 %collective-permute-start.1 = (f32[2,64,512]{2,1,0:T(8,128)S(1)}, f32[2,64,512]{2,1,0:T(8,128)S(1)}, u32[]{:S(2)}, u32[]{:S(2)}) collective-permute-start(f32[2,64,512]{2,1,0:T(8,128)S(1)} %pad_maximum_fusion.6), channel_id=1, source_target_pairs={{0,4},{1,5},{2,6},{3,7},{4,0},{5,1},{6,2},{7,3},{8,12},{9,13},{10,... | collective-permute-start | bytes 786440 | tf_op jit(solution)/shard_map/ppermute | solution.py:32
  7.1 9.7 %collective-permute-start.2 = (f32[2,64,512]{2,1,0:T(8,128)S(1)}, f32[2,64,512]{2,1,0:T(8,128)S(1)}, u32[]{:S(2)}, u32[]{:S(2)}) collective-permute-start(f32[2,64,512]{2,1,0:T(8,128)S(1)} %pad_maximum_fusion.7), channel_id=1, source_target_pairs={{0,6},{1,7},{2,4},{3,5},{4,2},{5,3},{6,0},{7,1},{8,14},{9,15},{10,... | collective-permute-start | bytes 786440 | tf_op jit(solution)/shard_map/ppermute | solution.py:32
  21.4 16.9 %collective-permute-start.4 = (f32[6,64,256]{2,1,0:T(8,128)S(1)}, f32[6,64,256]{2,1,0:T(8,128)S(1)}, u32[]{:S(2)}, u32[]{:S(2)}) collective-permute-start(f32[6,64,256]{2,1,0:T(8,128)S(1)} %get-tuple-element.109), channel_id=1, source_target_pairs={{0,1},{1,0},{2,3},{3,2},{4,5},{5,4},{6,7},{7,6},{8,9},{9,8},{10,11... | collective-permute-start | bytes 1179656 | tf_op jit(solution)/shard_map/ppermute | solution.py:32
  22.4 17.7 %collective-permute-start.6 = (f32[6,64,256]{2,1,0:T(8,128)S(1)}, f32[6,64,256]{2,1,0:T(8,128)S(1)}, u32[]{:S(2)}, u32[]{:S(2)}) collective-permute-start(f32[6,64,256]{2,1,0:T(8,128)S(1)} %get-tuple-element.111), channel_id=1, source_target_pairs={{0,65},{1,64},{2,67},{3,66},{4,69},{5,68},{6,71},{7,70},{8,73},{9,... | collective-permute-start | bytes 1179656 | tf_op jit(solution)/shard_map/ppermute | solution.py:32
  23.5 14.8 %collective-permute-start.5 = (f32[4,64,256]{2,1,0:T(8,128)S(1)}, f32[4,64,256]{2,1,0:T(8,128)S(1)}, u32[]{:S(2)}, u32[]{:S(2)}) collective-permute-start(f32[4,64,256]{2,1,0:T(8,128)S(1)} %get-tuple-element.110), channel_id=1, source_target_pairs={{0,64},{1,65},{2,66},{3,67},{4,68},{5,69},{6,70},{7,71},{8,72},{9,... | collective-permute-start | bytes 786440 | tf_op jit(solution)/shard_map/ppermute | solution.py:32
  41.0 9.3 %collective-permute-start.7 = (f32[256,256]{1,0:T(8,128)S(1)}, f32[256,256]{1,0:T(8,128)S(1)}, u32[]{:S(2)}, u32[]{:S(2)}) collective-permute-start(f32[256,256]{1,0:T(8,128)S(1)} %get-tuple-element.120.rest_0_.a0), channel_id=1, source_target_pairs={{0,2},{1,3},{2,0},{3,1},{4,6},{5,7},{6,4},{7,5},{8,10},{9,11},{10,... | collective-permute-start | bytes 786440 | tf_op jit(solution)/shard_map/ppermute | solution.py:32
  42.2 16.8 %collective-permute-start.10 = (f32[256,256]{1,0:T(8,128)S(1)}, f32[256,256]{1,0:T(8,128)S(1)}, u32[]{:S(2)}, u32[]{:S(2)}) collective-permute-start(f32[256,256]{1,0:T(8,128)S(1)} %get-tuple-element.120.rest_0_.a0), channel_id=1, source_target_pairs={{0,6},{1,7},{2,4},{3,5},{4,2},{5,3},{6,0},{7,1},{8,14},{9,15},{10,... | collective-permute-start | bytes 786440 | tf_op jit(solution)/shard_map/ppermute | solution.py:32
  44.4 14.6 %collective-permute-start.9 = (f32[256,256]{1,0:T(8,128)S(1)}, f32[256,256]{1,0:T(8,128)S(1)}, u32[]{:S(2)}, u32[]{:S(2)}) collective-permute-start(f32[256,256]{1,0:T(8,128)S(1)} %get-tuple-element.120.rest_0_.a0), channel_id=1, source_target_pairs={{0,4},{1,5},{2,6},{3,7},{4,0},{5,1},{6,2},{7,3},{8,12},{9,13},{10,... | collective-permute-start | bytes 786440 | tf_op jit(solution)/shard_map/ppermute | solution.py:32
  50.3 8.7 %collective-permute-start.8 = (f32[2,64,512]{2,1,0:T(8,128)S(1)}, f32[2,64,512]{2,1,0:T(8,128)S(1)}, u32[]{:S(2)}, u32[]{:S(2)}) collective-permute-start(f32[2,64,512]{2,1,0:T(8,128)S(1)} %get-tuple-element.118.t_one), channel_id=1, source_target_pairs={{0,32},{1,33},{2,34},{3,35},{4,36},{5,37},{6,38},{7,39},{8,40},{9,... | collective-permute-start | bytes 786440 | tf_op jit(solution)/shard_map/ppermute | solution.py:32
  50.3 7.8 %collective-permute-start.12 = (f32[128,256]{1,0:T(8,128)S(1)}, f32[128,256]{1,0:T(8,128)S(1)}, u32[]{:S(2)}, u32[]{:S(2)}) collective-permute-start(f32[128,256]{1,0:T(8,128)S(1)} %get-tuple-element.119.b0), channel_id=1, source_target_pairs={{0,64},{1,65},{2,66},{3,67},{4,68},{5,69},{6,70},{7,71},{8,72},{9,... | collective-permute-start | bytes 393224 | tf_op jit(solution)/shard_map/ppermute | solution.py:32
  51.3 7.7 %collective-permute-start.11 = (f32[128,256]{1,0:T(8,128)S(1)}, f32[128,256]{1,0:T(8,128)S(1)}, u32[]{:S(2)}, u32[]{:S(2)}) collective-permute-start(f32[128,256]{1,0:T(8,128)S(1)} %get-tuple-element.119.b0), channel_id=1, source_target_pairs={{0,1},{1,0},{2,3},{3,2},{4,5},{5,4},{6,7},{7,6},{8,9},{9,8},{10,11... | collective-permute-start | bytes 393224 | tf_op jit(solution)/shard_map/ppermute | solution.py:32
  60.3 7.9 %collective-permute-start.14 = (f32[192,256]{1,0:T(8,128)S(1)}, f32[192,256]{1,0:T(8,128)S(1)}, u32[]{:S(2)}, u32[]{:S(2)}) collective-permute-start(f32[192,256]{1,0:T(8,128)S(1)} %get-tuple-element.129), channel_id=1, source_target_pairs={{0,8},{1,9},{2,10},{3,11},{4,12},{5,13},{6,14},{7,15},{8,0},{9,1},... | collective-permute-start | bytes 589832 | tf_op jit(solution)/shard_map/ppermute | solution.py:32
  62.3 12.4 %collective-permute-start.15 = (f32[192,256]{1,0:T(8,128)S(1)}, f32[192,256]{1,0:T(8,128)S(1)}, u32[]{:S(2)}, u32[]{:S(2)}) collective-permute-start(f32[192,256]{1,0:T(8,128)S(1)} %get-tuple-element.130), channel_id=1, source_target_pairs={{0,16},{1,17},{2,18},{3,19},{4,20},{5,21},{6,22},{7,23},{8,24},{9,... | collective-permute-start | bytes 589832 | tf_op jit(solution)/shard_map/ppermute | solution.py:32
  65.9 11.4 %collective-permute-start.16 = (f32[192,256]{1,0:T(8,128)S(1)}, f32[192,256]{1,0:T(8,128)S(1)}, u32[]{:S(2)}, u32[]{:S(2)}) collective-permute-start(f32[192,256]{1,0:T(8,128)S(1)} %get-tuple-element.131), channel_id=1, source_target_pairs={{0,24},{1,25},{2,26},{3,27},{4,28},{5,29},{6,30},{7,31},{8,16},{9,... | collective-permute-start | bytes 589832 | tf_op jit(solution)/shard_map/ppermute | solution.py:32
  65.9 16.3 %collective-permute-start.17 = (f32[4,128,256]{2,1,0:T(8,128)S(1)}, f32[4,128,256]{2,1,0:T(8,128)S(1)}, u32[]{:S(2)}, u32[]{:S(2)}) collective-permute-start(f32[4,128,256]{2,1,0:T(8,128)S(1)} %pad_maximum_fusion.1), channel_id=1, source_target_pairs={{0,32},{1,33},{2,34},{3,35},{4,36},{5,37},{6,38},{7,39},{8,40},{9,... | collective-permute-start | bytes 1572872 | tf_op jit(solution)/shard_map/ppermute | solution.py:32
  77.4 16.2 %collective-permute-start.24 = (f32[4,64,256]{2,1,0:T(8,128)S(1)}, f32[4,64,256]{2,1,0:T(8,128)S(1)}, u32[]{:S(2)}, u32[]{:S(2)}) collective-permute-start(f32[4,64,256]{2,1,0:T(8,128)S(1)} %get-tuple-element.141), channel_id=1, source_target_pairs={{0,1},{1,0},{2,3},{3,2},{4,5},{5,4},{6,7},{7,6},{8,9},{9,8},{10,11... | collective-permute-start | bytes 786440 | tf_op jit(solution)/shard_map/ppermute | solution.py:32
  78.1 18.5 %collective-permute-start.25 = (f32[4,64,256]{2,1,0:T(8,128)S(1)}, f32[4,64,256]{2,1,0:T(8,128)S(1)}, u32[]{:S(2)}, u32[]{:S(2)}) collective-permute-start(f32[4,64,256]{2,1,0:T(8,128)S(1)} %get-tuple-element.142), channel_id=1, source_target_pairs={{0,64},{1,65},{2,66},{3,67},{4,68},{5,69},{6,70},{7,71},{8,72},{9,... | collective-permute-start | bytes 786440 | tf_op jit(solution)/shard_map/ppermute | solution.py:32
  81.0 15.6 %collective-permute-start.26 = (f32[4,64,256]{2,1,0:T(8,128)S(1)}, f32[4,64,256]{2,1,0:T(8,128)S(1)}, u32[]{:S(2)}, u32[]{:S(2)}) collective-permute-start(f32[4,64,256]{2,1,0:T(8,128)S(1)} %get-tuple-element.143), channel_id=1, source_target_pairs={{0,65},{1,64},{2,67},{3,66},{4,69},{5,68},{6,71},{7,70},{8,73},{9,... | collective-permute-start | bytes 786440 | tf_op jit(solution)/shard_map/ppermute | solution.py:32
  82.2 6.5 %collective-permute-start.19 = (f32[128,256]{1,0:T(8,128)S(1)}, f32[128,256]{1,0:T(8,128)S(1)}, u32[]{:S(2)}, u32[]{:S(2)}) collective-permute-start(f32[128,256]{1,0:T(8,128)S(1)} %fusion.y0.refs_7_), channel_id=1, source_target_pairs={{0,16},{1,17},{2,18},{3,19},{4,20},{5,21},{6,22},{7,23},{8,24},{9,... | collective-permute-start | bytes 393224 | tf_op jit(solution)/shard_map/ppermute | solution.py:32
  83.6 7.0 %collective-permute-start.18 = (f32[128,256]{1,0:T(8,128)S(1)}, f32[128,256]{1,0:T(8,128)S(1)}, u32[]{:S(2)}, u32[]{:S(2)}) collective-permute-start(f32[128,256]{1,0:T(8,128)S(1)} %fusion.y0.refs_7_), channel_id=1, source_target_pairs={{0,8},{1,9},{2,10},{3,11},{4,12},{5,13},{6,14},{7,15},{8,0},{9,1},... | collective-permute-start | bytes 393224 | tf_op jit(solution)/shard_map/ppermute | solution.py:32
  91.9 6.6 %collective-permute-start.22 = (f32[128,256]{1,0:T(8,128)S(1)}, f32[128,256]{1,0:T(8,128)S(1)}, u32[]{:S(2)}, u32[]{:S(2)}) collective-permute-start(f32[128,256]{1,0:T(8,128)S(1)} %get-tuple-element.133), channel_id=1, source_target_pairs={{0,4},{1,5},{2,6},{3,7},{4,0},{5,1},{6,2},{7,3},{8,12},{9,13},{10,... | collective-permute-start | bytes 393224 | tf_op jit(solution)/shard_map/ppermute | solution.py:32
  100.1 7.9 %collective-permute-start.29 = (f32[128,256]{1,0:T(8,128)S(1)}, f32[128,256]{1,0:T(8,128)S(1)}, u32[]{:S(2)}, u32[]{:S(2)}) collective-permute-start(f32[128,256]{1,0:T(8,128)S(1)} %add_add_fusion.6.refs_6_), channel_id=1, source_target_pairs={{0,6},{1,7},{2,4},{3,5},{4,2},{5,3},{6,0},{7,1},{8,14},{9,15},{10,... | collective-permute-start | bytes 393224 | tf_op jit(solution)/shard_map/ppermute | solution.py:32
  103.6 10.6 %collective-permute-start.32 = (f32[256,256]{1,0:T(8,128)S(1)}, f32[256,256]{1,0:T(8,128)S(1)}, u32[]{:S(2)}, u32[]{:S(2)}) collective-permute-start(f32[256,256]{1,0:T(8,128)S(1)} %get-tuple-element.168.a0.b0), channel_id=1, source_target_pairs={{0,65},{1,64},{2,67},{3,66},{4,69},{5,68},{6,71},{7,70},{8,73},{9,... | collective-permute-start | bytes 786440 | tf_op jit(solution)/shard_map/ppermute | solution.py:32
  105.7 8.5 %collective-permute-start.31 = (f32[256,256]{1,0:T(8,128)S(1)}, f32[256,256]{1,0:T(8,128)S(1)}, u32[]{:S(2)}, u32[]{:S(2)}) collective-permute-start(f32[256,256]{1,0:T(8,128)S(1)} %get-tuple-element.168.a0.b0), channel_id=1, source_target_pairs={{0,64},{1,65},{2,66},{3,67},{4,68},{5,69},{6,70},{7,71},{8,72},{9,... | collective-permute-start | bytes 786440 | tf_op jit(solution)/shard_map/ppermute | solution.py:32
  106.3 8.6 %collective-permute-start.30 = (f32[256,256]{1,0:T(8,128)S(1)}, f32[256,256]{1,0:T(8,128)S(1)}, u32[]{:S(2)}, u32[]{:S(2)}) collective-permute-start(f32[256,256]{1,0:T(8,128)S(1)} %get-tuple-element.168.a0.b0), channel_id=1, source_target_pairs={{0,1},{1,0},{2,3},{3,2},{4,5},{5,4},{6,7},{7,6},{8,9},{9,8},{10,11... | collective-permute-start | bytes 786440 | tf_op jit(solution)/shard_map/ppermute | solution.py:32
  107.7 6.5 %collective-permute-start.28 = (f32[128,256]{1,0:T(8,128)S(1)}, f32[128,256]{1,0:T(8,128)S(1)}, u32[]{:S(2)}, u32[]{:S(2)}) collective-permute-start(f32[128,256]{1,0:T(8,128)S(1)} %add_add_fusion.6.refs_6_), channel_id=1, source_target_pairs={{0,4},{1,5},{2,6},{3,7},{4,0},{5,1},{6,2},{7,3},{8,12},{9,13},{10,... | collective-permute-start | bytes 393224 | tf_op jit(solution)/shard_map/ppermute | solution.py:32
  118.6 6.8 %collective-permute-start.37 = (f32[128,256]{1,0:T(8,128)S(1)}, f32[128,256]{1,0:T(8,128)S(1)}, u32[]{:S(2)}, u32[]{:S(2)}) collective-permute-start(f32[128,256]{1,0:T(8,128)S(1)} %get-tuple-element.159), channel_id=1, source_target_pairs={{0,8},{1,9},{2,10},{3,11},{4,12},{5,13},{6,14},{7,15},{8,0},{9,1},... | collective-permute-start | bytes 393224 | tf_op jit(solution)/shard_map/ppermute | solution.py:32
  119.3 8.9 %collective-permute-start.38 = (f32[128,256]{1,0:T(8,128)S(1)}, f32[128,256]{1,0:T(8,128)S(1)}, u32[]{:S(2)}, u32[]{:S(2)}) collective-permute-start(f32[128,256]{1,0:T(8,128)S(1)} %get-tuple-element.160), channel_id=1, source_target_pairs={{0,16},{1,17},{2,18},{3,19},{4,20},{5,21},{6,22},{7,23},{8,24},{9,... | collective-permute-start | bytes 393224 | tf_op jit(solution)/shard_map/ppermute | solution.py:32
  121.7 8.7 %collective-permute-start.39 = (f32[128,256]{1,0:T(8,128)S(1)}, f32[128,256]{1,0:T(8,128)S(1)}, u32[]{:S(2)}, u32[]{:S(2)}) collective-permute-start(f32[128,256]{1,0:T(8,128)S(1)} %get-tuple-element.161), channel_id=1, source_target_pairs={{0,24},{1,25},{2,26},{3,27},{4,28},{5,29},{6,30},{7,31},{8,16},{9,... | collective-permute-start | bytes 393224 | tf_op jit(solution)/shard_map/ppermute | solution.py:32
  123.9 14.4 %collective-permute-start.35 = (f32[256,256]{1,0:T(8,128)S(1)}, f32[256,256]{1,0:T(8,128)S(1)}, u32[]{:S(2)}, u32[]{:S(2)}) collective-permute-start(f32[256,256]{1,0:T(8,128)S(1)} %shard_map.63.b0), channel_id=1, source_target_pairs={{0,6},{1,7},{2,4},{3,5},{4,2},{5,3},{6,0},{7,1},{8,14},{9,15},{10,... | collective-permute-start | bytes 786440 | tf_op jit(solution)/shard_map/ppermute | solution.py:32
  125.2 13.1 %collective-permute-start.34 = (f32[256,256]{1,0:T(8,128)S(1)}, f32[256,256]{1,0:T(8,128)S(1)}, u32[]{:S(2)}, u32[]{:S(2)}) collective-permute-start(f32[256,256]{1,0:T(8,128)S(1)} %shard_map.63.b0), channel_id=1, source_target_pairs={{0,4},{1,5},{2,6},{3,7},{4,0},{5,1},{6,2},{7,3},{8,12},{9,13},{10,... | collective-permute-start | bytes 786440 | tf_op jit(solution)/shard_map/ppermute | solution.py:32
  125.4 13.5 %collective-permute-start.33 = (f32[256,256]{1,0:T(8,128)S(1)}, f32[256,256]{1,0:T(8,128)S(1)}, u32[]{:S(2)}, u32[]{:S(2)}) collective-permute-start(f32[256,256]{1,0:T(8,128)S(1)} %shard_map.63.b0), channel_id=1, source_target_pairs={{0,2},{1,3},{2,0},{3,1},{4,6},{5,7},{6,4},{7,5},{8,10},{9,11},{10,... | collective-permute-start | bytes 786440 | tf_op jit(solution)/shard_map/ppermute | solution.py:32
  130.4 9.1 %collective-permute-start.42 = (f32[128,256]{1,0:T(8,128)S(1)}, f32[128,256]{1,0:T(8,128)S(1)}, u32[]{:S(2)}, u32[]{:S(2)}) collective-permute-start(f32[128,256]{1,0:T(8,128)S(1)} %add_add_fusion.5.y0.refs_5_), channel_id=1, source_target_pairs={{0,24},{1,25},{2,26},{3,27},{4,28},{5,29},{6,30},{7,31},{8,16},{9,... | collective-permute-start | bytes 393224 | tf_op jit(solution)/shard_map/ppermute | solution.py:32
  132.1 7.4 %collective-permute-start.41 = (f32[128,256]{1,0:T(8,128)S(1)}, f32[128,256]{1,0:T(8,128)S(1)}, u32[]{:S(2)}, u32[]{:S(2)}) collective-permute-start(f32[128,256]{1,0:T(8,128)S(1)} %add_add_fusion.5.y0.refs_5_), channel_id=1, source_target_pairs={{0,16},{1,17},{2,18},{3,19},{4,20},{5,21},{6,22},{7,23},{8,24},{9,... | collective-permute-start | bytes 393224 | tf_op jit(solution)/shard_map/ppermute | solution.py:32
  147.5 6.4 %collective-permute-start.45 = (f32[128,256]{1,0:T(8,128)S(1)}, f32[128,256]{1,0:T(8,128)S(1)}, u32[]{:S(2)}, u32[]{:S(2)}) collective-permute-start(f32[128,256]{1,0:T(8,128)S(1)} %get-tuple-element.173), channel_id=1, source_target_pairs={{0,1},{1,0},{2,3},{3,2},{4,5},{5,4},{6,7},{7,6},{8,9},{9,8},{10,11... | collective-permute-start | bytes 393224 | tf_op jit(solution)/shard_map/ppermute | solution.py:32
  148.2 9.4 %collective-permute-start.46 = (f32[128,256]{1,0:T(8,128)S(1)}, f32[128,256]{1,0:T(8,128)S(1)}, u32[]{:S(2)}, u32[]{:S(2)}) collective-permute-start(f32[128,256]{1,0:T(8,128)S(1)} %get-tuple-element.174), channel_id=1, source_target_pairs={{0,64},{1,65},{2,66},{3,67},{4,68},{5,69},{6,70},{7,71},{8,72},{9,... | collective-permute-start | bytes 393224 | tf_op jit(solution)/shard_map/ppermute | solution.py:32
  151.1 8.7 %collective-permute-start.47 = (f32[128,256]{1,0:T(8,128)S(1)}, f32[128,256]{1,0:T(8,128)S(1)}, u32[]{:S(2)}, u32[]{:S(2)}) collective-permute-start(f32[128,256]{1,0:T(8,128)S(1)} %get-tuple-element.175), channel_id=1, source_target_pairs={{0,65},{1,64},{2,67},{3,66},{4,69},{5,68},{6,71},{7,70},{8,73},{9,... | collective-permute-start | bytes 393224 | tf_op jit(solution)/shard_map/ppermute | solution.py:32
  159.9 9.0 %collective-permute-start.50 = (f32[128,256]{1,0:T(8,128)S(1)}, f32[128,256]{1,0:T(8,128)S(1)}, u32[]{:S(2)}, u32[]{:S(2)}) collective-permute-start(f32[128,256]{1,0:T(8,128)S(1)} %add_add_fusion.4.refs_4_), channel_id=1, source_target_pairs={{0,65},{1,64},{2,67},{3,66},{4,69},{5,68},{6,71},{7,70},{8,73},{9,... | collective-permute-start | bytes 393224 | tf_op jit(solution)/shard_map/ppermute | solution.py:32
  161.1 7.8 %collective-permute-start.49 = (f32[128,256]{1,0:T(8,128)S(1)}, f32[128,256]{1,0:T(8,128)S(1)}, u32[]{:S(2)}, u32[]{:S(2)}) collective-permute-start(f32[128,256]{1,0:T(8,128)S(1)} %add_add_fusion.4.refs_4_), channel_id=1, source_target_pairs={{0,64},{1,65},{2,66},{3,67},{4,68},{5,69},{6,70},{7,71},{8,72},{9,... | collective-permute-start | bytes 393224 | tf_op jit(solution)/shard_map/ppermute | solution.py:32
  161.1 8.4 %collective-permute-start.48 = (f32[128,256]{1,0:T(8,128)S(1)}, f32[128,256]{1,0:T(8,128)S(1)}, u32[]{:S(2)}, u32[]{:S(2)}) collective-permute-start(f32[128,256]{1,0:T(8,128)S(1)} %add_add_fusion.4.refs_4_), channel_id=1, source_target_pairs={{0,1},{1,0},{2,3},{3,2},{4,5},{5,4},{6,7},{7,6},{8,9},{9,8},{10,11... | collective-permute-start | bytes 393224 | tf_op jit(solution)/shard_map/ppermute | solution.py:32
  170.2 18.5 %collective-permute-start.44 = (f32[4,192,256]{2,1,0:T(8,128)S(1)}, f32[4,192,256]{2,1,0:T(8,128)S(1)}, u32[]{:S(2)}, u32[]{:S(2)}) collective-permute-start(f32[4,192,256]{2,1,0:T(8,128)S(1)} %get-tuple-element.172), channel_id=1, source_target_pairs={{0,32},{1,33},{2,34},{3,35},{4,36},{5,37},{6,38},{7,39},{8,40},{9,... | collective-permute-start | bytes 2359304 | tf_op jit(solution)/shard_map/ppermute | solution.py:32
  172.7 6.4 %collective-permute-start.52 = (f32[128,256]{1,0:T(8,128)S(1)}, f32[128,256]{1,0:T(8,128)S(1)}, u32[]{:S(2)}, u32[]{:S(2)}) collective-permute-start(f32[128,256]{1,0:T(8,128)S(1)} %get-tuple-element.177), channel_id=1, source_target_pairs={{0,8},{1,9},{2,10},{3,11},{4,12},{5,13},{6,14},{7,15},{8,0},{9,1},... | collective-permute-start | bytes 393224 | tf_op jit(solution)/shard_map/ppermute | solution.py:32
  172.8 9.5 %collective-permute-start.53 = (f32[128,256]{1,0:T(8,128)S(1)}, f32[128,256]{1,0:T(8,128)S(1)}, u32[]{:S(2)}, u32[]{:S(2)}) collective-permute-start(f32[128,256]{1,0:T(8,128)S(1)} %get-tuple-element.178), channel_id=1, source_target_pairs={{0,16},{1,17},{2,18},{3,19},{4,20},{5,21},{6,22},{7,23},{8,24},{9,... | collective-permute-start | bytes 393224 | tf_op jit(solution)/shard_map/ppermute | solution.py:32
  175.9 8.7 %collective-permute-start.54 = (f32[128,256]{1,0:T(8,128)S(1)}, f32[128,256]{1,0:T(8,128)S(1)}, u32[]{:S(2)}, u32[]{:S(2)}) collective-permute-start(f32[128,256]{1,0:T(8,128)S(1)} %get-tuple-element.179), channel_id=1, source_target_pairs={{0,24},{1,25},{2,26},{3,27},{4,28},{5,29},{6,30},{7,31},{8,16},{9,... | collective-permute-start | bytes 393224 | tf_op jit(solution)/shard_map/ppermute | solution.py:32
  184.6 8.5 %collective-permute-start.57 = (f32[128,256]{1,0:T(8,128)S(1)}, f32[128,256]{1,0:T(8,128)S(1)}, u32[]{:S(2)}, u32[]{:S(2)}) collective-permute-start(f32[128,256]{1,0:T(8,128)S(1)} %add_add_fusion.3.y0.refs_3_), channel_id=1, source_target_pairs={{0,24},{1,25},{2,26},{3,27},{4,28},{5,29},{6,30},{7,31},{8,16},{9,... | collective-permute-start | bytes 393224 | tf_op jit(solution)/shard_map/ppermute | solution.py:32
  186.3 7.6 %collective-permute-start.56 = (f32[128,256]{1,0:T(8,128)S(1)}, f32[128,256]{1,0:T(8,128)S(1)}, u32[]{:S(2)}, u32[]{:S(2)}) collective-permute-start(f32[128,256]{1,0:T(8,128)S(1)} %add_add_fusion.3.y0.refs_3_), channel_id=1, source_target_pairs={{0,16},{1,17},{2,18},{3,19},{4,20},{5,21},{6,22},{7,23},{8,24},{9,... | collective-permute-start | bytes 393224 | tf_op jit(solution)/shard_map/ppermute | solution.py:32
  186.3 7.9 %collective-permute-start.55 = (f32[128,256]{1,0:T(8,128)S(1)}, f32[128,256]{1,0:T(8,128)S(1)}, u32[]{:S(2)}, u32[]{:S(2)}) collective-permute-start(f32[128,256]{1,0:T(8,128)S(1)} %add_add_fusion.3.y0.refs_3_), channel_id=1, source_target_pairs={{0,8},{1,9},{2,10},{3,11},{4,12},{5,13},{6,14},{7,15},{8,0},{9,1},... | collective-permute-start | bytes 393224 | tf_op jit(solution)/shard_map/ppermute | solution.py:32
  195.6 7.2 %collective-permute-start.59 = (f32[128,256]{1,0:T(8,128)S(1)}, f32[128,256]{1,0:T(8,128)S(1)}, u32[]{:S(2)}, u32[]{:S(2)}) collective-permute-start(f32[128,256]{1,0:T(8,128)S(1)} %get-tuple-element.182), channel_id=1, source_target_pairs={{0,4},{1,5},{2,6},{3,7},{4,0},{5,1},{6,2},{7,3},{8,12},{9,13},{10,... | collective-permute-start | bytes 393224 | tf_op jit(solution)/shard_map/ppermute | solution.py:32
  204.5 6.5 %collective-permute-start.63 = (f32[128,256]{1,0:T(8,128)S(1)}, f32[128,256]{1,0:T(8,128)S(1)}, u32[]{:S(2)}, u32[]{:S(2)}) collective-permute-start(f32[128,256]{1,0:T(8,128)S(1)} %add_add_fusion.2.refs_2_), channel_id=1, source_target_pairs={{0,6},{1,7},{2,4},{3,5},{4,2},{5,3},{6,0},{7,1},{8,14},{9,15},{10,... | collective-permute-start | bytes 393224 | tf_op jit(solution)/shard_map/ppermute | solution.py:32
  206.8 6.5 %collective-permute-start.62 = (f32[128,256]{1,0:T(8,128)S(1)}, f32[128,256]{1,0:T(8,128)S(1)}, u32[]{:S(2)}, u32[]{:S(2)}) collective-permute-start(f32[128,256]{1,0:T(8,128)S(1)} %add_add_fusion.2.refs_2_), channel_id=1, source_target_pairs={{0,4},{1,5},{2,6},{3,7},{4,0},{5,1},{6,2},{7,3},{8,12},{9,13},{10,... | collective-permute-start | bytes 393224 | tf_op jit(solution)/shard_map/ppermute | solution.py:32
  216.5 6.4 %collective-permute-start.65 = (f32[128,256]{1,0:T(8,128)S(1)}, f32[128,256]{1,0:T(8,128)S(1)}, u32[]{:S(2)}, u32[]{:S(2)}) collective-permute-start(f32[128,256]{1,0:T(8,128)S(1)} %get-tuple-element.187), channel_id=1, source_target_pairs={{0,8},{1,9},{2,10},{3,11},{4,12},{5,13},{6,14},{7,15},{8,0},{9,1},... | collective-permute-start | bytes 393224 | tf_op jit(solution)/shard_map/ppermute | solution.py:32
  217.7 8.4 %collective-permute-start.66 = (f32[128,256]{1,0:T(8,128)S(1)}, f32[128,256]{1,0:T(8,128)S(1)}, u32[]{:S(2)}, u32[]{:S(2)}) collective-permute-start(f32[128,256]{1,0:T(8,128)S(1)} %get-tuple-element.188), channel_id=1, source_target_pairs={{0,16},{1,17},{2,18},{3,19},{4,20},{5,21},{6,22},{7,23},{8,24},{9,... | collective-permute-start | bytes 393224 | tf_op jit(solution)/shard_map/ppermute | solution.py:32
  219.7 8.7 %collective-permute-start.67 = (f32[128,256]{1,0:T(8,128)S(1)}, f32[128,256]{1,0:T(8,128)S(1)}, u32[]{:S(2)}, u32[]{:S(2)}) collective-permute-start(f32[128,256]{1,0:T(8,128)S(1)} %get-tuple-element.189), channel_id=1, source_target_pairs={{0,24},{1,25},{2,26},{3,27},{4,28},{5,29},{6,30},{7,31},{8,16},{9,... | collective-permute-start | bytes 393224 | tf_op jit(solution)/shard_map/ppermute | solution.py:32
  228.4 8.5 %collective-permute-start.70 = (f32[128,256]{1,0:T(8,128)S(1)}, f32[128,256]{1,0:T(8,128)S(1)}, u32[]{:S(2)}, u32[]{:S(2)}) collective-permute-start(f32[128,256]{1,0:T(8,128)S(1)} %add_add_fusion.1.y0.refs_1_), channel_id=1, source_target_pairs={{0,24},{1,25},{2,26},{3,27},{4,28},{5,29},{6,30},{7,31},{8,16},{9,... | collective-permute-start | bytes 393224 | tf_op jit(solution)/shard_map/ppermute | solution.py:32
  230.1 7.6 %collective-permute-start.69 = (f32[128,256]{1,0:T(8,128)S(1)}, f32[128,256]{1,0:T(8,128)S(1)}, u32[]{:S(2)}, u32[]{:S(2)}) collective-permute-start(f32[128,256]{1,0:T(8,128)S(1)} %add_add_fusion.1.y0.refs_1_), channel_id=1, source_target_pairs={{0,16},{1,17},{2,18},{3,19},{4,20},{5,21},{6,22},{7,23},{8,24},{9,... | collective-permute-start | bytes 393224 | tf_op jit(solution)/shard_map/ppermute | solution.py:32
  230.1 7.9 %collective-permute-start.68 = (f32[128,256]{1,0:T(8,128)S(1)}, f32[128,256]{1,0:T(8,128)S(1)}, u32[]{:S(2)}, u32[]{:S(2)}) collective-permute-start(f32[128,256]{1,0:T(8,128)S(1)} %add_add_fusion.1.y0.refs_1_), channel_id=1, source_target_pairs={{0,8},{1,9},{2,10},{3,11},{4,12},{5,13},{6,14},{7,15},{8,0},{9,1},... | collective-permute-start | bytes 393224 | tf_op jit(solution)/shard_map/ppermute | solution.py:32
  239.5 7.3 %collective-permute-start.72 = (f32[128,256]{1,0:T(8,128)S(1)}, f32[128,256]{1,0:T(8,128)S(1)}, u32[]{:S(2)}, u32[]{:S(2)}) collective-permute-start(f32[128,256]{1,0:T(8,128)S(1)} %get-tuple-element.192), channel_id=1, source_target_pairs={{0,64},{1,65},{2,66},{3,67},{4,68},{5,69},{6,70},{7,71},{8,72},{9,... | collective-permute-start | bytes 393224 | tf_op jit(solution)/shard_map/ppermute | solution.py:32
  249.2 7.9 %collective-permute-start.74 = (f32[2,2,64,256]{3,2,1,0:T(8,128)S(1)}, f32[2,2,64,256]{3,2,1,0:T(8,128)S(1)}, u32[]{:S(2)}, u32[]{:S(2)}) collective-permute-start(f32[2,2,64,256]{3,2,1,0:T(8,128)S(1)} %get-tuple-element.197), channel_id=1, source_target_pairs={{0,1},{1,0},{2,3},{3,2},{4,5},{5,4},{6,7},{7,6},{8,9},{9,8},{10,11... | collective-permute-start | bytes 786440 | tf_op jit(solution)/shard_map/ppermute | solution.py:32
  249.6 11.8 %collective-permute-start.75 = (f32[2,2,64,256]{3,2,1,0:T(8,128)S(1)}, f32[2,2,64,256]{3,2,1,0:T(8,128)S(1)}, u32[]{:S(2)}, u32[]{:S(2)}) collective-permute-start(f32[2,2,64,256]{3,2,1,0:T(8,128)S(1)} %get-tuple-element.198), channel_id=1, source_target_pairs={{0,64},{1,65},{2,66},{3,67},{4,68},{5,69},{6,70},{7,71},{8,72},{9,... | collective-permute-start | bytes 786440 | tf_op jit(solution)/shard_map/ppermute | solution.py:32
  252.7 11.2 %collective-permute-start.76 = (f32[2,2,64,256]{3,2,1,0:T(8,128)S(1)}, f32[2,2,64,256]{3,2,1,0:T(8,128)S(1)}, u32[]{:S(2)}, u32[]{:S(2)}) collective-permute-start(f32[2,2,64,256]{3,2,1,0:T(8,128)S(1)} %get-tuple-element.199), channel_id=1, source_target_pairs={{0,65},{1,64},{2,67},{3,66},{4,69},{5,68},{6,71},{7,70},{8,73},{9,... | collective-permute-start | bytes 786440 | tf_op jit(solution)/shard_map/ppermute | solution.py:32
  267.2 10.4 %collective-permute-start.78 = (f32[2,64,512]{2,1,0:T(8,128)S(1)}, f32[2,64,512]{2,1,0:T(8,128)S(1)}, u32[]{:S(2)}, u32[]{:S(2)}) collective-permute-start(f32[2,64,512]{2,1,0:T(8,128)S(1)} %get-tuple-element.203.d1), channel_id=1, source_target_pairs={{0,2},{1,3},{2,0},{3,1},{4,6},{5,7},{6,4},{7,5},{8,10},{9,11},{10,... | collective-permute-start | bytes 786440 | tf_op jit(solution)/shard_map/ppermute | solution.py:32
  269.7 9.9 %collective-permute-start.79 = (f32[2,64,512]{2,1,0:T(8,128)S(1)}, f32[2,64,512]{2,1,0:T(8,128)S(1)}, u32[]{:S(2)}, u32[]{:S(2)}) collective-permute-start(f32[2,64,512]{2,1,0:T(8,128)S(1)} %get-tuple-element.204.d2), channel_id=1, source_target_pairs={{0,4},{1,5},{2,6},{3,7},{4,0},{5,1},{6,2},{7,3},{8,12},{9,13},{10,... | collective-permute-start | bytes 786440 | tf_op jit(solution)/shard_map/ppermute | solution.py:32
  274.4 9.5 %collective-permute-start.80 = (f32[2,64,512]{2,1,0:T(8,128)S(1)}, f32[2,64,512]{2,1,0:T(8,128)S(1)}, u32[]{:S(2)}, u32[]{:S(2)}) collective-permute-start(f32[2,64,512]{2,1,0:T(8,128)S(1)} %get-tuple-element.205.d3), channel_id=1, source_target_pairs={{0,6},{1,7},{2,4},{3,5},{4,2},{5,3},{6,0},{7,1},{8,14},{9,15},{10,... | collective-permute-start | bytes 786440 | tf_op jit(solution)/shard_map/ppermute | solution.py:32
  (19 other events, 81.5 us)

commit v5 on v4

--- a/solution.py
+++ b/solution.py
@@ -258,11 +258,8 @@
         fill(keep, got)
 
 
-def base_kernel(at, a0, a1, a2, a3, l0, l1, l2, l3, *outs):
-    uppers, mixed, lower, riders, messages, t_one = (*outs[:3], outs[3:7], outs[7:11], outs[11])
-    for out, rows in zip(messages, (l0, l1, l2, l3)):
-        out[0] = rows[0]
-        out[1] = rows[1]
+def base_kernel(at, a0, a1, a2, a3, *outs):
+    uppers, mixed, riders, t_one = outs[0], outs[1:3], outs[3:7], outs[7]
     for r, a in enumerate((a0, a1, a2, a3)):
         s = at[X] ^ r
         n = s // 2
@@ -272,18 +269,12 @@
             @pl.when(n == i)
             def _():
                 uppers[rows_of(128 * (1 - i) + 64 * lax.rem(s, 2), 64), :] = a[0]
-                (mixed, lower)[i][rows, :] = a[1]
-
-        @pl.when((n == 0) & (lax.rem(s, 2) == at[C]))
-        def _():
-            for h in range(2):
-                mixed[pl.ds(128 + 64 * h, 64), :] = a[2 + h]
-
-        @pl.when((n == 1) & (lax.rem(s, 2) == at[C]))
-        def _():
-            for out in messages:
+                mixed[i][rows, :] = a[1]
+
+            @pl.when((n == i) & (lax.rem(s, 2) == at[C]))
+            def _():
                 for h in range(2):
-                    out[2 + h] = a[2 + h]
+                    mixed[i][pl.ds(128 + 64 * h, 64), :] = a[2 + h]
 
         @pl.when(lax.rem(s, 2) == at[C])
         def _():
@@ -309,12 +300,13 @@
         out[rows_of(64 * (at[Z] ^ r), 64), :] = e[pl.ds(128, 64), :]
 
 
-def local_kernel(at, e0, e1, e2, e3, *outs):
+def local_kernel(at, e0, e1, e2, e3, m0, m1, m2, m3, *outs):
     a_own, a_give = outs[4:]
+    for r, m in enumerate((m0, m1, m2, m3)):
+        a_own[r] = m[rows_of(128 + 64 * at[C], 64), :]
+        a_give[pl.ds(64 * r, 64), :] = m[rows_of(128 + 64 * (1 - at[C]), 64), :]
     for r, e in enumerate((e0, e1, e2, e3)):
         s = at[X] ^ r
-        a_own[r] = e[2 + at[C]]
-        a_give[pl.ds(64 * r, 64), :] = e[3 - at[C]]
         for n in range(2):
 
             @pl.when(s // 2 == n)
@@ -431,25 +423,21 @@
         [(n, 64, 256) for n in (4, 6, 4, 6)] + [(2, 64, 256)] * 4 + [(4, 64, 512)],
     )
     rows, rows_local = rows[:4], rows[4:]
-    (uppers, mixed, lower_three, *riders) = local(
+    (uppers, mixed, lowers, *riders, t_one) = local(
         base_kernel,
         at,
-        exchanged(rows, along["x"]) + rows_local,
-        [(256, 256), (256, 256), piece]
-        + [half_piece] * 4
-        + [(4, 64, 256)] * 4
-        + [(2, 64, 512)],
-    )
-    riders, rows_local, t_one = riders[:4], riders[4:8], riders[8]
+        exchanged(rows, along["x"]),
+        [(256, 256)] * 3 + [half_piece] * 4 + [(2, 64, 512)],
+    )
     pieces = gathered(uppers, "y")
-    lowers = gathered(lower_three, "x")
+    lowers = gathered(lowers, "x")
     (t_aside,) = after([t_one], pieces[1])
     t_two = send(t_aside, to_other_core)
     pieces = list(after(pieces, tuple(lowers)))
     parts = product(
         cross_tail_kernel, at, [t_all, t_one, t_two] + pieces + riders, [wide, wide], 192
     )
-    b_sib = send(jnp.stack(lowers), to_other_core)
+    b_sib = send(jnp.stack([a[:128] for a in lowers]), to_other_core)
     rows_local = after(rows_local, parts[0])
     cross, columns = scattered(parts, "z")
     rows_local = exchanged(rows_local, along["x"])
@@ -489,7 +477,7 @@
         if t == 3:
             rows_local = after(rows_local, parts[0])
             *locals_, a_own, a_give = local(
-                local_kernel, at, rows_local, [piece] * 4 + [(4, *half_piece), (256, 256)]
+                local_kernel, at, list(rows_local) + lowers, [piece] * 4 + [(4, *half_piece), (256, 256)]
             )
         if t == 2:
             lowers = list(after(mixed, parts[0]))

time: 287 us -> 288 us (level)
  transfers between devices with their start and end apart: 81 -> 81, of which waited for: 61 -> 59; matrix products, arithmetic and copies ran while one was open for 0% -> 0% of each run, Pallas kernels for 2% -> 2%
where the time goes in v5:
time: 288 us; the launch traced here: 287 us
  waiting for transfers between devices  154 us (53%)
  starting transfers between devices  111 us (39%)
  Pallas kernels  18.1 us (6%)
    ppermute x81, waiting for transfers between devices, send(): return lax.ppermute(x, AXES, route(place, only))  154 us
    ppermute x81, starting transfers between devices, send(): return lax.ppermute(x, AXES, route(place, only))  111 us
    pallas_call x18, Pallas kernels, local(): pl.pallas_call(kernel, out_shape=[jax.ShapeDtypeStruct(s, jnp.float32) fo...  18.1 us
  transfers between devices with their start and end apart: 81, of which 59 were waited for; matrix products, arithmetic and copies ran while one was open for 0% of the time, Pallas kernels for 2%

profile of v5, /device:TPU:6, one launch (start us, length us, event | category | flops | bytes accessed | tf_op | source)
XLA Modules:
  0.0 287.0 jit_solution(10218976598982189601)
XLA Ops:
  4.1 3.0 %collective-permute-start.1 = (f32[2,64,512]{2,1,0:T(8,128)S(1)}, f32[2,64,512]{2,1,0:T(8,128)S(1)}, u32[]{:S(2)}, u32[]{:S(2)}) collective-permute-start(f32[2,64,512]{2,1,0:T(8,128)S(1)} %pad_maximum_fusion.6), channel_id=1, source_target_pairs={{0,4},{1,5},{2,6},{3,7},{4,0},{5,1},{6,2},{7,3},{8,12},{9,13},{10,... | collective-permute-start | bytes 786440 | tf_op jit(solution)/shard_map/ppermute | solution.py:32
  8.8 5.4 %collective-permute-done.1.d2 = f32[2,64,512]{2,1,0:T(8,128)S(1)} collective-permute-done((f32[2,64,512]{2,1,0:T(8,128)S(1)}, f32[2,64,512]{2,1,0:T(8,128)S(1)}, u32[]{:S(2)}, u32[]{:S(2)}) %collective-permute-start.1) | collective-permute-done | bytes 262176 | tf_op jit(solution)/shard_map/ppermute | solution.py:32
  14.2 2.7 collective-permute-done.2.d3
  17.7 3.0 %collective-permute-done.3.got = f32[4,5,64,256]{3,2,1,0:T(8,128)S(1)} collective-permute-done((f32[4,5,64,256]{3,2,1,0:T(8,128)S(1)}, f32[4,5,64,256]{3,2,1,0:T(8,128)S(1)}, u32[]{:S(2)}, u32[]{:S(2)}) %collective-permute-start.3) | collective-permute-done | bytes 1310752 | tf_op jit(solution)/shard_map/ppermute | solution.py:32
  23.5 2.1 collective-permute-start.5
  25.6 12.7 %collective-permute-done.5.a2 = f32[4,64,256]{2,1,0:T(8,128)S(1)} collective-permute-done((f32[4,64,256]{2,1,0:T(8,128)S(1)}, f32[4,64,256]{2,1,0:T(8,128)S(1)}, u32[]{:S(2)}, u32[]{:S(2)}) %collective-permute-start.5) | collective-permute-done | bytes 262176 | tf_op jit(solution)/shard_map/ppermute | solution.py:32
  38.3 1.7 collective-permute-done.6.a3
  44.2 2.3 collective-permute-start.10
  47.3 2.4 collective-permute-done.7.rest_1_.a1
  49.7 6.4 %collective-permute-done.13.b3.m3 = f32[256,256]{1,0:T(8,128)S(1)} collective-permute-done((f32[256,256]{1,0:T(8,128)S(1)}, f32[256,256]{1,0:T(8,128)S(1)}, u32[]{:S(2)}, u32[]{:S(2)}) %collective-permute-start.13) | collective-permute-done | bytes 262176 | tf_op jit(solution)/shard_map/ppermute | solution.py:32
  59.9 3.6 %collective-permute-start.15 = (f32[192,256]{1,0:T(8,128)S(1)}, f32[192,256]{1,0:T(8,128)S(1)}, u32[]{:S(2)}, u32[]{:S(2)}) collective-permute-start(f32[192,256]{1,0:T(8,128)S(1)} %get-tuple-element.122), channel_id=1, source_target_pairs={{0,16},{1,17},{2,18},{3,19},{4,20},{5,21},{6,22},{7,23},{8,24},{9,... | collective-permute-start | bytes 589832 | tf_op jit(solution)/shard_map/ppermute | solution.py:32
  63.9 2.9 %collective-permute-done.14.e1 = f32[192,256]{1,0:T(8,128)S(1)} collective-permute-done((f32[192,256]{1,0:T(8,128)S(1)}, f32[192,256]{1,0:T(8,128)S(1)}, u32[]{:S(2)}, u32[]{:S(2)}) %collective-permute-start.14) | collective-permute-done | bytes 196640 | tf_op jit(solution)/shard_map/ppermute | solution.py:32
  66.8 6.0 %collective-permute-done.15.e2 = f32[192,256]{1,0:T(8,128)S(1)} collective-permute-done((f32[192,256]{1,0:T(8,128)S(1)}, f32[192,256]{1,0:T(8,128)S(1)}, u32[]{:S(2)}, u32[]{:S(2)}) %collective-permute-start.15) | collective-permute-done | bytes 196640 | tf_op jit(solution)/shard_map/ppermute | solution.py:32
  72.7 2.6 collective-permute-done.16.e3
  76.1 3.4 %collective-permute-start.18 = (f32[128,256]{1,0:T(8,128)S(1)}, f32[128,256]{1,0:T(8,128)S(1)}, u32[]{:S(2)}, u32[]{:S(2)}) collective-permute-start(f32[128,256]{1,0:T(8,128)S(1)} %fusion.y0.refs_7_), channel_id=1, source_target_pairs={{0,8},{1,9},{2,10},{3,11},{4,12},{5,13},{6,14},{7,15},{8,0},{9,1},... | collective-permute-start | bytes 393224 | tf_op jit(solution)/shard_map/ppermute | solution.py:32
  86.5 1.7 collective-permute-start.21
  88.2 3.1 %collective-permute-start.23 = (f32[128,256]{1,0:T(8,128)S(1)}, f32[128,256]{1,0:T(8,128)S(1)}, u32[]{:S(2)}, u32[]{:S(2)}) collective-permute-start(f32[128,256]{1,0:T(8,128)S(1)} %get-tuple-element.126), channel_id=1, source_target_pairs={{0,6},{1,7},{2,4},{3,5},{4,2},{5,3},{6,0},{7,1},{8,14},{9,15},{10,... | collective-permute-start | bytes 393224 | tf_op jit(solution)/shard_map/ppermute | solution.py:32
  92.6 2.2 collective-permute-done.22
  96.1 2.5 collective-permute-start.29
  98.6 1.9 collective-permute-start.32
  104.3 4.8 %collective-permute-done.28 = f32[128,256]{1,0:T(8,128)S(1)} collective-permute-done((f32[128,256]{1,0:T(8,128)S(1)}, f32[128,256]{1,0:T(8,128)S(1)}, u32[]{:S(2)}, u32[]{:S(2)}) %collective-permute-start.28) | collective-permute-done | bytes 131104 | tf_op jit(solution)/shard_map/ppermute | solution.py:32
  109.2 3.2 %collective-permute-done.32.a3.b3 = f32[256,256]{1,0:T(8,128)S(1)} collective-permute-done((f32[256,256]{1,0:T(8,128)S(1)}, f32[256,256]{1,0:T(8,128)S(1)}, u32[]{:S(2)}, u32[]{:S(2)}) %collective-permute-start.32) | collective-permute-done | bytes 262176 | tf_op jit(solution)/shard_map/ppermute | solution.py:32
  113.2 2.3 collective-permute-done.36.x_sib
  116.8 4.6 %collective-permute-start.39 = (f32[128,256]{1,0:T(8,128)S(1)}, f32[128,256]{1,0:T(8,128)S(1)}, u32[]{:S(2)}, u32[]{:S(2)}) collective-permute-start(f32[128,256]{1,0:T(8,128)S(1)} %get-tuple-element.153), channel_id=1, source_target_pairs={{0,24},{1,25},{2,26},{3,27},{4,28},{5,29},{6,30},{7,31},{8,16},{9,... | collective-permute-start | bytes 393224 | tf_op jit(solution)/shard_map/ppermute | solution.py:32
  123.1 3.1 %collective-permute-start.33 = (f32[256,256]{1,0:T(8,128)S(1)}, f32[256,256]{1,0:T(8,128)S(1)}, u32[]{:S(2)}, u32[]{:S(2)}) collective-permute-start(f32[256,256]{1,0:T(8,128)S(1)} %shard_map.63.b0), channel_id=1, source_target_pairs={{0,2},{1,3},{2,0},{3,1},{4,6},{5,7},{6,4},{7,5},{8,10},{9,11},{10,... | collective-permute-start | bytes 786440 | tf_op jit(solution)/shard_map/ppermute | solution.py:32
  126.7 3.5 %collective-permute-start.42 = (f32[128,256]{1,0:T(8,128)S(1)}, f32[128,256]{1,0:T(8,128)S(1)}, u32[]{:S(2)}, u32[]{:S(2)}) collective-permute-start(f32[128,256]{1,0:T(8,128)S(1)} %add_add_fusion.5.y0.refs_5_), channel_id=1, source_target_pairs={{0,24},{1,25},{2,26},{3,27},{4,28},{5,29},{6,30},{7,31},{8,16},{9,... | collective-permute-start | bytes 393224 | tf_op jit(solution)/shard_map/ppermute | solution.py:32
  130.2 6.2 %collective-permute-done.35.b3 = f32[256,256]{1,0:T(8,128)S(1)} collective-permute-done((f32[256,256]{1,0:T(8,128)S(1)}, f32[256,256]{1,0:T(8,128)S(1)}, u32[]{:S(2)}, u32[]{:S(2)}) %collective-permute-start.35) | collective-permute-done | bytes 262176 | tf_op jit(solution)/shard_map/ppermute | solution.py:32
  137.0 4.3 %collective-permute-done.40.y1 = f32[128,256]{1,0:T(8,128)S(1)} collective-permute-done((f32[128,256]{1,0:T(8,128)S(1)}, f32[128,256]{1,0:T(8,128)S(1)}, u32[]{:S(2)}, u32[]{:S(2)}) %collective-permute-start.40) | collective-permute-done | bytes 131104 | tf_op jit(solution)/shard_map/ppermute | solution.py:32
  141.6 2.6 collective-permute-done.43.b_sib
  146.4 2.7 collective-permute-start.46
  152.0 3.5 %collective-permute-done.46 = f32[128,256]{1,0:T(8,128)S(1)} collective-permute-done((f32[128,256]{1,0:T(8,128)S(1)}, f32[128,256]{1,0:T(8,128)S(1)}, u32[]{:S(2)}, u32[]{:S(2)}) %collective-permute-start.46) | collective-permute-done | bytes 131104 | tf_op jit(solution)/shard_map/ppermute | solution.py:32
  155.5 2.2 collective-permute-done.47
  159.3 2.6 collective-permute-start.48
  161.9 4.6 %collective-permute-done.50 = f32[128,256]{1,0:T(8,128)S(1)} collective-permute-done((f32[128,256]{1,0:T(8,128)S(1)}, f32[128,256]{1,0:T(8,128)S(1)}, u32[]{:S(2)}, u32[]{:S(2)}) %collective-permute-start.50) | collective-permute-done | bytes 131104 | tf_op jit(solution)/shard_map/ppermute | solution.py:32
  172.5 2.9 %collective-permute-start.54 = (f32[128,256]{1,0:T(8,128)S(1)}, f32[128,256]{1,0:T(8,128)S(1)}, u32[]{:S(2)}, u32[]{:S(2)}) collective-permute-start(f32[128,256]{1,0:T(8,128)S(1)} %get-tuple-element.171), channel_id=1, source_target_pairs={{0,24},{1,25},{2,26},{3,27},{4,28},{5,29},{6,30},{7,31},{8,16},{9,... | collective-permute-start | bytes 393224 | tf_op jit(solution)/shard_map/ppermute | solution.py:32
  177.0 1.8 collective-permute-done.53
  178.9 2.2 collective-permute-done.54
  181.2 3.0 %collective-permute-start.57 = (f32[128,256]{1,0:T(8,128)S(1)}, f32[128,256]{1,0:T(8,128)S(1)}, u32[]{:S(2)}, u32[]{:S(2)}) collective-permute-start(f32[128,256]{1,0:T(8,128)S(1)} %add_add_fusion.3.y0.refs_3_), channel_id=1, source_target_pairs={{0,24},{1,25},{2,26},{3,27},{4,28},{5,29},{6,30},{7,31},{8,16},{9,... | collective-permute-start | bytes 393224 | tf_op jit(solution)/shard_map/ppermute | solution.py:32
  185.3 4.1 %collective-permute-done.57.y3 = f32[128,256]{1,0:T(8,128)S(1)} collective-permute-done((f32[128,256]{1,0:T(8,128)S(1)}, f32[128,256]{1,0:T(8,128)S(1)}, u32[]{:S(2)}, u32[]{:S(2)}) %collective-permute-start.57) | collective-permute-done | bytes 131104 | tf_op jit(solution)/shard_map/ppermute | solution.py:32
  189.4 2.3 collective-permute-done.56.y2
  193.1 1.8 collective-permute-start.59
  194.9 2.9 %collective-permute-start.60 = (f32[128,256]{1,0:T(8,128)S(1)}, f32[128,256]{1,0:T(8,128)S(1)}, u32[]{:S(2)}, u32[]{:S(2)}) collective-permute-start(f32[128,256]{1,0:T(8,128)S(1)} %get-tuple-element.175), channel_id=1, source_target_pairs={{0,6},{1,7},{2,4},{3,5},{4,2},{5,3},{6,0},{7,1},{8,14},{9,15},{10,... | collective-permute-start | bytes 393224 | tf_op jit(solution)/shard_map/ppermute | solution.py:32
  201.2 3.3 %collective-permute-start.63 = (f32[128,256]{1,0:T(8,128)S(1)}, f32[128,256]{1,0:T(8,128)S(1)}, u32[]{:S(2)}, u32[]{:S(2)}) collective-permute-start(f32[128,256]{1,0:T(8,128)S(1)} %add_add_fusion.2.refs_2_), channel_id=1, source_target_pairs={{0,6},{1,7},{2,4},{3,5},{4,2},{5,3},{6,0},{7,1},{8,14},{9,15},{10,... | collective-permute-start | bytes 393224 | tf_op jit(solution)/shard_map/ppermute | solution.py:32
  205.7 2.8 collective-permute-done.63
  208.4 2.5 collective-permute-done.62
  211.1 1.9 collective-permute-done.64.x_sib
  214.3 4.2 %collective-permute-start.66 = (f32[128,256]{1,0:T(8,128)S(1)}, f32[128,256]{1,0:T(8,128)S(1)}, u32[]{:S(2)}, u32[]{:S(2)}) collective-permute-start(f32[128,256]{1,0:T(8,128)S(1)} %get-tuple-element.180), channel_id=1, source_target_pairs={{0,16},{1,17},{2,18},{3,19},{4,20},{5,21},{6,22},{7,23},{8,24},{9,... | collective-permute-start | bytes 393224 | tf_op jit(solution)/shard_map/ppermute | solution.py:32
  220.7 4.3 %collective-permute-done.66 = f32[128,256]{1,0:T(8,128)S(1)} collective-permute-done((f32[128,256]{1,0:T(8,128)S(1)}, f32[128,256]{1,0:T(8,128)S(1)}, u32[]{:S(2)}, u32[]{:S(2)}) %collective-permute-start.66) | collective-permute-done | bytes 131104 | tf_op jit(solution)/shard_map/ppermute | solution.py:32
  225.0 2.2 collective-permute-done.67
  228.3 3.1 %collective-permute-start.68 = (f32[128,256]{1,0:T(8,128)S(1)}, f32[128,256]{1,0:T(8,128)S(1)}, u32[]{:S(2)}, u32[]{:S(2)}) collective-permute-start(f32[128,256]{1,0:T(8,128)S(1)} %add_add_fusion.1.y0.refs_1_), channel_id=1, source_target_pairs={{0,8},{1,9},{2,10},{3,11},{4,12},{5,13},{6,14},{7,15},{8,0},{9,1},... | collective-permute-start | bytes 393224 | tf_op jit(solution)/shard_map/ppermute | solution.py:32
  231.4 4.8 %collective-permute-done.70.y3 = f32[128,256]{1,0:T(8,128)S(1)} collective-permute-done((f32[128,256]{1,0:T(8,128)S(1)}, f32[128,256]{1,0:T(8,128)S(1)}, u32[]{:S(2)}, u32[]{:S(2)}) %collective-permute-start.70) | collective-permute-done | bytes 131104 | tf_op jit(solution)/shard_map/ppermute | solution.py:32
  238.3 2.8 collective-permute-start.72
  241.1 1.9 collective-permute-start.73
  244.0 2.3 collective-permute-done.72
  248.7 3.4 %collective-permute-start.75 = (f32[2,2,64,256]{3,2,1,0:T(8,128)S(1)}, f32[2,2,64,256]{3,2,1,0:T(8,128)S(1)}, u32[]{:S(2)}, u32[]{:S(2)}) collective-permute-start(f32[2,2,64,256]{3,2,1,0:T(8,128)S(1)} %get-tuple-element.190), channel_id=1, source_target_pairs={{0,64},{1,65},{2,66},{3,67},{4,68},{5,69},{6,70},{7,71},{8,72},{9,... | collective-permute-start | bytes 786440 | tf_op jit(solution)/shard_map/ppermute | solution.py:32
  253.4 4.5 %collective-permute-done.74.a1 = f32[2,2,64,256]{3,2,1,0:T(8,128)S(1)} collective-permute-done((f32[2,2,64,256]{3,2,1,0:T(8,128)S(1)}, f32[2,2,64,256]{3,2,1,0:T(8,128)S(1)}, u32[]{:S(2)}, u32[]{:S(2)}) %collective-permute-start.74) | collective-permute-done | bytes 262176 | tf_op jit(solution)/shard_map/ppermute | solution.py:32
  258.0 4.8 %collective-permute-done.75.a2 = f32[2,2,64,256]{3,2,1,0:T(8,128)S(1)} collective-permute-done((f32[2,2,64,256]{3,2,1,0:T(8,128)S(1)}, f32[2,2,64,256]{3,2,1,0:T(8,128)S(1)}, u32[]{:S(2)}, u32[]{:S(2)}) %collective-permute-start.75) | collective-permute-done | bytes 262176 | tf_op jit(solution)/shard_map/ppermute | solution.py:32
  262.8 2.6 collective-permute-done.76.a3
  266.1 1.9 collective-permute-done.77.got
  268.6 2.3 collective-permute-start.78
  270.9 5.0 %collective-permute-start.79 = (f32[2,64,512]{2,1,0:T(8,128)S(1)}, f32[2,64,512]{2,1,0:T(8,128)S(1)}, u32[]{:S(2)}, u32[]{:S(2)}) collective-permute-start(f32[2,64,512]{2,1,0:T(8,128)S(1)} %get-tuple-element.196.d2), channel_id=1, source_target_pairs={{0,4},{1,5},{2,6},{3,7},{4,0},{5,1},{6,2},{7,3},{8,12},{9,13},{10,... | collective-permute-start | bytes 786440 | tf_op jit(solution)/shard_map/ppermute | solution.py:32
  275.9 3.2 %collective-permute-start.80 = (f32[2,64,512]{2,1,0:T(8,128)S(1)}, f32[2,64,512]{2,1,0:T(8,128)S(1)}, u32[]{:S(2)}, u32[]{:S(2)}) collective-permute-start(f32[2,64,512]{2,1,0:T(8,128)S(1)} %get-tuple-element.197.d3), channel_id=1, source_target_pairs={{0,6},{1,7},{2,4},{3,5},{4,2},{5,3},{6,0},{7,1},{8,14},{9,15},{10,... | collective-permute-start | bytes 786440 | tf_op jit(solution)/shard_map/ppermute | solution.py:32
  279.1 2.0 collective-permute-done.79.g2
  281.1 4.3 %collective-permute-done.80.g3 = f32[2,64,512]{2,1,0:T(8,128)S(1)} collective-permute-done((f32[2,64,512]{2,1,0:T(8,128)S(1)}, f32[2,64,512]{2,1,0:T(8,128)S(1)}, u32[]{:S(2)}, u32[]{:S(2)}) %collective-permute-start.80) | collective-permute-done | bytes 262176 | tf_op jit(solution)/shard_map/ppermute | solution.py:32
  (158 shorter events, 72.6 us)
Async XLA Ops:
  4.1 10.1 %collective-permute-start.1 = (f32[2,64,512]{2,1,0:T(8,128)S(1)}, f32[2,64,512]{2,1,0:T(8,128)S(1)}, u32[]{:S(2)}, u32[]{:S(2)}) collective-permute-start(f32[2,64,512]{2,1,0:T(8,128)S(1)} %pad_maximum_fusion.6), channel_id=1, source_target_pairs={{0,4},{1,5},{2,6},{3,7},{4,0},{5,1},{6,2},{7,3},{8,12},{9,13},{10,... | collective-permute-start | bytes 786440 | tf_op jit(solution)/shard_map/ppermute | solution.py:32
  7.1 9.7 %collective-permute-start.2 = (f32[2,64,512]{2,1,0:T(8,128)S(1)}, f32[2,64,512]{2,1,0:T(8,128)S(1)}, u32[]{:S(2)}, u32[]{:S(2)}) collective-permute-start(f32[2,64,512]{2,1,0:T(8,128)S(1)} %pad_maximum_fusion.7), channel_id=1, source_target_pairs={{0,6},{1,7},{2,4},{3,5},{4,2},{5,3},{6,0},{7,1},{8,14},{9,15},{10,... | collective-permute-start | bytes 786440 | tf_op jit(solution)/shard_map/ppermute | solution.py:32
  21.4 16.9 %collective-permute-start.4 = (f32[6,64,256]{2,1,0:T(8,128)S(1)}, f32[6,64,256]{2,1,0:T(8,128)S(1)}, u32[]{:S(2)}, u32[]{:S(2)}) collective-permute-start(f32[6,64,256]{2,1,0:T(8,128)S(1)} %get-tuple-element.105), channel_id=1, source_target_pairs={{0,1},{1,0},{2,3},{3,2},{4,5},{5,4},{6,7},{7,6},{8,9},{9,8},{10,11... | collective-permute-start | bytes 1179656 | tf_op jit(solution)/shard_map/ppermute | solution.py:32
  22.4 17.7 %collective-permute-start.6 = (f32[6,64,256]{2,1,0:T(8,128)S(1)}, f32[6,64,256]{2,1,0:T(8,128)S(1)}, u32[]{:S(2)}, u32[]{:S(2)}) collective-permute-start(f32[6,64,256]{2,1,0:T(8,128)S(1)} %get-tuple-element.107), channel_id=1, source_target_pairs={{0,65},{1,64},{2,67},{3,66},{4,69},{5,68},{6,71},{7,70},{8,73},{9,... | collective-permute-start | bytes 1179656 | tf_op jit(solution)/shard_map/ppermute | solution.py:32
  23.5 14.8 %collective-permute-start.5 = (f32[4,64,256]{2,1,0:T(8,128)S(1)}, f32[4,64,256]{2,1,0:T(8,128)S(1)}, u32[]{:S(2)}, u32[]{:S(2)}) collective-permute-start(f32[4,64,256]{2,1,0:T(8,128)S(1)} %get-tuple-element.106), channel_id=1, source_target_pairs={{0,64},{1,65},{2,66},{3,67},{4,68},{5,69},{6,70},{7,71},{8,72},{9,... | collective-permute-start | bytes 786440 | tf_op jit(solution)/shard_map/ppermute | solution.py:32
  40.9 8.8 %collective-permute-start.7 = (f32[256,256]{1,0:T(8,128)S(1)}, f32[256,256]{1,0:T(8,128)S(1)}, u32[]{:S(2)}, u32[]{:S(2)}) collective-permute-start(f32[256,256]{1,0:T(8,128)S(1)} %get-tuple-element.112.rest_0_.a0), channel_id=1, source_target_pairs={{0,2},{1,3},{2,0},{3,1},{4,6},{5,7},{6,4},{7,5},{8,10},{9,11},{10,... | collective-permute-start | bytes 786440 | tf_op jit(solution)/shard_map/ppermute | solution.py:32
  42.1 14.0 %collective-permute-start.13 = (f32[256,256]{1,0:T(8,128)S(1)}, f32[256,256]{1,0:T(8,128)S(1)}, u32[]{:S(2)}, u32[]{:S(2)}) collective-permute-start(f32[256,256]{1,0:T(8,128)S(1)} %get-tuple-element.111.b0.m0), channel_id=1, source_target_pairs={{0,65},{1,64},{2,67},{3,66},{4,69},{5,68},{6,71},{7,70},{8,73},{9,... | collective-permute-start | bytes 786440 | tf_op jit(solution)/shard_map/ppermute | solution.py:32
  43.3 12.9 %collective-permute-start.12 = (f32[256,256]{1,0:T(8,128)S(1)}, f32[256,256]{1,0:T(8,128)S(1)}, u32[]{:S(2)}, u32[]{:S(2)}) collective-permute-start(f32[256,256]{1,0:T(8,128)S(1)} %get-tuple-element.111.b0.m0), channel_id=1, source_target_pairs={{0,64},{1,65},{2,66},{3,67},{4,68},{5,69},{6,70},{7,71},{8,72},{9,... | collective-permute-start | bytes 786440 | tf_op jit(solution)/shard_map/ppermute | solution.py:32
  44.2 13.1 %collective-permute-start.10 = (f32[256,256]{1,0:T(8,128)S(1)}, f32[256,256]{1,0:T(8,128)S(1)}, u32[]{:S(2)}, u32[]{:S(2)}) collective-permute-start(f32[256,256]{1,0:T(8,128)S(1)} %get-tuple-element.112.rest_0_.a0), channel_id=1, source_target_pairs={{0,6},{1,7},{2,4},{3,5},{4,2},{5,3},{6,0},{7,1},{8,14},{9,15},{10,... | collective-permute-start | bytes 786440 | tf_op jit(solution)/shard_map/ppermute | solution.py:32
  46.5 10.8 %collective-permute-start.9 = (f32[256,256]{1,0:T(8,128)S(1)}, f32[256,256]{1,0:T(8,128)S(1)}, u32[]{:S(2)}, u32[]{:S(2)}) collective-permute-start(f32[256,256]{1,0:T(8,128)S(1)} %get-tuple-element.112.rest_0_.a0), channel_id=1, source_target_pairs={{0,4},{1,5},{2,6},{3,7},{4,0},{5,1},{6,2},{7,3},{8,12},{9,13},{10,... | collective-permute-start | bytes 786440 | tf_op jit(solution)/shard_map/ppermute | solution.py:32
  49.7 7.6 %collective-permute-start.11 = (f32[256,256]{1,0:T(8,128)S(1)}, f32[256,256]{1,0:T(8,128)S(1)}, u32[]{:S(2)}, u32[]{:S(2)}) collective-permute-start(f32[256,256]{1,0:T(8,128)S(1)} %get-tuple-element.111.b0.m0), channel_id=1, source_target_pairs={{0,1},{1,0},{2,3},{3,2},{4,5},{5,4},{6,7},{7,6},{8,9},{9,8},{10,11... | collective-permute-start | bytes 786440 | tf_op jit(solution)/shard_map/ppermute | solution.py:32
  59.0 7.8 %collective-permute-start.14 = (f32[192,256]{1,0:T(8,128)S(1)}, f32[192,256]{1,0:T(8,128)S(1)}, u32[]{:S(2)}, u32[]{:S(2)}) collective-permute-start(f32[192,256]{1,0:T(8,128)S(1)} %get-tuple-element.121), channel_id=1, source_target_pairs={{0,8},{1,9},{2,10},{3,11},{4,12},{5,13},{6,14},{7,15},{8,0},{9,1},... | collective-permute-start | bytes 589832 | tf_op jit(solution)/shard_map/ppermute | solution.py:32
  59.9 12.8 %collective-permute-start.15 = (f32[192,256]{1,0:T(8,128)S(1)}, f32[192,256]{1,0:T(8,128)S(1)}, u32[]{:S(2)}, u32[]{:S(2)}) collective-permute-start(f32[192,256]{1,0:T(8,128)S(1)} %get-tuple-element.122), channel_id=1, source_target_pairs={{0,16},{1,17},{2,18},{3,19},{4,20},{5,21},{6,22},{7,23},{8,24},{9,... | collective-permute-start | bytes 589832 | tf_op jit(solution)/shard_map/ppermute | solution.py:32
  63.5 11.8 %collective-permute-start.16 = (f32[192,256]{1,0:T(8,128)S(1)}, f32[192,256]{1,0:T(8,128)S(1)}, u32[]{:S(2)}, u32[]{:S(2)}) collective-permute-start(f32[192,256]{1,0:T(8,128)S(1)} %get-tuple-element.123), channel_id=1, source_target_pairs={{0,24},{1,25},{2,26},{3,27},{4,28},{5,29},{6,30},{7,31},{8,16},{9,... | collective-permute-start | bytes 589832 | tf_op jit(solution)/shard_map/ppermute | solution.py:32
  63.8 17.2 %collective-permute-start.17 = (f32[4,128,256]{2,1,0:T(8,128)S(1)}, f32[4,128,256]{2,1,0:T(8,128)S(1)}, u32[]{:S(2)}, u32[]{:S(2)}) collective-permute-start(f32[4,128,256]{2,1,0:T(8,128)S(1)} %pad_maximum_fusion.1), channel_id=1, source_target_pairs={{0,32},{1,33},{2,34},{3,35},{4,36},{5,37},{6,38},{7,39},{8,40},{9,... | collective-permute-start | bytes 1572872 | tf_op jit(solution)/shard_map/ppermute | solution.py:32
  75.4 8.5 %collective-permute-start.20 = (f32[128,256]{1,0:T(8,128)S(1)}, f32[128,256]{1,0:T(8,128)S(1)}, u32[]{:S(2)}, u32[]{:S(2)}) collective-permute-start(f32[128,256]{1,0:T(8,128)S(1)} %fusion.y0.refs_7_), channel_id=1, source_target_pairs={{0,24},{1,25},{2,26},{3,27},{4,28},{5,29},{6,30},{7,31},{8,16},{9,... | collective-permute-start | bytes 393224 | tf_op jit(solution)/shard_map/ppermute | solution.py:32
  75.7 9.4 %collective-permute-start.19 = (f32[128,256]{1,0:T(8,128)S(1)}, f32[128,256]{1,0:T(8,128)S(1)}, u32[]{:S(2)}, u32[]{:S(2)}) collective-permute-start(f32[128,256]{1,0:T(8,128)S(1)} %fusion.y0.refs_7_), channel_id=1, source_target_pairs={{0,16},{1,17},{2,18},{3,19},{4,20},{5,21},{6,22},{7,23},{8,24},{9,... | collective-permute-start | bytes 393224 | tf_op jit(solution)/shard_map/ppermute | solution.py:32
  76.1 9.1 %collective-permute-start.18 = (f32[128,256]{1,0:T(8,128)S(1)}, f32[128,256]{1,0:T(8,128)S(1)}, u32[]{:S(2)}, u32[]{:S(2)}) collective-permute-start(f32[128,256]{1,0:T(8,128)S(1)} %fusion.y0.refs_7_), channel_id=1, source_target_pairs={{0,8},{1,9},{2,10},{3,11},{4,12},{5,13},{6,14},{7,15},{8,0},{9,1},... | collective-permute-start | bytes 393224 | tf_op jit(solution)/shard_map/ppermute | solution.py:32
  79.5 8.7 %collective-permute-start.24 = (f32[2,64,256]{2,1,0:T(8,128)S(1)}, f32[2,64,256]{2,1,0:T(8,128)S(1)}, u32[]{:S(2)}, u32[]{:S(2)}) collective-permute-start(f32[2,64,256]{2,1,0:T(8,128)S(1)} %get-tuple-element.133), channel_id=1, source_target_pairs={{0,1},{1,0},{2,3},{3,2},{4,5},{5,4},{6,7},{7,6},{8,9},{9,8},{10,11... | collective-permute-start | bytes 393224 | tf_op jit(solution)/shard_map/ppermute | solution.py:32
  81.0 10.3 %collective-permute-start.25 = (f32[2,64,256]{2,1,0:T(8,128)S(1)}, f32[2,64,256]{2,1,0:T(8,128)S(1)}, u32[]{:S(2)}, u32[]{:S(2)}) collective-permute-start(f32[2,64,256]{2,1,0:T(8,128)S(1)} %get-tuple-element.134), channel_id=1, source_target_pairs={{0,64},{1,65},{2,66},{3,67},{4,68},{5,69},{6,70},{7,71},{8,72},{9,... | collective-permute-start | bytes 393224 | tf_op jit(solution)/shard_map/ppermute | solution.py:32
  83.8 7.4 %collective-permute-start.26 = (f32[2,64,256]{2,1,0:T(8,128)S(1)}, f32[2,64,256]{2,1,0:T(8,128)S(1)}, u32[]{:S(2)}, u32[]{:S(2)}) collective-permute-start(f32[2,64,256]{2,1,0:T(8,128)S(1)} %get-tuple-element.135), channel_id=1, source_target_pairs={{0,65},{1,64},{2,67},{3,66},{4,69},{5,68},{6,71},{7,70},{8,73},{9,... | collective-permute-start | bytes 393224 | tf_op jit(solution)/shard_map/ppermute | solution.py:32
  88.2 6.5 %collective-permute-start.22 = (f32[128,256]{1,0:T(8,128)S(1)}, f32[128,256]{1,0:T(8,128)S(1)}, u32[]{:S(2)}, u32[]{:S(2)}) collective-permute-start(f32[128,256]{1,0:T(8,128)S(1)} %get-tuple-element.125), channel_id=1, source_target_pairs={{0,4},{1,5},{2,6},{3,7},{4,0},{5,1},{6,2},{7,3},{8,12},{9,13},{10,... | collective-permute-start | bytes 393224 | tf_op jit(solution)/shard_map/ppermute | solution.py:32
  88.2 7.8 %collective-permute-start.23 = (f32[128,256]{1,0:T(8,128)S(1)}, f32[128,256]{1,0:T(8,128)S(1)}, u32[]{:S(2)}, u32[]{:S(2)}) collective-permute-start(f32[128,256]{1,0:T(8,128)S(1)} %get-tuple-element.126), channel_id=1, source_target_pairs={{0,6},{1,7},{2,4},{3,5},{4,2},{5,3},{6,0},{7,1},{8,14},{9,15},{10,... | collective-permute-start | bytes 393224 | tf_op jit(solution)/shard_map/ppermute | solution.py:32
  96.1 6.7 %collective-permute-start.29 = (f32[128,256]{1,0:T(8,128)S(1)}, f32[128,256]{1,0:T(8,128)S(1)}, u32[]{:S(2)}, u32[]{:S(2)}) collective-permute-start(f32[128,256]{1,0:T(8,128)S(1)} %add_add_fusion.6.refs_6_), channel_id=1, source_target_pairs={{0,6},{1,7},{2,4},{3,5},{4,2},{5,3},{6,0},{7,1},{8,14},{9,15},{10,... | collective-permute-start | bytes 393224 | tf_op jit(solution)/shard_map/ppermute | solution.py:32
  98.6 13.7 %collective-permute-start.32 = (f32[256,256]{1,0:T(8,128)S(1)}, f32[256,256]{1,0:T(8,128)S(1)}, u32[]{:S(2)}, u32[]{:S(2)}) collective-permute-start(f32[256,256]{1,0:T(8,128)S(1)} %get-tuple-element.160.a0.b0), channel_id=1, source_target_pairs={{0,65},{1,64},{2,67},{3,66},{4,69},{5,68},{6,71},{7,70},{8,73},{9,... | collective-permute-start | bytes 786440 | tf_op jit(solution)/shard_map/ppermute | solution.py:32
  100.5 11.8 %collective-permute-start.31 = (f32[256,256]{1,0:T(8,128)S(1)}, f32[256,256]{1,0:T(8,128)S(1)}, u32[]{:S(2)}, u32[]{:S(2)}) collective-permute-start(f32[256,256]{1,0:T(8,128)S(1)} %get-tuple-element.160.a0.b0), channel_id=1, source_target_pairs={{0,64},{1,65},{2,66},{3,67},{4,68},{5,69},{6,70},{7,71},{8,72},{9,... | collective-permute-start | bytes 786440 | tf_op jit(solution)/shard_map/ppermute | solution.py:32
  101.4 11.6 %collective-permute-start.30 = (f32[256,256]{1,0:T(8,128)S(1)}, f32[256,256]{1,0:T(8,128)S(1)}, u32[]{:S(2)}, u32[]{:S(2)}) collective-permute-start(f32[256,256]{1,0:T(8,128)S(1)} %get-tuple-element.160.a0.b0), channel_id=1, source_target_pairs={{0,1},{1,0},{2,3},{3,2},{4,5},{5,4},{6,7},{7,6},{8,9},{9,8},{10,11... | collective-permute-start | bytes 786440 | tf_op jit(solution)/shard_map/ppermute | solution.py:32
  102.7 6.5 %collective-permute-start.28 = (f32[128,256]{1,0:T(8,128)S(1)}, f32[128,256]{1,0:T(8,128)S(1)}, u32[]{:S(2)}, u32[]{:S(2)}) collective-permute-start(f32[128,256]{1,0:T(8,128)S(1)} %add_add_fusion.6.refs_6_), channel_id=1, source_target_pairs={{0,4},{1,5},{2,6},{3,7},{4,0},{5,1},{6,2},{7,3},{8,12},{9,13},{10,... | collective-permute-start | bytes 393224 | tf_op jit(solution)/shard_map/ppermute | solution.py:32
  102.7 6.5 %collective-permute-start.27 = (f32[128,256]{1,0:T(8,128)S(1)}, f32[128,256]{1,0:T(8,128)S(1)}, u32[]{:S(2)}, u32[]{:S(2)}) collective-permute-start(f32[128,256]{1,0:T(8,128)S(1)} %add_add_fusion.6.refs_6_), channel_id=1, source_target_pairs={{0,2},{1,3},{2,0},{3,1},{4,6},{5,7},{6,4},{7,5},{8,10},{9,11},{10,... | collective-permute-start | bytes 393224 | tf_op jit(solution)/shard_map/ppermute | solution.py:32
  116.7 9.4 %collective-permute-start.38 = (f32[128,256]{1,0:T(8,128)S(1)}, f32[128,256]{1,0:T(8,128)S(1)}, u32[]{:S(2)}, u32[]{:S(2)}) collective-permute-start(f32[128,256]{1,0:T(8,128)S(1)} %get-tuple-element.152), channel_id=1, source_target_pairs={{0,16},{1,17},{2,18},{3,19},{4,20},{5,21},{6,22},{7,23},{8,24},{9,... | collective-permute-start | bytes 393224 | tf_op jit(solution)/shard_map/ppermute | solution.py:32
  116.8 9.8 %collective-permute-start.39 = (f32[128,256]{1,0:T(8,128)S(1)}, f32[128,256]{1,0:T(8,128)S(1)}, u32[]{:S(2)}, u32[]{:S(2)}) collective-permute-start(f32[128,256]{1,0:T(8,128)S(1)} %get-tuple-element.153), channel_id=1, source_target_pairs={{0,24},{1,25},{2,26},{3,27},{4,28},{5,29},{6,30},{7,31},{8,16},{9,... | collective-permute-start | bytes 393224 | tf_op jit(solution)/shard_map/ppermute | solution.py:32
  122.0 14.4 %collective-permute-start.35 = (f32[256,256]{1,0:T(8,128)S(1)}, f32[256,256]{1,0:T(8,128)S(1)}, u32[]{:S(2)}, u32[]{:S(2)}) collective-permute-start(f32[256,256]{1,0:T(8,128)S(1)} %shard_map.63.b0), channel_id=1, source_target_pairs={{0,6},{1,7},{2,4},{3,5},{4,2},{5,3},{6,0},{7,1},{8,14},{9,15},{10,... | collective-permute-start | bytes 786440 | tf_op jit(solution)/shard_map/ppermute | solution.py:32
  122.7 13.7 %collective-permute-start.34 = (f32[256,256]{1,0:T(8,128)S(1)}, f32[256,256]{1,0:T(8,128)S(1)}, u32[]{:S(2)}, u32[]{:S(2)}) collective-permute-start(f32[256,256]{1,0:T(8,128)S(1)} %shard_map.63.b0), channel_id=1, source_target_pairs={{0,4},{1,5},{2,6},{3,7},{4,0},{5,1},{6,2},{7,3},{8,12},{9,13},{10,... | collective-permute-start | bytes 786440 | tf_op jit(solution)/shard_map/ppermute | solution.py:32
  123.1 14.0 %collective-permute-start.33 = (f32[256,256]{1,0:T(8,128)S(1)}, f32[256,256]{1,0:T(8,128)S(1)}, u32[]{:S(2)}, u32[]{:S(2)}) collective-permute-start(f32[256,256]{1,0:T(8,128)S(1)} %shard_map.63.b0), channel_id=1, source_target_pairs={{0,2},{1,3},{2,0},{3,1},{4,6},{5,7},{6,4},{7,5},{8,10},{9,11},{10,... | collective-permute-start | bytes 786440 | tf_op jit(solution)/shard_map/ppermute | solution.py:32
  126.7 10.3 %collective-permute-start.42 = (f32[128,256]{1,0:T(8,128)S(1)}, f32[128,256]{1,0:T(8,128)S(1)}, u32[]{:S(2)}, u32[]{:S(2)}) collective-permute-start(f32[128,256]{1,0:T(8,128)S(1)} %add_add_fusion.5.y0.refs_5_), channel_id=1, source_target_pairs={{0,24},{1,25},{2,26},{3,27},{4,28},{5,29},{6,30},{7,31},{8,16},{9,... | collective-permute-start | bytes 393224 | tf_op jit(solution)/shard_map/ppermute | solution.py:32
  130.2 6.8 %collective-permute-start.41 = (f32[128,256]{1,0:T(8,128)S(1)}, f32[128,256]{1,0:T(8,128)S(1)}, u32[]{:S(2)}, u32[]{:S(2)}) collective-permute-start(f32[128,256]{1,0:T(8,128)S(1)} %add_add_fusion.5.y0.refs_5_), channel_id=1, source_target_pairs={{0,16},{1,17},{2,18},{3,19},{4,20},{5,21},{6,22},{7,23},{8,24},{9,... | collective-permute-start | bytes 393224 | tf_op jit(solution)/shard_map/ppermute | solution.py:32
  146.4 9.1 %collective-permute-start.46 = (f32[128,256]{1,0:T(8,128)S(1)}, f32[128,256]{1,0:T(8,128)S(1)}, u32[]{:S(2)}, u32[]{:S(2)}) collective-permute-start(f32[128,256]{1,0:T(8,128)S(1)} %get-tuple-element.166), channel_id=1, source_target_pairs={{0,64},{1,65},{2,66},{3,67},{4,68},{5,69},{6,70},{7,71},{8,72},{9,... | collective-permute-start | bytes 393224 | tf_op jit(solution)/shard_map/ppermute | solution.py:32
  149.1 8.7 %collective-permute-start.47 = (f32[128,256]{1,0:T(8,128)S(1)}, f32[128,256]{1,0:T(8,128)S(1)}, u32[]{:S(2)}, u32[]{:S(2)}) collective-permute-start(f32[128,256]{1,0:T(8,128)S(1)} %get-tuple-element.167), channel_id=1, source_target_pairs={{0,65},{1,64},{2,67},{3,66},{4,69},{5,68},{6,71},{7,70},{8,73},{9,... | collective-permute-start | bytes 393224 | tf_op jit(solution)/shard_map/ppermute | solution.py:32
  157.8 8.8 %collective-permute-start.50 = (f32[128,256]{1,0:T(8,128)S(1)}, f32[128,256]{1,0:T(8,128)S(1)}, u32[]{:S(2)}, u32[]{:S(2)}) collective-permute-start(f32[128,256]{1,0:T(8,128)S(1)} %add_add_fusion.4.refs_4_), channel_id=1, source_target_pairs={{0,65},{1,64},{2,67},{3,66},{4,69},{5,68},{6,71},{7,70},{8,73},{9,... | collective-permute-start | bytes 393224 | tf_op jit(solution)/shard_map/ppermute | solution.py:32
  159.2 7.6 %collective-permute-start.49 = (f32[128,256]{1,0:T(8,128)S(1)}, f32[128,256]{1,0:T(8,128)S(1)}, u32[]{:S(2)}, u32[]{:S(2)}) collective-permute-start(f32[128,256]{1,0:T(8,128)S(1)} %add_add_fusion.4.refs_4_), channel_id=1, source_target_pairs={{0,64},{1,65},{2,66},{3,67},{4,68},{5,69},{6,70},{7,71},{8,72},{9,... | collective-permute-start | bytes 393224 | tf_op jit(solution)/shard_map/ppermute | solution.py:32
  159.3 8.0 %collective-permute-start.48 = (f32[128,256]{1,0:T(8,128)S(1)}, f32[128,256]{1,0:T(8,128)S(1)}, u32[]{:S(2)}, u32[]{:S(2)}) collective-permute-start(f32[128,256]{1,0:T(8,128)S(1)} %add_add_fusion.4.refs_4_), channel_id=1, source_target_pairs={{0,1},{1,0},{2,3},{3,2},{4,5},{5,4},{6,7},{7,6},{8,9},{9,8},{10,11... | collective-permute-start | bytes 393224 | tf_op jit(solution)/shard_map/ppermute | solution.py:32
  168.1 17.2 %collective-permute-start.44 = (f32[4,192,256]{2,1,0:T(8,128)S(1)}, f32[4,192,256]{2,1,0:T(8,128)S(1)}, u32[]{:S(2)}, u32[]{:S(2)}) collective-permute-start(f32[4,192,256]{2,1,0:T(8,128)S(1)} %get-tuple-element.164), channel_id=1, source_target_pairs={{0,32},{1,33},{2,34},{3,35},{4,36},{5,37},{6,38},{7,39},{8,40},{9,... | collective-permute-start | bytes 2359304 | tf_op jit(solution)/shard_map/ppermute | solution.py:32
  171.0 7.9 %collective-permute-start.53 = (f32[128,256]{1,0:T(8,128)S(1)}, f32[128,256]{1,0:T(8,128)S(1)}, u32[]{:S(2)}, u32[]{:S(2)}) collective-permute-start(f32[128,256]{1,0:T(8,128)S(1)} %get-tuple-element.170), channel_id=1, source_target_pairs={{0,16},{1,17},{2,18},{3,19},{4,20},{5,21},{6,22},{7,23},{8,24},{9,... | collective-permute-start | bytes 393224 | tf_op jit(solution)/shard_map/ppermute | solution.py:32
  172.5 8.7 %collective-permute-start.54 = (f32[128,256]{1,0:T(8,128)S(1)}, f32[128,256]{1,0:T(8,128)S(1)}, u32[]{:S(2)}, u32[]{:S(2)}) collective-permute-start(f32[128,256]{1,0:T(8,128)S(1)} %get-tuple-element.171), channel_id=1, source_target_pairs={{0,24},{1,25},{2,26},{3,27},{4,28},{5,29},{6,30},{7,31},{8,16},{9,... | collective-permute-start | bytes 393224 | tf_op jit(solution)/shard_map/ppermute | solution.py:32
  181.2 8.3 %collective-permute-start.57 = (f32[128,256]{1,0:T(8,128)S(1)}, f32[128,256]{1,0:T(8,128)S(1)}, u32[]{:S(2)}, u32[]{:S(2)}) collective-permute-start(f32[128,256]{1,0:T(8,128)S(1)} %add_add_fusion.3.y0.refs_3_), channel_id=1, source_target_pairs={{0,24},{1,25},{2,26},{3,27},{4,28},{5,29},{6,30},{7,31},{8,16},{9,... | collective-permute-start | bytes 393224 | tf_op jit(solution)/shard_map/ppermute | solution.py:32
  184.2 7.5 %collective-permute-start.56 = (f32[128,256]{1,0:T(8,128)S(1)}, f32[128,256]{1,0:T(8,128)S(1)}, u32[]{:S(2)}, u32[]{:S(2)}) collective-permute-start(f32[128,256]{1,0:T(8,128)S(1)} %add_add_fusion.3.y0.refs_3_), channel_id=1, source_target_pairs={{0,16},{1,17},{2,18},{3,19},{4,20},{5,21},{6,22},{7,23},{8,24},{9,... | collective-permute-start | bytes 393224 | tf_op jit(solution)/shard_map/ppermute | solution.py:32
  184.2 7.5 %collective-permute-start.55 = (f32[128,256]{1,0:T(8,128)S(1)}, f32[128,256]{1,0:T(8,128)S(1)}, u32[]{:S(2)}, u32[]{:S(2)}) collective-permute-start(f32[128,256]{1,0:T(8,128)S(1)} %add_add_fusion.3.y0.refs_3_), channel_id=1, source_target_pairs={{0,8},{1,9},{2,10},{3,11},{4,12},{5,13},{6,14},{7,15},{8,0},{9,1},... | collective-permute-start | bytes 393224 | tf_op jit(solution)/shard_map/ppermute | solution.py:32
  193.1 6.6 %collective-permute-start.59 = (f32[128,256]{1,0:T(8,128)S(1)}, f32[128,256]{1,0:T(8,128)S(1)}, u32[]{:S(2)}, u32[]{:S(2)}) collective-permute-start(f32[128,256]{1,0:T(8,128)S(1)} %get-tuple-element.174), channel_id=1, source_target_pairs={{0,4},{1,5},{2,6},{3,7},{4,0},{5,1},{6,2},{7,3},{8,12},{9,13},{10,... | collective-permute-start | bytes 393224 | tf_op jit(solution)/shard_map/ppermute | solution.py:32
  201.2 7.3 %collective-permute-start.63 = (f32[128,256]{1,0:T(8,128)S(1)}, f32[128,256]{1,0:T(8,128)S(1)}, u32[]{:S(2)}, u32[]{:S(2)}) collective-permute-start(f32[128,256]{1,0:T(8,128)S(1)} %add_add_fusion.2.refs_2_), channel_id=1, source_target_pairs={{0,6},{1,7},{2,4},{3,5},{4,2},{5,3},{6,0},{7,1},{8,14},{9,15},{10,... | collective-permute-start | bytes 393224 | tf_op jit(solution)/shard_map/ppermute | solution.py:32
  204.5 6.5 %collective-permute-start.62 = (f32[128,256]{1,0:T(8,128)S(1)}, f32[128,256]{1,0:T(8,128)S(1)}, u32[]{:S(2)}, u32[]{:S(2)}) collective-permute-start(f32[128,256]{1,0:T(8,128)S(1)} %add_add_fusion.2.refs_2_), channel_id=1, source_target_pairs={{0,4},{1,5},{2,6},{3,7},{4,0},{5,1},{6,2},{7,3},{8,12},{9,13},{10,... | collective-permute-start | bytes 393224 | tf_op jit(solution)/shard_map/ppermute | solution.py:32
  204.5 6.5 %collective-permute-start.61 = (f32[128,256]{1,0:T(8,128)S(1)}, f32[128,256]{1,0:T(8,128)S(1)}, u32[]{:S(2)}, u32[]{:S(2)}) collective-permute-start(f32[128,256]{1,0:T(8,128)S(1)} %add_add_fusion.2.refs_2_), channel_id=1, source_target_pairs={{0,2},{1,3},{2,0},{3,1},{4,6},{5,7},{6,4},{7,5},{8,10},{9,11},{10,... | collective-permute-start | bytes 393224 | tf_op jit(solution)/shard_map/ppermute | solution.py:32
  214.3 10.6 %collective-permute-start.66 = (f32[128,256]{1,0:T(8,128)S(1)}, f32[128,256]{1,0:T(8,128)S(1)}, u32[]{:S(2)}, u32[]{:S(2)}) collective-permute-start(f32[128,256]{1,0:T(8,128)S(1)} %get-tuple-element.180), channel_id=1, source_target_pairs={{0,16},{1,17},{2,18},{3,19},{4,20},{5,21},{6,22},{7,23},{8,24},{9,... | collective-permute-start | bytes 393224 | tf_op jit(solution)/shard_map/ppermute | solution.py:32
  218.5 8.7 %collective-permute-start.67 = (f32[128,256]{1,0:T(8,128)S(1)}, f32[128,256]{1,0:T(8,128)S(1)}, u32[]{:S(2)}, u32[]{:S(2)}) collective-permute-start(f32[128,256]{1,0:T(8,128)S(1)} %get-tuple-element.181), channel_id=1, source_target_pairs={{0,24},{1,25},{2,26},{3,27},{4,28},{5,29},{6,30},{7,31},{8,16},{9,... | collective-permute-start | bytes 393224 | tf_op jit(solution)/shard_map/ppermute | solution.py:32
  227.2 9.0 %collective-permute-start.70 = (f32[128,256]{1,0:T(8,128)S(1)}, f32[128,256]{1,0:T(8,128)S(1)}, u32[]{:S(2)}, u32[]{:S(2)}) collective-permute-start(f32[128,256]{1,0:T(8,128)S(1)} %add_add_fusion.1.y0.refs_1_), channel_id=1, source_target_pairs={{0,24},{1,25},{2,26},{3,27},{4,28},{5,29},{6,30},{7,31},{8,16},{9,... | collective-permute-start | bytes 393224 | tf_op jit(solution)/shard_map/ppermute | solution.py:32
  227.8 8.5 %collective-permute-start.69 = (f32[128,256]{1,0:T(8,128)S(1)}, f32[128,256]{1,0:T(8,128)S(1)}, u32[]{:S(2)}, u32[]{:S(2)}) collective-permute-start(f32[128,256]{1,0:T(8,128)S(1)} %add_add_fusion.1.y0.refs_1_), channel_id=1, source_target_pairs={{0,16},{1,17},{2,18},{3,19},{4,20},{5,21},{6,22},{7,23},{8,24},{9,... | collective-permute-start | bytes 393224 | tf_op jit(solution)/shard_map/ppermute | solution.py:32
  228.3 8.6 %collective-permute-start.68 = (f32[128,256]{1,0:T(8,128)S(1)}, f32[128,256]{1,0:T(8,128)S(1)}, u32[]{:S(2)}, u32[]{:S(2)}) collective-permute-start(f32[128,256]{1,0:T(8,128)S(1)} %add_add_fusion.1.y0.refs_1_), channel_id=1, source_target_pairs={{0,8},{1,9},{2,10},{3,11},{4,12},{5,13},{6,14},{7,15},{8,0},{9,1},... | collective-permute-start | bytes 393224 | tf_op jit(solution)/shard_map/ppermute | solution.py:32
  238.3 7.9 %collective-permute-start.72 = (f32[128,256]{1,0:T(8,128)S(1)}, f32[128,256]{1,0:T(8,128)S(1)}, u32[]{:S(2)}, u32[]{:S(2)}) collective-permute-start(f32[128,256]{1,0:T(8,128)S(1)} %get-tuple-element.184), channel_id=1, source_target_pairs={{0,64},{1,65},{2,66},{3,67},{4,68},{5,69},{6,70},{7,71},{8,72},{9,... | collective-permute-start | bytes 393224 | tf_op jit(solution)/shard_map/ppermute | solution.py:32
  241.1 6.8 %collective-permute-start.73 = (f32[128,256]{1,0:T(8,128)S(1)}, f32[128,256]{1,0:T(8,128)S(1)}, u32[]{:S(2)}, u32[]{:S(2)}) collective-permute-start(f32[128,256]{1,0:T(8,128)S(1)} %get-tuple-element.185), channel_id=1, source_target_pairs={{0,65},{1,64},{2,67},{3,66},{4,69},{5,68},{6,71},{7,70},{8,73},{9,... | collective-permute-start | bytes 393224 | tf_op jit(solution)/shard_map/ppermute | solution.py:32
  248.6 9.3 %collective-permute-start.74 = (f32[2,2,64,256]{3,2,1,0:T(8,128)S(1)}, f32[2,2,64,256]{3,2,1,0:T(8,128)S(1)}, u32[]{:S(2)}, u32[]{:S(2)}) collective-permute-start(f32[2,2,64,256]{3,2,1,0:T(8,128)S(1)} %get-tuple-element.189), channel_id=1, source_target_pairs={{0,1},{1,0},{2,3},{3,2},{4,5},{5,4},{6,7},{7,6},{8,9},{9,8},{10,11... | collective-permute-start | bytes 786440 | tf_op jit(solution)/shard_map/ppermute | solution.py:32
  248.7 14.1 %collective-permute-start.75 = (f32[2,2,64,256]{3,2,1,0:T(8,128)S(1)}, f32[2,2,64,256]{3,2,1,0:T(8,128)S(1)}, u32[]{:S(2)}, u32[]{:S(2)}) collective-permute-start(f32[2,2,64,256]{3,2,1,0:T(8,128)S(1)} %get-tuple-element.190), channel_id=1, source_target_pairs={{0,64},{1,65},{2,66},{3,67},{4,68},{5,69},{6,70},{7,71},{8,72},{9,... | collective-permute-start | bytes 786440 | tf_op jit(solution)/shard_map/ppermute | solution.py:32
  252.1 13.3 %collective-permute-start.76 = (f32[2,2,64,256]{3,2,1,0:T(8,128)S(1)}, f32[2,2,64,256]{3,2,1,0:T(8,128)S(1)}, u32[]{:S(2)}, u32[]{:S(2)}) collective-permute-start(f32[2,2,64,256]{3,2,1,0:T(8,128)S(1)} %get-tuple-element.191), channel_id=1, source_target_pairs={{0,65},{1,64},{2,67},{3,66},{4,69},{5,68},{6,71},{7,70},{8,73},{9,... | collective-permute-start | bytes 786440 | tf_op jit(solution)/shard_map/ppermute | solution.py:32
  268.6 10.4 %collective-permute-start.78 = (f32[2,64,512]{2,1,0:T(8,128)S(1)}, f32[2,64,512]{2,1,0:T(8,128)S(1)}, u32[]{:S(2)}, u32[]{:S(2)}) collective-permute-start(f32[2,64,512]{2,1,0:T(8,128)S(1)} %get-tuple-element.195.d1), channel_id=1, source_target_pairs={{0,2},{1,3},{2,0},{3,1},{4,6},{5,7},{6,4},{7,5},{8,10},{9,11},{10,... | collective-permute-start | bytes 786440 | tf_op jit(solution)/shard_map/ppermute | solution.py:32
  270.9 10.2 %collective-permute-start.79 = (f32[2,64,512]{2,1,0:T(8,128)S(1)}, f32[2,64,512]{2,1,0:T(8,128)S(1)}, u32[]{:S(2)}, u32[]{:S(2)}) collective-permute-start(f32[2,64,512]{2,1,0:T(8,128)S(1)} %get-tuple-element.196.d2), channel_id=1, source_target_pairs={{0,4},{1,5},{2,6},{3,7},{4,0},{5,1},{6,2},{7,3},{8,12},{9,13},{10,... | collective-permute-start | bytes 786440 | tf_op jit(solution)/shard_map/ppermute | solution.py:32
  275.9 9.5 %collective-permute-start.80 = (f32[2,64,512]{2,1,0:T(8,128)S(1)}, f32[2,64,512]{2,1,0:T(8,128)S(1)}, u32[]{:S(2)}, u32[]{:S(2)}) collective-permute-start(f32[2,64,512]{2,1,0:T(8,128)S(1)} %get-tuple-element.197.d3), channel_id=1, source_target_pairs={{0,6},{1,7},{2,4},{3,5},{4,2},{5,3},{6,0},{7,1},{8,14},{9,15},{10,... | collective-permute-start | bytes 786440 | tf_op jit(solution)/shard_map/ppermute | solution.py:32
  (19 other events, 78.8 us)

commit v6 on v5

--- a/solution.py
+++ b/solution.py
@@ -329,37 +329,40 @@
                         out[n, k] = ref[pl.ds(64 * (s % 2), 64), :]
 
 
-def meet_kernel(at, a0, a1, a2, a3, keep, give):
-    for r, a in enumerate((a0, a1, a2, a3)):
-        keep[at[X] ^ r] = a[at[C]]
-        give[at[X] ^ r] = a[1 - at[C]]
-
-
-def turn_kernel(at, keep, got, *outs):
-    mine, theirs = rows_of(256 * at[C], 256), rows_of(256 * (1 - at[C]), 256)
-    for r, out in enumerate(outs):
-        for k in range(2):
-            out[k, :, mine] = keep[at[Y] ^ r, k]
-            out[k, :, theirs] = got[at[Y] ^ r, k]
-
-
-def finish_kernel(at, mask, d0, d1, d2, d3, g1, g2, g3, diag, off):
-    def fill(parts):
-        for r, part in enumerate(parts):
-            s = at[Y] ^ r
-            for k in range(4):
-                cols = rows_of(512 * k + 128 * s, 128)
-                kept = mask[4 * k + s]
-                diag[:, cols] = part[0, :, pl.ds(128 * k, 128)] * kept
-                off[:, cols] = -part[1, :, pl.ds(128 * k, 128)] * kept
-
+def meet_kernel(at, a0, a1, a2, a3, *outs):
+    rest = outs[4]
+    for k, a in enumerate((a0, a1, a2, a3)):
+        rest[at[X] ^ k] = a[1]
+        for r in range(4):
+
+            @pl.when((at[X] ^ at[Y] ^ k) == r)
+            def _():
+                outs[r][...] = a[0]
+
+
+def turn_kernel(at, h0, h1, h2, h3, rest, keep, give):
     @pl.when(at[C] == 0)
     def _():
-        fill((d0, g1, g2, g3))
+        for r, h in enumerate((h0, h1, h2, h3)):
+            keep[at[Y] ^ r] = h[...]
+        give[...] = rest[...]
 
     @pl.when(at[C] == 1)
     def _():
-        fill((d0, d1, d2, d3))
+        for r, h in enumerate((h0, h1, h2, h3)):
+            give[at[Y] ^ r] = h[...]
+        keep[...] = rest[...]
+
+
+def finish_kernel(at, mask, keep, got, diag, off):
+    for ref, half in ((keep, at[C]), (got, 1 - at[C])):
+        for s in range(4):
+            for i in range(2):
+                block = 4 * (2 * half + i) + s
+                cols = rows_of(128 * block, 128)
+                kept = mask[block]
+                diag[:, cols] = ref[s, 0, :, pl.ds(128 * i, 128)] * kept
+                off[:, cols] = -ref[s, 1, :, pl.ds(128 * i, 128)] * kept
 
 
 def local(kernel, at, args, shapes, scratch=(), copies=0, scalars=(), far=(), flops=0, out_far=0):
@@ -487,14 +490,11 @@
 
     outs = [a[t] for t in range(4) for a in (blocks, crosses)]
     outs = exchanged(local(leave_kernel, at, outs, [(2, 2, 64, 256)] * 4), along["x"])
-    keep, give = local(meet_kernel, at, outs, [(4, 2, 64, 256)] * 2)
+    *turned, rest = local(meet_kernel, at, outs, [(2, 64, 256)] * 4 + [(4, 2, 64, 256)])
+    turned = exchanged(turned, along["y"])
+    keep, give = local(turn_kernel, at, turned + [rest], [(4, 2, 64, 256)] * 2)
     got = send(give, to_other_core)
-    turned = local(turn_kernel, at, [keep, got], [(2, 64, 512)] * 4)
-    back = exchanged(turned, along["y"], lambda co, **_: co == 0)
-
-    diag, off = local(
-        finish_kernel, at, list(turned) + back[1:], [(64, 2048)] * 2, scalars=[mask]
-    )
+    diag, off = local(finish_kernel, at, [keep, got], [(64, 2048)] * 2, scalars=[mask])
     return diag[None], off[None]
 
 

time: 288 us -> 282 us (0.979)
  starting transfers between devices: 111 us -> 105 us
    ppermute x81, starting transfers between devices: 111 us -> 105 us  [send(): return lax.ppermute(x, AXES, route(place, only))]
  transfers between devices with their start and end apart: 81 -> 81, of which waited for: 59 -> 60; matrix products, arithmetic and copies ran while one was open for 0% -> 0% of each run, Pallas kernels for 2% -> 2%
where the time goes in v6:
time: 282 us; the launch traced here: 280 us
  waiting for transfers between devices  152 us (54%)
  starting transfers between devices  105 us (37%)
  Pallas kernels  18.2 us (6%)
    ppermute x81, waiting for transfers between devices, send(): return lax.ppermute(x, AXES, route(place, only))  152 us
    ppermute x81, starting transfers between devices, send(): return lax.ppermute(x, AXES, route(place, only))  105 us
    pallas_call x18, Pallas kernels, local(): pl.pallas_call(kernel, out_shape=[jax.ShapeDtypeStruct(s, jnp.float32) fo...  18.2 us
  transfers between devices with their start and end apart: 81, of which 60 were waited for; matrix products, arithmetic and copies ran while one was open for 0% of the time, Pallas kernels for 2%

profile of v6, /device:TPU:6, one launch (start us, length us, event | category | flops | bytes accessed | tf_op | source)
XLA Modules:
  0.0 280.1 jit_solution(14226488576535754561)
XLA Ops:
  2.3 1.7 collective-permute-start
  4.1 3.0 %collective-permute-start.1 = (f32[2,64,512]{2,1,0:T(8,128)S(1)}, f32[2,64,512]{2,1,0:T(8,128)S(1)}, u32[]{:S(2)}, u32[]{:S(2)}) collective-permute-start(f32[2,64,512]{2,1,0:T(8,128)S(1)} %pad_maximum_fusion.6), channel_id=1, source_target_pairs={{0,4},{1,5},{2,6},{3,7},{4,0},{5,1},{6,2},{7,3},{8,12},{9,13},{10,... | collective-permute-start | bytes 786440 | tf_op jit(solution)/shard_map/ppermute | solution.py:32
  8.8 5.4 %collective-permute-done.1.d2 = f32[2,64,512]{2,1,0:T(8,128)S(1)} collective-permute-done((f32[2,64,512]{2,1,0:T(8,128)S(1)}, f32[2,64,512]{2,1,0:T(8,128)S(1)}, u32[]{:S(2)}, u32[]{:S(2)}) %collective-permute-start.1) | collective-permute-done | bytes 262176 | tf_op jit(solution)/shard_map/ppermute | solution.py:32
  14.2 2.7 collective-permute-done.2.d3
  17.7 3.0 %collective-permute-done.3.got = f32[4,5,64,256]{3,2,1,0:T(8,128)S(1)} collective-permute-done((f32[4,5,64,256]{3,2,1,0:T(8,128)S(1)}, f32[4,5,64,256]{3,2,1,0:T(8,128)S(1)}, u32[]{:S(2)}, u32[]{:S(2)}) %collective-permute-start.3) | collective-permute-done | bytes 1310752 | tf_op jit(solution)/shard_map/ppermute | solution.py:32
  23.5 2.1 collective-permute-start.5
  25.6 12.7 %collective-permute-done.5.a2 = f32[4,64,256]{2,1,0:T(8,128)S(1)} collective-permute-done((f32[4,64,256]{2,1,0:T(8,128)S(1)}, f32[4,64,256]{2,1,0:T(8,128)S(1)}, u32[]{:S(2)}, u32[]{:S(2)}) %collective-permute-start.5) | collective-permute-done | bytes 262176 | tf_op jit(solution)/shard_map/ppermute | solution.py:32
  38.3 1.7 collective-permute-done.6.a3
  44.2 2.3 collective-permute-start.10
  47.3 2.4 collective-permute-done.7.rest_1_.a1
  49.7 6.4 %collective-permute-done.13.b3.m3 = f32[256,256]{1,0:T(8,128)S(1)} collective-permute-done((f32[256,256]{1,0:T(8,128)S(1)}, f32[256,256]{1,0:T(8,128)S(1)}, u32[]{:S(2)}, u32[]{:S(2)}) %collective-permute-start.13) | collective-permute-done | bytes 262176 | tf_op jit(solution)/shard_map/ppermute | solution.py:32
  59.9 3.6 %collective-permute-start.15 = (f32[192,256]{1,0:T(8,128)S(1)}, f32[192,256]{1,0:T(8,128)S(1)}, u32[]{:S(2)}, u32[]{:S(2)}) collective-permute-start(f32[192,256]{1,0:T(8,128)S(1)} %get-tuple-element.123), channel_id=1, source_target_pairs={{0,16},{1,17},{2,18},{3,19},{4,20},{5,21},{6,22},{7,23},{8,24},{9,... | collective-permute-start | bytes 589832 | tf_op jit(solution)/shard_map/ppermute | solution.py:32
  63.9 2.9 %collective-permute-done.14.e1 = f32[192,256]{1,0:T(8,128)S(1)} collective-permute-done((f32[192,256]{1,0:T(8,128)S(1)}, f32[192,256]{1,0:T(8,128)S(1)}, u32[]{:S(2)}, u32[]{:S(2)}) %collective-permute-start.14) | collective-permute-done | bytes 196640 | tf_op jit(solution)/shard_map/ppermute | solution.py:32
  66.8 6.0 %collective-permute-done.15.e2 = f32[192,256]{1,0:T(8,128)S(1)} collective-permute-done((f32[192,256]{1,0:T(8,128)S(1)}, f32[192,256]{1,0:T(8,128)S(1)}, u32[]{:S(2)}, u32[]{:S(2)}) %collective-permute-start.15) | collective-permute-done | bytes 196640 | tf_op jit(solution)/shard_map/ppermute | solution.py:32
  72.7 2.6 collective-permute-done.16.e3
  76.1 3.4 %collective-permute-start.18 = (f32[128,256]{1,0:T(8,128)S(1)}, f32[128,256]{1,0:T(8,128)S(1)}, u32[]{:S(2)}, u32[]{:S(2)}) collective-permute-start(f32[128,256]{1,0:T(8,128)S(1)} %fusion.y0.refs_7_), channel_id=1, source_target_pairs={{0,8},{1,9},{2,10},{3,11},{4,12},{5,13},{6,14},{7,15},{8,0},{9,1},... | collective-permute-start | bytes 393224 | tf_op jit(solution)/shard_map/ppermute | solution.py:32
  86.5 1.7 collective-permute-start.21
  88.2 3.1 %collective-permute-start.23 = (f32[128,256]{1,0:T(8,128)S(1)}, f32[128,256]{1,0:T(8,128)S(1)}, u32[]{:S(2)}, u32[]{:S(2)}) collective-permute-start(f32[128,256]{1,0:T(8,128)S(1)} %get-tuple-element.127), channel_id=1, source_target_pairs={{0,6},{1,7},{2,4},{3,5},{4,2},{5,3},{6,0},{7,1},{8,14},{9,15},{10,... | collective-permute-start | bytes 393224 | tf_op jit(solution)/shard_map/ppermute | solution.py:32
  92.6 2.2 collective-permute-done.22
  96.1 2.5 collective-permute-start.29
  98.6 1.9 collective-permute-start.32
  104.3 4.8 %collective-permute-done.28 = f32[128,256]{1,0:T(8,128)S(1)} collective-permute-done((f32[128,256]{1,0:T(8,128)S(1)}, f32[128,256]{1,0:T(8,128)S(1)}, u32[]{:S(2)}, u32[]{:S(2)}) %collective-permute-start.28) | collective-permute-done | bytes 131104 | tf_op jit(solution)/shard_map/ppermute | solution.py:32
  109.2 3.2 %collective-permute-done.32.a3.b3 = f32[256,256]{1,0:T(8,128)S(1)} collective-permute-done((f32[256,256]{1,0:T(8,128)S(1)}, f32[256,256]{1,0:T(8,128)S(1)}, u32[]{:S(2)}, u32[]{:S(2)}) %collective-permute-start.32) | collective-permute-done | bytes 262176 | tf_op jit(solution)/shard_map/ppermute | solution.py:32
  113.2 2.3 collective-permute-done.36.x_sib
  116.8 4.6 %collective-permute-start.39 = (f32[128,256]{1,0:T(8,128)S(1)}, f32[128,256]{1,0:T(8,128)S(1)}, u32[]{:S(2)}, u32[]{:S(2)}) collective-permute-start(f32[128,256]{1,0:T(8,128)S(1)} %get-tuple-element.154), channel_id=1, source_target_pairs={{0,24},{1,25},{2,26},{3,27},{4,28},{5,29},{6,30},{7,31},{8,16},{9,... | collective-permute-start | bytes 393224 | tf_op jit(solution)/shard_map/ppermute | solution.py:32
  123.1 3.1 %collective-permute-start.33 = (f32[256,256]{1,0:T(8,128)S(1)}, f32[256,256]{1,0:T(8,128)S(1)}, u32[]{:S(2)}, u32[]{:S(2)}) collective-permute-start(f32[256,256]{1,0:T(8,128)S(1)} %shard_map.63.b0), channel_id=1, source_target_pairs={{0,2},{1,3},{2,0},{3,1},{4,6},{5,7},{6,4},{7,5},{8,10},{9,11},{10,... | collective-permute-start | bytes 786440 | tf_op jit(solution)/shard_map/ppermute | solution.py:32
  126.7 3.5 %collective-permute-start.42 = (f32[128,256]{1,0:T(8,128)S(1)}, f32[128,256]{1,0:T(8,128)S(1)}, u32[]{:S(2)}, u32[]{:S(2)}) collective-permute-start(f32[128,256]{1,0:T(8,128)S(1)} %add_add_fusion.5.y0.refs_5_), channel_id=1, source_target_pairs={{0,24},{1,25},{2,26},{3,27},{4,28},{5,29},{6,30},{7,31},{8,16},{9,... | collective-permute-start | bytes 393224 | tf_op jit(solution)/shard_map/ppermute | solution.py:32
  130.2 6.2 %collective-permute-done.35.b3 = f32[256,256]{1,0:T(8,128)S(1)} collective-permute-done((f32[256,256]{1,0:T(8,128)S(1)}, f32[256,256]{1,0:T(8,128)S(1)}, u32[]{:S(2)}, u32[]{:S(2)}) %collective-permute-start.35) | collective-permute-done | bytes 262176 | tf_op jit(solution)/shard_map/ppermute | solution.py:32
  137.0 4.3 %collective-permute-done.40.y1 = f32[128,256]{1,0:T(8,128)S(1)} collective-permute-done((f32[128,256]{1,0:T(8,128)S(1)}, f32[128,256]{1,0:T(8,128)S(1)}, u32[]{:S(2)}, u32[]{:S(2)}) %collective-permute-start.40) | collective-permute-done | bytes 131104 | tf_op jit(solution)/shard_map/ppermute | solution.py:32
  141.6 2.6 collective-permute-done.43.b_sib
  146.4 2.7 collective-permute-start.46
  152.0 3.5 %collective-permute-done.46 = f32[128,256]{1,0:T(8,128)S(1)} collective-permute-done((f32[128,256]{1,0:T(8,128)S(1)}, f32[128,256]{1,0:T(8,128)S(1)}, u32[]{:S(2)}, u32[]{:S(2)}) %collective-permute-start.46) | collective-permute-done | bytes 131104 | tf_op jit(solution)/shard_map/ppermute | solution.py:32
  155.5 2.2 collective-permute-done.47
  159.3 2.6 collective-permute-start.48
  161.9 4.6 %collective-permute-done.50 = f32[128,256]{1,0:T(8,128)S(1)} collective-permute-done((f32[128,256]{1,0:T(8,128)S(1)}, f32[128,256]{1,0:T(8,128)S(1)}, u32[]{:S(2)}, u32[]{:S(2)}) %collective-permute-start.50) | collective-permute-done | bytes 131104 | tf_op jit(solution)/shard_map/ppermute | solution.py:32
  172.5 2.9 %collective-permute-start.54 = (f32[128,256]{1,0:T(8,128)S(1)}, f32[128,256]{1,0:T(8,128)S(1)}, u32[]{:S(2)}, u32[]{:S(2)}) collective-permute-start(f32[128,256]{1,0:T(8,128)S(1)} %get-tuple-element.172), channel_id=1, source_target_pairs={{0,24},{1,25},{2,26},{3,27},{4,28},{5,29},{6,30},{7,31},{8,16},{9,... | collective-permute-start | bytes 393224 | tf_op jit(solution)/shard_map/ppermute | solution.py:32
  177.0 1.8 collective-permute-done.53
  178.9 2.2 collective-permute-done.54
  181.2 3.0 %collective-permute-start.57 = (f32[128,256]{1,0:T(8,128)S(1)}, f32[128,256]{1,0:T(8,128)S(1)}, u32[]{:S(2)}, u32[]{:S(2)}) collective-permute-start(f32[128,256]{1,0:T(8,128)S(1)} %add_add_fusion.3.y0.refs_3_), channel_id=1, source_target_pairs={{0,24},{1,25},{2,26},{3,27},{4,28},{5,29},{6,30},{7,31},{8,16},{9,... | collective-permute-start | bytes 393224 | tf_op jit(solution)/shard_map/ppermute | solution.py:32
  185.3 4.1 %collective-permute-done.57.y3 = f32[128,256]{1,0:T(8,128)S(1)} collective-permute-done((f32[128,256]{1,0:T(8,128)S(1)}, f32[128,256]{1,0:T(8,128)S(1)}, u32[]{:S(2)}, u32[]{:S(2)}) %collective-permute-start.57) | collective-permute-done | bytes 131104 | tf_op jit(solution)/shard_map/ppermute | solution.py:32
  189.4 2.3 collective-permute-done.56.y2
  193.1 1.8 collective-permute-start.59
  194.9 2.9 %collective-permute-start.60 = (f32[128,256]{1,0:T(8,128)S(1)}, f32[128,256]{1,0:T(8,128)S(1)}, u32[]{:S(2)}, u32[]{:S(2)}) collective-permute-start(f32[128,256]{1,0:T(8,128)S(1)} %get-tuple-element.176), channel_id=1, source_target_pairs={{0,6},{1,7},{2,4},{3,5},{4,2},{5,3},{6,0},{7,1},{8,14},{9,15},{10,... | collective-permute-start | bytes 393224 | tf_op jit(solution)/shard_map/ppermute | solution.py:32
  201.2 3.3 %collective-permute-start.63 = (f32[128,256]{1,0:T(8,128)S(1)}, f32[128,256]{1,0:T(8,128)S(1)}, u32[]{:S(2)}, u32[]{:S(2)}) collective-permute-start(f32[128,256]{1,0:T(8,128)S(1)} %add_add_fusion.2.refs_2_), channel_id=1, source_target_pairs={{0,6},{1,7},{2,4},{3,5},{4,2},{5,3},{6,0},{7,1},{8,14},{9,15},{10,... | collective-permute-start | bytes 393224 | tf_op jit(solution)/shard_map/ppermute | solution.py:32
  205.7 2.8 collective-permute-done.63
  208.4 2.5 collective-permute-done.62
  211.1 1.9 collective-permute-done.64.x_sib
  214.3 4.2 %collective-permute-start.66 = (f32[128,256]{1,0:T(8,128)S(1)}, f32[128,256]{1,0:T(8,128)S(1)}, u32[]{:S(2)}, u32[]{:S(2)}) collective-permute-start(f32[128,256]{1,0:T(8,128)S(1)} %get-tuple-element.181), channel_id=1, source_target_pairs={{0,16},{1,17},{2,18},{3,19},{4,20},{5,21},{6,22},{7,23},{8,24},{9,... | collective-permute-start | bytes 393224 | tf_op jit(solution)/shard_map/ppermute | solution.py:32
  220.7 4.3 %collective-permute-done.66 = f32[128,256]{1,0:T(8,128)S(1)} collective-permute-done((f32[128,256]{1,0:T(8,128)S(1)}, f32[128,256]{1,0:T(8,128)S(1)}, u32[]{:S(2)}, u32[]{:S(2)}) %collective-permute-start.66) | collective-permute-done | bytes 131104 | tf_op jit(solution)/shard_map/ppermute | solution.py:32
  225.0 2.2 collective-permute-done.67
  228.3 3.1 %collective-permute-start.68 = (f32[128,256]{1,0:T(8,128)S(1)}, f32[128,256]{1,0:T(8,128)S(1)}, u32[]{:S(2)}, u32[]{:S(2)}) collective-permute-start(f32[128,256]{1,0:T(8,128)S(1)} %add_add_fusion.1.y0.refs_1_), channel_id=1, source_target_pairs={{0,8},{1,9},{2,10},{3,11},{4,12},{5,13},{6,14},{7,15},{8,0},{9,1},... | collective-permute-start | bytes 393224 | tf_op jit(solution)/shard_map/ppermute | solution.py:32
  231.4 4.8 %collective-permute-done.70.y3 = f32[128,256]{1,0:T(8,128)S(1)} collective-permute-done((f32[128,256]{1,0:T(8,128)S(1)}, f32[128,256]{1,0:T(8,128)S(1)}, u32[]{:S(2)}, u32[]{:S(2)}) %collective-permute-start.70) | collective-permute-done | bytes 131104 | tf_op jit(solution)/shard_map/ppermute | solution.py:32
  238.3 2.8 collective-permute-start.72
  241.1 1.9 collective-permute-start.73
  244.0 2.3 collective-permute-done.72
  248.7 3.4 %collective-permute-start.75 = (f32[2,2,64,256]{3,2,1,0:T(8,128)S(1)}, f32[2,2,64,256]{3,2,1,0:T(8,128)S(1)}, u32[]{:S(2)}, u32[]{:S(2)}) collective-permute-start(f32[2,2,64,256]{3,2,1,0:T(8,128)S(1)} %get-tuple-element.191), channel_id=1, source_target_pairs={{0,64},{1,65},{2,66},{3,67},{4,68},{5,69},{6,70},{7,71},{8,72},{9,... | collective-permute-start | bytes 786440 | tf_op jit(solution)/shard_map/ppermute | solution.py:32
  253.4 4.5 %collective-permute-done.74.a1 = f32[2,2,64,256]{3,2,1,0:T(8,128)S(1)} collective-permute-done((f32[2,2,64,256]{3,2,1,0:T(8,128)S(1)}, f32[2,2,64,256]{3,2,1,0:T(8,128)S(1)}, u32[]{:S(2)}, u32[]{:S(2)}) %collective-permute-start.74) | collective-permute-done | bytes 262176 | tf_op jit(solution)/shard_map/ppermute | solution.py:32
  258.0 4.8 %collective-permute-done.75.a2 = f32[2,2,64,256]{3,2,1,0:T(8,128)S(1)} collective-permute-done((f32[2,2,64,256]{3,2,1,0:T(8,128)S(1)}, f32[2,2,64,256]{3,2,1,0:T(8,128)S(1)}, u32[]{:S(2)}, u32[]{:S(2)}) %collective-permute-start.75) | collective-permute-done | bytes 262176 | tf_op jit(solution)/shard_map/ppermute | solution.py:32
  262.8 2.6 collective-permute-done.76.a3
  266.5 3.1 %collective-permute-start.78 = (f32[2,64,256]{2,1,0:T(8,128)S(1)}, f32[2,64,256]{2,1,0:T(8,128)S(1)}, u32[]{:S(2)}, u32[]{:S(2)}) collective-permute-start(f32[2,64,256]{2,1,0:T(8,128)S(1)} %get-tuple-element.195), channel_id=1, source_target_pairs={{0,4},{1,5},{2,6},{3,7},{4,0},{5,1},{6,2},{7,3},{8,12},{9,13},{10,... | collective-permute-start | bytes 393224 | tf_op jit(solution)/shard_map/ppermute | solution.py:32
  271.3 2.8 %collective-permute-done.78.h2 = f32[2,64,256]{2,1,0:T(8,128)S(1)} collective-permute-done((f32[2,64,256]{2,1,0:T(8,128)S(1)}, f32[2,64,256]{2,1,0:T(8,128)S(1)}, u32[]{:S(2)}, u32[]{:S(2)}) %collective-permute-start.78) | collective-permute-done | bytes 131104 | tf_op jit(solution)/shard_map/ppermute | solution.py:32
  274.1 1.7 collective-permute-done.79.h3
  276.5 1.9 collective-permute-done.80.got
  278.4 1.7 shard_map.76
  (158 shorter events, 71.6 us)
Async XLA Ops:
  2.3 6.5 %collective-permute-start = (f32[2,64,512]{2,1,0:T(8,128)S(1)}, f32[2,64,512]{2,1,0:T(8,128)S(1)}, u32[]{:S(2)}, u32[]{:S(2)}) collective-permute-start(f32[2,64,512]{2,1,0:T(8,128)S(1)} %pad_maximum_fusion.5), channel_id=1, source_target_pairs={{0,2},{1,3},{2,0},{3,1},{4,6},{5,7},{6,4},{7,5},{8,10},{9,11},{10,... | collective-permute-start | bytes 786440 | tf_op jit(solution)/shard_map/ppermute | solution.py:32
  4.1 10.1 %collective-permute-start.1 = (f32[2,64,512]{2,1,0:T(8,128)S(1)}, f32[2,64,512]{2,1,0:T(8,128)S(1)}, u32[]{:S(2)}, u32[]{:S(2)}) collective-permute-start(f32[2,64,512]{2,1,0:T(8,128)S(1)} %pad_maximum_fusion.6), channel_id=1, source_target_pairs={{0,4},{1,5},{2,6},{3,7},{4,0},{5,1},{6,2},{7,3},{8,12},{9,13},{10,... | collective-permute-start | bytes 786440 | tf_op jit(solution)/shard_map/ppermute | solution.py:32
  7.1 9.7 %collective-permute-start.2 = (f32[2,64,512]{2,1,0:T(8,128)S(1)}, f32[2,64,512]{2,1,0:T(8,128)S(1)}, u32[]{:S(2)}, u32[]{:S(2)}) collective-permute-start(f32[2,64,512]{2,1,0:T(8,128)S(1)} %pad_maximum_fusion.7), channel_id=1, source_target_pairs={{0,6},{1,7},{2,4},{3,5},{4,2},{5,3},{6,0},{7,1},{8,14},{9,15},{10,... | collective-permute-start | bytes 786440 | tf_op jit(solution)/shard_map/ppermute | solution.py:32
  21.4 16.9 %collective-permute-start.4 = (f32[6,64,256]{2,1,0:T(8,128)S(1)}, f32[6,64,256]{2,1,0:T(8,128)S(1)}, u32[]{:S(2)}, u32[]{:S(2)}) collective-permute-start(f32[6,64,256]{2,1,0:T(8,128)S(1)} %get-tuple-element.106), channel_id=1, source_target_pairs={{0,1},{1,0},{2,3},{3,2},{4,5},{5,4},{6,7},{7,6},{8,9},{9,8},{10,11... | collective-permute-start | bytes 1179656 | tf_op jit(solution)/shard_map/ppermute | solution.py:32
  22.4 17.7 %collective-permute-start.6 = (f32[6,64,256]{2,1,0:T(8,128)S(1)}, f32[6,64,256]{2,1,0:T(8,128)S(1)}, u32[]{:S(2)}, u32[]{:S(2)}) collective-permute-start(f32[6,64,256]{2,1,0:T(8,128)S(1)} %get-tuple-element.108), channel_id=1, source_target_pairs={{0,65},{1,64},{2,67},{3,66},{4,69},{5,68},{6,71},{7,70},{8,73},{9,... | collective-permute-start | bytes 1179656 | tf_op jit(solution)/shard_map/ppermute | solution.py:32
  23.5 14.8 %collective-permute-start.5 = (f32[4,64,256]{2,1,0:T(8,128)S(1)}, f32[4,64,256]{2,1,0:T(8,128)S(1)}, u32[]{:S(2)}, u32[]{:S(2)}) collective-permute-start(f32[4,64,256]{2,1,0:T(8,128)S(1)} %get-tuple-element.107), channel_id=1, source_target_pairs={{0,64},{1,65},{2,66},{3,67},{4,68},{5,69},{6,70},{7,71},{8,72},{9,... | collective-permute-start | bytes 786440 | tf_op jit(solution)/shard_map/ppermute | solution.py:32
  40.9 8.8 %collective-permute-start.7 = (f32[256,256]{1,0:T(8,128)S(1)}, f32[256,256]{1,0:T(8,128)S(1)}, u32[]{:S(2)}, u32[]{:S(2)}) collective-permute-start(f32[256,256]{1,0:T(8,128)S(1)} %get-tuple-element.113.rest_0_.a0), channel_id=1, source_target_pairs={{0,2},{1,3},{2,0},{3,1},{4,6},{5,7},{6,4},{7,5},{8,10},{9,11},{10,... | collective-permute-start | bytes 786440 | tf_op jit(solution)/shard_map/ppermute | solution.py:32
  42.1 14.0 %collective-permute-start.13 = (f32[256,256]{1,0:T(8,128)S(1)}, f32[256,256]{1,0:T(8,128)S(1)}, u32[]{:S(2)}, u32[]{:S(2)}) collective-permute-start(f32[256,256]{1,0:T(8,128)S(1)} %get-tuple-element.112.b0.m0), channel_id=1, source_target_pairs={{0,65},{1,64},{2,67},{3,66},{4,69},{5,68},{6,71},{7,70},{8,73},{9,... | collective-permute-start | bytes 786440 | tf_op jit(solution)/shard_map/ppermute | solution.py:32
  43.3 12.9 %collective-permute-start.12 = (f32[256,256]{1,0:T(8,128)S(1)}, f32[256,256]{1,0:T(8,128)S(1)}, u32[]{:S(2)}, u32[]{:S(2)}) collective-permute-start(f32[256,256]{1,0:T(8,128)S(1)} %get-tuple-element.112.b0.m0), channel_id=1, source_target_pairs={{0,64},{1,65},{2,66},{3,67},{4,68},{5,69},{6,70},{7,71},{8,72},{9,... | collective-permute-start | bytes 786440 | tf_op jit(solution)/shard_map/ppermute | solution.py:32
  44.2 13.1 %collective-permute-start.10 = (f32[256,256]{1,0:T(8,128)S(1)}, f32[256,256]{1,0:T(8,128)S(1)}, u32[]{:S(2)}, u32[]{:S(2)}) collective-permute-start(f32[256,256]{1,0:T(8,128)S(1)} %get-tuple-element.113.rest_0_.a0), channel_id=1, source_target_pairs={{0,6},{1,7},{2,4},{3,5},{4,2},{5,3},{6,0},{7,1},{8,14},{9,15},{10,... | collective-permute-start | bytes 786440 | tf_op jit(solution)/shard_map/ppermute | solution.py:32
  46.5 10.8 %collective-permute-start.9 = (f32[256,256]{1,0:T(8,128)S(1)}, f32[256,256]{1,0:T(8,128)S(1)}, u32[]{:S(2)}, u32[]{:S(2)}) collective-permute-start(f32[256,256]{1,0:T(8,128)S(1)} %get-tuple-element.113.rest_0_.a0), channel_id=1, source_target_pairs={{0,4},{1,5},{2,6},{3,7},{4,0},{5,1},{6,2},{7,3},{8,12},{9,13},{10,... | collective-permute-start | bytes 786440 | tf_op jit(solution)/shard_map/ppermute | solution.py:32
  49.7 7.6 %collective-permute-start.11 = (f32[256,256]{1,0:T(8,128)S(1)}, f32[256,256]{1,0:T(8,128)S(1)}, u32[]{:S(2)}, u32[]{:S(2)}) collective-permute-start(f32[256,256]{1,0:T(8,128)S(1)} %get-tuple-element.112.b0.m0), channel_id=1, source_target_pairs={{0,1},{1,0},{2,3},{3,2},{4,5},{5,4},{6,7},{7,6},{8,9},{9,8},{10,11... | collective-permute-start | bytes 786440 | tf_op jit(solution)/shard_map/ppermute | solution.py:32
  59.0 7.8 %collective-permute-start.14 = (f32[192,256]{1,0:T(8,128)S(1)}, f32[192,256]{1,0:T(8,128)S(1)}, u32[]{:S(2)}, u32[]{:S(2)}) collective-permute-start(f32[192,256]{1,0:T(8,128)S(1)} %get-tuple-element.122), channel_id=1, source_target_pairs={{0,8},{1,9},{2,10},{3,11},{4,12},{5,13},{6,14},{7,15},{8,0},{9,1},... | collective-permute-start | bytes 589832 | tf_op jit(solution)/shard_map/ppermute | solution.py:32
  59.9 12.8 %collective-permute-start.15 = (f32[192,256]{1,0:T(8,128)S(1)}, f32[192,256]{1,0:T(8,128)S(1)}, u32[]{:S(2)}, u32[]{:S(2)}) collective-permute-start(f32[192,256]{1,0:T(8,128)S(1)} %get-tuple-element.123), channel_id=1, source_target_pairs={{0,16},{1,17},{2,18},{3,19},{4,20},{5,21},{6,22},{7,23},{8,24},{9,... | collective-permute-start | bytes 589832 | tf_op jit(solution)/shard_map/ppermute | solution.py:32
  63.5 11.8 %collective-permute-start.16 = (f32[192,256]{1,0:T(8,128)S(1)}, f32[192,256]{1,0:T(8,128)S(1)}, u32[]{:S(2)}, u32[]{:S(2)}) collective-permute-start(f32[192,256]{1,0:T(8,128)S(1)} %get-tuple-element.124), channel_id=1, source_target_pairs={{0,24},{1,25},{2,26},{3,27},{4,28},{5,29},{6,30},{7,31},{8,16},{9,... | collective-permute-start | bytes 589832 | tf_op jit(solution)/shard_map/ppermute | solution.py:32
  63.8 17.2 %collective-permute-start.17 = (f32[4,128,256]{2,1,0:T(8,128)S(1)}, f32[4,128,256]{2,1,0:T(8,128)S(1)}, u32[]{:S(2)}, u32[]{:S(2)}) collective-permute-start(f32[4,128,256]{2,1,0:T(8,128)S(1)} %pad_maximum_fusion.1), channel_id=1, source_target_pairs={{0,32},{1,33},{2,34},{3,35},{4,36},{5,37},{6,38},{7,39},{8,40},{9,... | collective-permute-start | bytes 1572872 | tf_op jit(solution)/shard_map/ppermute | solution.py:32
  75.4 8.5 %collective-permute-start.20 = (f32[128,256]{1,0:T(8,128)S(1)}, f32[128,256]{1,0:T(8,128)S(1)}, u32[]{:S(2)}, u32[]{:S(2)}) collective-permute-start(f32[128,256]{1,0:T(8,128)S(1)} %fusion.y0.refs_7_), channel_id=1, source_target_pairs={{0,24},{1,25},{2,26},{3,27},{4,28},{5,29},{6,30},{7,31},{8,16},{9,... | collective-permute-start | bytes 393224 | tf_op jit(solution)/shard_map/ppermute | solution.py:32
  75.7 9.4 %collective-permute-start.19 = (f32[128,256]{1,0:T(8,128)S(1)}, f32[128,256]{1,0:T(8,128)S(1)}, u32[]{:S(2)}, u32[]{:S(2)}) collective-permute-start(f32[128,256]{1,0:T(8,128)S(1)} %fusion.y0.refs_7_), channel_id=1, source_target_pairs={{0,16},{1,17},{2,18},{3,19},{4,20},{5,21},{6,22},{7,23},{8,24},{9,... | collective-permute-start | bytes 393224 | tf_op jit(solution)/shard_map/ppermute | solution.py:32
  76.1 9.1 %collective-permute-start.18 = (f32[128,256]{1,0:T(8,128)S(1)}, f32[128,256]{1,0:T(8,128)S(1)}, u32[]{:S(2)}, u32[]{:S(2)}) collective-permute-start(f32[128,256]{1,0:T(8,128)S(1)} %fusion.y0.refs_7_), channel_id=1, source_target_pairs={{0,8},{1,9},{2,10},{3,11},{4,12},{5,13},{6,14},{7,15},{8,0},{9,1},... | collective-permute-start | bytes 393224 | tf_op jit(solution)/shard_map/ppermute | solution.py:32
  79.5 8.7 %collective-permute-start.24 = (f32[2,64,256]{2,1,0:T(8,128)S(1)}, f32[2,64,256]{2,1,0:T(8,128)S(1)}, u32[]{:S(2)}, u32[]{:S(2)}) collective-permute-start(f32[2,64,256]{2,1,0:T(8,128)S(1)} %get-tuple-element.134), channel_id=1, source_target_pairs={{0,1},{1,0},{2,3},{3,2},{4,5},{5,4},{6,7},{7,6},{8,9},{9,8},{10,11... | collective-permute-start | bytes 393224 | tf_op jit(solution)/shard_map/ppermute | solution.py:32
  81.0 10.3 %collective-permute-start.25 = (f32[2,64,256]{2,1,0:T(8,128)S(1)}, f32[2,64,256]{2,1,0:T(8,128)S(1)}, u32[]{:S(2)}, u32[]{:S(2)}) collective-permute-start(f32[2,64,256]{2,1,0:T(8,128)S(1)} %get-tuple-element.135), channel_id=1, source_target_pairs={{0,64},{1,65},{2,66},{3,67},{4,68},{5,69},{6,70},{7,71},{8,72},{9,... | collective-permute-start | bytes 393224 | tf_op jit(solution)/shard_map/ppermute | solution.py:32
  83.8 7.4 %collective-permute-start.26 = (f32[2,64,256]{2,1,0:T(8,128)S(1)}, f32[2,64,256]{2,1,0:T(8,128)S(1)}, u32[]{:S(2)}, u32[]{:S(2)}) collective-permute-start(f32[2,64,256]{2,1,0:T(8,128)S(1)} %get-tuple-element.136), channel_id=1, source_target_pairs={{0,65},{1,64},{2,67},{3,66},{4,69},{5,68},{6,71},{7,70},{8,73},{9,... | collective-permute-start | bytes 393224 | tf_op jit(solution)/shard_map/ppermute | solution.py:32
  88.2 6.5 %collective-permute-start.22 = (f32[128,256]{1,0:T(8,128)S(1)}, f32[128,256]{1,0:T(8,128)S(1)}, u32[]{:S(2)}, u32[]{:S(2)}) collective-permute-start(f32[128,256]{1,0:T(8,128)S(1)} %get-tuple-element.126), channel_id=1, source_target_pairs={{0,4},{1,5},{2,6},{3,7},{4,0},{5,1},{6,2},{7,3},{8,12},{9,13},{10,... | collective-permute-start | bytes 393224 | tf_op jit(solution)/shard_map/ppermute | solution.py:32
  88.2 7.8 %collective-permute-start.23 = (f32[128,256]{1,0:T(8,128)S(1)}, f32[128,256]{1,0:T(8,128)S(1)}, u32[]{:S(2)}, u32[]{:S(2)}) collective-permute-start(f32[128,256]{1,0:T(8,128)S(1)} %get-tuple-element.127), channel_id=1, source_target_pairs={{0,6},{1,7},{2,4},{3,5},{4,2},{5,3},{6,0},{7,1},{8,14},{9,15},{10,... | collective-permute-start | bytes 393224 | tf_op jit(solution)/shard_map/ppermute | solution.py:32
  96.1 6.7 %collective-permute-start.29 = (f32[128,256]{1,0:T(8,128)S(1)}, f32[128,256]{1,0:T(8,128)S(1)}, u32[]{:S(2)}, u32[]{:S(2)}) collective-permute-start(f32[128,256]{1,0:T(8,128)S(1)} %add_add_fusion.6.refs_6_), channel_id=1, source_target_pairs={{0,6},{1,7},{2,4},{3,5},{4,2},{5,3},{6,0},{7,1},{8,14},{9,15},{10,... | collective-permute-start | bytes 393224 | tf_op jit(solution)/shard_map/ppermute | solution.py:32
  98.6 13.7 %collective-permute-start.32 = (f32[256,256]{1,0:T(8,128)S(1)}, f32[256,256]{1,0:T(8,128)S(1)}, u32[]{:S(2)}, u32[]{:S(2)}) collective-permute-start(f32[256,256]{1,0:T(8,128)S(1)} %get-tuple-element.161.a0.b0), channel_id=1, source_target_pairs={{0,65},{1,64},{2,67},{3,66},{4,69},{5,68},{6,71},{7,70},{8,73},{9,... | collective-permute-start | bytes 786440 | tf_op jit(solution)/shard_map/ppermute | solution.py:32
  100.5 11.8 %collective-permute-start.31 = (f32[256,256]{1,0:T(8,128)S(1)}, f32[256,256]{1,0:T(8,128)S(1)}, u32[]{:S(2)}, u32[]{:S(2)}) collective-permute-start(f32[256,256]{1,0:T(8,128)S(1)} %get-tuple-element.161.a0.b0), channel_id=1, source_target_pairs={{0,64},{1,65},{2,66},{3,67},{4,68},{5,69},{6,70},{7,71},{8,72},{9,... | collective-permute-start | bytes 786440 | tf_op jit(solution)/shard_map/ppermute | solution.py:32
  101.4 11.6 %collective-permute-start.30 = (f32[256,256]{1,0:T(8,128)S(1)}, f32[256,256]{1,0:T(8,128)S(1)}, u32[]{:S(2)}, u32[]{:S(2)}) collective-permute-start(f32[256,256]{1,0:T(8,128)S(1)} %get-tuple-element.161.a0.b0), channel_id=1, source_target_pairs={{0,1},{1,0},{2,3},{3,2},{4,5},{5,4},{6,7},{7,6},{8,9},{9,8},{10,11... | collective-permute-start | bytes 786440 | tf_op jit(solution)/shard_map/ppermute | solution.py:32
  102.7 6.5 %collective-permute-start.28 = (f32[128,256]{1,0:T(8,128)S(1)}, f32[128,256]{1,0:T(8,128)S(1)}, u32[]{:S(2)}, u32[]{:S(2)}) collective-permute-start(f32[128,256]{1,0:T(8,128)S(1)} %add_add_fusion.6.refs_6_), channel_id=1, source_target_pairs={{0,4},{1,5},{2,6},{3,7},{4,0},{5,1},{6,2},{7,3},{8,12},{9,13},{10,... | collective-permute-start | bytes 393224 | tf_op jit(solution)/shard_map/ppermute | solution.py:32
  102.7 6.5 %collective-permute-start.27 = (f32[128,256]{1,0:T(8,128)S(1)}, f32[128,256]{1,0:T(8,128)S(1)}, u32[]{:S(2)}, u32[]{:S(2)}) collective-permute-start(f32[128,256]{1,0:T(8,128)S(1)} %add_add_fusion.6.refs_6_), channel_id=1, source_target_pairs={{0,2},{1,3},{2,0},{3,1},{4,6},{5,7},{6,4},{7,5},{8,10},{9,11},{10,... | collective-permute-start | bytes 393224 | tf_op jit(solution)/shard_map/ppermute | solution.py:32
  116.7 9.4 %collective-permute-start.38 = (f32[128,256]{1,0:T(8,128)S(1)}, f32[128,256]{1,0:T(8,128)S(1)}, u32[]{:S(2)}, u32[]{:S(2)}) collective-permute-start(f32[128,256]{1,0:T(8,128)S(1)} %get-tuple-element.153), channel_id=1, source_target_pairs={{0,16},{1,17},{2,18},{3,19},{4,20},{5,21},{6,22},{7,23},{8,24},{9,... | collective-permute-start | bytes 393224 | tf_op jit(solution)/shard_map/ppermute | solution.py:32
  116.8 9.8 %collective-permute-start.39 = (f32[128,256]{1,0:T(8,128)S(1)}, f32[128,256]{1,0:T(8,128)S(1)}, u32[]{:S(2)}, u32[]{:S(2)}) collective-permute-start(f32[128,256]{1,0:T(8,128)S(1)} %get-tuple-element.154), channel_id=1, source_target_pairs={{0,24},{1,25},{2,26},{3,27},{4,28},{5,29},{6,30},{7,31},{8,16},{9,... | collective-permute-start | bytes 393224 | tf_op jit(solution)/shard_map/ppermute | solution.py:32
  122.0 14.4 %collective-permute-start.35 = (f32[256,256]{1,0:T(8,128)S(1)}, f32[256,256]{1,0:T(8,128)S(1)}, u32[]{:S(2)}, u32[]{:S(2)}) collective-permute-start(f32[256,256]{1,0:T(8,128)S(1)} %shard_map.63.b0), channel_id=1, source_target_pairs={{0,6},{1,7},{2,4},{3,5},{4,2},{5,3},{6,0},{7,1},{8,14},{9,15},{10,... | collective-permute-start | bytes 786440 | tf_op jit(solution)/shard_map/ppermute | solution.py:32
  122.7 13.7 %collective-permute-start.34 = (f32[256,256]{1,0:T(8,128)S(1)}, f32[256,256]{1,0:T(8,128)S(1)}, u32[]{:S(2)}, u32[]{:S(2)}) collective-permute-start(f32[256,256]{1,0:T(8,128)S(1)} %shard_map.63.b0), channel_id=1, source_target_pairs={{0,4},{1,5},{2,6},{3,7},{4,0},{5,1},{6,2},{7,3},{8,12},{9,13},{10,... | collective-permute-start | bytes 786440 | tf_op jit(solution)/shard_map/ppermute | solution.py:32
  123.1 14.0 %collective-permute-start.33 = (f32[256,256]{1,0:T(8,128)S(1)}, f32[256,256]{1,0:T(8,128)S(1)}, u32[]{:S(2)}, u32[]{:S(2)}) collective-permute-start(f32[256,256]{1,0:T(8,128)S(1)} %shard_map.63.b0), channel_id=1, source_target_pairs={{0,2},{1,3},{2,0},{3,1},{4,6},{5,7},{6,4},{7,5},{8,10},{9,11},{10,... | collective-permute-start | bytes 786440 | tf_op jit(solution)/shard_map/ppermute | solution.py:32
  126.7 10.3 %collective-permute-start.42 = (f32[128,256]{1,0:T(8,128)S(1)}, f32[128,256]{1,0:T(8,128)S(1)}, u32[]{:S(2)}, u32[]{:S(2)}) collective-permute-start(f32[128,256]{1,0:T(8,128)S(1)} %add_add_fusion.5.y0.refs_5_), channel_id=1, source_target_pairs={{0,24},{1,25},{2,26},{3,27},{4,28},{5,29},{6,30},{7,31},{8,16},{9,... | collective-permute-start | bytes 393224 | tf_op jit(solution)/shard_map/ppermute | solution.py:32
  130.2 6.8 %collective-permute-start.41 = (f32[128,256]{1,0:T(8,128)S(1)}, f32[128,256]{1,0:T(8,128)S(1)}, u32[]{:S(2)}, u32[]{:S(2)}) collective-permute-start(f32[128,256]{1,0:T(8,128)S(1)} %add_add_fusion.5.y0.refs_5_), channel_id=1, source_target_pairs={{0,16},{1,17},{2,18},{3,19},{4,20},{5,21},{6,22},{7,23},{8,24},{9,... | collective-permute-start | bytes 393224 | tf_op jit(solution)/shard_map/ppermute | solution.py:32
  146.4 9.1 %collective-permute-start.46 = (f32[128,256]{1,0:T(8,128)S(1)}, f32[128,256]{1,0:T(8,128)S(1)}, u32[]{:S(2)}, u32[]{:S(2)}) collective-permute-start(f32[128,256]{1,0:T(8,128)S(1)} %get-tuple-element.167), channel_id=1, source_target_pairs={{0,64},{1,65},{2,66},{3,67},{4,68},{5,69},{6,70},{7,71},{8,72},{9,... | collective-permute-start | bytes 393224 | tf_op jit(solution)/shard_map/ppermute | solution.py:32
  149.1 8.7 %collective-permute-start.47 = (f32[128,256]{1,0:T(8,128)S(1)}, f32[128,256]{1,0:T(8,128)S(1)}, u32[]{:S(2)}, u32[]{:S(2)}) collective-permute-start(f32[128,256]{1,0:T(8,128)S(1)} %get-tuple-element.168), channel_id=1, source_target_pairs={{0,65},{1,64},{2,67},{3,66},{4,69},{5,68},{6,71},{7,70},{8,73},{9,... | collective-permute-start | bytes 393224 | tf_op jit(solution)/shard_map/ppermute | solution.py:32
  157.8 8.8 %collective-permute-start.50 = (f32[128,256]{1,0:T(8,128)S(1)}, f32[128,256]{1,0:T(8,128)S(1)}, u32[]{:S(2)}, u32[]{:S(2)}) collective-permute-start(f32[128,256]{1,0:T(8,128)S(1)} %add_add_fusion.4.refs_4_), channel_id=1, source_target_pairs={{0,65},{1,64},{2,67},{3,66},{4,69},{5,68},{6,71},{7,70},{8,73},{9,... | collective-permute-start | bytes 393224 | tf_op jit(solution)/shard_map/ppermute | solution.py:32
  159.2 7.6 %collective-permute-start.49 = (f32[128,256]{1,0:T(8,128)S(1)}, f32[128,256]{1,0:T(8,128)S(1)}, u32[]{:S(2)}, u32[]{:S(2)}) collective-permute-start(f32[128,256]{1,0:T(8,128)S(1)} %add_add_fusion.4.refs_4_), channel_id=1, source_target_pairs={{0,64},{1,65},{2,66},{3,67},{4,68},{5,69},{6,70},{7,71},{8,72},{9,... | collective-permute-start | bytes 393224 | tf_op jit(solution)/shard_map/ppermute | solution.py:32
  159.3 8.0 %collective-permute-start.48 = (f32[128,256]{1,0:T(8,128)S(1)}, f32[128,256]{1,0:T(8,128)S(1)}, u32[]{:S(2)}, u32[]{:S(2)}) collective-permute-start(f32[128,256]{1,0:T(8,128)S(1)} %add_add_fusion.4.refs_4_), channel_id=1, source_target_pairs={{0,1},{1,0},{2,3},{3,2},{4,5},{5,4},{6,7},{7,6},{8,9},{9,8},{10,11... | collective-permute-start | bytes 393224 | tf_op jit(solution)/shard_map/ppermute | solution.py:32
  168.1 17.2 %collective-permute-start.44 = (f32[4,192,256]{2,1,0:T(8,128)S(1)}, f32[4,192,256]{2,1,0:T(8,128)S(1)}, u32[]{:S(2)}, u32[]{:S(2)}) collective-permute-start(f32[4,192,256]{2,1,0:T(8,128)S(1)} %get-tuple-element.165), channel_id=1, source_target_pairs={{0,32},{1,33},{2,34},{3,35},{4,36},{5,37},{6,38},{7,39},{8,40},{9,... | collective-permute-start | bytes 2359304 | tf_op jit(solution)/shard_map/ppermute | solution.py:32
  171.0 7.9 %collective-permute-start.53 = (f32[128,256]{1,0:T(8,128)S(1)}, f32[128,256]{1,0:T(8,128)S(1)}, u32[]{:S(2)}, u32[]{:S(2)}) collective-permute-start(f32[128,256]{1,0:T(8,128)S(1)} %get-tuple-element.171), channel_id=1, source_target_pairs={{0,16},{1,17},{2,18},{3,19},{4,20},{5,21},{6,22},{7,23},{8,24},{9,... | collective-permute-start | bytes 393224 | tf_op jit(solution)/shard_map/ppermute | solution.py:32
  172.5 8.7 %collective-permute-start.54 = (f32[128,256]{1,0:T(8,128)S(1)}, f32[128,256]{1,0:T(8,128)S(1)}, u32[]{:S(2)}, u32[]{:S(2)}) collective-permute-start(f32[128,256]{1,0:T(8,128)S(1)} %get-tuple-element.172), channel_id=1, source_target_pairs={{0,24},{1,25},{2,26},{3,27},{4,28},{5,29},{6,30},{7,31},{8,16},{9,... | collective-permute-start | bytes 393224 | tf_op jit(solution)/shard_map/ppermute | solution.py:32
  181.2 8.3 %collective-permute-start.57 = (f32[128,256]{1,0:T(8,128)S(1)}, f32[128,256]{1,0:T(8,128)S(1)}, u32[]{:S(2)}, u32[]{:S(2)}) collective-permute-start(f32[128,256]{1,0:T(8,128)S(1)} %add_add_fusion.3.y0.refs_3_), channel_id=1, source_target_pairs={{0,24},{1,25},{2,26},{3,27},{4,28},{5,29},{6,30},{7,31},{8,16},{9,... | collective-permute-start | bytes 393224 | tf_op jit(solution)/shard_map/ppermute | solution.py:32
  184.2 7.5 %collective-permute-start.56 = (f32[128,256]{1,0:T(8,128)S(1)}, f32[128,256]{1,0:T(8,128)S(1)}, u32[]{:S(2)}, u32[]{:S(2)}) collective-permute-start(f32[128,256]{1,0:T(8,128)S(1)} %add_add_fusion.3.y0.refs_3_), channel_id=1, source_target_pairs={{0,16},{1,17},{2,18},{3,19},{4,20},{5,21},{6,22},{7,23},{8,24},{9,... | collective-permute-start | bytes 393224 | tf_op jit(solution)/shard_map/ppermute | solution.py:32
  184.2 7.5 %collective-permute-start.55 = (f32[128,256]{1,0:T(8,128)S(1)}, f32[128,256]{1,0:T(8,128)S(1)}, u32[]{:S(2)}, u32[]{:S(2)}) collective-permute-start(f32[128,256]{1,0:T(8,128)S(1)} %add_add_fusion.3.y0.refs_3_), channel_id=1, source_target_pairs={{0,8},{1,9},{2,10},{3,11},{4,12},{5,13},{6,14},{7,15},{8,0},{9,1},... | collective-permute-start | bytes 393224 | tf_op jit(solution)/shard_map/ppermute | solution.py:32
  193.1 6.6 %collective-permute-start.59 = (f32[128,256]{1,0:T(8,128)S(1)}, f32[128,256]{1,0:T(8,128)S(1)}, u32[]{:S(2)}, u32[]{:S(2)}) collective-permute-start(f32[128,256]{1,0:T(8,128)S(1)} %get-tuple-element.175), channel_id=1, source_target_pairs={{0,4},{1,5},{2,6},{3,7},{4,0},{5,1},{6,2},{7,3},{8,12},{9,13},{10,... | collective-permute-start | bytes 393224 | tf_op jit(solution)/shard_map/ppermute | solution.py:32
  201.2 7.3 %collective-permute-start.63 = (f32[128,256]{1,0:T(8,128)S(1)}, f32[128,256]{1,0:T(8,128)S(1)}, u32[]{:S(2)}, u32[]{:S(2)}) collective-permute-start(f32[128,256]{1,0:T(8,128)S(1)} %add_add_fusion.2.refs_2_), channel_id=1, source_target_pairs={{0,6},{1,7},{2,4},{3,5},{4,2},{5,3},{6,0},{7,1},{8,14},{9,15},{10,... | collective-permute-start | bytes 393224 | tf_op jit(solution)/shard_map/ppermute | solution.py:32
  204.5 6.5 %collective-permute-start.62 = (f32[128,256]{1,0:T(8,128)S(1)}, f32[128,256]{1,0:T(8,128)S(1)}, u32[]{:S(2)}, u32[]{:S(2)}) collective-permute-start(f32[128,256]{1,0:T(8,128)S(1)} %add_add_fusion.2.refs_2_), channel_id=1, source_target_pairs={{0,4},{1,5},{2,6},{3,7},{4,0},{5,1},{6,2},{7,3},{8,12},{9,13},{10,... | collective-permute-start | bytes 393224 | tf_op jit(solution)/shard_map/ppermute | solution.py:32
  204.5 6.5 %collective-permute-start.61 = (f32[128,256]{1,0:T(8,128)S(1)}, f32[128,256]{1,0:T(8,128)S(1)}, u32[]{:S(2)}, u32[]{:S(2)}) collective-permute-start(f32[128,256]{1,0:T(8,128)S(1)} %add_add_fusion.2.refs_2_), channel_id=1, source_target_pairs={{0,2},{1,3},{2,0},{3,1},{4,6},{5,7},{6,4},{7,5},{8,10},{9,11},{10,... | collective-permute-start | bytes 393224 | tf_op jit(solution)/shard_map/ppermute | solution.py:32
  214.2 6.4 %collective-permute-start.65 = (f32[128,256]{1,0:T(8,128)S(1)}, f32[128,256]{1,0:T(8,128)S(1)}, u32[]{:S(2)}, u32[]{:S(2)}) collective-permute-start(f32[128,256]{1,0:T(8,128)S(1)} %get-tuple-element.180), channel_id=1, source_target_pairs={{0,8},{1,9},{2,10},{3,11},{4,12},{5,13},{6,14},{7,15},{8,0},{9,1},... | collective-permute-start | bytes 393224 | tf_op jit(solution)/shard_map/ppermute | solution.py:32
  214.3 10.6 %collective-permute-start.66 = (f32[128,256]{1,0:T(8,128)S(1)}, f32[128,256]{1,0:T(8,128)S(1)}, u32[]{:S(2)}, u32[]{:S(2)}) collective-permute-start(f32[128,256]{1,0:T(8,128)S(1)} %get-tuple-element.181), channel_id=1, source_target_pairs={{0,16},{1,17},{2,18},{3,19},{4,20},{5,21},{6,22},{7,23},{8,24},{9,... | collective-permute-start | bytes 393224 | tf_op jit(solution)/shard_map/ppermute | solution.py:32
  218.5 8.7 %collective-permute-start.67 = (f32[128,256]{1,0:T(8,128)S(1)}, f32[128,256]{1,0:T(8,128)S(1)}, u32[]{:S(2)}, u32[]{:S(2)}) collective-permute-start(f32[128,256]{1,0:T(8,128)S(1)} %get-tuple-element.182), channel_id=1, source_target_pairs={{0,24},{1,25},{2,26},{3,27},{4,28},{5,29},{6,30},{7,31},{8,16},{9,... | collective-permute-start | bytes 393224 | tf_op jit(solution)/shard_map/ppermute | solution.py:32
  227.2 9.0 %collective-permute-start.70 = (f32[128,256]{1,0:T(8,128)S(1)}, f32[128,256]{1,0:T(8,128)S(1)}, u32[]{:S(2)}, u32[]{:S(2)}) collective-permute-start(f32[128,256]{1,0:T(8,128)S(1)} %add_add_fusion.1.y0.refs_1_), channel_id=1, source_target_pairs={{0,24},{1,25},{2,26},{3,27},{4,28},{5,29},{6,30},{7,31},{8,16},{9,... | collective-permute-start | bytes 393224 | tf_op jit(solution)/shard_map/ppermute | solution.py:32
  227.8 8.5 %collective-permute-start.69 = (f32[128,256]{1,0:T(8,128)S(1)}, f32[128,256]{1,0:T(8,128)S(1)}, u32[]{:S(2)}, u32[]{:S(2)}) collective-permute-start(f32[128,256]{1,0:T(8,128)S(1)} %add_add_fusion.1.y0.refs_1_), channel_id=1, source_target_pairs={{0,16},{1,17},{2,18},{3,19},{4,20},{5,21},{6,22},{7,23},{8,24},{9,... | collective-permute-start | bytes 393224 | tf_op jit(solution)/shard_map/ppermute | solution.py:32
  228.3 8.6 %collective-permute-start.68 = (f32[128,256]{1,0:T(8,128)S(1)}, f32[128,256]{1,0:T(8,128)S(1)}, u32[]{:S(2)}, u32[]{:S(2)}) collective-permute-start(f32[128,256]{1,0:T(8,128)S(1)} %add_add_fusion.1.y0.refs_1_), channel_id=1, source_target_pairs={{0,8},{1,9},{2,10},{3,11},{4,12},{5,13},{6,14},{7,15},{8,0},{9,1},... | collective-permute-start | bytes 393224 | tf_op jit(solution)/shard_map/ppermute | solution.py:32
  238.3 7.9 %collective-permute-start.72 = (f32[128,256]{1,0:T(8,128)S(1)}, f32[128,256]{1,0:T(8,128)S(1)}, u32[]{:S(2)}, u32[]{:S(2)}) collective-permute-start(f32[128,256]{1,0:T(8,128)S(1)} %get-tuple-element.185), channel_id=1, source_target_pairs={{0,64},{1,65},{2,66},{3,67},{4,68},{5,69},{6,70},{7,71},{8,72},{9,... | collective-permute-start | bytes 393224 | tf_op jit(solution)/shard_map/ppermute | solution.py:32
  241.1 6.8 %collective-permute-start.73 = (f32[128,256]{1,0:T(8,128)S(1)}, f32[128,256]{1,0:T(8,128)S(1)}, u32[]{:S(2)}, u32[]{:S(2)}) collective-permute-start(f32[128,256]{1,0:T(8,128)S(1)} %get-tuple-element.186), channel_id=1, source_target_pairs={{0,65},{1,64},{2,67},{3,66},{4,69},{5,68},{6,71},{7,70},{8,73},{9,... | collective-permute-start | bytes 393224 | tf_op jit(solution)/shard_map/ppermute | solution.py:32
  248.6 9.3 %collective-permute-start.74 = (f32[2,2,64,256]{3,2,1,0:T(8,128)S(1)}, f32[2,2,64,256]{3,2,1,0:T(8,128)S(1)}, u32[]{:S(2)}, u32[]{:S(2)}) collective-permute-start(f32[2,2,64,256]{3,2,1,0:T(8,128)S(1)} %get-tuple-element.190), channel_id=1, source_target_pairs={{0,1},{1,0},{2,3},{3,2},{4,5},{5,4},{6,7},{7,6},{8,9},{9,8},{10,11... | collective-permute-start | bytes 786440 | tf_op jit(solution)/shard_map/ppermute | solution.py:32
  248.7 14.1 %collective-permute-start.75 = (f32[2,2,64,256]{3,2,1,0:T(8,128)S(1)}, f32[2,2,64,256]{3,2,1,0:T(8,128)S(1)}, u32[]{:S(2)}, u32[]{:S(2)}) collective-permute-start(f32[2,2,64,256]{3,2,1,0:T(8,128)S(1)} %get-tuple-element.191), channel_id=1, source_target_pairs={{0,64},{1,65},{2,66},{3,67},{4,68},{5,69},{6,70},{7,71},{8,72},{9,... | collective-permute-start | bytes 786440 | tf_op jit(solution)/shard_map/ppermute | solution.py:32
  252.1 13.3 %collective-permute-start.76 = (f32[2,2,64,256]{3,2,1,0:T(8,128)S(1)}, f32[2,2,64,256]{3,2,1,0:T(8,128)S(1)}, u32[]{:S(2)}, u32[]{:S(2)}) collective-permute-start(f32[2,2,64,256]{3,2,1,0:T(8,128)S(1)} %get-tuple-element.192), channel_id=1, source_target_pairs={{0,65},{1,64},{2,67},{3,66},{4,69},{5,68},{6,71},{7,70},{8,73},{9,... | collective-permute-start | bytes 786440 | tf_op jit(solution)/shard_map/ppermute | solution.py:32
  266.5 7.6 %collective-permute-start.78 = (f32[2,64,256]{2,1,0:T(8,128)S(1)}, f32[2,64,256]{2,1,0:T(8,128)S(1)}, u32[]{:S(2)}, u32[]{:S(2)}) collective-permute-start(f32[2,64,256]{2,1,0:T(8,128)S(1)} %get-tuple-element.195), channel_id=1, source_target_pairs={{0,4},{1,5},{2,6},{3,7},{4,0},{5,1},{6,2},{7,3},{8,12},{9,13},{10,... | collective-permute-start | bytes 393224 | tf_op jit(solution)/shard_map/ppermute | solution.py:32
  (19 other events, 77.3 us)

commit v7 on v6

--- a/solution.py
+++ b/solution.py
@@ -316,28 +316,40 @@
                 outs[2 * n + 1][rows, :] = e[0]
 
 
-def leave_kernel(at, *refs):
-    kept, outs = refs[:8], refs[8:]
+def early_kernel(at, x1, y1, x2, y2, x3, y3, *outs):
     for r, out in enumerate(outs):
         for s in range(4):
 
             @pl.when((at[X] ^ r) == s)
             def _():
-                for n in range(2):
-                    for k in range(2):
-                        ref = kept[2 * (2 * (s // 2) + n) + k]
-                        out[n, k] = ref[pl.ds(64 * (s % 2), 64), :]
-
-
-def meet_kernel(at, a0, a1, a2, a3, *outs):
+                rows = pl.ds(64 * (s % 2), 64)
+                steps = ((x2, y2), (x3, y3)) if s // 2 else ((x1, y1), (x1, y1))
+                for n, step in enumerate(steps):
+                    for k, ref in enumerate(step):
+                        out[n, k] = ref[rows, :]
+
+
+def late_kernel(at, x0, y0, *outs):
+    for r, out in enumerate(outs):
+        rows = rows_of(64 * lax.rem(at[X] ^ r, 2), 64)
+        out[0] = x0[rows, :]
+        out[1] = y0[rows, :]
+
+
+def meet_kernel(at, e0, e1, e2, e3, l0, l1, l2, l3, *outs):
     rest = outs[4]
-    for k, a in enumerate((a0, a1, a2, a3)):
-        rest[at[X] ^ k] = a[1]
+    for k, (early, late) in enumerate(((e0, l0), (e1, l1), (e2, l2), (e3, l3))):
+        rest[at[X] ^ k] = early[1]
         for r in range(4):
-
-            @pl.when((at[X] ^ at[Y] ^ k) == r)
+            here = (at[X] ^ at[Y] ^ k) == r
+
+            @pl.when(here & (at[X] // 2 == 0))
             def _():
-                outs[r][...] = a[0]
+                outs[r][...] = late[...]
+
+            @pl.when(here & (at[X] // 2 == 1))
+            def _():
+                outs[r][...] = early[0]
 
 
 def turn_kernel(at, h0, h1, h2, h3, rest, keep, give):
@@ -450,6 +462,10 @@
     for t in (3, 2, 1, 0):
         odd = t % 2 == 1
         first, second = ("y", "x") if odd else ("x", "y")
+        if t == 0:
+            early = [a[s] for s in (1, 2, 3) for a in (blocks, crosses)]
+            early = local(early_kernel, at, early, [(2, 2, 64, 256)] * 4)
+            early = exchanged(early, along["x"])
         if t < 3:
             mine = gathered(blocks[t + 1], second)
             if t == 2:
@@ -470,6 +486,8 @@
             cross, _ = scattered(parts, "z")
             crosses[t] = cross
         whole = gathered(cross, "z")
+        if t == 0:
+            whole = list(after(whole, tuple(early)))
         if t == 2:
             on_y = list(after(on_y, tuple(whole)))
             on_y_sib = send(jnp.stack(on_y), to_other_core)
@@ -488,9 +506,13 @@
             b_sib = send(give, to_other_core)
         blocks[t] = scattered(parts, first)[0] + locals_[t]
 
-    outs = [a[t] for t in range(4) for a in (blocks, crosses)]
-    outs = exchanged(local(leave_kernel, at, outs, [(2, 2, 64, 256)] * 4), along["x"])
-    *turned, rest = local(meet_kernel, at, outs, [(2, 64, 256)] * 4 + [(4, 2, 64, 256)])
+    late = local(late_kernel, at, [blocks[0], crosses[0]], [(2, 64, 256)] * 4)
+    late = [late[0]] + [
+        send(late[r], along["x"](r), lambda x, **_: (x ^ r) // 2 == 0) for r in (1, 2, 3)
+    ]
+    *turned, rest = local(
+        meet_kernel, at, early + late, [(2, 64, 256)] * 4 + [(4, 2, 64, 256)]
+    )
     turned = exchanged(turned, along["y"])
     keep, give = local(turn_kernel, at, turned + [rest], [(4, 2, 64, 256)] * 2)
     got = send(give, to_other_core)

time: 282 us -> 280 us (level)
  waiting for transfers between devices: 152 us -> 139 us
  starting transfers between devices: 105 us -> 113 us
    ppermute x81 -> x84, waiting for transfers between devices: 152 us -> 139 us  [send(): return lax.ppermute(x, AXES, route(place, only))]
    ppermute x81 -> x84, starting transfers between devices: 105 us -> 113 us  [send(): return lax.ppermute(x, AXES, route(place, only))]
    pallas_call x18 -> x19, Pallas kernels: 18.2 us -> 19.1 us  [local(): pl.pallas_call(kernel, out_shape=[jax.ShapeDtypeStruct(s, jnp.float32) fo...]
  transfers between devices with their start and end apart: 81 -> 84, of which waited for: 60 -> 60; matrix products, arithmetic and copies ran while one was open for 0% -> 0% of each run, Pallas kernels for 2% -> 2%
where the time goes in v7:
time: 280 us; the launch traced here: 276 us
  waiting for transfers between devices  139 us (50%)
  starting transfers between devices  113 us (40%)
  Pallas kernels  19.1 us (7%)
    ppermute x84, waiting for transfers between devices, send(): return lax.ppermute(x, AXES, route(place, only))  139 us
    ppermute x84, starting transfers between devices, send(): return lax.ppermute(x, AXES, route(place, only))  113 us
    pallas_call x19, Pallas kernels, local(): pl.pallas_call(kernel, out_shape=[jax.ShapeDtypeStruct(s, jnp.float32) fo...  19.1 us
  transfers between devices with their start and end apart: 84, of which 60 were waited for; matrix products, arithmetic and copies ran while one was open for 0% of the time, Pallas kernels for 2%

profile of v7, /device:TPU:6, one launch (start us, length us, event | category | flops | bytes accessed | tf_op | source)
XLA Modules:
  0.0 275.5 jit_solution(12572953518711387861)
XLA Ops:
  2.3 1.7 collective-permute-start
  4.1 3.0 %collective-permute-start.1 = (f32[2,64,512]{2,1,0:T(8,128)S(1)}, f32[2,64,512]{2,1,0:T(8,128)S(1)}, u32[]{:S(2)}, u32[]{:S(2)}) collective-permute-start(f32[2,64,512]{2,1,0:T(8,128)S(1)} %pad_maximum_fusion.6), channel_id=1, source_target_pairs={{0,4},{1,5},{2,6},{3,7},{4,0},{5,1},{6,2},{7,3},{8,12},{9,13},{10,... | collective-permute-start | bytes 786440 | tf_op jit(solution)/shard_map/ppermute | solution.py:32
  8.8 5.4 %collective-permute-done.1.d2 = f32[2,64,512]{2,1,0:T(8,128)S(1)} collective-permute-done((f32[2,64,512]{2,1,0:T(8,128)S(1)}, f32[2,64,512]{2,1,0:T(8,128)S(1)}, u32[]{:S(2)}, u32[]{:S(2)}) %collective-permute-start.1) | collective-permute-done | bytes 262176 | tf_op jit(solution)/shard_map/ppermute | solution.py:32
  14.2 2.7 collective-permute-done.2.d3
  17.7 3.0 %collective-permute-done.3.got = f32[4,5,64,256]{3,2,1,0:T(8,128)S(1)} collective-permute-done((f32[4,5,64,256]{3,2,1,0:T(8,128)S(1)}, f32[4,5,64,256]{3,2,1,0:T(8,128)S(1)}, u32[]{:S(2)}, u32[]{:S(2)}) %collective-permute-start.3) | collective-permute-done | bytes 1310752 | tf_op jit(solution)/shard_map/ppermute | solution.py:32
  23.5 2.1 collective-permute-start.5
  25.6 12.7 %collective-permute-done.5.a2 = f32[4,64,256]{2,1,0:T(8,128)S(1)} collective-permute-done((f32[4,64,256]{2,1,0:T(8,128)S(1)}, f32[4,64,256]{2,1,0:T(8,128)S(1)}, u32[]{:S(2)}, u32[]{:S(2)}) %collective-permute-start.5) | collective-permute-done | bytes 262176 | tf_op jit(solution)/shard_map/ppermute | solution.py:32
  38.3 1.7 collective-permute-done.6.a3
  44.2 2.3 collective-permute-start.14
  47.3 2.4 collective-permute-done.11.rest_1_.a1
  49.7 6.4 %collective-permute-done.9.b3.m3 = f32[256,256]{1,0:T(8,128)S(1)} collective-permute-done((f32[256,256]{1,0:T(8,128)S(1)}, f32[256,256]{1,0:T(8,128)S(1)}, u32[]{:S(2)}, u32[]{:S(2)}) %collective-permute-start.9) | collective-permute-done | bytes 262176 | tf_op jit(solution)/shard_map/ppermute | solution.py:32
  59.9 3.6 %collective-permute-start.16 = (f32[192,256]{1,0:T(8,128)S(1)}, f32[192,256]{1,0:T(8,128)S(1)}, u32[]{:S(2)}, u32[]{:S(2)}) collective-permute-start(f32[192,256]{1,0:T(8,128)S(1)} %get-tuple-element.131), channel_id=1, source_target_pairs={{0,16},{1,17},{2,18},{3,19},{4,20},{5,21},{6,22},{7,23},{8,24},{9,... | collective-permute-start | bytes 589832 | tf_op jit(solution)/shard_map/ppermute | solution.py:32
  63.9 2.9 %collective-permute-done.15.e1 = f32[192,256]{1,0:T(8,128)S(1)} collective-permute-done((f32[192,256]{1,0:T(8,128)S(1)}, f32[192,256]{1,0:T(8,128)S(1)}, u32[]{:S(2)}, u32[]{:S(2)}) %collective-permute-start.15) | collective-permute-done | bytes 196640 | tf_op jit(solution)/shard_map/ppermute | solution.py:32
  66.8 6.0 %collective-permute-done.16.e2 = f32[192,256]{1,0:T(8,128)S(1)} collective-permute-done((f32[192,256]{1,0:T(8,128)S(1)}, f32[192,256]{1,0:T(8,128)S(1)}, u32[]{:S(2)}, u32[]{:S(2)}) %collective-permute-start.16) | collective-permute-done | bytes 196640 | tf_op jit(solution)/shard_map/ppermute | solution.py:32
  72.7 2.6 collective-permute-done.17.e3
  76.1 3.4 %collective-permute-start.18 = (f32[128,256]{1,0:T(8,128)S(1)}, f32[128,256]{1,0:T(8,128)S(1)}, u32[]{:S(2)}, u32[]{:S(2)}) collective-permute-start(f32[128,256]{1,0:T(8,128)S(1)} %fusion.y0.y3), channel_id=1, source_target_pairs={{0,8},{1,9},{2,10},{3,11},{4,12},{5,13},{6,14},{7,15},{8,0},{9,1},... | collective-permute-start | bytes 393224 | tf_op jit(solution)/shard_map/ppermute | solution.py:32
  86.5 1.7 collective-permute-start.21
  88.2 3.1 %collective-permute-start.23 = (f32[128,256]{1,0:T(8,128)S(1)}, f32[128,256]{1,0:T(8,128)S(1)}, u32[]{:S(2)}, u32[]{:S(2)}) collective-permute-start(f32[128,256]{1,0:T(8,128)S(1)} %get-tuple-element.136), channel_id=1, source_target_pairs={{0,6},{1,7},{2,4},{3,5},{4,2},{5,3},{6,0},{7,1},{8,14},{9,15},{10,... | collective-permute-start | bytes 393224 | tf_op jit(solution)/shard_map/ppermute | solution.py:32
  92.6 2.2 collective-permute-done.22
  96.1 2.5 collective-permute-start.32
  98.6 1.9 collective-permute-start.29
  104.3 4.8 %collective-permute-done.31 = f32[128,256]{1,0:T(8,128)S(1)} collective-permute-done((f32[128,256]{1,0:T(8,128)S(1)}, f32[128,256]{1,0:T(8,128)S(1)}, u32[]{:S(2)}, u32[]{:S(2)}) %collective-permute-start.31) | collective-permute-done | bytes 131104 | tf_op jit(solution)/shard_map/ppermute | solution.py:32
  109.2 3.2 %collective-permute-done.29.a3.b3 = f32[256,256]{1,0:T(8,128)S(1)} collective-permute-done((f32[256,256]{1,0:T(8,128)S(1)}, f32[256,256]{1,0:T(8,128)S(1)}, u32[]{:S(2)}, u32[]{:S(2)}) %collective-permute-start.29) | collective-permute-done | bytes 262176 | tf_op jit(solution)/shard_map/ppermute | solution.py:32
  113.2 2.3 collective-permute-done.36.x_sib
  116.8 4.6 %collective-permute-start.39 = (f32[128,256]{1,0:T(8,128)S(1)}, f32[128,256]{1,0:T(8,128)S(1)}, u32[]{:S(2)}, u32[]{:S(2)}) collective-permute-start(f32[128,256]{1,0:T(8,128)S(1)} %get-tuple-element.162), channel_id=1, source_target_pairs={{0,24},{1,25},{2,26},{3,27},{4,28},{5,29},{6,30},{7,31},{8,16},{9,... | collective-permute-start | bytes 393224 | tf_op jit(solution)/shard_map/ppermute | solution.py:32
  123.1 3.1 %collective-permute-start.33 = (f32[256,256]{1,0:T(8,128)S(1)}, f32[256,256]{1,0:T(8,128)S(1)}, u32[]{:S(2)}, u32[]{:S(2)}) collective-permute-start(f32[256,256]{1,0:T(8,128)S(1)} %shard_map.65.b0), channel_id=1, source_target_pairs={{0,2},{1,3},{2,0},{3,1},{4,6},{5,7},{6,4},{7,5},{8,10},{9,11},{10,... | collective-permute-start | bytes 786440 | tf_op jit(solution)/shard_map/ppermute | solution.py:32
  126.7 3.5 %collective-permute-start.42 = (f32[128,256]{1,0:T(8,128)S(1)}, f32[128,256]{1,0:T(8,128)S(1)}, u32[]{:S(2)}, u32[]{:S(2)}) collective-permute-start(f32[128,256]{1,0:T(8,128)S(1)} %add_add_fusion.5.y0.y2), channel_id=1, source_target_pairs={{0,24},{1,25},{2,26},{3,27},{4,28},{5,29},{6,30},{7,31},{8,16},{9,... | collective-permute-start | bytes 393224 | tf_op jit(solution)/shard_map/ppermute | solution.py:32
  130.2 6.2 %collective-permute-done.35.b3 = f32[256,256]{1,0:T(8,128)S(1)} collective-permute-done((f32[256,256]{1,0:T(8,128)S(1)}, f32[256,256]{1,0:T(8,128)S(1)}, u32[]{:S(2)}, u32[]{:S(2)}) %collective-permute-start.35) | collective-permute-done | bytes 262176 | tf_op jit(solution)/shard_map/ppermute | solution.py:32
  137.0 4.3 %collective-permute-done.40.y1 = f32[128,256]{1,0:T(8,128)S(1)} collective-permute-done((f32[128,256]{1,0:T(8,128)S(1)}, f32[128,256]{1,0:T(8,128)S(1)}, u32[]{:S(2)}, u32[]{:S(2)}) %collective-permute-start.40) | collective-permute-done | bytes 131104 | tf_op jit(solution)/shard_map/ppermute | solution.py:32
  141.6 2.6 collective-permute-done.43.b_sib
  146.4 2.7 collective-permute-start.46
  150.4 1.6 collective-permute-done.45
  152.0 3.5 %collective-permute-done.46 = f32[128,256]{1,0:T(8,128)S(1)} collective-permute-done((f32[128,256]{1,0:T(8,128)S(1)}, f32[128,256]{1,0:T(8,128)S(1)}, u32[]{:S(2)}, u32[]{:S(2)}) %collective-permute-start.46) | collective-permute-done | bytes 131104 | tf_op jit(solution)/shard_map/ppermute | solution.py:32
  155.5 2.2 collective-permute-done.47
  159.3 2.6 collective-permute-start.48
  161.9 4.6 %collective-permute-done.50 = f32[128,256]{1,0:T(8,128)S(1)} collective-permute-done((f32[128,256]{1,0:T(8,128)S(1)}, f32[128,256]{1,0:T(8,128)S(1)}, u32[]{:S(2)}, u32[]{:S(2)}) %collective-permute-start.50) | collective-permute-done | bytes 131104 | tf_op jit(solution)/shard_map/ppermute | solution.py:32
  172.5 2.9 %collective-permute-start.54 = (f32[128,256]{1,0:T(8,128)S(1)}, f32[128,256]{1,0:T(8,128)S(1)}, u32[]{:S(2)}, u32[]{:S(2)}) collective-permute-start(f32[128,256]{1,0:T(8,128)S(1)} %get-tuple-element.180), channel_id=1, source_target_pairs={{0,24},{1,25},{2,26},{3,27},{4,28},{5,29},{6,30},{7,31},{8,16},{9,... | collective-permute-start | bytes 393224 | tf_op jit(solution)/shard_map/ppermute | solution.py:32
  175.4 1.6 collective-permute-done.52
  177.0 1.8 collective-permute-done.53
  178.9 2.2 collective-permute-done.54
  181.2 3.0 %collective-permute-start.57 = (f32[128,256]{1,0:T(8,128)S(1)}, f32[128,256]{1,0:T(8,128)S(1)}, u32[]{:S(2)}, u32[]{:S(2)}) collective-permute-start(f32[128,256]{1,0:T(8,128)S(1)} %add_add_fusion.3.y0.y1), channel_id=1, source_target_pairs={{0,24},{1,25},{2,26},{3,27},{4,28},{5,29},{6,30},{7,31},{8,16},{9,... | collective-permute-start | bytes 393224 | tf_op jit(solution)/shard_map/ppermute | solution.py:32
  185.3 4.1 %collective-permute-done.57.y3 = f32[128,256]{1,0:T(8,128)S(1)} collective-permute-done((f32[128,256]{1,0:T(8,128)S(1)}, f32[128,256]{1,0:T(8,128)S(1)}, u32[]{:S(2)}, u32[]{:S(2)}) %collective-permute-start.57) | collective-permute-done | bytes 131104 | tf_op jit(solution)/shard_map/ppermute | solution.py:32
  189.4 2.3 collective-permute-done.56.y2
  193.1 1.8 collective-permute-start.59
  194.9 2.9 %collective-permute-start.60 = (f32[128,256]{1,0:T(8,128)S(1)}, f32[128,256]{1,0:T(8,128)S(1)}, u32[]{:S(2)}, u32[]{:S(2)}) collective-permute-start(f32[128,256]{1,0:T(8,128)S(1)} %get-tuple-element.184), channel_id=1, source_target_pairs={{0,6},{1,7},{2,4},{3,5},{4,2},{5,3},{6,0},{7,1},{8,14},{9,15},{10,... | collective-permute-start | bytes 393224 | tf_op jit(solution)/shard_map/ppermute | solution.py:32
  201.2 3.3 %collective-permute-start.66 = (f32[128,256]{1,0:T(8,128)S(1)}, f32[128,256]{1,0:T(8,128)S(1)}, u32[]{:S(2)}, u32[]{:S(2)}) collective-permute-start(f32[128,256]{1,0:T(8,128)S(1)} %add_add_fusion.2.x1), channel_id=1, source_target_pairs={{0,6},{1,7},{2,4},{3,5},{4,2},{5,3},{6,0},{7,1},{8,14},{9,15},{10,... | collective-permute-start | bytes 393224 | tf_op jit(solution)/shard_map/ppermute | solution.py:32
  205.7 2.8 collective-permute-done.66
  208.4 2.5 collective-permute-done.65
  211.1 1.9 collective-permute-done.67.x_sib
  214.3 4.2 %collective-permute-start.69 = (f32[128,256]{1,0:T(8,128)S(1)}, f32[128,256]{1,0:T(8,128)S(1)}, u32[]{:S(2)}, u32[]{:S(2)}) collective-permute-start(f32[128,256]{1,0:T(8,128)S(1)} %get-tuple-element.193), channel_id=1, source_target_pairs={{0,16},{1,17},{2,18},{3,19},{4,20},{5,21},{6,22},{7,23},{8,24},{9,... | collective-permute-start | bytes 393224 | tf_op jit(solution)/shard_map/ppermute | solution.py:32
  219.8 2.8 collective-permute-start.62
  222.6 1.9 collective-permute-start.63
  225.0 2.2 collective-permute-done.70
  229.1 2.4 collective-permute-start.71
  231.4 2.4 collective-permute-done.62.e2
  233.8 2.6 collective-permute-done.63.e3
  238.3 2.9 %collective-permute-start.75 = (f32[128,256]{1,0:T(8,128)S(1)}, f32[128,256]{1,0:T(8,128)S(1)}, u32[]{:S(2)}, u32[]{:S(2)}) collective-permute-start(f32[128,256]{1,0:T(8,128)S(1)} %get-tuple-element.201), channel_id=1, source_target_pairs={{0,64},{1,65},{2,66},{3,67},{4,68},{5,69},{6,70},{7,71},{8,72},{9,... | collective-permute-start | bytes 393224 | tf_op jit(solution)/shard_map/ppermute | solution.py:32
  241.3 1.8 collective-permute-start.76
  244.0 2.3 collective-permute-done.75
  249.1 6.6 %collective-permute-start.78 = (f32[2,64,256]{2,1,0:T(8,128)S(1)}, f32[2,64,256]{2,1,0:T(8,128)S(1)}, u32[]{:S(2)}, u32[]{:S(2)}) collective-permute-start(f32[2,64,256]{2,1,0:T(8,128)S(1)} %get-tuple-element.207), channel_id=1, source_target_pairs={{64,0},{65,1},{66,2},{67,3},{68,4},{69,5},{70,6},{71,7},{72,8},{73... | collective-permute-start | bytes 393224 | tf_op jit(solution)/shard_map/ppermute | solution.py:32
  261.2 3.1 %collective-permute-start.81 = (f32[2,64,256]{2,1,0:T(8,128)S(1)}, f32[2,64,256]{2,1,0:T(8,128)S(1)}, u32[]{:S(2)}, u32[]{:S(2)}) collective-permute-start(f32[2,64,256]{2,1,0:T(8,128)S(1)} %get-tuple-element.211), channel_id=1, source_target_pairs={{0,4},{1,5},{2,6},{3,7},{4,0},{5,1},{6,2},{7,3},{8,12},{9,13},{10,... | collective-permute-start | bytes 393224 | tf_op jit(solution)/shard_map/ppermute | solution.py:32
  266.7 2.9 %collective-permute-done.81.h2 = f32[2,64,256]{2,1,0:T(8,128)S(1)} collective-permute-done((f32[2,64,256]{2,1,0:T(8,128)S(1)}, f32[2,64,256]{2,1,0:T(8,128)S(1)}, u32[]{:S(2)}, u32[]{:S(2)}) %collective-permute-start.81) | collective-permute-done | bytes 131104 | tf_op jit(solution)/shard_map/ppermute | solution.py:32
  272.0 1.9 collective-permute-done.83.got
  273.9 1.7 shard_map.77
  (165 shorter events, 74.2 us)
Async XLA Ops:
  4.1 10.1 %collective-permute-start.1 = (f32[2,64,512]{2,1,0:T(8,128)S(1)}, f32[2,64,512]{2,1,0:T(8,128)S(1)}, u32[]{:S(2)}, u32[]{:S(2)}) collective-permute-start(f32[2,64,512]{2,1,0:T(8,128)S(1)} %pad_maximum_fusion.6), channel_id=1, source_target_pairs={{0,4},{1,5},{2,6},{3,7},{4,0},{5,1},{6,2},{7,3},{8,12},{9,13},{10,... | collective-permute-start | bytes 786440 | tf_op jit(solution)/shard_map/ppermute | solution.py:32
  7.1 9.7 %collective-permute-start.2 = (f32[2,64,512]{2,1,0:T(8,128)S(1)}, f32[2,64,512]{2,1,0:T(8,128)S(1)}, u32[]{:S(2)}, u32[]{:S(2)}) collective-permute-start(f32[2,64,512]{2,1,0:T(8,128)S(1)} %pad_maximum_fusion.7), channel_id=1, source_target_pairs={{0,6},{1,7},{2,4},{3,5},{4,2},{5,3},{6,0},{7,1},{8,14},{9,15},{10,... | collective-permute-start | bytes 786440 | tf_op jit(solution)/shard_map/ppermute | solution.py:32
  21.4 16.9 %collective-permute-start.4 = (f32[6,64,256]{2,1,0:T(8,128)S(1)}, f32[6,64,256]{2,1,0:T(8,128)S(1)}, u32[]{:S(2)}, u32[]{:S(2)}) collective-permute-start(f32[6,64,256]{2,1,0:T(8,128)S(1)} %get-tuple-element.113), channel_id=1, source_target_pairs={{0,1},{1,0},{2,3},{3,2},{4,5},{5,4},{6,7},{7,6},{8,9},{9,8},{10,11... | collective-permute-start | bytes 1179656 | tf_op jit(solution)/shard_map/ppermute | solution.py:32
  22.4 17.7 %collective-permute-start.6 = (f32[6,64,256]{2,1,0:T(8,128)S(1)}, f32[6,64,256]{2,1,0:T(8,128)S(1)}, u32[]{:S(2)}, u32[]{:S(2)}) collective-permute-start(f32[6,64,256]{2,1,0:T(8,128)S(1)} %get-tuple-element.115), channel_id=1, source_target_pairs={{0,65},{1,64},{2,67},{3,66},{4,69},{5,68},{6,71},{7,70},{8,73},{9,... | collective-permute-start | bytes 1179656 | tf_op jit(solution)/shard_map/ppermute | solution.py:32
  23.5 14.8 %collective-permute-start.5 = (f32[4,64,256]{2,1,0:T(8,128)S(1)}, f32[4,64,256]{2,1,0:T(8,128)S(1)}, u32[]{:S(2)}, u32[]{:S(2)}) collective-permute-start(f32[4,64,256]{2,1,0:T(8,128)S(1)} %get-tuple-element.114), channel_id=1, source_target_pairs={{0,64},{1,65},{2,66},{3,67},{4,68},{5,69},{6,70},{7,71},{8,72},{9,... | collective-permute-start | bytes 786440 | tf_op jit(solution)/shard_map/ppermute | solution.py:32
  40.9 8.8 %collective-permute-start.11 = (f32[256,256]{1,0:T(8,128)S(1)}, f32[256,256]{1,0:T(8,128)S(1)}, u32[]{:S(2)}, u32[]{:S(2)}) collective-permute-start(f32[256,256]{1,0:T(8,128)S(1)} %get-tuple-element.122.rest_0_.a0), channel_id=1, source_target_pairs={{0,2},{1,3},{2,0},{3,1},{4,6},{5,7},{6,4},{7,5},{8,10},{9,11},{10,... | collective-permute-start | bytes 786440 | tf_op jit(solution)/shard_map/ppermute | solution.py:32
  42.1 14.0 %collective-permute-start.9 = (f32[256,256]{1,0:T(8,128)S(1)}, f32[256,256]{1,0:T(8,128)S(1)}, u32[]{:S(2)}, u32[]{:S(2)}) collective-permute-start(f32[256,256]{1,0:T(8,128)S(1)} %get-tuple-element.117.b0.m0), channel_id=1, source_target_pairs={{0,65},{1,64},{2,67},{3,66},{4,69},{5,68},{6,71},{7,70},{8,73},{9,... | collective-permute-start | bytes 786440 | tf_op jit(solution)/shard_map/ppermute | solution.py:32
  43.3 12.9 %collective-permute-start.8 = (f32[256,256]{1,0:T(8,128)S(1)}, f32[256,256]{1,0:T(8,128)S(1)}, u32[]{:S(2)}, u32[]{:S(2)}) collective-permute-start(f32[256,256]{1,0:T(8,128)S(1)} %get-tuple-element.117.b0.m0), channel_id=1, source_target_pairs={{0,64},{1,65},{2,66},{3,67},{4,68},{5,69},{6,70},{7,71},{8,72},{9,... | collective-permute-start | bytes 786440 | tf_op jit(solution)/shard_map/ppermute | solution.py:32
  44.2 13.1 %collective-permute-start.14 = (f32[256,256]{1,0:T(8,128)S(1)}, f32[256,256]{1,0:T(8,128)S(1)}, u32[]{:S(2)}, u32[]{:S(2)}) collective-permute-start(f32[256,256]{1,0:T(8,128)S(1)} %get-tuple-element.122.rest_0_.a0), channel_id=1, source_target_pairs={{0,6},{1,7},{2,4},{3,5},{4,2},{5,3},{6,0},{7,1},{8,14},{9,15},{10,... | collective-permute-start | bytes 786440 | tf_op jit(solution)/shard_map/ppermute | solution.py:32
  46.5 10.8 %collective-permute-start.13 = (f32[256,256]{1,0:T(8,128)S(1)}, f32[256,256]{1,0:T(8,128)S(1)}, u32[]{:S(2)}, u32[]{:S(2)}) collective-permute-start(f32[256,256]{1,0:T(8,128)S(1)} %get-tuple-element.122.rest_0_.a0), channel_id=1, source_target_pairs={{0,4},{1,5},{2,6},{3,7},{4,0},{5,1},{6,2},{7,3},{8,12},{9,13},{10,... | collective-permute-start | bytes 786440 | tf_op jit(solution)/shard_map/ppermute | solution.py:32
  49.7 7.6 %collective-permute-start.7 = (f32[256,256]{1,0:T(8,128)S(1)}, f32[256,256]{1,0:T(8,128)S(1)}, u32[]{:S(2)}, u32[]{:S(2)}) collective-permute-start(f32[256,256]{1,0:T(8,128)S(1)} %get-tuple-element.117.b0.m0), channel_id=1, source_target_pairs={{0,1},{1,0},{2,3},{3,2},{4,5},{5,4},{6,7},{7,6},{8,9},{9,8},{10,11... | collective-permute-start | bytes 786440 | tf_op jit(solution)/shard_map/ppermute | solution.py:32
  59.0 7.8 %collective-permute-start.15 = (f32[192,256]{1,0:T(8,128)S(1)}, f32[192,256]{1,0:T(8,128)S(1)}, u32[]{:S(2)}, u32[]{:S(2)}) collective-permute-start(f32[192,256]{1,0:T(8,128)S(1)} %get-tuple-element.130), channel_id=1, source_target_pairs={{0,8},{1,9},{2,10},{3,11},{4,12},{5,13},{6,14},{7,15},{8,0},{9,1},... | collective-permute-start | bytes 589832 | tf_op jit(solution)/shard_map/ppermute | solution.py:32
  59.9 12.8 %collective-permute-start.16 = (f32[192,256]{1,0:T(8,128)S(1)}, f32[192,256]{1,0:T(8,128)S(1)}, u32[]{:S(2)}, u32[]{:S(2)}) collective-permute-start(f32[192,256]{1,0:T(8,128)S(1)} %get-tuple-element.131), channel_id=1, source_target_pairs={{0,16},{1,17},{2,18},{3,19},{4,20},{5,21},{6,22},{7,23},{8,24},{9,... | collective-permute-start | bytes 589832 | tf_op jit(solution)/shard_map/ppermute | solution.py:32
  63.5 11.8 %collective-permute-start.17 = (f32[192,256]{1,0:T(8,128)S(1)}, f32[192,256]{1,0:T(8,128)S(1)}, u32[]{:S(2)}, u32[]{:S(2)}) collective-permute-start(f32[192,256]{1,0:T(8,128)S(1)} %get-tuple-element.132), channel_id=1, source_target_pairs={{0,24},{1,25},{2,26},{3,27},{4,28},{5,29},{6,30},{7,31},{8,16},{9,... | collective-permute-start | bytes 589832 | tf_op jit(solution)/shard_map/ppermute | solution.py:32
  63.8 17.2 %collective-permute-start.10 = (f32[4,128,256]{2,1,0:T(8,128)S(1)}, f32[4,128,256]{2,1,0:T(8,128)S(1)}, u32[]{:S(2)}, u32[]{:S(2)}) collective-permute-start(f32[4,128,256]{2,1,0:T(8,128)S(1)} %pad_maximum_fusion.1), channel_id=1, source_target_pairs={{0,32},{1,33},{2,34},{3,35},{4,36},{5,37},{6,38},{7,39},{8,40},{9,... | collective-permute-start | bytes 1572872 | tf_op jit(solution)/shard_map/ppermute | solution.py:32
  75.4 8.5 %collective-permute-start.20 = (f32[128,256]{1,0:T(8,128)S(1)}, f32[128,256]{1,0:T(8,128)S(1)}, u32[]{:S(2)}, u32[]{:S(2)}) collective-permute-start(f32[128,256]{1,0:T(8,128)S(1)} %fusion.y0.y3), channel_id=1, source_target_pairs={{0,24},{1,25},{2,26},{3,27},{4,28},{5,29},{6,30},{7,31},{8,16},{9,... | collective-permute-start | bytes 393224 | tf_op jit(solution)/shard_map/ppermute | solution.py:32
  75.7 9.4 %collective-permute-start.19 = (f32[128,256]{1,0:T(8,128)S(1)}, f32[128,256]{1,0:T(8,128)S(1)}, u32[]{:S(2)}, u32[]{:S(2)}) collective-permute-start(f32[128,256]{1,0:T(8,128)S(1)} %fusion.y0.y3), channel_id=1, source_target_pairs={{0,16},{1,17},{2,18},{3,19},{4,20},{5,21},{6,22},{7,23},{8,24},{9,... | collective-permute-start | bytes 393224 | tf_op jit(solution)/shard_map/ppermute | solution.py:32
  76.1 9.1 %collective-permute-start.18 = (f32[128,256]{1,0:T(8,128)S(1)}, f32[128,256]{1,0:T(8,128)S(1)}, u32[]{:S(2)}, u32[]{:S(2)}) collective-permute-start(f32[128,256]{1,0:T(8,128)S(1)} %fusion.y0.y3), channel_id=1, source_target_pairs={{0,8},{1,9},{2,10},{3,11},{4,12},{5,13},{6,14},{7,15},{8,0},{9,1},... | collective-permute-start | bytes 393224 | tf_op jit(solution)/shard_map/ppermute | solution.py:32
  79.5 8.7 %collective-permute-start.24 = (f32[2,64,256]{2,1,0:T(8,128)S(1)}, f32[2,64,256]{2,1,0:T(8,128)S(1)}, u32[]{:S(2)}, u32[]{:S(2)}) collective-permute-start(f32[2,64,256]{2,1,0:T(8,128)S(1)} %get-tuple-element.143), channel_id=1, source_target_pairs={{0,1},{1,0},{2,3},{3,2},{4,5},{5,4},{6,7},{7,6},{8,9},{9,8},{10,11... | collective-permute-start | bytes 393224 | tf_op jit(solution)/shard_map/ppermute | solution.py:32
  81.0 10.3 %collective-permute-start.25 = (f32[2,64,256]{2,1,0:T(8,128)S(1)}, f32[2,64,256]{2,1,0:T(8,128)S(1)}, u32[]{:S(2)}, u32[]{:S(2)}) collective-permute-start(f32[2,64,256]{2,1,0:T(8,128)S(1)} %get-tuple-element.144), channel_id=1, source_target_pairs={{0,64},{1,65},{2,66},{3,67},{4,68},{5,69},{6,70},{7,71},{8,72},{9,... | collective-permute-start | bytes 393224 | tf_op jit(solution)/shard_map/ppermute | solution.py:32
  83.8 7.4 %collective-permute-start.26 = (f32[2,64,256]{2,1,0:T(8,128)S(1)}, f32[2,64,256]{2,1,0:T(8,128)S(1)}, u32[]{:S(2)}, u32[]{:S(2)}) collective-permute-start(f32[2,64,256]{2,1,0:T(8,128)S(1)} %get-tuple-element.145), channel_id=1, source_target_pairs={{0,65},{1,64},{2,67},{3,66},{4,69},{5,68},{6,71},{7,70},{8,73},{9,... | collective-permute-start | bytes 393224 | tf_op jit(solution)/shard_map/ppermute | solution.py:32
  88.2 6.5 %collective-permute-start.22 = (f32[128,256]{1,0:T(8,128)S(1)}, f32[128,256]{1,0:T(8,128)S(1)}, u32[]{:S(2)}, u32[]{:S(2)}) collective-permute-start(f32[128,256]{1,0:T(8,128)S(1)} %get-tuple-element.135), channel_id=1, source_target_pairs={{0,4},{1,5},{2,6},{3,7},{4,0},{5,1},{6,2},{7,3},{8,12},{9,13},{10,... | collective-permute-start | bytes 393224 | tf_op jit(solution)/shard_map/ppermute | solution.py:32
  88.2 7.8 %collective-permute-start.23 = (f32[128,256]{1,0:T(8,128)S(1)}, f32[128,256]{1,0:T(8,128)S(1)}, u32[]{:S(2)}, u32[]{:S(2)}) collective-permute-start(f32[128,256]{1,0:T(8,128)S(1)} %get-tuple-element.136), channel_id=1, source_target_pairs={{0,6},{1,7},{2,4},{3,5},{4,2},{5,3},{6,0},{7,1},{8,14},{9,15},{10,... | collective-permute-start | bytes 393224 | tf_op jit(solution)/shard_map/ppermute | solution.py:32
  96.1 6.7 %collective-permute-start.32 = (f32[128,256]{1,0:T(8,128)S(1)}, f32[128,256]{1,0:T(8,128)S(1)}, u32[]{:S(2)}, u32[]{:S(2)}) collective-permute-start(f32[128,256]{1,0:T(8,128)S(1)} %add_add_fusion.6.x3), channel_id=1, source_target_pairs={{0,6},{1,7},{2,4},{3,5},{4,2},{5,3},{6,0},{7,1},{8,14},{9,15},{10,... | collective-permute-start | bytes 393224 | tf_op jit(solution)/shard_map/ppermute | solution.py:32
  98.6 13.7 %collective-permute-start.29 = (f32[256,256]{1,0:T(8,128)S(1)}, f32[256,256]{1,0:T(8,128)S(1)}, u32[]{:S(2)}, u32[]{:S(2)}) collective-permute-start(f32[256,256]{1,0:T(8,128)S(1)} %get-tuple-element.169.a0.b0), channel_id=1, source_target_pairs={{0,65},{1,64},{2,67},{3,66},{4,69},{5,68},{6,71},{7,70},{8,73},{9,... | collective-permute-start | bytes 786440 | tf_op jit(solution)/shard_map/ppermute | solution.py:32
  100.5 11.8 %collective-permute-start.28 = (f32[256,256]{1,0:T(8,128)S(1)}, f32[256,256]{1,0:T(8,128)S(1)}, u32[]{:S(2)}, u32[]{:S(2)}) collective-permute-start(f32[256,256]{1,0:T(8,128)S(1)} %get-tuple-element.169.a0.b0), channel_id=1, source_target_pairs={{0,64},{1,65},{2,66},{3,67},{4,68},{5,69},{6,70},{7,71},{8,72},{9,... | collective-permute-start | bytes 786440 | tf_op jit(solution)/shard_map/ppermute | solution.py:32
  101.4 11.6 %collective-permute-start.27 = (f32[256,256]{1,0:T(8,128)S(1)}, f32[256,256]{1,0:T(8,128)S(1)}, u32[]{:S(2)}, u32[]{:S(2)}) collective-permute-start(f32[256,256]{1,0:T(8,128)S(1)} %get-tuple-element.169.a0.b0), channel_id=1, source_target_pairs={{0,1},{1,0},{2,3},{3,2},{4,5},{5,4},{6,7},{7,6},{8,9},{9,8},{10,11... | collective-permute-start | bytes 786440 | tf_op jit(solution)/shard_map/ppermute | solution.py:32
  102.7 6.5 %collective-permute-start.31 = (f32[128,256]{1,0:T(8,128)S(1)}, f32[128,256]{1,0:T(8,128)S(1)}, u32[]{:S(2)}, u32[]{:S(2)}) collective-permute-start(f32[128,256]{1,0:T(8,128)S(1)} %add_add_fusion.6.x3), channel_id=1, source_target_pairs={{0,4},{1,5},{2,6},{3,7},{4,0},{5,1},{6,2},{7,3},{8,12},{9,13},{10,... | collective-permute-start | bytes 393224 | tf_op jit(solution)/shard_map/ppermute | solution.py:32
  116.7 9.4 %collective-permute-start.38 = (f32[128,256]{1,0:T(8,128)S(1)}, f32[128,256]{1,0:T(8,128)S(1)}, u32[]{:S(2)}, u32[]{:S(2)}) collective-permute-start(f32[128,256]{1,0:T(8,128)S(1)} %get-tuple-element.161), channel_id=1, source_target_pairs={{0,16},{1,17},{2,18},{3,19},{4,20},{5,21},{6,22},{7,23},{8,24},{9,... | collective-permute-start | bytes 393224 | tf_op jit(solution)/shard_map/ppermute | solution.py:32
  116.8 9.8 %collective-permute-start.39 = (f32[128,256]{1,0:T(8,128)S(1)}, f32[128,256]{1,0:T(8,128)S(1)}, u32[]{:S(2)}, u32[]{:S(2)}) collective-permute-start(f32[128,256]{1,0:T(8,128)S(1)} %get-tuple-element.162), channel_id=1, source_target_pairs={{0,24},{1,25},{2,26},{3,27},{4,28},{5,29},{6,30},{7,31},{8,16},{9,... | collective-permute-start | bytes 393224 | tf_op jit(solution)/shard_map/ppermute | solution.py:32
  122.0 14.4 %collective-permute-start.35 = (f32[256,256]{1,0:T(8,128)S(1)}, f32[256,256]{1,0:T(8,128)S(1)}, u32[]{:S(2)}, u32[]{:S(2)}) collective-permute-start(f32[256,256]{1,0:T(8,128)S(1)} %shard_map.65.b0), channel_id=1, source_target_pairs={{0,6},{1,7},{2,4},{3,5},{4,2},{5,3},{6,0},{7,1},{8,14},{9,15},{10,... | collective-permute-start | bytes 786440 | tf_op jit(solution)/shard_map/ppermute | solution.py:32
  122.7 13.7 %collective-permute-start.34 = (f32[256,256]{1,0:T(8,128)S(1)}, f32[256,256]{1,0:T(8,128)S(1)}, u32[]{:S(2)}, u32[]{:S(2)}) collective-permute-start(f32[256,256]{1,0:T(8,128)S(1)} %shard_map.65.b0), channel_id=1, source_target_pairs={{0,4},{1,5},{2,6},{3,7},{4,0},{5,1},{6,2},{7,3},{8,12},{9,13},{10,... | collective-permute-start | bytes 786440 | tf_op jit(solution)/shard_map/ppermute | solution.py:32
  123.1 14.0 %collective-permute-start.33 = (f32[256,256]{1,0:T(8,128)S(1)}, f32[256,256]{1,0:T(8,128)S(1)}, u32[]{:S(2)}, u32[]{:S(2)}) collective-permute-start(f32[256,256]{1,0:T(8,128)S(1)} %shard_map.65.b0), channel_id=1, source_target_pairs={{0,2},{1,3},{2,0},{3,1},{4,6},{5,7},{6,4},{7,5},{8,10},{9,11},{10,... | collective-permute-start | bytes 786440 | tf_op jit(solution)/shard_map/ppermute | solution.py:32
  126.7 10.3 %collective-permute-start.42 = (f32[128,256]{1,0:T(8,128)S(1)}, f32[128,256]{1,0:T(8,128)S(1)}, u32[]{:S(2)}, u32[]{:S(2)}) collective-permute-start(f32[128,256]{1,0:T(8,128)S(1)} %add_add_fusion.5.y0.y2), channel_id=1, source_target_pairs={{0,24},{1,25},{2,26},{3,27},{4,28},{5,29},{6,30},{7,31},{8,16},{9,... | collective-permute-start | bytes 393224 | tf_op jit(solution)/shard_map/ppermute | solution.py:32
  130.2 6.8 %collective-permute-start.41 = (f32[128,256]{1,0:T(8,128)S(1)}, f32[128,256]{1,0:T(8,128)S(1)}, u32[]{:S(2)}, u32[]{:S(2)}) collective-permute-start(f32[128,256]{1,0:T(8,128)S(1)} %add_add_fusion.5.y0.y2), channel_id=1, source_target_pairs={{0,16},{1,17},{2,18},{3,19},{4,20},{5,21},{6,22},{7,23},{8,24},{9,... | collective-permute-start | bytes 393224 | tf_op jit(solution)/shard_map/ppermute | solution.py:32
  146.4 9.1 %collective-permute-start.46 = (f32[128,256]{1,0:T(8,128)S(1)}, f32[128,256]{1,0:T(8,128)S(1)}, u32[]{:S(2)}, u32[]{:S(2)}) collective-permute-start(f32[128,256]{1,0:T(8,128)S(1)} %get-tuple-element.175), channel_id=1, source_target_pairs={{0,64},{1,65},{2,66},{3,67},{4,68},{5,69},{6,70},{7,71},{8,72},{9,... | collective-permute-start | bytes 393224 | tf_op jit(solution)/shard_map/ppermute | solution.py:32
  149.1 8.7 %collective-permute-start.47 = (f32[128,256]{1,0:T(8,128)S(1)}, f32[128,256]{1,0:T(8,128)S(1)}, u32[]{:S(2)}, u32[]{:S(2)}) collective-permute-start(f32[128,256]{1,0:T(8,128)S(1)} %get-tuple-element.176), channel_id=1, source_target_pairs={{0,65},{1,64},{2,67},{3,66},{4,69},{5,68},{6,71},{7,70},{8,73},{9,... | collective-permute-start | bytes 393224 | tf_op jit(solution)/shard_map/ppermute | solution.py:32
  157.8 8.8 %collective-permute-start.50 = (f32[128,256]{1,0:T(8,128)S(1)}, f32[128,256]{1,0:T(8,128)S(1)}, u32[]{:S(2)}, u32[]{:S(2)}) collective-permute-start(f32[128,256]{1,0:T(8,128)S(1)} %add_add_fusion.4.x2), channel_id=1, source_target_pairs={{0,65},{1,64},{2,67},{3,66},{4,69},{5,68},{6,71},{7,70},{8,73},{9,... | collective-permute-start | bytes 393224 | tf_op jit(solution)/shard_map/ppermute | solution.py:32
  159.2 7.6 %collective-permute-start.49 = (f32[128,256]{1,0:T(8,128)S(1)}, f32[128,256]{1,0:T(8,128)S(1)}, u32[]{:S(2)}, u32[]{:S(2)}) collective-permute-start(f32[128,256]{1,0:T(8,128)S(1)} %add_add_fusion.4.x2), channel_id=1, source_target_pairs={{0,64},{1,65},{2,66},{3,67},{4,68},{5,69},{6,70},{7,71},{8,72},{9,... | collective-permute-start | bytes 393224 | tf_op jit(solution)/shard_map/ppermute | solution.py:32
  159.3 8.0 %collective-permute-start.48 = (f32[128,256]{1,0:T(8,128)S(1)}, f32[128,256]{1,0:T(8,128)S(1)}, u32[]{:S(2)}, u32[]{:S(2)}) collective-permute-start(f32[128,256]{1,0:T(8,128)S(1)} %add_add_fusion.4.x2), channel_id=1, source_target_pairs={{0,1},{1,0},{2,3},{3,2},{4,5},{5,4},{6,7},{7,6},{8,9},{9,8},{10,11... | collective-permute-start | bytes 393224 | tf_op jit(solution)/shard_map/ppermute | solution.py:32
  168.1 17.2 %collective-permute-start.44 = (f32[4,192,256]{2,1,0:T(8,128)S(1)}, f32[4,192,256]{2,1,0:T(8,128)S(1)}, u32[]{:S(2)}, u32[]{:S(2)}) collective-permute-start(f32[4,192,256]{2,1,0:T(8,128)S(1)} %get-tuple-element.173), channel_id=1, source_target_pairs={{0,32},{1,33},{2,34},{3,35},{4,36},{5,37},{6,38},{7,39},{8,40},{9,... | collective-permute-start | bytes 2359304 | tf_op jit(solution)/shard_map/ppermute | solution.py:32
  171.0 7.9 %collective-permute-start.53 = (f32[128,256]{1,0:T(8,128)S(1)}, f32[128,256]{1,0:T(8,128)S(1)}, u32[]{:S(2)}, u32[]{:S(2)}) collective-permute-start(f32[128,256]{1,0:T(8,128)S(1)} %get-tuple-element.179), channel_id=1, source_target_pairs={{0,16},{1,17},{2,18},{3,19},{4,20},{5,21},{6,22},{7,23},{8,24},{9,... | collective-permute-start | bytes 393224 | tf_op jit(solution)/shard_map/ppermute | solution.py:32
  172.5 8.7 %collective-permute-start.54 = (f32[128,256]{1,0:T(8,128)S(1)}, f32[128,256]{1,0:T(8,128)S(1)}, u32[]{:S(2)}, u32[]{:S(2)}) collective-permute-start(f32[128,256]{1,0:T(8,128)S(1)} %get-tuple-element.180), channel_id=1, source_target_pairs={{0,24},{1,25},{2,26},{3,27},{4,28},{5,29},{6,30},{7,31},{8,16},{9,... | collective-permute-start | bytes 393224 | tf_op jit(solution)/shard_map/ppermute | solution.py:32
  181.2 8.3 %collective-permute-start.57 = (f32[128,256]{1,0:T(8,128)S(1)}, f32[128,256]{1,0:T(8,128)S(1)}, u32[]{:S(2)}, u32[]{:S(2)}) collective-permute-start(f32[128,256]{1,0:T(8,128)S(1)} %add_add_fusion.3.y0.y1), channel_id=1, source_target_pairs={{0,24},{1,25},{2,26},{3,27},{4,28},{5,29},{6,30},{7,31},{8,16},{9,... | collective-permute-start | bytes 393224 | tf_op jit(solution)/shard_map/ppermute | solution.py:32
  184.2 7.5 %collective-permute-start.56 = (f32[128,256]{1,0:T(8,128)S(1)}, f32[128,256]{1,0:T(8,128)S(1)}, u32[]{:S(2)}, u32[]{:S(2)}) collective-permute-start(f32[128,256]{1,0:T(8,128)S(1)} %add_add_fusion.3.y0.y1), channel_id=1, source_target_pairs={{0,16},{1,17},{2,18},{3,19},{4,20},{5,21},{6,22},{7,23},{8,24},{9,... | collective-permute-start | bytes 393224 | tf_op jit(solution)/shard_map/ppermute | solution.py:32
  184.2 7.5 %collective-permute-start.55 = (f32[128,256]{1,0:T(8,128)S(1)}, f32[128,256]{1,0:T(8,128)S(1)}, u32[]{:S(2)}, u32[]{:S(2)}) collective-permute-start(f32[128,256]{1,0:T(8,128)S(1)} %add_add_fusion.3.y0.y1), channel_id=1, source_target_pairs={{0,8},{1,9},{2,10},{3,11},{4,12},{5,13},{6,14},{7,15},{8,0},{9,1},... | collective-permute-start | bytes 393224 | tf_op jit(solution)/shard_map/ppermute | solution.py:32
  193.1 6.6 %collective-permute-start.59 = (f32[128,256]{1,0:T(8,128)S(1)}, f32[128,256]{1,0:T(8,128)S(1)}, u32[]{:S(2)}, u32[]{:S(2)}) collective-permute-start(f32[128,256]{1,0:T(8,128)S(1)} %get-tuple-element.183), channel_id=1, source_target_pairs={{0,4},{1,5},{2,6},{3,7},{4,0},{5,1},{6,2},{7,3},{8,12},{9,13},{10,... | collective-permute-start | bytes 393224 | tf_op jit(solution)/shard_map/ppermute | solution.py:32
  201.2 7.3 %collective-permute-start.66 = (f32[128,256]{1,0:T(8,128)S(1)}, f32[128,256]{1,0:T(8,128)S(1)}, u32[]{:S(2)}, u32[]{:S(2)}) collective-permute-start(f32[128,256]{1,0:T(8,128)S(1)} %add_add_fusion.2.x1), channel_id=1, source_target_pairs={{0,6},{1,7},{2,4},{3,5},{4,2},{5,3},{6,0},{7,1},{8,14},{9,15},{10,... | collective-permute-start | bytes 393224 | tf_op jit(solution)/shard_map/ppermute | solution.py:32
  204.5 6.5 %collective-permute-start.65 = (f32[128,256]{1,0:T(8,128)S(1)}, f32[128,256]{1,0:T(8,128)S(1)}, u32[]{:S(2)}, u32[]{:S(2)}) collective-permute-start(f32[128,256]{1,0:T(8,128)S(1)} %add_add_fusion.2.x1), channel_id=1, source_target_pairs={{0,4},{1,5},{2,6},{3,7},{4,0},{5,1},{6,2},{7,3},{8,12},{9,13},{10,... | collective-permute-start | bytes 393224 | tf_op jit(solution)/shard_map/ppermute | solution.py:32
  214.2 8.4 %collective-permute-start.68 = (f32[128,256]{1,0:T(8,128)S(1)}, f32[128,256]{1,0:T(8,128)S(1)}, u32[]{:S(2)}, u32[]{:S(2)}) collective-permute-start(f32[128,256]{1,0:T(8,128)S(1)} %get-tuple-element.192), channel_id=1, source_target_pairs={{0,8},{1,9},{2,10},{3,11},{4,12},{5,13},{6,14},{7,15},{8,0},{9,1},... | collective-permute-start | bytes 393224 | tf_op jit(solution)/shard_map/ppermute | solution.py:32
  214.3 10.6 %collective-permute-start.69 = (f32[128,256]{1,0:T(8,128)S(1)}, f32[128,256]{1,0:T(8,128)S(1)}, u32[]{:S(2)}, u32[]{:S(2)}) collective-permute-start(f32[128,256]{1,0:T(8,128)S(1)} %get-tuple-element.193), channel_id=1, source_target_pairs={{0,16},{1,17},{2,18},{3,19},{4,20},{5,21},{6,22},{7,23},{8,24},{9,... | collective-permute-start | bytes 393224 | tf_op jit(solution)/shard_map/ppermute | solution.py:32
  218.5 8.7 %collective-permute-start.70 = (f32[128,256]{1,0:T(8,128)S(1)}, f32[128,256]{1,0:T(8,128)S(1)}, u32[]{:S(2)}, u32[]{:S(2)}) collective-permute-start(f32[128,256]{1,0:T(8,128)S(1)} %get-tuple-element.194), channel_id=1, source_target_pairs={{0,24},{1,25},{2,26},{3,27},{4,28},{5,29},{6,30},{7,31},{8,16},{9,... | collective-permute-start | bytes 393224 | tf_op jit(solution)/shard_map/ppermute | solution.py:32
  219.7 9.3 %collective-permute-start.61 = (f32[2,2,64,256]{3,2,1,0:T(8,128)S(1)}, f32[2,2,64,256]{3,2,1,0:T(8,128)S(1)}, u32[]{:S(2)}, u32[]{:S(2)}) collective-permute-start(f32[2,2,64,256]{3,2,1,0:T(8,128)S(1)} %get-tuple-element.188), channel_id=1, source_target_pairs={{0,1},{1,0},{2,3},{3,2},{4,5},{5,4},{6,7},{7,6},{8,9},{9,8},{10,11... | collective-permute-start | bytes 786440 | tf_op jit(solution)/shard_map/ppermute | solution.py:32
  219.8 14.0 %collective-permute-start.62 = (f32[2,2,64,256]{3,2,1,0:T(8,128)S(1)}, f32[2,2,64,256]{3,2,1,0:T(8,128)S(1)}, u32[]{:S(2)}, u32[]{:S(2)}) collective-permute-start(f32[2,2,64,256]{3,2,1,0:T(8,128)S(1)} %get-tuple-element.189), channel_id=1, source_target_pairs={{0,64},{1,65},{2,66},{3,67},{4,68},{5,69},{6,70},{7,71},{8,72},{9,... | collective-permute-start | bytes 786440 | tf_op jit(solution)/shard_map/ppermute | solution.py:32
  222.6 13.8 %collective-permute-start.63 = (f32[2,2,64,256]{3,2,1,0:T(8,128)S(1)}, f32[2,2,64,256]{3,2,1,0:T(8,128)S(1)}, u32[]{:S(2)}, u32[]{:S(2)}) collective-permute-start(f32[2,2,64,256]{3,2,1,0:T(8,128)S(1)} %get-tuple-element.190), channel_id=1, source_target_pairs={{0,65},{1,64},{2,67},{3,66},{4,69},{5,68},{6,71},{7,70},{8,73},{9,... | collective-permute-start | bytes 786440 | tf_op jit(solution)/shard_map/ppermute | solution.py:32
  227.2 9.1 %collective-permute-start.73 = (f32[128,256]{1,0:T(8,128)S(1)}, f32[128,256]{1,0:T(8,128)S(1)}, u32[]{:S(2)}, u32[]{:S(2)}) collective-permute-start(f32[128,256]{1,0:T(8,128)S(1)} %add_add_fusion.1.y0), channel_id=1, source_target_pairs={{0,24},{1,25},{2,26},{3,27},{4,28},{5,29},{6,30},{7,31},{8,16},{9,... | collective-permute-start | bytes 393224 | tf_op jit(solution)/shard_map/ppermute | solution.py:32
  227.8 8.6 %collective-permute-start.72 = (f32[128,256]{1,0:T(8,128)S(1)}, f32[128,256]{1,0:T(8,128)S(1)}, u32[]{:S(2)}, u32[]{:S(2)}) collective-permute-start(f32[128,256]{1,0:T(8,128)S(1)} %add_add_fusion.1.y0), channel_id=1, source_target_pairs={{0,16},{1,17},{2,18},{3,19},{4,20},{5,21},{6,22},{7,23},{8,24},{9,... | collective-permute-start | bytes 393224 | tf_op jit(solution)/shard_map/ppermute | solution.py:32
  229.1 7.8 %collective-permute-start.71 = (f32[128,256]{1,0:T(8,128)S(1)}, f32[128,256]{1,0:T(8,128)S(1)}, u32[]{:S(2)}, u32[]{:S(2)}) collective-permute-start(f32[128,256]{1,0:T(8,128)S(1)} %add_add_fusion.1.y0), channel_id=1, source_target_pairs={{0,8},{1,9},{2,10},{3,11},{4,12},{5,13},{6,14},{7,15},{8,0},{9,1},... | collective-permute-start | bytes 393224 | tf_op jit(solution)/shard_map/ppermute | solution.py:32
  238.3 7.9 %collective-permute-start.75 = (f32[128,256]{1,0:T(8,128)S(1)}, f32[128,256]{1,0:T(8,128)S(1)}, u32[]{:S(2)}, u32[]{:S(2)}) collective-permute-start(f32[128,256]{1,0:T(8,128)S(1)} %get-tuple-element.201), channel_id=1, source_target_pairs={{0,64},{1,65},{2,66},{3,67},{4,68},{5,69},{6,70},{7,71},{8,72},{9,... | collective-permute-start | bytes 393224 | tf_op jit(solution)/shard_map/ppermute | solution.py:32
  241.3 6.5 %collective-permute-start.76 = (f32[128,256]{1,0:T(8,128)S(1)}, f32[128,256]{1,0:T(8,128)S(1)}, u32[]{:S(2)}, u32[]{:S(2)}) collective-permute-start(f32[128,256]{1,0:T(8,128)S(1)} %get-tuple-element.202), channel_id=1, source_target_pairs={{0,65},{1,64},{2,67},{3,66},{4,69},{5,68},{6,71},{7,70},{8,73},{9,... | collective-permute-start | bytes 393224 | tf_op jit(solution)/shard_map/ppermute | solution.py:32
  248.4 8.6 %collective-permute-start.77 = (f32[2,64,256]{2,1,0:T(8,128)S(1)}, f32[2,64,256]{2,1,0:T(8,128)S(1)}, u32[]{:S(2)}, u32[]{:S(2)}) collective-permute-start(f32[2,64,256]{2,1,0:T(8,128)S(1)} %get-tuple-element.206), channel_id=1, source_target_pairs={{0,1},{1,0},{2,3},{3,2},{4,5},{5,4},{6,7},{7,6},{8,9},{9,8},{10,11... | collective-permute-start | bytes 393224 | tf_op jit(solution)/shard_map/ppermute | solution.py:32
  249.1 9.1 %collective-permute-start.78 = (f32[2,64,256]{2,1,0:T(8,128)S(1)}, f32[2,64,256]{2,1,0:T(8,128)S(1)}, u32[]{:S(2)}, u32[]{:S(2)}) collective-permute-start(f32[2,64,256]{2,1,0:T(8,128)S(1)} %get-tuple-element.207), channel_id=1, source_target_pairs={{64,0},{65,1},{66,2},{67,3},{68,4},{69,5},{70,6},{71,7},{72,8},{73... | collective-permute-start | bytes 393224 | tf_op jit(solution)/shard_map/ppermute | solution.py:32
  261.2 8.4 %collective-permute-start.81 = (f32[2,64,256]{2,1,0:T(8,128)S(1)}, f32[2,64,256]{2,1,0:T(8,128)S(1)}, u32[]{:S(2)}, u32[]{:S(2)}) collective-permute-start(f32[2,64,256]{2,1,0:T(8,128)S(1)} %get-tuple-element.211), channel_id=1, source_target_pairs={{0,4},{1,5},{2,6},{3,7},{4,0},{5,1},{6,2},{7,3},{8,12},{9,13},{10,... | collective-permute-start | bytes 393224 | tf_op jit(solution)/shard_map/ppermute | solution.py:32
  264.4 6.9 %collective-permute-start.82 = (f32[2,64,256]{2,1,0:T(8,128)S(1)}, f32[2,64,256]{2,1,0:T(8,128)S(1)}, u32[]{:S(2)}, u32[]{:S(2)}) collective-permute-start(f32[2,64,256]{2,1,0:T(8,128)S(1)} %get-tuple-element.212), channel_id=1, source_target_pairs={{0,6},{1,7},{2,4},{3,5},{4,2},{5,3},{6,0},{7,1},{8,14},{9,15},{10,... | collective-permute-start | bytes 393224 | tf_op jit(solution)/shard_map/ppermute | solution.py:32
  (22 other events, 95.3 us)

commit v8 on v7

--- a/solution.py
+++ b/solution.py
@@ -489,7 +489,7 @@
         if t == 0:
             whole = list(after(whole, tuple(early)))
         if t == 2:
-            on_y = list(after(on_y, tuple(whole)))
+            on_y = list(after(on_y, whole[2]))
             on_y_sib = send(jnp.stack(on_y), to_other_core)
         args = list(lowers) + [b_sib] if odd else on_y + [on_y_sib]
         kernel = close_odd_kernel if odd else functools.partial(close_even_kernel, t // 2)

time: 280 us -> 277 us (0.989)
  starting transfers between devices: 113 us -> 110 us
    ppermute x84, starting transfers between devices: 113 us -> 110 us  [send(): return lax.ppermute(x, AXES, route(place, only))]
  transfers between devices with their start and end apart: 84 -> 84, of which waited for: 60 -> 57; matrix products, arithmetic and copies ran while one was open for 0% -> 0% of each run, Pallas kernels for 2% -> 2%
where the time goes in v8:
time: 277 us; the launch traced here: 272 us
  waiting for transfers between devices  139 us (50%)
  starting transfers between devices  110 us (40%)
  Pallas kernels  19.1 us (7%)
    ppermute x84, waiting for transfers between devices, send(): return lax.ppermute(x, AXES, route(place, only))  139 us
    ppermute x84, starting transfers between devices, send(): return lax.ppermute(x, AXES, route(place, only))  110 us
    pallas_call x19, Pallas kernels, local(): pl.pallas_call(kernel, out_shape=[jax.ShapeDtypeStruct(s, jnp.float32) fo...  19.1 us
  transfers between devices with their start and end apart: 84, of which 57 were waited for; matrix products, arithmetic and copies ran while one was open for 0% of the time, Pallas kernels for 2%

profile of v8, /device:TPU:6, one launch (start us, length us, event | category | flops | bytes accessed | tf_op | source)
XLA Modules:
  0.0 272.2 jit_solution(1319117121597336487)
XLA Ops:
  4.1 3.0 %collective-permute-start.1 = (f32[2,64,512]{2,1,0:T(8,128)S(1)}, f32[2,64,512]{2,1,0:T(8,128)S(1)}, u32[]{:S(2)}, u32[]{:S(2)}) collective-permute-start(f32[2,64,512]{2,1,0:T(8,128)S(1)} %pad_maximum_fusion.6), channel_id=1, source_target_pairs={{0,4},{1,5},{2,6},{3,7},{4,0},{5,1},{6,2},{7,3},{8,12},{9,13},{10,... | collective-permute-start | bytes 786440 | tf_op jit(solution)/shard_map/ppermute | solution.py:32
  8.8 5.4 %collective-permute-done.1.d2 = f32[2,64,512]{2,1,0:T(8,128)S(1)} collective-permute-done((f32[2,64,512]{2,1,0:T(8,128)S(1)}, f32[2,64,512]{2,1,0:T(8,128)S(1)}, u32[]{:S(2)}, u32[]{:S(2)}) %collective-permute-start.1) | collective-permute-done | bytes 262176 | tf_op jit(solution)/shard_map/ppermute | solution.py:32
  14.2 2.7 collective-permute-done.2.d3
  17.7 3.0 %collective-permute-done.3.got = f32[4,5,64,256]{3,2,1,0:T(8,128)S(1)} collective-permute-done((f32[4,5,64,256]{3,2,1,0:T(8,128)S(1)}, f32[4,5,64,256]{3,2,1,0:T(8,128)S(1)}, u32[]{:S(2)}, u32[]{:S(2)}) %collective-permute-start.3) | collective-permute-done | bytes 1310752 | tf_op jit(solution)/shard_map/ppermute | solution.py:32
  23.5 2.1 collective-permute-start.5
  25.6 12.7 %collective-permute-done.5.a2 = f32[4,64,256]{2,1,0:T(8,128)S(1)} collective-permute-done((f32[4,64,256]{2,1,0:T(8,128)S(1)}, f32[4,64,256]{2,1,0:T(8,128)S(1)}, u32[]{:S(2)}, u32[]{:S(2)}) %collective-permute-start.5) | collective-permute-done | bytes 262176 | tf_op jit(solution)/shard_map/ppermute | solution.py:32
  38.3 1.7 collective-permute-done.6.a3
  44.2 2.3 collective-permute-start.14
  47.3 2.4 collective-permute-done.11.rest_1_.a1
  49.7 6.4 %collective-permute-done.9.b3.m3 = f32[256,256]{1,0:T(8,128)S(1)} collective-permute-done((f32[256,256]{1,0:T(8,128)S(1)}, f32[256,256]{1,0:T(8,128)S(1)}, u32[]{:S(2)}, u32[]{:S(2)}) %collective-permute-start.9) | collective-permute-done | bytes 262176 | tf_op jit(solution)/shard_map/ppermute | solution.py:32
  59.9 3.6 %collective-permute-start.16 = (f32[192,256]{1,0:T(8,128)S(1)}, f32[192,256]{1,0:T(8,128)S(1)}, u32[]{:S(2)}, u32[]{:S(2)}) collective-permute-start(f32[192,256]{1,0:T(8,128)S(1)} %get-tuple-element.131), channel_id=1, source_target_pairs={{0,16},{1,17},{2,18},{3,19},{4,20},{5,21},{6,22},{7,23},{8,24},{9,... | collective-permute-start | bytes 589832 | tf_op jit(solution)/shard_map/ppermute | solution.py:32
  63.9 2.9 %collective-permute-done.15.e1 = f32[192,256]{1,0:T(8,128)S(1)} collective-permute-done((f32[192,256]{1,0:T(8,128)S(1)}, f32[192,256]{1,0:T(8,128)S(1)}, u32[]{:S(2)}, u32[]{:S(2)}) %collective-permute-start.15) | collective-permute-done | bytes 196640 | tf_op jit(solution)/shard_map/ppermute | solution.py:32
  66.8 6.0 %collective-permute-done.16.e2 = f32[192,256]{1,0:T(8,128)S(1)} collective-permute-done((f32[192,256]{1,0:T(8,128)S(1)}, f32[192,256]{1,0:T(8,128)S(1)}, u32[]{:S(2)}, u32[]{:S(2)}) %collective-permute-start.16) | collective-permute-done | bytes 196640 | tf_op jit(solution)/shard_map/ppermute | solution.py:32
  72.7 2.6 collective-permute-done.17.e3
  76.1 3.4 %collective-permute-start.18 = (f32[128,256]{1,0:T(8,128)S(1)}, f32[128,256]{1,0:T(8,128)S(1)}, u32[]{:S(2)}, u32[]{:S(2)}) collective-permute-start(f32[128,256]{1,0:T(8,128)S(1)} %fusion.y0.y3), channel_id=1, source_target_pairs={{0,8},{1,9},{2,10},{3,11},{4,12},{5,13},{6,14},{7,15},{8,0},{9,1},... | collective-permute-start | bytes 393224 | tf_op jit(solution)/shard_map/ppermute | solution.py:32
  86.5 1.7 collective-permute-start.21
  88.2 3.1 %collective-permute-start.23 = (f32[128,256]{1,0:T(8,128)S(1)}, f32[128,256]{1,0:T(8,128)S(1)}, u32[]{:S(2)}, u32[]{:S(2)}) collective-permute-start(f32[128,256]{1,0:T(8,128)S(1)} %get-tuple-element.136), channel_id=1, source_target_pairs={{0,6},{1,7},{2,4},{3,5},{4,2},{5,3},{6,0},{7,1},{8,14},{9,15},{10,... | collective-permute-start | bytes 393224 | tf_op jit(solution)/shard_map/ppermute | solution.py:32
  92.6 2.2 collective-permute-done.22
  96.1 2.5 collective-permute-start.32
  98.6 1.9 collective-permute-start.29
  104.3 4.8 %collective-permute-done.31 = f32[128,256]{1,0:T(8,128)S(1)} collective-permute-done((f32[128,256]{1,0:T(8,128)S(1)}, f32[128,256]{1,0:T(8,128)S(1)}, u32[]{:S(2)}, u32[]{:S(2)}) %collective-permute-start.31) | collective-permute-done | bytes 131104 | tf_op jit(solution)/shard_map/ppermute | solution.py:32
  109.2 3.2 %collective-permute-done.29.a3.b3 = f32[256,256]{1,0:T(8,128)S(1)} collective-permute-done((f32[256,256]{1,0:T(8,128)S(1)}, f32[256,256]{1,0:T(8,128)S(1)}, u32[]{:S(2)}, u32[]{:S(2)}) %collective-permute-start.29) | collective-permute-done | bytes 262176 | tf_op jit(solution)/shard_map/ppermute | solution.py:32
  113.2 2.3 collective-permute-done.36.x_sib
  116.8 4.6 %collective-permute-start.39 = (f32[128,256]{1,0:T(8,128)S(1)}, f32[128,256]{1,0:T(8,128)S(1)}, u32[]{:S(2)}, u32[]{:S(2)}) collective-permute-start(f32[128,256]{1,0:T(8,128)S(1)} %get-tuple-element.162), channel_id=1, source_target_pairs={{0,24},{1,25},{2,26},{3,27},{4,28},{5,29},{6,30},{7,31},{8,16},{9,... | collective-permute-start | bytes 393224 | tf_op jit(solution)/shard_map/ppermute | solution.py:32
  123.1 3.1 %collective-permute-start.33 = (f32[256,256]{1,0:T(8,128)S(1)}, f32[256,256]{1,0:T(8,128)S(1)}, u32[]{:S(2)}, u32[]{:S(2)}) collective-permute-start(f32[256,256]{1,0:T(8,128)S(1)} %shard_map.65.b0), channel_id=1, source_target_pairs={{0,2},{1,3},{2,0},{3,1},{4,6},{5,7},{6,4},{7,5},{8,10},{9,11},{10,... | collective-permute-start | bytes 786440 | tf_op jit(solution)/shard_map/ppermute | solution.py:32
  126.7 1.8 collective-permute-start.40
  128.5 7.9 %collective-permute-done.35.b3 = f32[256,256]{1,0:T(8,128)S(1)} collective-permute-done((f32[256,256]{1,0:T(8,128)S(1)}, f32[256,256]{1,0:T(8,128)S(1)}, u32[]{:S(2)}, u32[]{:S(2)}) %collective-permute-start.35) | collective-permute-done | bytes 262176 | tf_op jit(solution)/shard_map/ppermute | solution.py:32
  137.6 6.8 %collective-permute-done.43.y3 = f32[128,256]{1,0:T(8,128)S(1)} collective-permute-done((f32[128,256]{1,0:T(8,128)S(1)}, f32[128,256]{1,0:T(8,128)S(1)}, u32[]{:S(2)}, u32[]{:S(2)}) %collective-permute-start.43) | collective-permute-done | bytes 131104 | tf_op jit(solution)/shard_map/ppermute | solution.py:32
  146.6 2.7 collective-permute-start.46
  150.5 1.7 collective-permute-done.45
  152.2 2.9 %collective-permute-done.46 = f32[128,256]{1,0:T(8,128)S(1)} collective-permute-done((f32[128,256]{1,0:T(8,128)S(1)}, f32[128,256]{1,0:T(8,128)S(1)}, u32[]{:S(2)}, u32[]{:S(2)}) %collective-permute-start.46) | collective-permute-done | bytes 131104 | tf_op jit(solution)/shard_map/ppermute | solution.py:32
  155.1 1.9 collective-permute-done.47
  159.0 2.3 collective-permute-start.48
  161.3 4.3 %collective-permute-done.50 = f32[128,256]{1,0:T(8,128)S(1)} collective-permute-done((f32[128,256]{1,0:T(8,128)S(1)}, f32[128,256]{1,0:T(8,128)S(1)}, u32[]{:S(2)}, u32[]{:S(2)}) %collective-permute-start.50) | collective-permute-done | bytes 131104 | tf_op jit(solution)/shard_map/ppermute | solution.py:32
  169.8 2.5 collective-permute-start.53
  172.3 2.2 collective-permute-start.54
  176.1 2.6 collective-permute-done.53
  178.7 2.2 collective-permute-done.54
  181.0 2.3 collective-permute-start.57
  183.3 1.9 collective-permute-start.55
  185.2 3.7 %collective-permute-done.57.y3 = f32[128,256]{1,0:T(8,128)S(1)} collective-permute-done((f32[128,256]{1,0:T(8,128)S(1)}, f32[128,256]{1,0:T(8,128)S(1)}, u32[]{:S(2)}, u32[]{:S(2)}) %collective-permute-start.57) | collective-permute-done | bytes 131104 | tf_op jit(solution)/shard_map/ppermute | solution.py:32
  188.9 1.9 collective-permute-done.56.y2
  192.2 2.2 collective-permute-start.59
  194.5 2.5 collective-permute-start.60
  197.2 1.7 collective-permute-done.59
  198.9 1.7 collective-permute-done.60
  200.7 2.5 collective-permute-start.66
  204.9 2.3 collective-permute-done.66
  207.2 2.5 collective-permute-done.65
  209.8 1.9 collective-permute-done.67.x_sib
  213.4 3.1 %collective-permute-start.69 = (f32[128,256]{1,0:T(8,128)S(1)}, f32[128,256]{1,0:T(8,128)S(1)}, u32[]{:S(2)}, u32[]{:S(2)}) collective-permute-start(f32[128,256]{1,0:T(8,128)S(1)} %get-tuple-element.193), channel_id=1, source_target_pairs={{0,16},{1,17},{2,18},{3,19},{4,20},{5,21},{6,22},{7,23},{8,24},{9,... | collective-permute-start | bytes 393224 | tf_op jit(solution)/shard_map/ppermute | solution.py:32
  218.8 2.5 collective-permute-start.62
  221.3 1.9 collective-permute-start.63
  223.3 1.9 collective-permute-done.70
  229.3 3.2 %collective-permute-done.62.e2 = f32[2,2,64,256]{3,2,1,0:T(8,128)S(1)} collective-permute-done((f32[2,2,64,256]{3,2,1,0:T(8,128)S(1)}, f32[2,2,64,256]{3,2,1,0:T(8,128)S(1)}, u32[]{:S(2)}, u32[]{:S(2)}) %collective-permute-start.62) | collective-permute-done | bytes 262176 | tf_op jit(solution)/shard_map/ppermute | solution.py:32
  232.5 2.6 collective-permute-done.63.e3
  236.6 3.4 %collective-permute-start.75 = (f32[128,256]{1,0:T(8,128)S(1)}, f32[128,256]{1,0:T(8,128)S(1)}, u32[]{:S(2)}, u32[]{:S(2)}) collective-permute-start(f32[128,256]{1,0:T(8,128)S(1)} %get-tuple-element.201), channel_id=1, source_target_pairs={{0,64},{1,65},{2,66},{3,67},{4,68},{5,69},{6,70},{7,71},{8,72},{9,... | collective-permute-start | bytes 393224 | tf_op jit(solution)/shard_map/ppermute | solution.py:32
  241.7 2.8 %collective-permute-done.75 = f32[128,256]{1,0:T(8,128)S(1)} collective-permute-done((f32[128,256]{1,0:T(8,128)S(1)}, f32[128,256]{1,0:T(8,128)S(1)}, u32[]{:S(2)}, u32[]{:S(2)}) %collective-permute-start.75) | collective-permute-done | bytes 131104 | tf_op jit(solution)/shard_map/ppermute | solution.py:32
  244.5 1.7 collective-permute-done.76
  247.5 5.9 %collective-permute-start.78 = (f32[2,64,256]{2,1,0:T(8,128)S(1)}, f32[2,64,256]{2,1,0:T(8,128)S(1)}, u32[]{:S(2)}, u32[]{:S(2)}) collective-permute-start(f32[2,64,256]{2,1,0:T(8,128)S(1)} %get-tuple-element.207), channel_id=1, source_target_pairs={{64,0},{65,1},{66,2},{67,3},{68,4},{69,5},{70,6},{71,7},{72,8},{73... | collective-permute-start | bytes 393224 | tf_op jit(solution)/shard_map/ppermute | solution.py:32
  258.7 3.1 %collective-permute-start.81 = (f32[2,64,256]{2,1,0:T(8,128)S(1)}, f32[2,64,256]{2,1,0:T(8,128)S(1)}, u32[]{:S(2)}, u32[]{:S(2)}) collective-permute-start(f32[2,64,256]{2,1,0:T(8,128)S(1)} %get-tuple-element.211), channel_id=1, source_target_pairs={{0,4},{1,5},{2,6},{3,7},{4,0},{5,1},{6,2},{7,3},{8,12},{9,13},{10,... | collective-permute-start | bytes 393224 | tf_op jit(solution)/shard_map/ppermute | solution.py:32
  263.3 2.8 %collective-permute-done.81.h2 = f32[2,64,256]{2,1,0:T(8,128)S(1)} collective-permute-done((f32[2,64,256]{2,1,0:T(8,128)S(1)}, f32[2,64,256]{2,1,0:T(8,128)S(1)}, u32[]{:S(2)}, u32[]{:S(2)}) %collective-permute-start.81) | collective-permute-done | bytes 131104 | tf_op jit(solution)/shard_map/ppermute | solution.py:32
  266.1 1.8 collective-permute-done.82.h3
  268.6 1.9 collective-permute-done.83.got
  (165 shorter events, 73.8 us)
Async XLA Ops:
  4.1 10.1 %collective-permute-start.1 = (f32[2,64,512]{2,1,0:T(8,128)S(1)}, f32[2,64,512]{2,1,0:T(8,128)S(1)}, u32[]{:S(2)}, u32[]{:S(2)}) collective-permute-start(f32[2,64,512]{2,1,0:T(8,128)S(1)} %pad_maximum_fusion.6), channel_id=1, source_target_pairs={{0,4},{1,5},{2,6},{3,7},{4,0},{5,1},{6,2},{7,3},{8,12},{9,13},{10,... | collective-permute-start | bytes 786440 | tf_op jit(solution)/shard_map/ppermute | solution.py:32
  7.1 9.7 %collective-permute-start.2 = (f32[2,64,512]{2,1,0:T(8,128)S(1)}, f32[2,64,512]{2,1,0:T(8,128)S(1)}, u32[]{:S(2)}, u32[]{:S(2)}) collective-permute-start(f32[2,64,512]{2,1,0:T(8,128)S(1)} %pad_maximum_fusion.7), channel_id=1, source_target_pairs={{0,6},{1,7},{2,4},{3,5},{4,2},{5,3},{6,0},{7,1},{8,14},{9,15},{10,... | collective-permute-start | bytes 786440 | tf_op jit(solution)/shard_map/ppermute | solution.py:32
  21.4 16.9 %collective-permute-start.4 = (f32[6,64,256]{2,1,0:T(8,128)S(1)}, f32[6,64,256]{2,1,0:T(8,128)S(1)}, u32[]{:S(2)}, u32[]{:S(2)}) collective-permute-start(f32[6,64,256]{2,1,0:T(8,128)S(1)} %get-tuple-element.113), channel_id=1, source_target_pairs={{0,1},{1,0},{2,3},{3,2},{4,5},{5,4},{6,7},{7,6},{8,9},{9,8},{10,11... | collective-permute-start | bytes 1179656 | tf_op jit(solution)/shard_map/ppermute | solution.py:32
  22.4 17.7 %collective-permute-start.6 = (f32[6,64,256]{2,1,0:T(8,128)S(1)}, f32[6,64,256]{2,1,0:T(8,128)S(1)}, u32[]{:S(2)}, u32[]{:S(2)}) collective-permute-start(f32[6,64,256]{2,1,0:T(8,128)S(1)} %get-tuple-element.115), channel_id=1, source_target_pairs={{0,65},{1,64},{2,67},{3,66},{4,69},{5,68},{6,71},{7,70},{8,73},{9,... | collective-permute-start | bytes 1179656 | tf_op jit(solution)/shard_map/ppermute | solution.py:32
  23.5 14.8 %collective-permute-start.5 = (f32[4,64,256]{2,1,0:T(8,128)S(1)}, f32[4,64,256]{2,1,0:T(8,128)S(1)}, u32[]{:S(2)}, u32[]{:S(2)}) collective-permute-start(f32[4,64,256]{2,1,0:T(8,128)S(1)} %get-tuple-element.114), channel_id=1, source_target_pairs={{0,64},{1,65},{2,66},{3,67},{4,68},{5,69},{6,70},{7,71},{8,72},{9,... | collective-permute-start | bytes 786440 | tf_op jit(solution)/shard_map/ppermute | solution.py:32
  40.9 8.8 %collective-permute-start.11 = (f32[256,256]{1,0:T(8,128)S(1)}, f32[256,256]{1,0:T(8,128)S(1)}, u32[]{:S(2)}, u32[]{:S(2)}) collective-permute-start(f32[256,256]{1,0:T(8,128)S(1)} %get-tuple-element.122.rest_0_.a0), channel_id=1, source_target_pairs={{0,2},{1,3},{2,0},{3,1},{4,6},{5,7},{6,4},{7,5},{8,10},{9,11},{10,... | collective-permute-start | bytes 786440 | tf_op jit(solution)/shard_map/ppermute | solution.py:32
  42.1 14.0 %collective-permute-start.9 = (f32[256,256]{1,0:T(8,128)S(1)}, f32[256,256]{1,0:T(8,128)S(1)}, u32[]{:S(2)}, u32[]{:S(2)}) collective-permute-start(f32[256,256]{1,0:T(8,128)S(1)} %get-tuple-element.117.b0.m0), channel_id=1, source_target_pairs={{0,65},{1,64},{2,67},{3,66},{4,69},{5,68},{6,71},{7,70},{8,73},{9,... | collective-permute-start | bytes 786440 | tf_op jit(solution)/shard_map/ppermute | solution.py:32
  43.3 12.9 %collective-permute-start.8 = (f32[256,256]{1,0:T(8,128)S(1)}, f32[256,256]{1,0:T(8,128)S(1)}, u32[]{:S(2)}, u32[]{:S(2)}) collective-permute-start(f32[256,256]{1,0:T(8,128)S(1)} %get-tuple-element.117.b0.m0), channel_id=1, source_target_pairs={{0,64},{1,65},{2,66},{3,67},{4,68},{5,69},{6,70},{7,71},{8,72},{9,... | collective-permute-start | bytes 786440 | tf_op jit(solution)/shard_map/ppermute | solution.py:32
  44.2 13.1 %collective-permute-start.14 = (f32[256,256]{1,0:T(8,128)S(1)}, f32[256,256]{1,0:T(8,128)S(1)}, u32[]{:S(2)}, u32[]{:S(2)}) collective-permute-start(f32[256,256]{1,0:T(8,128)S(1)} %get-tuple-element.122.rest_0_.a0), channel_id=1, source_target_pairs={{0,6},{1,7},{2,4},{3,5},{4,2},{5,3},{6,0},{7,1},{8,14},{9,15},{10,... | collective-permute-start | bytes 786440 | tf_op jit(solution)/shard_map/ppermute | solution.py:32
  46.5 10.8 %collective-permute-start.13 = (f32[256,256]{1,0:T(8,128)S(1)}, f32[256,256]{1,0:T(8,128)S(1)}, u32[]{:S(2)}, u32[]{:S(2)}) collective-permute-start(f32[256,256]{1,0:T(8,128)S(1)} %get-tuple-element.122.rest_0_.a0), channel_id=1, source_target_pairs={{0,4},{1,5},{2,6},{3,7},{4,0},{5,1},{6,2},{7,3},{8,12},{9,13},{10,... | collective-permute-start | bytes 786440 | tf_op jit(solution)/shard_map/ppermute | solution.py:32
  49.7 7.6 %collective-permute-start.7 = (f32[256,256]{1,0:T(8,128)S(1)}, f32[256,256]{1,0:T(8,128)S(1)}, u32[]{:S(2)}, u32[]{:S(2)}) collective-permute-start(f32[256,256]{1,0:T(8,128)S(1)} %get-tuple-element.117.b0.m0), channel_id=1, source_target_pairs={{0,1},{1,0},{2,3},{3,2},{4,5},{5,4},{6,7},{7,6},{8,9},{9,8},{10,11... | collective-permute-start | bytes 786440 | tf_op jit(solution)/shard_map/ppermute | solution.py:32
  59.0 7.8 %collective-permute-start.15 = (f32[192,256]{1,0:T(8,128)S(1)}, f32[192,256]{1,0:T(8,128)S(1)}, u32[]{:S(2)}, u32[]{:S(2)}) collective-permute-start(f32[192,256]{1,0:T(8,128)S(1)} %get-tuple-element.130), channel_id=1, source_target_pairs={{0,8},{1,9},{2,10},{3,11},{4,12},{5,13},{6,14},{7,15},{8,0},{9,1},... | collective-permute-start | bytes 589832 | tf_op jit(solution)/shard_map/ppermute | solution.py:32
  59.9 12.8 %collective-permute-start.16 = (f32[192,256]{1,0:T(8,128)S(1)}, f32[192,256]{1,0:T(8,128)S(1)}, u32[]{:S(2)}, u32[]{:S(2)}) collective-permute-start(f32[192,256]{1,0:T(8,128)S(1)} %get-tuple-element.131), channel_id=1, source_target_pairs={{0,16},{1,17},{2,18},{3,19},{4,20},{5,21},{6,22},{7,23},{8,24},{9,... | collective-permute-start | bytes 589832 | tf_op jit(solution)/shard_map/ppermute | solution.py:32
  63.5 11.8 %collective-permute-start.17 = (f32[192,256]{1,0:T(8,128)S(1)}, f32[192,256]{1,0:T(8,128)S(1)}, u32[]{:S(2)}, u32[]{:S(2)}) collective-permute-start(f32[192,256]{1,0:T(8,128)S(1)} %get-tuple-element.132), channel_id=1, source_target_pairs={{0,24},{1,25},{2,26},{3,27},{4,28},{5,29},{6,30},{7,31},{8,16},{9,... | collective-permute-start | bytes 589832 | tf_op jit(solution)/shard_map/ppermute | solution.py:32
  63.8 17.2 %collective-permute-start.10 = (f32[4,128,256]{2,1,0:T(8,128)S(1)}, f32[4,128,256]{2,1,0:T(8,128)S(1)}, u32[]{:S(2)}, u32[]{:S(2)}) collective-permute-start(f32[4,128,256]{2,1,0:T(8,128)S(1)} %pad_maximum_fusion.1), channel_id=1, source_target_pairs={{0,32},{1,33},{2,34},{3,35},{4,36},{5,37},{6,38},{7,39},{8,40},{9,... | collective-permute-start | bytes 1572872 | tf_op jit(solution)/shard_map/ppermute | solution.py:32
  75.4 8.5 %collective-permute-start.20 = (f32[128,256]{1,0:T(8,128)S(1)}, f32[128,256]{1,0:T(8,128)S(1)}, u32[]{:S(2)}, u32[]{:S(2)}) collective-permute-start(f32[128,256]{1,0:T(8,128)S(1)} %fusion.y0.y3), channel_id=1, source_target_pairs={{0,24},{1,25},{2,26},{3,27},{4,28},{5,29},{6,30},{7,31},{8,16},{9,... | collective-permute-start | bytes 393224 | tf_op jit(solution)/shard_map/ppermute | solution.py:32
  75.7 9.4 %collective-permute-start.19 = (f32[128,256]{1,0:T(8,128)S(1)}, f32[128,256]{1,0:T(8,128)S(1)}, u32[]{:S(2)}, u32[]{:S(2)}) collective-permute-start(f32[128,256]{1,0:T(8,128)S(1)} %fusion.y0.y3), channel_id=1, source_target_pairs={{0,16},{1,17},{2,18},{3,19},{4,20},{5,21},{6,22},{7,23},{8,24},{9,... | collective-permute-start | bytes 393224 | tf_op jit(solution)/shard_map/ppermute | solution.py:32
  76.1 9.1 %collective-permute-start.18 = (f32[128,256]{1,0:T(8,128)S(1)}, f32[128,256]{1,0:T(8,128)S(1)}, u32[]{:S(2)}, u32[]{:S(2)}) collective-permute-start(f32[128,256]{1,0:T(8,128)S(1)} %fusion.y0.y3), channel_id=1, source_target_pairs={{0,8},{1,9},{2,10},{3,11},{4,12},{5,13},{6,14},{7,15},{8,0},{9,1},... | collective-permute-start | bytes 393224 | tf_op jit(solution)/shard_map/ppermute | solution.py:32
  79.5 8.7 %collective-permute-start.24 = (f32[2,64,256]{2,1,0:T(8,128)S(1)}, f32[2,64,256]{2,1,0:T(8,128)S(1)}, u32[]{:S(2)}, u32[]{:S(2)}) collective-permute-start(f32[2,64,256]{2,1,0:T(8,128)S(1)} %get-tuple-element.143), channel_id=1, source_target_pairs={{0,1},{1,0},{2,3},{3,2},{4,5},{5,4},{6,7},{7,6},{8,9},{9,8},{10,11... | collective-permute-start | bytes 393224 | tf_op jit(solution)/shard_map/ppermute | solution.py:32
  81.0 10.3 %collective-permute-start.25 = (f32[2,64,256]{2,1,0:T(8,128)S(1)}, f32[2,64,256]{2,1,0:T(8,128)S(1)}, u32[]{:S(2)}, u32[]{:S(2)}) collective-permute-start(f32[2,64,256]{2,1,0:T(8,128)S(1)} %get-tuple-element.144), channel_id=1, source_target_pairs={{0,64},{1,65},{2,66},{3,67},{4,68},{5,69},{6,70},{7,71},{8,72},{9,... | collective-permute-start | bytes 393224 | tf_op jit(solution)/shard_map/ppermute | solution.py:32
  83.8 7.4 %collective-permute-start.26 = (f32[2,64,256]{2,1,0:T(8,128)S(1)}, f32[2,64,256]{2,1,0:T(8,128)S(1)}, u32[]{:S(2)}, u32[]{:S(2)}) collective-permute-start(f32[2,64,256]{2,1,0:T(8,128)S(1)} %get-tuple-element.145), channel_id=1, source_target_pairs={{0,65},{1,64},{2,67},{3,66},{4,69},{5,68},{6,71},{7,70},{8,73},{9,... | collective-permute-start | bytes 393224 | tf_op jit(solution)/shard_map/ppermute | solution.py:32
  88.2 6.5 %collective-permute-start.22 = (f32[128,256]{1,0:T(8,128)S(1)}, f32[128,256]{1,0:T(8,128)S(1)}, u32[]{:S(2)}, u32[]{:S(2)}) collective-permute-start(f32[128,256]{1,0:T(8,128)S(1)} %get-tuple-element.135), channel_id=1, source_target_pairs={{0,4},{1,5},{2,6},{3,7},{4,0},{5,1},{6,2},{7,3},{8,12},{9,13},{10,... | collective-permute-start | bytes 393224 | tf_op jit(solution)/shard_map/ppermute | solution.py:32
  88.2 7.8 %collective-permute-start.23 = (f32[128,256]{1,0:T(8,128)S(1)}, f32[128,256]{1,0:T(8,128)S(1)}, u32[]{:S(2)}, u32[]{:S(2)}) collective-permute-start(f32[128,256]{1,0:T(8,128)S(1)} %get-tuple-element.136), channel_id=1, source_target_pairs={{0,6},{1,7},{2,4},{3,5},{4,2},{5,3},{6,0},{7,1},{8,14},{9,15},{10,... | collective-permute-start | bytes 393224 | tf_op jit(solution)/shard_map/ppermute | solution.py:32
  96.1 6.7 %collective-permute-start.32 = (f32[128,256]{1,0:T(8,128)S(1)}, f32[128,256]{1,0:T(8,128)S(1)}, u32[]{:S(2)}, u32[]{:S(2)}) collective-permute-start(f32[128,256]{1,0:T(8,128)S(1)} %add_add_fusion.6.x3), channel_id=1, source_target_pairs={{0,6},{1,7},{2,4},{3,5},{4,2},{5,3},{6,0},{7,1},{8,14},{9,15},{10,... | collective-permute-start | bytes 393224 | tf_op jit(solution)/shard_map/ppermute | solution.py:32
  98.6 13.7 %collective-permute-start.29 = (f32[256,256]{1,0:T(8,128)S(1)}, f32[256,256]{1,0:T(8,128)S(1)}, u32[]{:S(2)}, u32[]{:S(2)}) collective-permute-start(f32[256,256]{1,0:T(8,128)S(1)} %get-tuple-element.169.a0.b0), channel_id=1, source_target_pairs={{0,65},{1,64},{2,67},{3,66},{4,69},{5,68},{6,71},{7,70},{8,73},{9,... | collective-permute-start | bytes 786440 | tf_op jit(solution)/shard_map/ppermute | solution.py:32
  100.5 11.8 %collective-permute-start.28 = (f32[256,256]{1,0:T(8,128)S(1)}, f32[256,256]{1,0:T(8,128)S(1)}, u32[]{:S(2)}, u32[]{:S(2)}) collective-permute-start(f32[256,256]{1,0:T(8,128)S(1)} %get-tuple-element.169.a0.b0), channel_id=1, source_target_pairs={{0,64},{1,65},{2,66},{3,67},{4,68},{5,69},{6,70},{7,71},{8,72},{9,... | collective-permute-start | bytes 786440 | tf_op jit(solution)/shard_map/ppermute | solution.py:32
  101.4 11.6 %collective-permute-start.27 = (f32[256,256]{1,0:T(8,128)S(1)}, f32[256,256]{1,0:T(8,128)S(1)}, u32[]{:S(2)}, u32[]{:S(2)}) collective-permute-start(f32[256,256]{1,0:T(8,128)S(1)} %get-tuple-element.169.a0.b0), channel_id=1, source_target_pairs={{0,1},{1,0},{2,3},{3,2},{4,5},{5,4},{6,7},{7,6},{8,9},{9,8},{10,11... | collective-permute-start | bytes 786440 | tf_op jit(solution)/shard_map/ppermute | solution.py:32
  102.7 6.5 %collective-permute-start.31 = (f32[128,256]{1,0:T(8,128)S(1)}, f32[128,256]{1,0:T(8,128)S(1)}, u32[]{:S(2)}, u32[]{:S(2)}) collective-permute-start(f32[128,256]{1,0:T(8,128)S(1)} %add_add_fusion.6.x3), channel_id=1, source_target_pairs={{0,4},{1,5},{2,6},{3,7},{4,0},{5,1},{6,2},{7,3},{8,12},{9,13},{10,... | collective-permute-start | bytes 393224 | tf_op jit(solution)/shard_map/ppermute | solution.py:32
  116.7 9.4 %collective-permute-start.38 = (f32[128,256]{1,0:T(8,128)S(1)}, f32[128,256]{1,0:T(8,128)S(1)}, u32[]{:S(2)}, u32[]{:S(2)}) collective-permute-start(f32[128,256]{1,0:T(8,128)S(1)} %get-tuple-element.161), channel_id=1, source_target_pairs={{0,16},{1,17},{2,18},{3,19},{4,20},{5,21},{6,22},{7,23},{8,24},{9,... | collective-permute-start | bytes 393224 | tf_op jit(solution)/shard_map/ppermute | solution.py:32
  116.8 9.8 %collective-permute-start.39 = (f32[128,256]{1,0:T(8,128)S(1)}, f32[128,256]{1,0:T(8,128)S(1)}, u32[]{:S(2)}, u32[]{:S(2)}) collective-permute-start(f32[128,256]{1,0:T(8,128)S(1)} %get-tuple-element.162), channel_id=1, source_target_pairs={{0,24},{1,25},{2,26},{3,27},{4,28},{5,29},{6,30},{7,31},{8,16},{9,... | collective-permute-start | bytes 393224 | tf_op jit(solution)/shard_map/ppermute | solution.py:32
  122.0 14.4 %collective-permute-start.35 = (f32[256,256]{1,0:T(8,128)S(1)}, f32[256,256]{1,0:T(8,128)S(1)}, u32[]{:S(2)}, u32[]{:S(2)}) collective-permute-start(f32[256,256]{1,0:T(8,128)S(1)} %shard_map.65.b0), channel_id=1, source_target_pairs={{0,6},{1,7},{2,4},{3,5},{4,2},{5,3},{6,0},{7,1},{8,14},{9,15},{10,... | collective-permute-start | bytes 786440 | tf_op jit(solution)/shard_map/ppermute | solution.py:32
  122.7 13.7 %collective-permute-start.34 = (f32[256,256]{1,0:T(8,128)S(1)}, f32[256,256]{1,0:T(8,128)S(1)}, u32[]{:S(2)}, u32[]{:S(2)}) collective-permute-start(f32[256,256]{1,0:T(8,128)S(1)} %shard_map.65.b0), channel_id=1, source_target_pairs={{0,4},{1,5},{2,6},{3,7},{4,0},{5,1},{6,2},{7,3},{8,12},{9,13},{10,... | collective-permute-start | bytes 786440 | tf_op jit(solution)/shard_map/ppermute | solution.py:32
  123.1 14.0 %collective-permute-start.33 = (f32[256,256]{1,0:T(8,128)S(1)}, f32[256,256]{1,0:T(8,128)S(1)}, u32[]{:S(2)}, u32[]{:S(2)}) collective-permute-start(f32[256,256]{1,0:T(8,128)S(1)} %shard_map.65.b0), channel_id=1, source_target_pairs={{0,2},{1,3},{2,0},{3,1},{4,6},{5,7},{6,4},{7,5},{8,10},{9,11},{10,... | collective-permute-start | bytes 786440 | tf_op jit(solution)/shard_map/ppermute | solution.py:32
  126.7 10.3 %collective-permute-start.40 = (f32[128,256]{1,0:T(8,128)S(1)}, f32[128,256]{1,0:T(8,128)S(1)}, u32[]{:S(2)}, u32[]{:S(2)}) collective-permute-start(f32[128,256]{1,0:T(8,128)S(1)} %add_add_fusion.5.y0.y2), channel_id=1, source_target_pairs={{0,16},{1,17},{2,18},{3,19},{4,20},{5,21},{6,22},{7,23},{8,24},{9,... | collective-permute-start | bytes 393224 | tf_op jit(solution)/shard_map/ppermute | solution.py:32
  137.1 7.2 %collective-permute-start.41 = (f32[4,256,256]{2,1,0:T(8,128)S(1)}, f32[4,256,256]{2,1,0:T(8,128)S(1)}, u32[]{:S(2)}, u32[]{:S(2)}) collective-permute-start(f32[4,256,256]{2,1,0:T(8,128)S(1)} %pad_maximum_fusion), channel_id=1, source_target_pairs={{0,32},{1,33},{2,34},{3,35},{4,36},{5,37},{6,38},{7,39},{8,40},{9,... | collective-permute-start | bytes 3145736 | tf_op jit(solution)/shard_map/ppermute | solution.py:32
  137.2 7.1 %collective-permute-start.43 = (f32[128,256]{1,0:T(8,128)S(1)}, f32[128,256]{1,0:T(8,128)S(1)}, u32[]{:S(2)}, u32[]{:S(2)}) collective-permute-start(f32[128,256]{1,0:T(8,128)S(1)} %add_add_fusion.5.y0.y2), channel_id=1, source_target_pairs={{0,24},{1,25},{2,26},{3,27},{4,28},{5,29},{6,30},{7,31},{8,16},{9,... | collective-permute-start | bytes 393224 | tf_op jit(solution)/shard_map/ppermute | solution.py:32
  137.6 6.8 %collective-permute-start.42 = (f32[128,256]{1,0:T(8,128)S(1)}, f32[128,256]{1,0:T(8,128)S(1)}, u32[]{:S(2)}, u32[]{:S(2)}) collective-permute-start(f32[128,256]{1,0:T(8,128)S(1)} %add_add_fusion.5.y0.y2), channel_id=1, source_target_pairs={{0,8},{1,9},{2,10},{3,11},{4,12},{5,13},{6,14},{7,15},{8,0},{9,1},... | collective-permute-start | bytes 393224 | tf_op jit(solution)/shard_map/ppermute | solution.py:32
  145.8 6.5 %collective-permute-start.45 = (f32[128,256]{1,0:T(8,128)S(1)}, f32[128,256]{1,0:T(8,128)S(1)}, u32[]{:S(2)}, u32[]{:S(2)}) collective-permute-start(f32[128,256]{1,0:T(8,128)S(1)} %get-tuple-element.174), channel_id=1, source_target_pairs={{0,1},{1,0},{2,3},{3,2},{4,5},{5,4},{6,7},{7,6},{8,9},{9,8},{10,11... | collective-permute-start | bytes 393224 | tf_op jit(solution)/shard_map/ppermute | solution.py:32
  146.6 8.6 %collective-permute-start.46 = (f32[128,256]{1,0:T(8,128)S(1)}, f32[128,256]{1,0:T(8,128)S(1)}, u32[]{:S(2)}, u32[]{:S(2)}) collective-permute-start(f32[128,256]{1,0:T(8,128)S(1)} %get-tuple-element.175), channel_id=1, source_target_pairs={{0,64},{1,65},{2,66},{3,67},{4,68},{5,69},{6,70},{7,71},{8,72},{9,... | collective-permute-start | bytes 393224 | tf_op jit(solution)/shard_map/ppermute | solution.py:32
  149.2 7.9 %collective-permute-start.47 = (f32[128,256]{1,0:T(8,128)S(1)}, f32[128,256]{1,0:T(8,128)S(1)}, u32[]{:S(2)}, u32[]{:S(2)}) collective-permute-start(f32[128,256]{1,0:T(8,128)S(1)} %get-tuple-element.176), channel_id=1, source_target_pairs={{0,65},{1,64},{2,67},{3,66},{4,69},{5,68},{6,71},{7,70},{8,73},{9,... | collective-permute-start | bytes 393224 | tf_op jit(solution)/shard_map/ppermute | solution.py:32
  157.1 8.4 %collective-permute-start.50 = (f32[128,256]{1,0:T(8,128)S(1)}, f32[128,256]{1,0:T(8,128)S(1)}, u32[]{:S(2)}, u32[]{:S(2)}) collective-permute-start(f32[128,256]{1,0:T(8,128)S(1)} %add_add_fusion.4.x2), channel_id=1, source_target_pairs={{0,65},{1,64},{2,67},{3,66},{4,69},{5,68},{6,71},{7,70},{8,73},{9,... | collective-permute-start | bytes 393224 | tf_op jit(solution)/shard_map/ppermute | solution.py:32
  158.5 7.3 %collective-permute-start.49 = (f32[128,256]{1,0:T(8,128)S(1)}, f32[128,256]{1,0:T(8,128)S(1)}, u32[]{:S(2)}, u32[]{:S(2)}) collective-permute-start(f32[128,256]{1,0:T(8,128)S(1)} %add_add_fusion.4.x2), channel_id=1, source_target_pairs={{0,64},{1,65},{2,66},{3,67},{4,68},{5,69},{6,70},{7,71},{8,72},{9,... | collective-permute-start | bytes 393224 | tf_op jit(solution)/shard_map/ppermute | solution.py:32
  159.0 7.5 %collective-permute-start.48 = (f32[128,256]{1,0:T(8,128)S(1)}, f32[128,256]{1,0:T(8,128)S(1)}, u32[]{:S(2)}, u32[]{:S(2)}) collective-permute-start(f32[128,256]{1,0:T(8,128)S(1)} %add_add_fusion.4.x2), channel_id=1, source_target_pairs={{0,1},{1,0},{2,3},{3,2},{4,5},{5,4},{6,7},{7,6},{8,9},{9,8},{10,11... | collective-permute-start | bytes 393224 | tf_op jit(solution)/shard_map/ppermute | solution.py:32
  167.2 18.0 %collective-permute-start.44 = (f32[4,192,256]{2,1,0:T(8,128)S(1)}, f32[4,192,256]{2,1,0:T(8,128)S(1)}, u32[]{:S(2)}, u32[]{:S(2)}) collective-permute-start(f32[4,192,256]{2,1,0:T(8,128)S(1)} %get-tuple-element.173), channel_id=1, source_target_pairs={{0,32},{1,33},{2,34},{3,35},{4,36},{5,37},{6,38},{7,39},{8,40},{9,... | collective-permute-start | bytes 2359304 | tf_op jit(solution)/shard_map/ppermute | solution.py:32
  169.8 8.9 %collective-permute-start.53 = (f32[128,256]{1,0:T(8,128)S(1)}, f32[128,256]{1,0:T(8,128)S(1)}, u32[]{:S(2)}, u32[]{:S(2)}) collective-permute-start(f32[128,256]{1,0:T(8,128)S(1)} %get-tuple-element.179), channel_id=1, source_target_pairs={{0,16},{1,17},{2,18},{3,19},{4,20},{5,21},{6,22},{7,23},{8,24},{9,... | collective-permute-start | bytes 393224 | tf_op jit(solution)/shard_map/ppermute | solution.py:32
  172.3 8.7 %collective-permute-start.54 = (f32[128,256]{1,0:T(8,128)S(1)}, f32[128,256]{1,0:T(8,128)S(1)}, u32[]{:S(2)}, u32[]{:S(2)}) collective-permute-start(f32[128,256]{1,0:T(8,128)S(1)} %get-tuple-element.180), channel_id=1, source_target_pairs={{0,24},{1,25},{2,26},{3,27},{4,28},{5,29},{6,30},{7,31},{8,16},{9,... | collective-permute-start | bytes 393224 | tf_op jit(solution)/shard_map/ppermute | solution.py:32
  181.0 7.9 %collective-permute-start.57 = (f32[128,256]{1,0:T(8,128)S(1)}, f32[128,256]{1,0:T(8,128)S(1)}, u32[]{:S(2)}, u32[]{:S(2)}) collective-permute-start(f32[128,256]{1,0:T(8,128)S(1)} %add_add_fusion.3.y0.y1), channel_id=1, source_target_pairs={{0,24},{1,25},{2,26},{3,27},{4,28},{5,29},{6,30},{7,31},{8,16},{9,... | collective-permute-start | bytes 393224 | tf_op jit(solution)/shard_map/ppermute | solution.py:32
  183.2 7.6 %collective-permute-start.56 = (f32[128,256]{1,0:T(8,128)S(1)}, f32[128,256]{1,0:T(8,128)S(1)}, u32[]{:S(2)}, u32[]{:S(2)}) collective-permute-start(f32[128,256]{1,0:T(8,128)S(1)} %add_add_fusion.3.y0.y1), channel_id=1, source_target_pairs={{0,16},{1,17},{2,18},{3,19},{4,20},{5,21},{6,22},{7,23},{8,24},{9,... | collective-permute-start | bytes 393224 | tf_op jit(solution)/shard_map/ppermute | solution.py:32
  183.3 7.6 %collective-permute-start.55 = (f32[128,256]{1,0:T(8,128)S(1)}, f32[128,256]{1,0:T(8,128)S(1)}, u32[]{:S(2)}, u32[]{:S(2)}) collective-permute-start(f32[128,256]{1,0:T(8,128)S(1)} %add_add_fusion.3.y0.y1), channel_id=1, source_target_pairs={{0,8},{1,9},{2,10},{3,11},{4,12},{5,13},{6,14},{7,15},{8,0},{9,1},... | collective-permute-start | bytes 393224 | tf_op jit(solution)/shard_map/ppermute | solution.py:32
  192.2 6.7 %collective-permute-start.59 = (f32[128,256]{1,0:T(8,128)S(1)}, f32[128,256]{1,0:T(8,128)S(1)}, u32[]{:S(2)}, u32[]{:S(2)}) collective-permute-start(f32[128,256]{1,0:T(8,128)S(1)} %get-tuple-element.183), channel_id=1, source_target_pairs={{0,4},{1,5},{2,6},{3,7},{4,0},{5,1},{6,2},{7,3},{8,12},{9,13},{10,... | collective-permute-start | bytes 393224 | tf_op jit(solution)/shard_map/ppermute | solution.py:32
  203.2 6.5 %collective-permute-start.65 = (f32[128,256]{1,0:T(8,128)S(1)}, f32[128,256]{1,0:T(8,128)S(1)}, u32[]{:S(2)}, u32[]{:S(2)}) collective-permute-start(f32[128,256]{1,0:T(8,128)S(1)} %add_add_fusion.2.x1), channel_id=1, source_target_pairs={{0,4},{1,5},{2,6},{3,7},{4,0},{5,1},{6,2},{7,3},{8,12},{9,13},{10,... | collective-permute-start | bytes 393224 | tf_op jit(solution)/shard_map/ppermute | solution.py:32
  213.0 8.4 %collective-permute-start.68 = (f32[128,256]{1,0:T(8,128)S(1)}, f32[128,256]{1,0:T(8,128)S(1)}, u32[]{:S(2)}, u32[]{:S(2)}) collective-permute-start(f32[128,256]{1,0:T(8,128)S(1)} %get-tuple-element.192), channel_id=1, source_target_pairs={{0,8},{1,9},{2,10},{3,11},{4,12},{5,13},{6,14},{7,15},{8,0},{9,1},... | collective-permute-start | bytes 393224 | tf_op jit(solution)/shard_map/ppermute | solution.py:32
  213.4 9.9 %collective-permute-start.69 = (f32[128,256]{1,0:T(8,128)S(1)}, f32[128,256]{1,0:T(8,128)S(1)}, u32[]{:S(2)}, u32[]{:S(2)}) collective-permute-start(f32[128,256]{1,0:T(8,128)S(1)} %get-tuple-element.193), channel_id=1, source_target_pairs={{0,16},{1,17},{2,18},{3,19},{4,20},{5,21},{6,22},{7,23},{8,24},{9,... | collective-permute-start | bytes 393224 | tf_op jit(solution)/shard_map/ppermute | solution.py:32
  216.5 8.7 %collective-permute-start.70 = (f32[128,256]{1,0:T(8,128)S(1)}, f32[128,256]{1,0:T(8,128)S(1)}, u32[]{:S(2)}, u32[]{:S(2)}) collective-permute-start(f32[128,256]{1,0:T(8,128)S(1)} %get-tuple-element.194), channel_id=1, source_target_pairs={{0,24},{1,25},{2,26},{3,27},{4,28},{5,29},{6,30},{7,31},{8,16},{9,... | collective-permute-start | bytes 393224 | tf_op jit(solution)/shard_map/ppermute | solution.py:32
  218.5 9.3 %collective-permute-start.61 = (f32[2,2,64,256]{3,2,1,0:T(8,128)S(1)}, f32[2,2,64,256]{3,2,1,0:T(8,128)S(1)}, u32[]{:S(2)}, u32[]{:S(2)}) collective-permute-start(f32[2,2,64,256]{3,2,1,0:T(8,128)S(1)} %get-tuple-element.188), channel_id=1, source_target_pairs={{0,1},{1,0},{2,3},{3,2},{4,5},{5,4},{6,7},{7,6},{8,9},{9,8},{10,11... | collective-permute-start | bytes 786440 | tf_op jit(solution)/shard_map/ppermute | solution.py:32
  218.8 13.7 %collective-permute-start.62 = (f32[2,2,64,256]{3,2,1,0:T(8,128)S(1)}, f32[2,2,64,256]{3,2,1,0:T(8,128)S(1)}, u32[]{:S(2)}, u32[]{:S(2)}) collective-permute-start(f32[2,2,64,256]{3,2,1,0:T(8,128)S(1)} %get-tuple-element.189), channel_id=1, source_target_pairs={{0,64},{1,65},{2,66},{3,67},{4,68},{5,69},{6,70},{7,71},{8,72},{9,... | collective-permute-start | bytes 786440 | tf_op jit(solution)/shard_map/ppermute | solution.py:32
  221.3 13.8 %collective-permute-start.63 = (f32[2,2,64,256]{3,2,1,0:T(8,128)S(1)}, f32[2,2,64,256]{3,2,1,0:T(8,128)S(1)}, u32[]{:S(2)}, u32[]{:S(2)}) collective-permute-start(f32[2,2,64,256]{3,2,1,0:T(8,128)S(1)} %get-tuple-element.190), channel_id=1, source_target_pairs={{0,65},{1,64},{2,67},{3,66},{4,69},{5,68},{6,71},{7,70},{8,73},{9,... | collective-permute-start | bytes 786440 | tf_op jit(solution)/shard_map/ppermute | solution.py:32
  225.2 9.9 %collective-permute-start.73 = (f32[128,256]{1,0:T(8,128)S(1)}, f32[128,256]{1,0:T(8,128)S(1)}, u32[]{:S(2)}, u32[]{:S(2)}) collective-permute-start(f32[128,256]{1,0:T(8,128)S(1)} %add_add_fusion.1.y0), channel_id=1, source_target_pairs={{0,24},{1,25},{2,26},{3,27},{4,28},{5,29},{6,30},{7,31},{8,16},{9,... | collective-permute-start | bytes 393224 | tf_op jit(solution)/shard_map/ppermute | solution.py:32
  226.5 8.6 %collective-permute-start.72 = (f32[128,256]{1,0:T(8,128)S(1)}, f32[128,256]{1,0:T(8,128)S(1)}, u32[]{:S(2)}, u32[]{:S(2)}) collective-permute-start(f32[128,256]{1,0:T(8,128)S(1)} %add_add_fusion.1.y0), channel_id=1, source_target_pairs={{0,16},{1,17},{2,18},{3,19},{4,20},{5,21},{6,22},{7,23},{8,24},{9,... | collective-permute-start | bytes 393224 | tf_op jit(solution)/shard_map/ppermute | solution.py:32
  227.8 7.3 %collective-permute-start.71 = (f32[128,256]{1,0:T(8,128)S(1)}, f32[128,256]{1,0:T(8,128)S(1)}, u32[]{:S(2)}, u32[]{:S(2)}) collective-permute-start(f32[128,256]{1,0:T(8,128)S(1)} %add_add_fusion.1.y0), channel_id=1, source_target_pairs={{0,8},{1,9},{2,10},{3,11},{4,12},{5,13},{6,14},{7,15},{8,0},{9,1},... | collective-permute-start | bytes 393224 | tf_op jit(solution)/shard_map/ppermute | solution.py:32
  236.6 7.9 %collective-permute-start.75 = (f32[128,256]{1,0:T(8,128)S(1)}, f32[128,256]{1,0:T(8,128)S(1)}, u32[]{:S(2)}, u32[]{:S(2)}) collective-permute-start(f32[128,256]{1,0:T(8,128)S(1)} %get-tuple-element.201), channel_id=1, source_target_pairs={{0,64},{1,65},{2,66},{3,67},{4,68},{5,69},{6,70},{7,71},{8,72},{9,... | collective-permute-start | bytes 393224 | tf_op jit(solution)/shard_map/ppermute | solution.py:32
  246.8 7.9 %collective-permute-start.77 = (f32[2,64,256]{2,1,0:T(8,128)S(1)}, f32[2,64,256]{2,1,0:T(8,128)S(1)}, u32[]{:S(2)}, u32[]{:S(2)}) collective-permute-start(f32[2,64,256]{2,1,0:T(8,128)S(1)} %get-tuple-element.206), channel_id=1, source_target_pairs={{0,1},{1,0},{2,3},{3,2},{4,5},{5,4},{6,7},{7,6},{8,9},{9,8},{10,11... | collective-permute-start | bytes 393224 | tf_op jit(solution)/shard_map/ppermute | solution.py:32
  247.5 8.4 %collective-permute-start.78 = (f32[2,64,256]{2,1,0:T(8,128)S(1)}, f32[2,64,256]{2,1,0:T(8,128)S(1)}, u32[]{:S(2)}, u32[]{:S(2)}) collective-permute-start(f32[2,64,256]{2,1,0:T(8,128)S(1)} %get-tuple-element.207), channel_id=1, source_target_pairs={{64,0},{65,1},{66,2},{67,3},{68,4},{69,5},{70,6},{71,7},{72,8},{73... | collective-permute-start | bytes 393224 | tf_op jit(solution)/shard_map/ppermute | solution.py:32
  258.7 7.4 %collective-permute-start.81 = (f32[2,64,256]{2,1,0:T(8,128)S(1)}, f32[2,64,256]{2,1,0:T(8,128)S(1)}, u32[]{:S(2)}, u32[]{:S(2)}) collective-permute-start(f32[2,64,256]{2,1,0:T(8,128)S(1)} %get-tuple-element.211), channel_id=1, source_target_pairs={{0,4},{1,5},{2,6},{3,7},{4,0},{5,1},{6,2},{7,3},{8,12},{9,13},{10,... | collective-permute-start | bytes 393224 | tf_op jit(solution)/shard_map/ppermute | solution.py:32
  (22 other events, 97.9 us)
